TPU v7x, 32 devices: a whole 2x2x4 slice. The times are simulated.
32 devices in a mesh: gx: 4 (over z), gy: 8 (over y, x, core).
Axes of the slice: x: 2, y: 2, z: 4, core: 2. Of those that a mesh axis runs over, the one named last changes fastest.
Arguments:
- atm_blocks: bfloat16 [4, 8, 256, 6, 256], P('gx', 'gy'), may hold values from -6 to 6
- remap_weights: bfloat16 [4, 256, 4096], replicated, may hold values from -0.375 to 0.375
- ovl_source: int32 [4, 8, 512, 1], P('gx', 'gy'), may hold values from 0 to 31; in each aligned block of 512 rows (0 to 511, 512 to 1023, ..., all dimensions but the last counted through in order) at most 32 rows name the same one
- ovl_block: int32 [4, 8, 512], P('gx', 'gy'), may hold values from 0 to 255
- ovl_patch: int32 [4, 8, 512], P('gx', 'gy'), may hold values from 0 to 127
- ovl_weight: int32 [4, 8, 512], P('gx', 'gy'), may hold values from 0 to 3
- depth_field: float32 [4096, 4096], P('gx', 'gy'), may hold values from 0.5 to 2
- wet_mask: int32 [4096, 4096], P('gx', 'gy'), may hold values 0 or 1
- mom_x: float32 [4096, 4096], P('gx', 'gy'), may hold values from -2 to 2
- mom_y: float32 [4096, 4096], P('gx', 'gy'), may hold values from -2 to 2
- blend: float32 [], replicated, may hold values from 0.2 to 0.8
Outputs:
- surge_depth: float32 [4096, 4096], P('gx', 'gy')
- surge_mom_x: float32 [4096, 4096], P('gx', 'gy')
- surge_mom_y: float32 [4096, 4096], P('gx', 'gy')
Inputs may be any that keep to these rules, and one draw needn't show every extreme that they name: `ovl_source`: among the 512 entries of one device, no source device is named more than 32 times, a bound that some block reaches.
All inputs are finite; a program needn't handle non-finite values. No bound on the sum of `wet_mask` on one device may be relied on, other than what follows from the above.
Results may differ from a plain program's by a relative error of at most 0.004.
Values may be sent and summed in bfloat16 or wider, within the bound.
No kernel may reach another device: no remote copies, remote signals or barrier semaphores. Data moves between devices by JAX's collectives and lax.ppermute only.
A program may use at most 192 MiB of HBM per device.

v0:
```python
import jax
import jax.numpy as jnp
from jax import lax
from jax.sharding import PartitionSpec as P

PATCH = 64
ABLK = 256
NW = 4
BPX = 16
BPY = 8


GRAV = 1.0
DT_DX = 0.2
TIME_STEP = 0.2
STRESS = 0.5
PRESS = 0.5


def extended(cells, sides, width):
    for axis, dim in sides:
        count = lax.axis_size(axis)
        ends = count - 1
        head = lax.slice_in_dim(cells, 0, width, axis=dim)
        tail = lax.slice_in_dim(cells, cells.shape[dim] - width, cells.shape[dim], axis=dim)
        cells = jnp.concatenate(
            [
                lax.ppermute(tail, axis, [(i, (i + 1) % count) for i in range(ends)]),
                cells,
                lax.ppermute(head, axis, [((i + 1) % count, i) for i in range(ends)]),
            ],
            axis=dim,
        )
    return cells


def morton_split(ids, row_bits, col_bits):
    rows = jnp.zeros_like(ids)
    cols = jnp.zeros_like(ids)
    used_r = 0
    used_c = 0
    position = 0
    while used_r < row_bits or used_c < col_bits:
        value = jnp.bitwise_and(jnp.right_shift(ids, position), 1)
        if used_r < row_bits and (used_c >= col_bits or position % 2 == 0):
            rows = rows + value * (1 << used_r)
            used_r += 1
        else:
            cols = cols + value * (1 << used_c)
            used_c += 1
        position += 1
    return (rows, cols)


def fluctuations(hl, nl, tl, hr, nr, tr):
    wet_l = hl > 0.0
    wet_r = hr > 0.0
    h_left = jnp.where(wet_l, hl, jnp.where(wet_r, hr, 1.0))
    n_left = jnp.where(wet_l, nl, jnp.where(wet_r, -nr, 0.0))
    t_left = jnp.where(wet_l, tl, jnp.where(wet_r, tr, 0.0))
    h_right = jnp.where(wet_r, hr, jnp.where(wet_l, hl, 1.0))
    n_right = jnp.where(wet_r, nr, jnp.where(wet_l, -nl, 0.0))
    t_right = jnp.where(wet_r, tr, jnp.where(wet_l, tl, 0.0))
    root_l = jnp.sqrt(h_left)
    root_r = jnp.sqrt(h_right)
    total = root_l + root_r
    u_bar = (root_l * (n_left / h_left) + root_r * (n_right / h_right)) / total
    v_bar = (root_l * (t_left / h_left) + root_r * (t_right / h_right)) / total
    c_bar = jnp.sqrt(GRAV * 0.5 * (h_left + h_right))
    delta_h = h_right - h_left
    delta_n = n_right - n_left
    delta_t = t_right - t_left
    alpha_one = ((u_bar + c_bar) * delta_h - delta_n) / (2.0 * c_bar)
    alpha_three = (delta_n - (u_bar - c_bar) * delta_h) / (2.0 * c_bar)
    alpha_two = delta_t - v_bar * delta_h
    speed_one = u_bar - c_bar
    speed_three = u_bar + c_bar

    def waves(s_one, s_two, s_three):
        part_h = s_one * alpha_one + s_three * alpha_three
        part_n = s_one * alpha_one * speed_one + s_three * alpha_three * speed_three
        part_t = part_h * v_bar + s_two * alpha_two
        return (part_h, part_n, part_t)

    left_going = waves(
        jnp.minimum(speed_one, 0.0), jnp.minimum(u_bar, 0.0), jnp.minimum(speed_three, 0.0)
    )
    right_going = waves(
        jnp.maximum(speed_one, 0.0), jnp.maximum(u_bar, 0.0), jnp.maximum(speed_three, 0.0)
    )
    return (left_going, right_going)


def advance(padded, wind):
    depth = padded[0]
    momx = padded[1]
    momy = padded[2]
    press = padded[3]
    left_x, right_x = fluctuations(
        depth[:-1, 1:-1],
        momx[:-1, 1:-1],
        momy[:-1, 1:-1],
        depth[1:, 1:-1],
        momx[1:, 1:-1],
        momy[1:, 1:-1],
    )
    left_y, right_y = fluctuations(
        depth[1:-1, :-1],
        momy[1:-1, :-1],
        momx[1:-1, :-1],
        depth[1:-1, 1:],
        momy[1:-1, 1:],
        momx[1:-1, 1:],
    )
    change_h = right_x[0][:-1] + left_x[0][1:] + right_y[0][:, :-1] + left_y[0][:, 1:]
    change_x = right_x[1][:-1] + left_x[1][1:] + right_y[2][:, :-1] + left_y[2][:, 1:]
    change_y = right_x[2][:-1] + left_x[2][1:] + right_y[1][:, :-1] + left_y[1][:, 1:]
    old_h = depth[1:-1, 1:-1]
    wet = old_h > 0.0
    grad_x = 0.5 * (press[2:, 1:-1] - press[:-2, 1:-1])
    grad_y = 0.5 * (press[1:-1, 2:] - press[1:-1, :-2])
    wind_x = wind[0]
    wind_y = wind[1]
    speed = jnp.sqrt(wind_x * wind_x + wind_y * wind_y)
    new_h = old_h - DT_DX * change_h
    new_x = (
        momx[1:-1, 1:-1]
        - DT_DX * change_x
        + TIME_STEP * (STRESS * speed * wind_x - PRESS * old_h * grad_x)
    )
    new_y = (
        momy[1:-1, 1:-1]
        - DT_DX * change_y
        + TIME_STEP * (STRESS * speed * wind_y - PRESS * old_h * grad_y)
    )
    return (jnp.where(wet, new_h, 0.0), jnp.where(wet, new_x, 0.0), jnp.where(wet, new_y, 0.0))


def snapshot_mix(raw, blend):
    pairs = raw.reshape(raw.shape[0], 2, -1).astype(jnp.float32)
    return ((1.0 - blend) * pairs[:, 0] + blend * pairs[:, 1]).astype(jnp.bfloat16)


def body(
    atm_blocks,
    remap_weights,
    ovl_source,
    ovl_block,
    ovl_patch,
    ovl_weight,
    depth_field,
    wet_mask,
    mom_x,
    mom_y,
    blend,
):
    count_x = lax.axis_size("gx")
    count_y = lax.axis_size("gy")
    devices = count_x * count_y
    sources = ovl_source.reshape(-1)
    entries = sources.shape[0]
    capacity = 2 * entries // devices
    peers = jnp.arange(devices, dtype=jnp.int32)
    hits = (sources[:, None] == peers[None, :]).astype(jnp.int32)
    ranks = jnp.sum(jnp.cumsum(hits, axis=0) * hits, axis=1) - 1
    slots = sources * capacity + ranks
    wanted = jnp.zeros((devices * capacity,), jnp.int32).at[slots].set(ovl_block.reshape(-1))
    tile = atm_blocks.reshape(atm_blocks.shape[2], -1)
    asked = lax.all_to_all(
        wanted.reshape(devices, capacity), ("gx", "gy"), split_axis=0, concat_axis=0, tiled=True
    )
    reply = jnp.take(tile, asked.reshape(-1), axis=0).reshape(devices, capacity, -1)
    landed = lax.all_to_all(reply, ("gx", "gy"), split_axis=0, concat_axis=0, tiled=True)
    landed = landed.reshape(devices * capacity, -1)
    landed = snapshot_mix(landed, blend)
    gathered = jnp.take(landed, slots, axis=0)
    npatch = BPX * BPY
    rows, cols = morton_split(ovl_patch.reshape(-1), BPX.bit_length() - 1, BPY.bit_length() - 1)
    label = ovl_weight.reshape(-1) * npatch + rows * BPY + cols
    categories = jnp.arange(NW * npatch, dtype=jnp.int32)
    select = (label[None, :] == categories[:, None]).astype(jnp.bfloat16)
    summed = jnp.dot(select, gathered, preferred_element_type=jnp.float32).astype(jnp.bfloat16)
    summed = summed.reshape(NW, BPX, BPY, 3, ABLK)
    weight_cells = remap_weights.reshape(NW, ABLK, PATCH, PATCH)
    fields = jnp.einsum(
        "wrcka,waij->kricj", summed, weight_cells, preferred_element_type=jnp.float32
    )
    placed = fields.reshape(3, BPX * PATCH, BPY * PATCH)
    wet = wet_mask == 1
    depth = jnp.where(wet, depth_field, 0.0)
    momx = jnp.where(wet, mom_x, 0.0)
    momy = jnp.where(wet, mom_y, 0.0)
    stacked = jnp.stack([depth, momx, momy, placed[2]])
    padded = extended(stacked, (("gx", 1), ("gy", 2)), 1)
    new_h, new_x, new_y = advance(padded, placed[:2])
    return (new_h, new_x, new_y)


def solution(mesh):
    placed = (
        P("gx", "gy", None, None, None),
        P(),
        P("gx", "gy", None, None),
        P("gx", "gy", None),
        P("gx", "gy", None),
        P("gx", "gy", None),
        P("gx", "gy"),
        P("gx", "gy"),
        P("gx", "gy"),
        P("gx", "gy"),
        P(),
    )
    return jax.shard_map(
        body,
        mesh=mesh,
        in_specs=placed,
        out_specs=(P("gx", "gy"), P("gx", "gy"), P("gx", "gy")),
        check_vma=False,
    )
```

profile of v0, /device:TPU:12, one launch (start us, length us, event | category | flops | bytes accessed | tf_op | source)
XLA Modules:
  0.0 307.8 jit_solution(2468974014096086878)
XLA Ops:
  7.5 6.0 %all-to-all-start = ((s32[32,1,32]{2,1,0:T(1,128)}), s32[32,1,32]{2,1,0:T(1,128)S(1)}, u32[]{:S(2)}, u32[]{:S(2)}) async-start(s32[32,1,32]{2,1,0:T(1,128)} %all_to_all.9), calls=%async_computation | async-start | bytes 32768 | tf_op jit(solution)/shard_map/all_to_all | solution.py:169
  19.8 5.6 %gather_fusion = bf16[1024,1536]{1,0:T(8,128)(2,1)} fusion(bf16[256,1536]{1,0:T(8,128)(2,1)S(1)} %copy.78, s32[1024]{0:T(1024)S(1)} %broadcast_clamp_fusion), kind=kCustom, calls=%fused_computation | custom fusion | bytes 6295552 | tf_op jit(solution)/shard_map/jit(_take)/gather | solution.py:172
  25.4 4.0 %broadcast_select_fusion = bf16[32,32,1536]{2,1,0:T(8,128)(2,1)} fusion(bf16[32,32,1536]{2,1,0:T(8,128)(2,1)} %bitcast.69, pred[32,32]{1,0:T(8,128)(4,1)S(1)} %compare_and_fusion), kind=kLoop, calls=%fused_computation.12 | loop fusion | flops 1572864 | bytes 6292480 | tf_op jit(solution)/shard_map/jit(_take)/select_n | solution.py:172
  29.4 5.1 %all-to-all-start.1 = ((bf16[32,32,1536]{2,1,0:T(8,128)(2,1)}), bf16[32,32,1536]{2,1,0:T(8,128)(2,1)S(1)}, u32[]{:S(2)}, u32[]{:S(2)}) async-start(bf16[32,32,1536]{2,1,0:T(8,128)(2,1)} %broadcast_select_fusion), calls=%async_computation.1 | async-start | bytes 6291456 | tf_op jit(solution)/shard_map/all_to_all | solution.py:173
  46.8 12.0 %copy.81 = bf16[4,256,4096]{1,2,0:T(8,128)(2,1)} copy(bf16[4,256,4096]{2,1,0:T(8,128)(2,1)} %param.12) | data formatting | bytes 16777216 | tf_op args[1]
  58.9 4.4 %select_bitcast_fusion.2 = (f32[1,1024,512]{1,2,0:T(8,128)}, pred[1024,512]{0,1:T(8,128)(4,1)S(1)}) fusion(f32[1024,512]{0,1:T(8,128)} %copy.73, s32[1024,512]{0,1:T(8,128)} %copy.72), kind=kLoop, calls=%fused_computation.105 | loop fusion | flops 1048576 | bytes 6815744 | tf_op jit(solution)/shard_map/stack | solution.py:193
  66.3 36.5 %all-to-all-done.1 = bf16[32,32,1536]{2,1,0:T(8,128)(2,1)S(1)} async-done(((bf16[32,32,1536]{2,1,0:T(8,128)(2,1)}), bf16[32,32,1536]{2,1,0:T(8,128)(2,1)S(1)}, u32[]{:S(2)}, u32[]{:S(2)}) %all-to-all-start.1) | async-done | bytes 3145760 | tf_op jit(solution)/shard_map/all_to_all | solution.py:173
  102.8 5.5 %reshape.253 = f32[1024,2,768]{2,1,0:T(2,128)} reshape(bf16[32,32,1536]{2,1,0:T(8,128)(2,1)S(1)} %all-to-all-done.1) | data formatting | bytes 9437184 | tf_op jit(solution)/shard_map/convert_element_type | solution.py:140
  108.3 12.7 %fusion.56 = (f32[1024,1,768]{2,1,0:T(1,128)}, f32[1024,1,768]{2,1,0:T(1,128)}) fusion(f32[1024,2,768]{2,1,0:T(2,128)} %reshape.253), kind=kLoop, calls=%fused_computation.151 | loop fusion | bytes 12582912 | tf_op jit(solution)/shard_map/slice | solution.py:141
  127.0 12.0 %fusion.2 = f32[3,16,64,8,64]{4,3,2,0,1:T(8,128)} fusion(bf16[4,256,64,64,1,1]{1,3,2,0,5,4:T(8,128)(2,1)} %bitcast.70, bf16[4,16,8,3,256,1]{4,2,3,1,0,5:T(8,128)(2,1)S(1)} %bitcast.82), kind=kOutput, calls=%fused_computation.7 | convolution fusion | flops 3221225472 | bytes 15466496 | tf_op jit(solution)/shard_map/wrcka,waij->kricj/dot_general | solution.py:185
  139.0 9.8 %fusion.53 = (f32[1,16,64,8,64]{4,3,2,0,1:T(8,128)}, f32[1,16,64,8,64]{4,3,2,0,1:T(8,128)}, f32[1,16,64,8,64]{4,3,2,0,1:T(8,128)}) fusion(f32[3,16,64,8,64]{4,3,2,0,1:T(8,128)} %fusion.2), kind=kLoop, calls=%fused_computation.148 | loop fusion | bytes 12582912 | tf_op jit(solution)/shard_map/slice | solution.py:122
  154.0 3.7 %pad_maximum_fusion.1 = f32[4,1024,512]{1,2,0:T(8,128)S(1)} fusion(f32[1,1024,512]{1,2,0:T(8,128)} %copy.84, f32[1,1024,512]{1,2,0:T(8,128)} %get-tuple-element.65, f32[1,1024,512]{1,2,0:T(8,128)} %get-tuple-element.64, f32[1,1024,512]{1,2,0:T(8,128)} %get-tuple-element.45), kind=kLoop, calls=%fused_computation.4 | loop fusion | flops 6291456 | bytes 16777216 | tf_op jit(solution)/shard_map/stack | solution.py:193
  161.8 5.0 %collective-permute-start.1 = (f32[4,1,512]{2,0,1:T(4,128)S(1)}, f32[4,1,512]{2,0,1:T(4,128)S(1)}, u32[]{:S(2)}, u32[]{:S(2)}) collective-permute-start(f32[4,1,512]{2,0,1:T(4,128)S(1)} %copy.86), channel_id=1, source_target_pairs={{8,0},{16,8},{24,16},{9,1},{17,9},{25,17},{10,2},{18,10},{26,18},{... | collective-permute-start | bytes 24584 | tf_op jit(solution)/shard_map/ppermute | solution.py:30
  173.1 11.4 %concatenate.6 = f32[4,1026,512]{1,2,0:T(8,128)} concatenate(f32[4,1,512]{1,2,0:T(8,128)S(1)} %copy.87, f32[4,1024,512]{1,2,0:T(8,128)} %copy-done.2, f32[4,1,512]{1,2,0:T(8,128)S(1)} %copy.88), dimensions={1} | concatenate | bytes 16809984 | tf_op jit(solution)/shard_map/concatenate | solution.py:26
  200.4 8.0 %pad_maximum_fusion = f32[4,1026,514]{1,2,0:T(8,128)} fusion(f32[4,1026,1]{1,2,0:T(1,128)S(1)} %copy.92, f32[4,1026,512]{1,2,0:T(8,128)} %concatenate.6, f32[4,1026,1]{1,2,0:T(1,128)S(1)} %copy.91), kind=kLoop, calls=%fused_computation.3 | loop fusion | flops 4218912 | bytes 16875648 | tf_op jit(solution)/shard_map/concatenate | solution.py:26
  208.4 5.8 %slice_bitcast_fusion.1 = (f32[1026,514]{0,1:T(8,128)S(1)}, f32[1026,514]{0,1:T(8,128)}, f32[1026,514]{0,1:T(8,128)S(1)}, f32[1026,514]{0,1:T(8,128)S(1)}) fusion(f32[4,1026,514]{1,2,0:T(8,128)} %pad_maximum_fusion), kind=kLoop, calls=%fused_computation.14 | loop fusion | bytes 16875648 | tf_op jit(solution)/shard_map/squeeze | solution.py:97
  214.3 5.8 %multiply_subtract_fusion.1 = (f32[1024,513]{0,1:T(8,128)}, f32[1024,513]{0,1:T(8,128)}, f32[1024,513]{0,1:T(8,128)S(1)}, f32[1024,513]{0,1:T(8,128)S(1)}, pred[...) fusion(f32[1026,514]{0,1:T(8,128)S(1)} %get-tuple-element.52, f32[1026,514]{0,1:T(8,128)S(1)} %get-tuple-element.53), kind=kLoop, calls=%fused_computation.33 | loop fusion | flops 11031552 | bytes 17860608 | tf_op jit(solution)/shard_map/sub | solution.py:75
  220.1 5.8 %multiply_subtract_fusion = (f32[1025,512]{0,1:T(8,128)}, f32[1025,512]{0,1:T(8,128)}, f32[1025,512]{0,1:T(8,128)S(1)}, f32[1025,512]{0,1:T(8,128)S(1)}, pred[10...) fusion(f32[1026,514]{0,1:T(8,128)S(1)} %get-tuple-element.50, f32[1026,514]{0,1:T(8,128)S(1)} %get-tuple-element.53), kind=kLoop, calls=%fused_computation.17 | loop fusion | flops 11020800 | bytes 17843200 | tf_op jit(solution)/shard_map/sub | solution.py:75
  230.6 8.7 %fusion.51 = (f32[1024,513]{0,1:T(8,128)}, f32[1024,513]{0,1:T(8,128)}, f32[1024,513]{0,1:T(8,128)}, f32[1024,513]{0,1:T(8,128)S(1)}, f32[1024,513]{0,1:T(8,128)...) fusion(f32[1024,513]{0,1:T(8,128)S(1)} %get-tuple-element.20, ...), kind=kLoop, calls=%fused_computation.146 | loop fusion | flops 13132800 | bytes 25214976 | tf_op jit(solution)/shard_map/add | solution.py:80
  239.3 3.9 %fusion.52 = (f32[1024,513]{0,1:T(8,128)}, f32[1024,513]{0,1:T(8,128)}, f32[1024,513]{0,1:T(8,128)}) fusion(f32[1024,513]{0,1:T(8,128)S(1)} %get-tuple-element.37, f32[1024,513]{0,1:T(8,128)S(1)} %get-tuple-element.40, f32[1024,513]{0,1:T(8,128)S(1)} %get-tuple-element.39, f32[1024,513]{0,1:T(8,128)S(1)} %get-tuple-element.38), kind=kLoop, calls=%fused_computation.147 | loop fusion | flops 2626560 | bytes 14708736 | tf_op jit(solution)/shard_map/add | solution.py:80
  243.2 7.4 %fusion.49 = (f32[1025,512]{0,1:T(8,128)}, f32[1025,512]{0,1:T(8,128)}, f32[1025,512]{0,1:T(8,128)}, f32[1025,512]{0,1:T(8,128)S(1)}, f32[1025,512]{0,1:T(8,128)...) fusion(f32[1025,512]{0,1:T(8,128)S(1)} %get-tuple-element.14, ...), kind=kLoop, calls=%fused_computation.144 | loop fusion | flops 13120000 | bytes 25190400 | tf_op jit(solution)/shard_map/add | solution.py:80
  255.0 18.8 %fusion.12 = (f32[1024,512]{0,1:T(8,128)}, pred[1024,512]{0,1:T(8,128)(4,1)S(1)}) fusion(f32[1026,514]{0,1:T(8,128)} %get-tuple-element.51, f32[1024,513]{0,1:T(8,128)} %copy-done.6, f32[1024,513]{0,1:T(8,128)} %get-tuple-element.43, f32[1024,513]{0,1:T(8,128)} %copy-done.5, f32[1024,513]{0,1:T(8,128)} %get-tuple-element.44, ...), kind=kLoop, calls=%fused_computation.55 | loop fusion | flops 17301504 | bytes 48758784 | tf_op jit(solution)/shard_map/jit(_where)/select_n | solution.py:136
  276.7 6.2 %subtract_select_fusion = f32[1024,512]{0,1:T(8,128)} fusion(pred[1024,512]{0,1:T(8,128)(4,1)S(1)} %get-tuple-element.10, f32[1024,513]{0,1:T(8,128)} %get-tuple-element.42, f32[1024,513]{0,1:T(8,128)} %get-tuple-element.34, f32[1025,512]{0,1:T(8,128)} %get-tuple-element.31, f32[1025,512]{0,1:T(8,128)} %get-tuple-element.23, ...), kind=kLoop, calls=%fused_computation.102 | loop fusion | flops 3145728 | bytes 13107200 | tf_op jit(solution)/shard_map/jit(_where)/select_n | solution.py:136
  285.8 18.8 %fusion.27 = f32[1024,512]{0,1:T(8,128)} fusion(pred[1024,512]{0,1:T(8,128)(4,1)S(1)} %get-tuple-element.10, f32[1026,514]{0,1:T(8,128)} %get-tuple-element.51, f32[1024,513]{0,1:T(8,128)} %get-tuple-element.17, f32[1024,513]{0,1:T(8,128)} %get-tuple-element.18, f32[1024,513]{0,1:T(8,128)} %get-tuple-element.41, f32[1025,512]{0,1:T(8,128)} %copy-done.4, ...), kind=kLoop, calls=%fused_computation.81 | loop fusion | flops 16777216 | bytes 48758784 | tf_op jit(solution)/shard_map/jit(_where)/select_n | solution.py:136
  (83 shorter events, 82.9 us)
Async XLA Ops:
  7.5 11.0 %all-to-all-start = ((s32[32,1,32]{2,1,0:T(1,128)}), s32[32,1,32]{2,1,0:T(1,128)S(1)}, u32[]{:S(2)}, u32[]{:S(2)}) async-start(s32[32,1,32]{2,1,0:T(1,128)} %all_to_all.9), calls=%async_computation | async-start | bytes 32768 | tf_op jit(solution)/shard_map/all_to_all | solution.py:169
  29.4 73.4 %all-to-all-start.1 = ((bf16[32,32,1536]{2,1,0:T(8,128)(2,1)}), bf16[32,32,1536]{2,1,0:T(8,128)(2,1)S(1)}, u32[]{:S(2)}, u32[]{:S(2)}) async-start(bf16[32,32,1536]{2,1,0:T(8,128)(2,1)} %broadcast_select_fusion), calls=%async_computation.1 | async-start | bytes 6291456 | tf_op jit(solution)/shard_map/all_to_all | solution.py:173
  46.8 12.0 %copy-start.9 = (s32[1,1,512,1]{2,3,1,0:T(1,128)S(1)}, s32[1,1,512,1]{2,3,1,0:T(1,128)}, u32[]{:S(2)}) copy-start(s32[1,1,512,1]{2,3,1,0:T(1,128)} %param.13) | copy-start | bytes 6148
  46.8 12.0 %copy-start.10 = (s32[1,1,512]{2,1,0:T(1,128)S(1)}, s32[1,1,512]{2,1,0:T(1,128)}, u32[]{:S(2)}) copy-start(s32[1,1,512]{2,1,0:T(1,128)} %param.15) | copy-start | bytes 6148
  46.8 12.0 %copy-start.11 = (s32[1,1,512]{2,1,0:T(1,128)S(1)}, s32[1,1,512]{2,1,0:T(1,128)}, u32[]{:S(2)}) copy-start(s32[1,1,512]{2,1,0:T(1,128)} %param.16) | copy-start | bytes 6148
  58.8 4.5 %copy-start.7 = (f32[1024,512]{0,1:T(8,128)S(1)}, f32[1024,512]{0,1:T(8,128)}, u32[]{:S(2)}) copy-start(f32[1024,512]{0,1:T(8,128)} %copy.74) | copy-start | bytes 6291460
  58.9 4.4 %copy-start.8 = (f32[1024,512]{0,1:T(8,128)S(1)}, f32[1024,512]{0,1:T(8,128)}, u32[]{:S(2)}) copy-start(f32[1024,512]{0,1:T(8,128)} %copy.75) | copy-start | bytes 6291460
  157.7 3.3 %copy-start.2 = (f32[4,1024,512]{1,2,0:T(8,128)}, f32[4,1024,512]{1,2,0:T(8,128)S(1)}, u32[]{:S(2)}) copy-start(f32[4,1024,512]{1,2,0:T(8,128)S(1)} %pad_maximum_fusion.1) | copy-start | bytes 25165828
  161.8 7.3 %collective-permute-start.1 = (f32[4,1,512]{2,0,1:T(4,128)S(1)}, f32[4,1,512]{2,0,1:T(4,128)S(1)}, u32[]{:S(2)}, u32[]{:S(2)}) collective-permute-start(f32[4,1,512]{2,0,1:T(4,128)S(1)} %copy.86), channel_id=1, source_target_pairs={{8,0},{16,8},{24,16},{9,1},{17,9},{25,17},{10,2},{18,10},{26,18},{... | collective-permute-start | bytes 24584 | tf_op jit(solution)/shard_map/ppermute | solution.py:30
  167.2 5.5 %collective-permute-start = (f32[4,1,512]{2,0,1:T(4,128)S(1)}, f32[4,1,512]{2,0,1:T(4,128)S(1)}, u32[]{:S(2)}, u32[]{:S(2)}) collective-permute-start(f32[4,1,512]{2,0,1:T(4,128)S(1)} %copy.85), channel_id=1, source_target_pairs={{0,8},{8,16},{16,24},{1,9},{9,17},{17,25},{2,10},{10,18},{18,26},{... | collective-permute-start | bytes 24584 | tf_op jit(solution)/shard_map/ppermute | solution.py:28
  185.5 14.9 %collective-permute-start.3 = (f32[4,1026,1]{1,0,2:T(4,128)S(1)}, f32[4,1026,1]{1,0,2:T(4,128)S(1)}, u32[]{:S(2)}, u32[]{:S(2)}) collective-permute-start(f32[4,1026,1]{1,0,2:T(4,128)S(1)} %copy.90), channel_id=1, source_target_pairs={{1,0},{2,1},{3,2},{4,3},{5,4},{6,5},{7,6},{9,8},{10,9},{11,10},{12... | collective-permute-start | bytes 49256 | tf_op jit(solution)/shard_map/ppermute | solution.py:30
  187.4 13.0 %collective-permute-start.2 = (f32[4,1026,1]{1,0,2:T(4,128)S(1)}, f32[4,1026,1]{1,0,2:T(4,128)S(1)}, u32[]{:S(2)}, u32[]{:S(2)}) collective-permute-start(f32[4,1026,1]{1,0,2:T(4,128)S(1)} %copy.89), channel_id=1, source_target_pairs={{0,1},{1,2},{2,3},{3,4},{4,5},{5,6},{6,7},{8,9},{9,10},{10,11},{11... | collective-permute-start | bytes 49256 | tf_op jit(solution)/shard_map/ppermute | solution.py:28
  214.3 11.6 %copy-start = (f32[1026,514]{0,1:T(8,128)}, f32[1026,514]{0,1:T(8,128)S(1)}, u32[]{:S(2)}) copy-start(f32[1026,514]{0,1:T(8,128)S(1)} %get-tuple-element.50) | copy-start | bytes 6328372
  214.3 14.9 %copy-start.1 = (f32[1026,514]{0,1:T(8,128)}, f32[1026,514]{0,1:T(8,128)S(1)}, u32[]{:S(2)}) copy-start(f32[1026,514]{0,1:T(8,128)S(1)} %get-tuple-element.52) | copy-start | bytes 6328372
  239.3 3.9 %copy-start.5 = (f32[1024,513]{0,1:T(8,128)}, f32[1024,513]{0,1:T(8,128)S(1)}, u32[]{:S(2)}) copy-start(f32[1024,513]{0,1:T(8,128)S(1)} %get-tuple-element.38) | copy-start | bytes 6303748
  239.3 3.9 %copy-start.6 = (f32[1024,513]{0,1:T(8,128)}, f32[1024,513]{0,1:T(8,128)S(1)}, u32[]{:S(2)}) copy-start(f32[1024,513]{0,1:T(8,128)S(1)} %get-tuple-element.40) | copy-start | bytes 6303748
  250.6 3.7 %copy-start.3 = (f32[1025,512]{0,1:T(8,128)}, f32[1025,512]{0,1:T(8,128)S(1)}, u32[]{:S(2)}) copy-start(f32[1025,512]{0,1:T(8,128)S(1)} %get-tuple-element.27) | copy-start | bytes 6297604
  250.6 4.4 %copy-start.4 = (f32[1025,512]{0,1:T(8,128)}, f32[1025,512]{0,1:T(8,128)S(1)}, u32[]{:S(2)}) copy-start(f32[1025,512]{0,1:T(8,128)S(1)} %get-tuple-element.29) | copy-start | bytes 6297604
where the time goes:
time: 314 us; the launch traced here: 308 us
  other arithmetic  114 us (36%)
  local copies, waits for them, and re-layouts  114 us (36%)
  waiting for transfers between devices  43.1 us (14%)
  starting transfers between devices  22.4 us (7%)
  matrix products  12.6 us (4%)
    unnamed x33, local copies, waits for them, and re-layouts  37.9 us
    all_to_all x1, waiting for transfers between devices, body(): lax.all_to_all(reply, ('gx', 'gy'), split_axis=0, concat_axis=0, tiled=True)  36.5 us
    add x4, other arithmetic, waves(): part_h = s_one * alpha_one + s_three * alpha_three  23.5 us
    select_n x1, other arithmetic, advance(): jnp.where(wet, new_x, 0.0)  18.8 us
    select_n x1, other arithmetic, advance(): jnp.where(wet, new_y, 0.0)  18.8 us
    slice x1, local copies, waits for them, and re-layouts, snapshot_mix(): pairs[:, 0]  12.7 us
    dot_general x1, matrix products, body(): jnp.einsum('wrcka,waij->kricj', summed, weight_cells, preferred_element_t...  12 us
    sub x2, other arithmetic, fluctuations(): alpha_two = delta_t - v_bar * delta_h  11.6 us
  transfers between devices with their start and end apart: 6, of which 3 were waited for; matrix products, arithmetic and copies ran while one was open for 14% of the time, Pallas kernels for 0%

commit v1 on v0

v1 whole, which is shorter than its diff:
```python
import functools

import jax
import jax.numpy as jnp
from jax import lax
from jax.experimental import pallas as pl
from jax.experimental.pallas import tpu as pltpu
from jax.sharding import PartitionSpec as P

PATCH = 64
ABLK = 256
NW = 4
BPX = 16
BPY = 8
NPATCH = BPX * BPY

GRAV = 1.0
DT_DX = 0.2
TIME_STEP = 0.2
STRESS = 0.5
PRESS = 0.5

F32 = jnp.float32
BF16 = jnp.bfloat16
VMEM = pl.BlockSpec(memory_space=pltpu.VMEM)
SMEM = pl.BlockSpec(memory_space=pltpu.SMEM)
LANES = 128
TILE = 8
HALVES = BPX // TILE
QUADS = BPY // 2
SLAB = HALVES * QUADS * TILE


def params(limit=56 << 20, **kw):
    return pltpu.CompilerParams(vmem_limit_bytes=limit, **kw)


def iota(shape, dim):
    return lax.broadcasted_iota(jnp.int32, shape, dim)


def rank_kernel(capacity, src_ref, blk_ref, pat_ref, wgt_ref, want_ref, lab_ref):
    devices = want_ref.shape[0]
    src = src_ref[...]
    ent = src.shape[1]
    hits = (iota((devices, ent), 0) == src).astype(F32)
    order = (iota((ent, ent), 0) <= iota((ent, ent), 1)).astype(BF16)
    ranks = jnp.dot(hits.astype(BF16), order, preferred_element_type=F32)
    mine = jnp.sum(hits * ranks, axis=0, keepdims=True).astype(jnp.int32) - 1
    place = iota((capacity, ent), 0) == mine
    pat = pat_ref[...]
    row_bits = BPX.bit_length() - 1
    col_bits = BPY.bit_length() - 1
    rows = jnp.zeros_like(pat)
    cols = jnp.zeros_like(pat)
    used_r = used_c = position = 0
    while used_r < row_bits or used_c < col_bits:
        value = jnp.bitwise_and(jnp.right_shift(pat, position), 1)
        if used_r < row_bits and (used_c >= col_bits or position % 2 == 0):
            rows = rows + value * (1 << used_r)
            used_r += 1
        else:
            cols = cols + value * (1 << used_c)
            used_c += 1
        position += 1

    def spread(row):
        picked = jnp.where(place, row.astype(F32), 0.0).astype(BF16)
        return lax.dot_general(
            hits.astype(BF16), picked, (((1,), (1,)), ((), ())),
            preferred_element_type=F32,
        ).astype(jnp.int32)

    want_ref[...] = spread(blk_ref[...])
    slot = spread(cols * BPX + rows)
    group = spread(wgt_ref[...] + 1)
    lab_ref[...] = jnp.where(group > 0, (group - 1) * NPATCH + slot, -1)


def make_requests(src, blk, pat, wgt, devices, capacity):
    shape = jax.ShapeDtypeStruct((devices, capacity), jnp.int32)
    return pl.pallas_call(
        functools.partial(rank_kernel, capacity),
        out_shape=(shape, shape),
        in_specs=[VMEM] * 4,
        out_specs=(VMEM, VMEM),
        compiler_params=params(),
        name="requests",
    )(src, blk, pat, wgt)


def serve_kernel(blend_ref, asked_ref, atm_ref, press_ref, wind_ref):
    blend = blend_ref[0]
    keep = 1.0 - blend
    asked = asked_ref[...]
    pick = (asked == iota((asked.shape[0], atm_ref.shape[1]), 1)).astype(BF16)

    def mixed(k):
        first = atm_ref[k].astype(F32)
        second = atm_ref[3 + k].astype(F32)
        return (keep * first + blend * second).astype(BF16)

    press_ref[...] = jnp.dot(pick, mixed(2), preferred_element_type=F32).astype(BF16)
    for k in range(2):
        wind_ref[:, k * ABLK:(k + 1) * ABLK] = jnp.dot(
            pick, mixed(k), preferred_element_type=F32
        ).astype(BF16)


def serve(blend, asked, atm):
    slots = asked.shape[0]
    return pl.pallas_call(
        serve_kernel,
        out_shape=(
            jax.ShapeDtypeStruct((slots, ABLK), BF16),
            jax.ShapeDtypeStruct((slots, 2 * ABLK), BF16),
        ),
        in_specs=[SMEM, VMEM, VMEM],
        out_specs=(VMEM, VMEM),
        compiler_params=params(),
        name="serve",
    )(blend, asked, atm)


def edges_kernel(
    dl, ml, xl, yl, dr, mr, xr, yr, dt, mt, xt, yt, db, mb, xb, yb,
    top_ref, bottom_ref, left_ref, right_ref,
):
    def rows(d, m, x, y, at, out):
        wet = m[...] == 1
        for f, ref in enumerate((d, x, y)):
            out[f:f + 1, :] = jnp.where(wet, ref[...], 0.0)[at:at + 1]

    rows(dt, mt, xt, yt, 0, top_ref)
    rows(db, mb, xb, yb, TILE - 1, bottom_ref)
    lane = iota((LANES, LANES), 1)

    def step(b, carry):
        at = pl.ds(pl.multiple_of(b * LANES, LANES), LANES)
        wl = ml[at, :] == 1
        wr = mr[at, :] == 1
        packed = jnp.where(wl, dl[at, :], 0.0)
        packed = jnp.where(lane == 1, pltpu.roll(jnp.where(wl, xl[at, :], 0.0), 1, 1), packed)
        packed = jnp.where(lane == 2, pltpu.roll(jnp.where(wl, yl[at, :], 0.0), 2, 1), packed)
        packed = jnp.where(lane == 8, pltpu.roll(jnp.where(wr, dr[at, :], 0.0), 9, 1), packed)
        packed = jnp.where(lane == 9, pltpu.roll(jnp.where(wr, xr[at, :], 0.0), 10, 1), packed)
        packed = jnp.where(lane == 10, pltpu.roll(jnp.where(wr, yr[at, :], 0.0), 11, 1), packed)
        turned = packed.T
        left_ref[:, at] = turned[0:TILE]
        right_ref[:, at] = turned[TILE:2 * TILE]
        return carry

    lax.fori_loop(0, dl.shape[0] // LANES, step, 0)


def edge_cells(depth, mask, momx, momy):
    rows, cols = depth.shape
    fields = (depth, mask, momx, momy)
    left = pl.BlockSpec((rows, LANES), lambda i: (0, 0))
    right = pl.BlockSpec((rows, LANES), lambda i: (0, cols // LANES - 1))
    top = pl.BlockSpec((TILE, cols), lambda i: (0, 0))
    bottom = pl.BlockSpec((TILE, cols), lambda i: (rows // TILE - 1, 0))
    line = jax.ShapeDtypeStruct((TILE, cols), F32)
    column = jax.ShapeDtypeStruct((TILE, rows), F32)
    return pl.pallas_call(
        edges_kernel,
        grid=(1,),
        out_shape=(line, line, column, column),
        in_specs=[left] * 4 + [right] * 4 + [top] * 4 + [bottom] * 4,
        out_specs=(
            pl.BlockSpec((TILE, cols), lambda i: (0, 0)),
            pl.BlockSpec((TILE, cols), lambda i: (0, 0)),
            pl.BlockSpec((TILE, rows), lambda i: (0, 0)),
            pl.BlockSpec((TILE, rows), lambda i: (0, 0)),
        ),
        compiler_params=params(),
        name="edges",
    )(*(fields * 4))


def send(value, axis, step):
    count = lax.axis_size(axis)
    if step > 0:
        pairs = [(i, i + 1) for i in range(count - 1)]
    else:
        pairs = [(i + 1, i) for i in range(count - 1)]
    return lax.ppermute(value, axis, pairs)


def roe(hl, nl, tl, sl, ql, pl_, hr, nr, tr, sr, qr, pr, left=True, right=True):
    both = jnp.minimum(hl, hr) > 0.0
    half = jnp.where(both, 0.5, 1.0)
    level = (hl + hr) * half
    rc = lax.rsqrt(level)
    c = level * rc
    inv = 1.0 / (sl + sr)
    u = jnp.where(both, (ql + qr) * inv, 0.0)
    v = (pl_ + pr) * inv
    dh = jnp.where(both, hr - hl, 0.0)
    dn = (nr - nl) * (half + half)
    dt = jnp.where(both, tr - tl, 0.0)
    e = (dn - u * dh) * (0.5 * rc)
    mid = 0.5 * dh
    a1 = mid - e
    a3 = mid + e
    a2 = dt - v * dh
    s1 = u - c
    s3 = u + c
    w1 = s1 * a1
    w3 = s3 * a3
    w2 = u * a2
    zero = jnp.zeros_like(w1)
    n1 = s1 < 0.0
    n3 = s3 < 0.0
    n2 = u < 0.0
    out = []
    for going in ((True, left), (False, right)):
        if not going[1]:
            continue
        if going[0]:
            m1 = jnp.where(n1, w1, zero)
            m3 = jnp.where(n3, w3, zero)
            m2 = jnp.where(n2, w2, zero)
        else:
            m1 = jnp.where(n1, zero, w1)
            m3 = jnp.where(n3, zero, w3)
            m2 = jnp.where(n2, zero, w2)
        ph = m1 + m3
        out.append((ph, m1 * s1 + m3 * s3, ph * v + m2))
    return out


def stencil_kernel(
    d_ref, m_ref, x_ref, y_ref, up_ref, dn_ref, lh_ref, rh_ref, lo_ref, ro_ref,
    newh_ref, hu_ref, hv_ref, h_ref,
    sh, su, sv, ss, sq, sp, edge, ecol,
):
    rows, cols = d_ref.shape
    tiles = rows // TILE
    store = (sh, su, sv, ss, sq, sp)

    def derived(h, u, v):
        r = jnp.where(h > 0.0, lax.rsqrt(h), 0.0)
        return (h, u, v, h * r, u * r, v * r)

    for at, ref in ((0, up_ref), (rows + TILE, dn_ref)):
        vals = derived(ref[0:1, :], ref[1:2, :], ref[2:3, :])
        for dst, val in zip(store, vals):
            dst[at:at + TILE, :] = jnp.broadcast_to(val, (TILE, cols))

    def fill(t, carry):
        at = pl.ds(pl.multiple_of(t * TILE, TILE), TILE)
        wet = m_ref[at, :] == 1
        h = jnp.where(wet, d_ref[at, :], 0.0)
        u = jnp.where(wet, x_ref[at, :], 0.0)
        v = jnp.where(wet, y_ref[at, :], 0.0)
        to = pl.ds(pl.multiple_of(t * TILE + TILE, TILE), TILE)
        for dst, val in zip(store, derived(h, u, v)):
            dst[to, :] = val
        return carry

    lax.fori_loop(0, tiles, fill, 0, unroll=4)

    def line(ref):
        h, u, v, s, q, p = derived(ref[0:1, :], ref[1:2, :], ref[2:3, :])
        return (h, v, u, s, p, q)

    first = roe(*line(lh_ref), *line(lo_ref), left=False)[0]
    last = roe(*line(ro_ref), *line(rh_ref), right=False)[0]
    edge[...] = jnp.zeros_like(edge)
    for f, val in enumerate(first + last):
        edge[f:f + 1, :] = val

    def turn(b, carry):
        at = pl.ds(pl.multiple_of(b * LANES, LANES), LANES)
        ecol[at, :] = edge[:, at].T
        return carry

    lax.fori_loop(0, rows // LANES, turn, 0)

    row = iota((TILE, cols), 0)
    lane = iota((TILE, cols), 1)

    def down(value, before):
        rolled = pltpu.roll(value, 1, 0)
        return jnp.where(row == 0, before, rolled), rolled

    def load(start):
        return [ref[pl.ds(start, TILE), :] for ref in store]

    def below(now, after):
        return jnp.where(row == TILE - 1, pltpu.roll(after, TILE - 1, 0), pltpu.roll(now, TILE - 1, 0))

    def body(t, before):
        base = pl.multiple_of(t * TILE + TILE, TILE)
        now = load(base)
        after = load(pl.multiple_of(base + TILE, TILE))
        nxt = [below(a, b) for a, b in zip(now, after)]
        lx, rx = roe(*now, *nxt)
        moved, carry = [], []
        for a, b in zip(rx, before):
            m, c = down(a, b)
            moved.append(m)
            carry.append(c)
        h, u, v, s, q, p = now
        side = (h, v, u, s, p, q)
        other = [pltpu.roll(a, cols - 1, 1) for a in side]
        ly, ry = roe(*side, *other)
        at = pl.ds(pl.multiple_of(t * TILE, TILE), TILE)
        fl = ecol[at, :]
        ly = [jnp.where(lane == cols - 1, fl[:, 3 + f:4 + f], a) for f, a in enumerate(ly)]
        ry = [jnp.where(lane == 0, fl[:, f:f + 1], pltpu.roll(a, 1, 1)) for f, a in enumerate(ry)]
        ch = lx[0] + moved[0] + ly[0] + ry[0]
        cx = lx[1] + moved[1] + ly[2] + ry[2]
        cy = lx[2] + moved[2] + ly[1] + ry[1]
        wet = h > 0.0
        newh_ref[at, :] = jnp.where(wet, h - DT_DX * ch, 0.0)
        hu = u - DT_DX * cx
        hv = v - DT_DX * cy
        r = t // (PATCH // TILE)
        i0 = (t % (PATCH // TILE)) * TILE
        start = i0 * SLAB + (r // TILE) * (QUADS * TILE) + r % TILE
        for g in range(QUADS):
            to = pl.ds(start + g * TILE, TILE, stride=SLAB)
            cut = slice(g * LANES, (g + 1) * LANES)
            hu_ref[to, :] = hu[:, cut]
            hv_ref[to, :] = hv[:, cut]
            h_ref[to, :] = h[:, cut]
        return tuple(carry)

    lead = load(0)
    after = load(TILE)
    nxt = [below(a, b) for a, b in zip(lead, after)]
    rx = roe(*lead, *nxt, left=False)[0]
    start = tuple(pltpu.roll(a, 1, 0) for a in rx)
    lax.fori_loop(0, tiles, body, start)


def stencil(depth, mask, momx, momy, up, dn, lh, rh, lo, ro):
    rows, cols = depth.shape
    grouped = jax.ShapeDtypeStruct((rows * cols // LANES, LANES), F32)
    pad = pltpu.VMEM((rows + 2 * TILE, cols), F32)
    return pl.pallas_call(
        stencil_kernel,
        out_shape=(jax.ShapeDtypeStruct((rows, cols), F32), grouped, grouped, grouped),
        in_specs=[VMEM] * 10,
        out_specs=(VMEM,) * 4,
        scratch_shapes=[pad] * 6 + [pltpu.VMEM((LANES, rows), F32), pltpu.VMEM((rows, LANES), F32)],
        compiler_params=params(),
        cost_estimate=pl.CostEstimate(flops=200 * rows * cols, bytes_accessed=32 * rows * cols, transcendentals=0),
        name="stencil",
    )(depth, mask, momx, momy, up, dn, lh, rh, lo, ro)


def summed_of(lab, landed):
    select = (iota((NW * NPATCH, lab.shape[1]), 0) == lab).astype(BF16)
    return jnp.dot(select, landed, preferred_element_type=F32).astype(BF16)


def stack_left(left, summed, channels):
    for k in range(channels):
        for w in range(NW):
            left[k * NPATCH:(k + 1) * NPATCH, w * ABLK:(w + 1) * ABLK] = summed[
                w * NPATCH:(w + 1) * NPATCH, k * ABLK:(k + 1) * ABLK
            ]


def pair_rows(acc, k, t, half, g, low):
    cut = slice(t * LANES, (t + 1) * LANES)
    base = k * NPATCH + half * TILE
    even = acc[base + (2 * g) * BPX:base + (2 * g) * BPX + TILE, cut]
    odd = acc[base + (2 * g + 1) * BPX:base + (2 * g + 1) * BPX + TILE, cut]
    return (
        jnp.where(low, even, pltpu.roll(odd, LANES // 2, 1)),
        jnp.where(low, pltpu.roll(even, LANES // 2, 1), odd),
    )


def press_kernel(lab_ref, landed_ref, w_ref, out_ref, left, acc):
    @pl.when(pl.program_id(0) == 0)
    def _():
        stack_left(left, summed_of(lab_ref[...], landed_ref[...]), 1)

    acc[...] = jnp.dot(left[...], w_ref[...], preferred_element_type=F32)
    low = iota((TILE, LANES), 1) < LANES // 2
    for t in range(TILE // 2):
        for half in range(HALVES):
            for g in range(QUADS):
                pair = pair_rows(acc, 0, t, half, g, low)
                for odd in range(2):
                    at = (2 * t + odd) * SLAB + (half * QUADS + g) * TILE
                    out_ref[at:at + TILE, :] = pair[odd]


def pressure_field(lab, landed, weights):
    steps = PATCH // TILE
    chunk = TILE * PATCH
    cells = PATCH * SLAB
    return pl.pallas_call(
        press_kernel,
        grid=(steps,),
        out_shape=jax.ShapeDtypeStruct((cells, LANES), F32),
        in_specs=[
            pl.BlockSpec(lab.shape, lambda i: (0, 0)),
            pl.BlockSpec(landed.shape, lambda i: (0, 0)),
            pl.BlockSpec((NW * ABLK, chunk), lambda i: (0, i)),
        ],
        out_specs=pl.BlockSpec((cells // steps, LANES), lambda i: (i, 0)),
        scratch_shapes=[
            pltpu.VMEM((NPATCH, NW * ABLK), BF16),
            pltpu.VMEM((NPATCH, chunk), F32),
        ],
        compiler_params=params(),
        cost_estimate=pl.CostEstimate(
            flops=2 * NPATCH * NW * ABLK * PATCH * PATCH, bytes_accessed=12 << 20, transcendentals=0
        ),
        name="pressure",
    )(lab, landed, weights)


def press_edges_kernel(p_ref, top_ref, bottom_ref, left_ref, right_ref):
    last = (PATCH - 1) * SLAB
    for g in range(QUADS):
        cut = slice(g * LANES, (g + 1) * LANES)
        top_ref[:, cut] = p_ref[g * TILE:(g + 1) * TILE, :]
        at = last + (QUADS + g) * TILE
        bottom_ref[:, cut] = pltpu.roll(p_ref[at:at + TILE, :], 1, 0)
    lane = iota((LANES, LANES), 1)
    per = LANES // (HALVES * TILE)
    for b in range(PATCH // per):
        firsts, lasts = [], []
        for i in range(b * per, (b + 1) * per):
            for half in range(HALVES):
                at = i * SLAB + half * QUADS * TILE
                firsts.append(p_ref[at:at + TILE, :])
                at = at + (QUADS - 1) * TILE
                lasts.append(p_ref[at:at + TILE, :])
        packed = jnp.where(
            lane == TILE,
            pltpu.roll(jnp.concatenate(lasts, axis=0), TILE + 1, 1),
            jnp.concatenate(firsts, axis=0),
        )
        turned = packed.T
        left_ref[:, b * LANES:(b + 1) * LANES] = turned[0:TILE]
        right_ref[:, b * LANES:(b + 1) * LANES] = turned[TILE:2 * TILE]


def press_edges(p):
    rows = PATCH * BPX
    cols = PATCH * BPY
    line = jax.ShapeDtypeStruct((TILE, cols), F32)
    column = jax.ShapeDtypeStruct((TILE, rows), F32)
    return pl.pallas_call(
        press_edges_kernel,
        out_shape=(line, line, column, column),
        in_specs=[VMEM],
        out_specs=(VMEM,) * 4,
        compiler_params=params(),
        name="press_edges",
    )(p)


def gradient_kernel(
    p_ref, hu_ref, hv_ref, h_ref, up_ref, dn_ref, lh_ref, rh_ref,
    ox_ref, oy_ref, fac_ref, turned, ends,
):
    stacked = jnp.concatenate([lh_ref[...], rh_ref[...]], axis=0)
    for b in range(stacked.shape[1] // LANES):
        cut = slice(b * LANES, (b + 1) * LANES)
        square = jnp.concatenate(
            [stacked[:, cut], jnp.zeros((LANES - 2 * TILE, LANES), F32)], axis=0
        )
        turned[cut, :] = square.T
    row = iota((BPX, LANES), 0)
    last = (PATCH - 1) * SLAB
    for g in range(QUADS):
        cut = slice(g * LANES, (g + 1) * LANES)
        for at, end, halo, shift, edge in (
            (last, 0, up_ref, 1, 0),
            (0, 1, dn_ref, BPX - 1, BPX - 1),
        ):
            parts = [
                p_ref[at + (half * QUADS + g) * TILE:at + (half * QUADS + g + 1) * TILE, :]
                for half in range(HALVES)
            ]
            whole = pltpu.roll(jnp.concatenate(parts, axis=0), shift, 0)
            whole = jnp.where(row == edge, jnp.broadcast_to(halo[0:1, cut], (BPX, LANES)), whole)
            for half in range(HALVES):
                to = end * SLAB + (half * QUADS + g) * TILE
                ends[to:to + TILE, :] = whole[half * TILE:(half + 1) * TILE]

    lane = iota((TILE, LANES), 1)

    def cells(i, before, after):
        at = i * SLAB
        for half in range(HALVES):
            rows = pl.ds(pl.multiple_of((i * HALVES + half) * TILE, TILE), TILE)
            sides = turned[rows, :]
            tiles = [
                p_ref[pl.ds(pl.multiple_of(at + (half * QUADS + g) * TILE, TILE), TILE), :]
                for g in range(QUADS)
            ]
            ups = [pltpu.roll(a, 1, 1) for a in tiles]
            downs = [pltpu.roll(a, LANES - 1, 1) for a in tiles]
            for g in range(QUADS):
                off = (half * QUADS + g) * TILE
                here = pl.ds(pl.multiple_of(at + off, TILE), TILE)
                prev = jnp.where(lane == 0, ups[g - 1] if g else sides[:, 0:1], ups[g])
                if g < QUADS - 1:
                    nxt = jnp.where(lane == LANES - 1, downs[g + 1], downs[g])
                else:
                    nxt = jnp.where(lane == LANES - 1, sides[:, TILE:TILE + 1], downs[g])
                h = h_ref[here, :]
                wet = h > 0.0
                scale = (TIME_STEP * PRESS * 0.5) * h
                gx = after(off) - before(off)
                ox_ref[here, :] = jnp.where(wet, hu_ref[here, :] - scale * gx, 0.0)
                oy_ref[here, :] = jnp.where(wet, hv_ref[here, :] - scale * (nxt - prev), 0.0)
                fac_ref[here, :] = jnp.where(wet, TIME_STEP * STRESS, 0.0)

    def at_end(end):
        return lambda off: ends[end * SLAB + off:end * SLAB + off + TILE, :]

    def at_slab(i):
        return lambda off: p_ref[pl.ds(pl.multiple_of(i * SLAB + off, TILE), TILE), :]

    cells(0, at_end(0), at_slab(1))
    lax.fori_loop(
        1, PATCH - 1, lambda i, c: (cells(i, at_slab(i - 1), at_slab(i + 1)), c)[1], 0
    )
    cells(PATCH - 1, at_slab(PATCH - 2), at_end(1))


def gradient(p, hu, hv, h, up, dn, lh, rh):
    grouped = jax.ShapeDtypeStruct(p.shape, F32)
    return pl.pallas_call(
        gradient_kernel,
        out_shape=(grouped,) * 3,
        in_specs=[VMEM] * 8,
        out_specs=(VMEM,) * 3,
        scratch_shapes=[
            pltpu.VMEM((PATCH * BPX, LANES), F32),
            pltpu.VMEM((2 * SLAB, LANES), F32),
        ],
        compiler_params=params(),
        cost_estimate=pl.CostEstimate(
            flops=20 * p.size, bytes_accessed=28 * p.size, transcendentals=0
        ),
        name="gradient",
    )(p, hu, hv, h, up, dn, lh, rh)


def wind_kernel(lab_ref, landed_ref, w_ref, hu_ref, hv_ref, fac_ref, ox_ref, oy_ref, left, acc, sx, sy):
    @pl.when(pl.program_id(0) == 0)
    def _():
        stack_left(left, summed_of(lab_ref[...], landed_ref[...]), 2)

    acc[...] = jnp.dot(left[...], w_ref[...], preferred_element_type=F32)
    low = iota((TILE, LANES), 1) < LANES // 2
    for t in range(TILE // 2):
        for half in range(HALVES):
            for g in range(QUADS):
                xs = pair_rows(acc, 0, t, half, g, low)
                ys = pair_rows(acc, 1, t, half, g, low)
                for odd in range(2):
                    i = 2 * t + odd
                    at = i * SLAB + (half * QUADS + g) * TILE
                    wx = xs[odd]
                    wy = ys[odd]
                    speed = jnp.sqrt(wx * wx + wy * wy) * fac_ref[at:at + TILE, :]
                    to = pl.ds(half * TILE * TILE + i, TILE, stride=TILE)
                    sx[g, to, :] = hu_ref[at:at + TILE, :] + speed * wx
                    sy[g, to, :] = hv_ref[at:at + TILE, :] + speed * wy
    for src, dst in ((sx, ox_ref), (sy, oy_ref)):
        for g in range(QUADS):
            for r in range(BPX):
                dst[r, :, g * LANES:(g + 1) * LANES] = src[g, r * TILE:(r + 1) * TILE, :]


def wind_field(lab, landed, weights, hu, hv, fac):
    steps = PATCH // TILE
    chunk = TILE * PATCH
    cols = BPY * PATCH
    slab = pl.BlockSpec((TILE * SLAB, LANES), lambda i: (i, 0))
    out = pl.BlockSpec((BPX, TILE, cols), lambda i: (0, i, 0))
    shape = jax.ShapeDtypeStruct((BPX, PATCH, cols), F32)
    return pl.pallas_call(
        wind_kernel,
        grid=(steps,),
        out_shape=(shape, shape),
        in_specs=[
            pl.BlockSpec(lab.shape, lambda i: (0, 0)),
            pl.BlockSpec(landed.shape, lambda i: (0, 0)),
            pl.BlockSpec((NW * ABLK, chunk), lambda i: (0, i)),
            slab, slab, slab,
        ],
        out_specs=(out, out),
        scratch_shapes=[
            pltpu.VMEM((2 * NPATCH, NW * ABLK), BF16),
            pltpu.VMEM((2 * NPATCH, chunk), F32),
            pltpu.VMEM((QUADS, BPX * TILE, LANES), F32),
            pltpu.VMEM((QUADS, BPX * TILE, LANES), F32),
        ],
        compiler_params=params(),
        cost_estimate=pl.CostEstimate(
            flops=4 * NPATCH * NW * ABLK * PATCH * PATCH, bytes_accessed=20 << 20, transcendentals=0
        ),
        name="wind",
    )(lab, landed, weights, hu, hv, fac)


def body(
    atm_blocks,
    remap_weights,
    ovl_source,
    ovl_block,
    ovl_patch,
    ovl_weight,
    depth_field,
    wet_mask,
    mom_x,
    mom_y,
    blend,
):
    devices = lax.axis_size("gx") * lax.axis_size("gy")
    entries = ovl_source.size
    capacity = 2 * entries // devices
    both = ("gx", "gy")
    want, lab = make_requests(
        ovl_source.reshape(1, entries), ovl_block.reshape(1, entries),
        ovl_patch.reshape(1, entries), ovl_weight.reshape(1, entries), devices, capacity,
    )
    asked = lax.all_to_all(want, both, split_axis=0, concat_axis=0, tiled=True)
    atm = atm_blocks.reshape(atm_blocks.shape[2:]).transpose(1, 0, 2)
    press, wind = serve(blend.reshape(1), asked.reshape(devices * capacity, 1), atm)

    def exchange(rows):
        parts = rows.reshape(devices, capacity, rows.shape[1])
        got = lax.all_to_all(parts, both, split_axis=0, concat_axis=0, tiled=True)
        return got.reshape(rows.shape)

    press = exchange(press)
    wind = exchange(wind)
    lab = lab.reshape(1, devices * capacity)

    top, bottom, left, right = edge_cells(depth_field, wet_mask, mom_x, mom_y)
    newh, hu, hv, h = stencil(
        depth_field, wet_mask, mom_x, mom_y,
        send(bottom, "gx", 1), send(top, "gx", -1),
        send(right, "gy", 1), send(left, "gy", -1), left, right,
    )
    weights = remap_weights.reshape(NW * ABLK, PATCH * PATCH)
    p = pressure_field(lab, press, weights)
    top, bottom, left, right = press_edges(p)
    hu, hv, fac = gradient(
        p, hu, hv, h,
        send(bottom, "gx", 1), send(top, "gx", -1),
        send(right, "gy", 1), send(left, "gy", -1),
    )
    new_x, new_y = wind_field(lab, wind, weights, hu, hv, fac)
    return (newh, new_x.reshape(newh.shape), new_y.reshape(newh.shape))


def solution(mesh):
    placed = (
        P("gx", "gy", None, None, None),
        P(),
        P("gx", "gy", None, None),
        P("gx", "gy", None),
        P("gx", "gy", None),
        P("gx", "gy", None),
        P("gx", "gy"),
        P("gx", "gy"),
        P("gx", "gy"),
        P("gx", "gy"),
        P(),
    )
    return jax.shard_map(
        body,
        mesh=mesh,
        in_specs=placed,
        out_specs=(P("gx", "gy"), P("gx", "gy"), P("gx", "gy")),
        check_vma=False,
    )
```

time: 314 us -> 146 us (0.46); the launches traced: 308 us -> 146 us
  other arithmetic: 114 us -> 0.69 us
  local copies, waits for them, and re-layouts: 114 us -> 4.75 us
  Pallas kernels: 0 us -> 79.7 us
  waiting for transfers between devices: 43.1 us -> 4.34 us
  blocking collectives: 0 us -> 19.8 us
  matrix products: 12.6 us -> 0 us
  starting transfers between devices: 22.4 us -> 34.7 us
    pallas_call x0 -> x8, Pallas kernels: none -> 79.7 us  [the longest x1 34.3 us: stencil(): pl.pallas_call(stencil_kernel, out_shape=(jax.ShapeDtypeStruct((rows, col...]
    select_n x8 -> x0, other arithmetic: 53.2 us -> none  [the longest x1 18.8 us: advance(): jnp.where(wet, new_x, 0.0)]
    unnamed x33 -> x20, local copies, waits for them, and re-layouts: 37.9 us -> 2.24 us
    all_to_all x2, waiting for transfers between devices: 39.8 us -> 4.31 us  [the longest x1 4.31 us: body(): asked = lax.all_to_all(want, both, split_axis=0, concat_axis=0, tiled=True)]
    slice x11 -> x0, local copies, waits for them, and re-layouts: 30 us -> none  [the longest x1 12.7 us: snapshot_mix(): pairs[:, 0]]
    add x5 -> x0, other arithmetic: 23.5 us -> none  [the longest x4 23.5 us: waves(): part_h = s_one * alpha_one + s_three * alpha_three]
    all_to_all x0 -> x1, blocking collectives: none -> 19.8 us  [exchange(): got = lax.all_to_all(parts, both, split_axis=0, concat_axis=0, tiled=True)]
    squeeze x5 -> x0, local copies, waits for them, and re-layouts: 16.4 us -> none  [the longest x1 5.85 us: advance(): momy = padded[2]]
  transfers between devices with their start and end apart: 6 -> 10, of which waited for: 3 -> 1; matrix products, arithmetic and copies ran while one was open for 14% -> 0% of each run, Pallas kernels for 0% -> 43%
where the time goes in v1:
time: 146 us
  Pallas kernels  79.7 us (55%)
  starting transfers between devices  34.7 us (24%)
  blocking collectives  19.8 us (14%)
  local copies, waits for them, and re-layouts  4.75 us (3%)
  waiting for transfers between devices  4.34 us (3%)
  between operations  1.54 us (1%)
    pallas_call x1, Pallas kernels, stencil(): pl.pallas_call(stencil_kernel, out_shape=(jax.ShapeDtypeStruct((rows, col...  34.3 us
    ppermute x8, starting transfers between devices, send(): return lax.ppermute(value, axis, pairs)  24.6 us
    all_to_all x1, blocking collectives, exchange(): got = lax.all_to_all(parts, both, split_axis=0, concat_axis=0, tiled=True)  19.8 us
    pallas_call x1, Pallas kernels, wind_field(): pl.pallas_call(wind_kernel, grid=(steps,), out_shape=(shape, shape), in_s...  12.4 us
    pallas_call x1, Pallas kernels, gradient(): pl.pallas_call(gradient_kernel, out_shape=(grouped,) * 3, in_specs=[VMEM]...  12.3 us
    pallas_call x1, Pallas kernels, pressure_field(): pl.pallas_call(press_kernel, grid=(steps,), out_shape=jax.ShapeDtypeStruc...  9.01 us
    all_to_all x1, starting transfers between devices, body(): asked = lax.all_to_all(want, both, split_axis=0, concat_axis=0, tiled=True)  5.99 us
    pallas_call x1, Pallas kernels, edge_cells(): pl.pallas_call(edges_kernel, grid=(1,), out_shape=(line, line, column, co...  4.47 us
  transfers between devices with their start and end apart: 10, of which 1 were waited for; matrix products, arithmetic and copies ran while one was open for 0% of the time, Pallas kernels for 43%

profile of v1, /device:TPU:12, one launch (start us, length us, event | category | flops | bytes accessed | tf_op | source)
XLA Modules:
  0.0 145.5 jit_solution(1204877870036813349)
XLA Ops:
  0.6 1.7 %requests.1 = (s32[32,32]{1,0:T(8,128)}, s32[32,32]{1,0:T(8,128)}) custom-call(s32[1,512]{1,0:T(1,128)} %bitcast.27, s32[1,512]{1,0:T(1,128)} %bitcast.28, s32[1,512]{1,0:T(1,128)} %bitcast.29, s32[1,512]{1,0:T(1,128)} %bitcast.30), custom_call_target="tpu_custom_call" | custom-call | tf_op jit(solution)/shard_map/requests/pallas_call | solution.py:82
  2.3 6.0 %all-to-all-start = ((s32[32,1,32]{2,1,0:T(1,128)}), s32[32,1,32]{2,1,0:T(1,128)S(1)}, u32[]{:S(2)}, u32[]{:S(2)}) async-start(s32[32,1,32]{2,1,0:T(1,128)} %bitcast.26), calls=%async_computation | async-start | bytes 32768 | tf_op jit(solution)/shard_map/all_to_all | solution.py:633
  9.0 4.3 %all-to-all-done = s32[32,1,32]{2,1,0:T(1,128)S(1)} async-done(((s32[32,1,32]{2,1,0:T(1,128)}), s32[32,1,32]{2,1,0:T(1,128)S(1)}, u32[]{:S(2)}, u32[]{:S(2)}) %all-to-all-start) | async-done | bytes 4128 | tf_op jit(solution)/shard_map/all_to_all | solution.py:633
  13.8 0.7 reduce.3
  14.5 1.3 reshape.69.asked_ref
  15.8 2.9 %serve.1 = (bf16[1024,256]{1,0:T(8,128)(2,1)}, bf16[1024,512]{1,0:T(8,128)(2,1)}) custom-call(f32[1]{0:T(128)} %bitcast.18.blend_ref, s32[1024,1]{1,0:T(8,128)} %reshape.69.asked_ref, bf16[6,256,256]{2,1,0:T(8,128)(2,1)} %bitcast.24), custom_call_target="tpu_custom_call" | custom-call | tf_op jit(solution)/shard_map/serve/pallas_call | solution.py:112
  18.8 19.8 %all_to_all.19 = bf16[32,32,256]{2,1,0:T(8,128)(2,1)} all-to-all(bf16[32,32,256]{2,1,0:T(8,128)(2,1)} %bitcast.25), channel_id=1, replica_groups=mesh['gx'=4,'gy'=8] {'gx','gy'}, dimensions={0} | all-to-all | bytes 1048576 | tf_op jit(solution)/shard_map/all_to_all | solution.py:639
  38.5 4.2 %all-to-all-start.1 = ((bf16[32,32,512]{2,1,0:T(8,128)(2,1)}), bf16[32,32,512]{2,1,0:T(8,128)(2,1)S(1)}, u32[]{:S(2)}, u32[]{:S(2)}) async-start(bf16[32,32,512]{2,1,0:T(8,128)(2,1)} %bitcast.23), calls=%async_computation.1 | async-start | bytes 2097152 | tf_op jit(solution)/shard_map/all_to_all | solution.py:639
  42.7 4.5 %edges.1 = (f32[8,512]{1,0:T(8,128)}, f32[8,512]{1,0:T(8,128)}, f32[8,1024]{1,0:T(8,128)}, f32[8,1024]{1,0:T(8,128)}) custom-call(f32[1024,512]{1,0:T(8,128)} %d_ref.1, s32[1024,512]{1,0:T(8,128)} %m_ref.1, f32[1024,512]{1,0:T(8,128)} %x_ref.1, f32[1024,512]{1,0:T(8,128)} %y_ref.1, f32[1024,512]{1,0:T(8,128)} %d_ref.1, s32[1024,512]{1,0:T(8,128)} %m_ref.1, ...), custom_call_target="tpu_custom_call" | custom-call | tf_op jit(solution)/shard_map/edges/pallas_call | solution.py:165
  47.2 3.4 %collective-permute-start = (f32[8,512]{1,0:T(8,128)}, f32[8,512]{1,0:T(8,128)S(1)}, u32[]{:S(2)}, u32[]{:S(2)}) collective-permute-start(f32[8,512]{1,0:T(8,128)} %get-tuple-element.24), channel_id=1, source_target_pairs={{0,8},{8,16},{16,24},{1,9},{9,17},{17,25},{2,10},{10,18},{18,26},{... | collective-permute-start | bytes 49160 | tf_op jit(solution)/shard_map/ppermute | solution.py:187
  50.6 2.5 %collective-permute-start.1 = (f32[8,512]{1,0:T(8,128)}, f32[8,512]{1,0:T(8,128)S(1)}, u32[]{:S(2)}, u32[]{:S(2)}) collective-permute-start(f32[8,512]{1,0:T(8,128)} %get-tuple-element.25), channel_id=1, source_target_pairs={{8,0},{16,8},{24,16},{9,1},{17,9},{25,17},{10,2},{18,10},{26,18},{... | collective-permute-start | bytes 49160 | tf_op jit(solution)/shard_map/ppermute | solution.py:187
  53.0 1.9 %collective-permute-start.2 = (f32[8,1024]{1,0:T(8,128)}, f32[8,1024]{1,0:T(8,128)S(1)}, u32[]{:S(2)}, u32[]{:S(2)}) collective-permute-start(f32[8,1024]{1,0:T(8,128)} %get-tuple-element.26.ro_ref), channel_id=1, source_target_pairs={{0,1},{1,2},{2,3},{3,4},{4,5},{5,6},{6,7},{8,9},{9,10},{10,11},{11... | collective-permute-start | bytes 98312 | tf_op jit(solution)/shard_map/ppermute | solution.py:187
  55.0 4.5 %collective-permute-start.3 = (f32[8,1024]{1,0:T(8,128)}, f32[8,1024]{1,0:T(8,128)S(1)}, u32[]{:S(2)}, u32[]{:S(2)}) collective-permute-start(f32[8,1024]{1,0:T(8,128)} %get-tuple-element.27.lo_ref), channel_id=1, source_target_pairs={{1,0},{2,1},{3,2},{4,3},{5,4},{6,5},{7,6},{9,8},{10,9},{11,10},{12... | collective-permute-start | bytes 98312 | tf_op jit(solution)/shard_map/ppermute | solution.py:187
  59.5 0.7 reshape.58.lab_ref
  60.2 9.0 %pressure.1.p_ref = f32[4096,128]{1,0:T(8,128)} custom-call(s32[1,1024]{1,0:T(1,128)} %reshape.58.lab_ref, bf16[1024,256]{1,0:T(8,128)(2,1)} %bitcast.22, bf16[1024,4096]{1,0:T(8,128)(2,1)} %bitcast.19), custom_call_target="tpu_custom_call" | custom-call | flops 1073741824 | bytes 12582912 | tf_op jit(solution)/shard_map/pressure/pallas_call | solution.py:399
  69.2 2.6 %press_edges.1 = (f32[8,512]{1,0:T(8,128)}, f32[8,512]{1,0:T(8,128)}, f32[8,1024]{1,0:T(8,128)}, f32[8,1024]{1,0:T(8,128)}) custom-call(f32[4096,128]{1,0:T(8,128)} %pressure.1.p_ref), custom_call_target="tpu_custom_call" | custom-call | tf_op jit(solution)/shard_map/press_edges/pallas_call | solution.py:453
  71.8 1.9 %collective-permute-start.6 = (f32[8,1024]{1,0:T(8,128)}, f32[8,1024]{1,0:T(8,128)S(1)}, u32[]{:S(2)}, u32[]{:S(2)}) collective-permute-start(f32[8,1024]{1,0:T(8,128)} %get-tuple-element.38), channel_id=1, source_target_pairs={{0,1},{1,2},{2,3},{3,4},{4,5},{5,6},{6,7},{8,9},{9,10},{10,11},{11... | collective-permute-start | bytes 98312 | tf_op jit(solution)/shard_map/ppermute | solution.py:187
  73.7 4.5 %collective-permute-start.7 = (f32[8,1024]{1,0:T(8,128)}, f32[8,1024]{1,0:T(8,128)S(1)}, u32[]{:S(2)}, u32[]{:S(2)}) collective-permute-start(f32[8,1024]{1,0:T(8,128)} %get-tuple-element.39), channel_id=1, source_target_pairs={{1,0},{2,1},{3,2},{4,3},{5,4},{6,5},{7,6},{9,8},{10,9},{11,10},{12... | collective-permute-start | bytes 98312 | tf_op jit(solution)/shard_map/ppermute | solution.py:187
  78.3 3.4 %collective-permute-start.4 = (f32[8,512]{1,0:T(8,128)}, f32[8,512]{1,0:T(8,128)S(1)}, u32[]{:S(2)}, u32[]{:S(2)}) collective-permute-start(f32[8,512]{1,0:T(8,128)} %get-tuple-element.36), channel_id=1, source_target_pairs={{0,8},{8,16},{16,24},{1,9},{9,17},{17,25},{2,10},{10,18},{18,26},{... | collective-permute-start | bytes 49160 | tf_op jit(solution)/shard_map/ppermute | solution.py:187
  81.7 2.4 %collective-permute-start.5 = (f32[8,512]{1,0:T(8,128)}, f32[8,512]{1,0:T(8,128)S(1)}, u32[]{:S(2)}, u32[]{:S(2)}) collective-permute-start(f32[8,512]{1,0:T(8,128)} %get-tuple-element.37), channel_id=1, source_target_pairs={{8,0},{16,8},{24,16},{9,1},{17,9},{25,17},{10,2},{18,10},{26,18},{... | collective-permute-start | bytes 49160 | tf_op jit(solution)/shard_map/ppermute | solution.py:187
  84.8 34.3 %stencil.1 = (f32[1024,512]{1,0:T(8,128)}, f32[4096,128]{1,0:T(8,128)}, f32[4096,128]{1,0:T(8,128)}, f32[4096,128]{1,0:T(8,128)}) custom-call(f32[1024,512]{1,0:T(8,128)} %d_ref.1, s32[1024,512]{1,0:T(8,128)} %m_ref.1, f32[1024,512]{1,0:T(8,128)} %x_ref.1, f32[1024,512]{1,0:T(8,128)} %y_ref.1, f32[8,512]{1,0:T(8,128)} %copy-done.5, f32[8,512]{1,0:T(8,128)} %copy-done.6, ...), custom_call_target="tpu_custom_call" | custom-call | flops 104857600 | bytes 16777216 | tf_op jit(solution)/shard_map/stencil/pallas_call | solution.py:343
  119.8 12.3 %gradient.1 = (f32[4096,128]{1,0:T(8,128)}, f32[4096,128]{1,0:T(8,128)}, f32[4096,128]{1,0:T(8,128)}) custom-call(f32[4096,128]{1,0:T(8,128)} %pressure.1.p_ref, f32[4096,128]{1,0:T(8,128)} %get-tuple-element.33.hu_ref, f32[4096,128]{1,0:T(8,128)} %get-tuple-element.34.hv_ref, f32[4096,128]{1,0:T(8,128)} %get-tuple-element.35.h_ref, f32[8,512]{1,0:T(8,128)} %copy-done.7, ...), custom_call_target="tpu_custom_call" | custom-call | flops 10485760 | bytes 14680064 | tf_op jit(solution)/shard_map/gradient/pallas_call | solution.py:536
  132.1 1.0 copy-done
  133.1 12.4 %wind.1 = (f32[16,64,512]{2,1,0:T(8,128)}, f32[16,64,512]{2,1,0:T(8,128)}) custom-call(s32[1,1024]{1,0:T(1,128)} %reshape.58.lab_ref, bf16[1024,512]{1,0:T(8,128)(2,1)} %bitcast.21, bf16[1024,4096]{1,0:T(8,128)(2,1)} %bitcast.20, f32[4096,128]{1,0:T(8,128)} %get-tuple-element.40.hu_ref, f32[4096,128]{1,0:T(8,128)} %get-tuple-element.41.hv_ref, ...), custom_call_target="tpu_custom_call" | custom-call | flops 2147483648 | bytes 20971520 | tf_op jit(solution)/shard_map/wind/pallas_call | solution.py:587
  (29 shorter events, 1.8 us)
Async XLA Ops:
  2.3 11.0 %all-to-all-start = ((s32[32,1,32]{2,1,0:T(1,128)}), s32[32,1,32]{2,1,0:T(1,128)S(1)}, u32[]{:S(2)}, u32[]{:S(2)}) async-start(s32[32,1,32]{2,1,0:T(1,128)} %bitcast.26), calls=%async_computation | async-start | bytes 32768 | tf_op jit(solution)/shard_map/all_to_all | solution.py:633
  38.5 93.6 %all-to-all-start.1 = ((bf16[32,32,512]{2,1,0:T(8,128)(2,1)}), bf16[32,32,512]{2,1,0:T(8,128)(2,1)S(1)}, u32[]{:S(2)}, u32[]{:S(2)}) async-start(bf16[32,32,512]{2,1,0:T(8,128)(2,1)} %bitcast.23), calls=%async_computation.1 | async-start | bytes 2097152 | tf_op jit(solution)/shard_map/all_to_all | solution.py:639
  42.7 16.8 %copy-start.9 = (s32[32,32]{1,0:T(8,128)S(1)}, s32[32,32]{1,0:T(8,128)}, u32[]{:S(2)}) copy-start(s32[32,32]{1,0:T(8,128)} %get-tuple-element.29) | copy-start | bytes 12292
  47.2 26.5 %collective-permute-start = (f32[8,512]{1,0:T(8,128)}, f32[8,512]{1,0:T(8,128)S(1)}, u32[]{:S(2)}, u32[]{:S(2)}) collective-permute-start(f32[8,512]{1,0:T(8,128)} %get-tuple-element.24), channel_id=1, source_target_pairs={{0,8},{8,16},{16,24},{1,9},{9,17},{17,25},{2,10},{10,18},{18,26},{... | collective-permute-start | bytes 49160 | tf_op jit(solution)/shard_map/ppermute | solution.py:187
  50.6 27.7 %collective-permute-start.1 = (f32[8,512]{1,0:T(8,128)}, f32[8,512]{1,0:T(8,128)S(1)}, u32[]{:S(2)}, u32[]{:S(2)}) collective-permute-start(f32[8,512]{1,0:T(8,128)} %get-tuple-element.25), channel_id=1, source_target_pairs={{8,0},{16,8},{24,16},{9,1},{17,9},{25,17},{10,2},{18,10},{26,18},{... | collective-permute-start | bytes 49160 | tf_op jit(solution)/shard_map/ppermute | solution.py:187
  53.0 28.6 %collective-permute-start.2 = (f32[8,1024]{1,0:T(8,128)}, f32[8,1024]{1,0:T(8,128)S(1)}, u32[]{:S(2)}, u32[]{:S(2)}) collective-permute-start(f32[8,1024]{1,0:T(8,128)} %get-tuple-element.26.ro_ref), channel_id=1, source_target_pairs={{0,1},{1,2},{2,3},{3,4},{4,5},{5,6},{6,7},{8,9},{9,10},{10,11},{11... | collective-permute-start | bytes 98312 | tf_op jit(solution)/shard_map/ppermute | solution.py:187
  55.0 29.2 %collective-permute-start.3 = (f32[8,1024]{1,0:T(8,128)}, f32[8,1024]{1,0:T(8,128)S(1)}, u32[]{:S(2)}, u32[]{:S(2)}) collective-permute-start(f32[8,1024]{1,0:T(8,128)} %get-tuple-element.27.lo_ref), channel_id=1, source_target_pairs={{1,0},{2,1},{3,2},{4,3},{5,4},{6,5},{7,6},{9,8},{10,9},{11,10},{12... | collective-permute-start | bytes 98312 | tf_op jit(solution)/shard_map/ppermute | solution.py:187
  71.8 47.3 %collective-permute-start.6 = (f32[8,1024]{1,0:T(8,128)}, f32[8,1024]{1,0:T(8,128)S(1)}, u32[]{:S(2)}, u32[]{:S(2)}) collective-permute-start(f32[8,1024]{1,0:T(8,128)} %get-tuple-element.38), channel_id=1, source_target_pairs={{0,1},{1,2},{2,3},{3,4},{4,5},{5,6},{6,7},{8,9},{9,10},{10,11},{11... | collective-permute-start | bytes 98312 | tf_op jit(solution)/shard_map/ppermute | solution.py:187
  73.7 10.5 %copy-start.5 = (f32[8,512]{1,0:T(8,128)}, f32[8,512]{1,0:T(8,128)S(1)}, u32[]{:S(2)}) copy-start(f32[8,512]{1,0:T(8,128)S(1)} %collective-permute-done.up_ref) | copy-start | bytes 49156
  73.7 45.4 %collective-permute-start.7 = (f32[8,1024]{1,0:T(8,128)}, f32[8,1024]{1,0:T(8,128)S(1)}, u32[]{:S(2)}, u32[]{:S(2)}) collective-permute-start(f32[8,1024]{1,0:T(8,128)} %get-tuple-element.39), channel_id=1, source_target_pairs={{1,0},{2,1},{3,2},{4,3},{5,4},{6,5},{7,6},{9,8},{10,9},{11,10},{12... | collective-permute-start | bytes 98312 | tf_op jit(solution)/shard_map/ppermute | solution.py:187
  78.3 5.9 %copy-start.6 = (f32[8,512]{1,0:T(8,128)}, f32[8,512]{1,0:T(8,128)S(1)}, u32[]{:S(2)}) copy-start(f32[8,512]{1,0:T(8,128)S(1)} %collective-permute-done.1.dn_ref) | copy-start | bytes 49156
  78.3 40.8 %collective-permute-start.4 = (f32[8,512]{1,0:T(8,128)}, f32[8,512]{1,0:T(8,128)S(1)}, u32[]{:S(2)}, u32[]{:S(2)}) collective-permute-start(f32[8,512]{1,0:T(8,128)} %get-tuple-element.36), channel_id=1, source_target_pairs={{0,8},{8,16},{16,24},{1,9},{9,17},{17,25},{2,10},{10,18},{18,26},{... | collective-permute-start | bytes 49160 | tf_op jit(solution)/shard_map/ppermute | solution.py:187
  81.7 2.5 %copy-start.2 = (f32[8,1024]{1,0:T(8,128)}, f32[8,1024]{1,0:T(8,128)S(1)}, u32[]{:S(2)}) copy-start(f32[8,1024]{1,0:T(8,128)S(1)} %collective-permute-done.2.lh_ref) | copy-start | bytes 98308
  81.7 37.4 %collective-permute-start.5 = (f32[8,512]{1,0:T(8,128)}, f32[8,512]{1,0:T(8,128)S(1)}, u32[]{:S(2)}, u32[]{:S(2)}) collective-permute-start(f32[8,512]{1,0:T(8,128)} %get-tuple-element.37), channel_id=1, source_target_pairs={{8,0},{16,8},{24,16},{9,1},{17,9},{25,17},{10,2},{18,10},{26,18},{... | collective-permute-start | bytes 49160 | tf_op jit(solution)/shard_map/ppermute | solution.py:187
  84.2 0.6 copy-start.4
  119.1 0.6 copy-start.7
  119.1 0.6 copy-start.8
  119.1 0.6 copy-start.1
  119.2 0.6 copy-start.3
  132.1 1.0 copy-start

commit v2 on v1

--- a/solution.py
+++ b/solution.py
@@ -39,16 +39,36 @@
     return lax.broadcasted_iota(jnp.int32, shape, dim)
 
 
-def rank_kernel(capacity, src_ref, blk_ref, pat_ref, wgt_ref, want_ref, lab_ref):
-    devices = want_ref.shape[0]
-    src = src_ref[...]
-    ent = src.shape[1]
-    hits = (iota((devices, ent), 0) == src).astype(F32)
-    order = (iota((ent, ent), 0) <= iota((ent, ent), 1)).astype(BF16)
-    ranks = jnp.dot(hits.astype(BF16), order, preferred_element_type=F32)
-    mine = jnp.sum(hits * ranks, axis=0, keepdims=True).astype(jnp.int32) - 1
-    place = iota((capacity, ent), 0) == mine
-    pat = pat_ref[...]
+def mix_kernel(blend_ref, atm_ref, press_ref, wind_ref):
+    blend = blend_ref[0]
+    keep = 1.0 - blend
+
+    def mixed(k):
+        first = atm_ref[k].astype(F32)
+        second = atm_ref[3 + k].astype(F32)
+        return (keep * first + blend * second).astype(BF16)
+
+    press_ref[...] = mixed(2)
+    for k in range(2):
+        wind_ref[:, k * ABLK:(k + 1) * ABLK] = mixed(k)
+
+
+def mix(blend, atm):
+    blocks = atm.shape[1]
+    return pl.pallas_call(
+        mix_kernel,
+        out_shape=(
+            jax.ShapeDtypeStruct((blocks, ABLK), BF16),
+            jax.ShapeDtypeStruct((blocks, 2 * ABLK), BF16),
+        ),
+        in_specs=[SMEM, VMEM],
+        out_specs=(VMEM, VMEM),
+        compiler_params=params(),
+        name="mix",
+    )(blend, atm)
+
+
+def morton_slot(pat):
     row_bits = BPX.bit_length() - 1
     col_bits = BPY.bit_length() - 1
     rows = jnp.zeros_like(pat)
@@ -63,63 +83,63 @@
             cols = cols + value * (1 << used_c)
             used_c += 1
         position += 1
-
-    def spread(row):
-        picked = jnp.where(place, row.astype(F32), 0.0).astype(BF16)
-        return lax.dot_general(
-            hits.astype(BF16), picked, (((1,), (1,)), ((), ())),
-            preferred_element_type=F32,
-        ).astype(jnp.int32)
-
-    want_ref[...] = spread(blk_ref[...])
-    slot = spread(cols * BPX + rows)
-    group = spread(wgt_ref[...] + 1)
-    lab_ref[...] = jnp.where(group > 0, (group - 1) * NPATCH + slot, -1)
-
-
-def make_requests(src, blk, pat, wgt, devices, capacity):
-    shape = jax.ShapeDtypeStruct((devices, capacity), jnp.int32)
-    return pl.pallas_call(
-        functools.partial(rank_kernel, capacity),
-        out_shape=(shape, shape),
-        in_specs=[VMEM] * 4,
-        out_specs=(VMEM, VMEM),
-        compiler_params=params(),
-        name="requests",
-    )(src, blk, pat, wgt)
-
-
-def serve_kernel(blend_ref, asked_ref, atm_ref, press_ref, wind_ref):
-    blend = blend_ref[0]
-    keep = 1.0 - blend
-    asked = asked_ref[...]
-    pick = (asked == iota((asked.shape[0], atm_ref.shape[1]), 1)).astype(BF16)
-
-    def mixed(k):
-        first = atm_ref[k].astype(F32)
-        second = atm_ref[3 + k].astype(F32)
-        return (keep * first + blend * second).astype(BF16)
-
-    press_ref[...] = jnp.dot(pick, mixed(2), preferred_element_type=F32).astype(BF16)
-    for k in range(2):
-        wind_ref[:, k * ABLK:(k + 1) * ABLK] = jnp.dot(
-            pick, mixed(k), preferred_element_type=F32
-        ).astype(BF16)
-
-
-def serve(blend, asked, atm):
-    slots = asked.shape[0]
-    return pl.pallas_call(
-        serve_kernel,
-        out_shape=(
-            jax.ShapeDtypeStruct((slots, ABLK), BF16),
-            jax.ShapeDtypeStruct((slots, 2 * ABLK), BF16),
-        ),
-        in_specs=[SMEM, VMEM, VMEM],
-        out_specs=(VMEM, VMEM),
-        compiler_params=params(),
-        name="serve",
-    )(blend, asked, atm)
+    return cols * BPX + rows
+
+
+STEP = 2048
+
+
+def count_kernel(lab_ref, block_ref, out_ref):
+    ent = lab_ref.shape[1]
+    labels = (iota((NW * NPATCH, ent), 0) == lab_ref[...]).astype(BF16)
+    base = pl.program_id(0) * STEP
+    blocks = (iota((ent, STEP), 1) + base == block_ref[...]).astype(BF16)
+    out_ref[...] = jnp.dot(labels, blocks, preferred_element_type=F32).astype(BF16)
+
+
+def count_matrix(lab, block, total):
+    ent = lab.shape[1]
+    return pl.pallas_call(
+        count_kernel,
+        grid=(total // STEP,),
+        out_shape=jax.ShapeDtypeStruct((NW * NPATCH, total), BF16),
+        in_specs=[pl.BlockSpec((1, ent), lambda i: (0, 0)), pl.BlockSpec((ent, 1), lambda i: (0, 0))],
+        out_specs=pl.BlockSpec((NW * NPATCH, STEP), lambda i: (0, i)),
+        compiler_params=params(),
+        name="counts",
+    )(lab, block)
+
+
+def sum_kernel(s_ref, tiles_ref, out_ref, acc):
+    at = pl.program_id(0)
+
+    @pl.when(at == 0)
+    def _():
+        acc[...] = jnp.zeros_like(acc)
+
+    acc[...] += jnp.dot(s_ref[...], tiles_ref[...], preferred_element_type=F32)
+
+    @pl.when(at == pl.num_programs(0) - 1)
+    def _():
+        out_ref[...] = acc[...].astype(BF16)
+
+
+def summed_blocks(counts, tiles):
+    total, width = tiles.shape
+    labels = counts.shape[0]
+    return pl.pallas_call(
+        sum_kernel,
+        grid=(total // STEP,),
+        out_shape=jax.ShapeDtypeStruct((labels, width), BF16),
+        in_specs=[
+            pl.BlockSpec((labels, STEP), lambda i: (0, i)),
+            pl.BlockSpec((STEP, width), lambda i: (i, 0)),
+        ],
+        out_specs=pl.BlockSpec((labels, width), lambda i: (0, 0)),
+        scratch_shapes=[pltpu.VMEM((labels, width), F32)],
+        compiler_params=params(),
+        name="summed",
+    )(counts, tiles)
 
 
 def edges_kernel(
@@ -352,11 +372,6 @@
     )(depth, mask, momx, momy, up, dn, lh, rh, lo, ro)
 
 
-def summed_of(lab, landed):
-    select = (iota((NW * NPATCH, lab.shape[1]), 0) == lab).astype(BF16)
-    return jnp.dot(select, landed, preferred_element_type=F32).astype(BF16)
-
-
 def stack_left(left, summed, channels):
     for k in range(channels):
         for w in range(NW):
@@ -376,10 +391,10 @@
     )
 
 
-def press_kernel(lab_ref, landed_ref, w_ref, out_ref, left, acc):
+def press_kernel(summed_ref, w_ref, out_ref, left, acc):
     @pl.when(pl.program_id(0) == 0)
     def _():
-        stack_left(left, summed_of(lab_ref[...], landed_ref[...]), 1)
+        stack_left(left, summed_ref, 1)
 
     acc[...] = jnp.dot(left[...], w_ref[...], preferred_element_type=F32)
     low = iota((TILE, LANES), 1) < LANES // 2
@@ -392,7 +407,7 @@
                     out_ref[at:at + TILE, :] = pair[odd]
 
 
-def pressure_field(lab, landed, weights):
+def pressure_field(summed, weights):
     steps = PATCH // TILE
     chunk = TILE * PATCH
     cells = PATCH * SLAB
@@ -401,8 +416,7 @@
         grid=(steps,),
         out_shape=jax.ShapeDtypeStruct((cells, LANES), F32),
         in_specs=[
-            pl.BlockSpec(lab.shape, lambda i: (0, 0)),
-            pl.BlockSpec(landed.shape, lambda i: (0, 0)),
+            pl.BlockSpec(summed.shape, lambda i: (0, 0)),
             pl.BlockSpec((NW * ABLK, chunk), lambda i: (0, i)),
         ],
         out_specs=pl.BlockSpec((cells // steps, LANES), lambda i: (i, 0)),
@@ -415,7 +429,7 @@
             flops=2 * NPATCH * NW * ABLK * PATCH * PATCH, bytes_accessed=12 << 20, transcendentals=0
         ),
         name="pressure",
-    )(lab, landed, weights)
+    )(summed, weights)
 
 
 def press_edges_kernel(p_ref, top_ref, bottom_ref, left_ref, right_ref):
@@ -550,10 +564,10 @@
     )(p, hu, hv, h, up, dn, lh, rh)
 
 
-def wind_kernel(lab_ref, landed_ref, w_ref, hu_ref, hv_ref, fac_ref, ox_ref, oy_ref, left, acc, sx, sy):
+def wind_kernel(summed_ref, w_ref, hu_ref, hv_ref, fac_ref, ox_ref, oy_ref, left, acc, sx, sy):
     @pl.when(pl.program_id(0) == 0)
     def _():
-        stack_left(left, summed_of(lab_ref[...], landed_ref[...]), 2)
+        stack_left(left, summed_ref, 2)
 
     acc[...] = jnp.dot(left[...], w_ref[...], preferred_element_type=F32)
     low = iota((TILE, LANES), 1) < LANES // 2
@@ -577,7 +591,7 @@
                 dst[r, :, g * LANES:(g + 1) * LANES] = src[g, r * TILE:(r + 1) * TILE, :]
 
 
-def wind_field(lab, landed, weights, hu, hv, fac):
+def wind_field(summed, weights, hu, hv, fac):
     steps = PATCH // TILE
     chunk = TILE * PATCH
     cols = BPY * PATCH
@@ -589,8 +603,7 @@
         grid=(steps,),
         out_shape=(shape, shape),
         in_specs=[
-            pl.BlockSpec(lab.shape, lambda i: (0, 0)),
-            pl.BlockSpec(landed.shape, lambda i: (0, 0)),
+            pl.BlockSpec(summed.shape, lambda i: (0, 0)),
             pl.BlockSpec((NW * ABLK, chunk), lambda i: (0, i)),
             slab, slab, slab,
         ],
@@ -606,7 +619,7 @@
             flops=4 * NPATCH * NW * ABLK * PATCH * PATCH, bytes_accessed=20 << 20, transcendentals=0
         ),
         name="wind",
-    )(lab, landed, weights, hu, hv, fac)
+    )(summed, weights, hu, hv, fac)
 
 
 def body(
@@ -624,24 +637,15 @@
 ):
     devices = lax.axis_size("gx") * lax.axis_size("gy")
     entries = ovl_source.size
-    capacity = 2 * entries // devices
     both = ("gx", "gy")
-    want, lab = make_requests(
-        ovl_source.reshape(1, entries), ovl_block.reshape(1, entries),
-        ovl_patch.reshape(1, entries), ovl_weight.reshape(1, entries), devices, capacity,
-    )
-    asked = lax.all_to_all(want, both, split_axis=0, concat_axis=0, tiled=True)
     atm = atm_blocks.reshape(atm_blocks.shape[2:]).transpose(1, 0, 2)
-    press, wind = serve(blend.reshape(1), asked.reshape(devices * capacity, 1), atm)
-
-    def exchange(rows):
-        parts = rows.reshape(devices, capacity, rows.shape[1])
-        got = lax.all_to_all(parts, both, split_axis=0, concat_axis=0, tiled=True)
-        return got.reshape(rows.shape)
-
-    press = exchange(press)
-    wind = exchange(wind)
-    lab = lab.reshape(1, devices * capacity)
+    blocks = atm.shape[1]
+    press, wind = mix(blend.reshape(1), atm)
+    press = lax.all_gather(press, both, axis=0, tiled=True)
+    wind = lax.all_gather(wind, both, axis=0, tiled=True)
+    lab = ovl_weight.reshape(1, entries) * NPATCH + morton_slot(ovl_patch.reshape(1, entries))
+    block = ovl_source.reshape(entries, 1) * blocks + ovl_block.reshape(entries, 1)
+    counts = count_matrix(lab, block, devices * blocks)
 
     top, bottom, left, right = edge_cells(depth_field, wet_mask, mom_x, mom_y)
     newh, hu, hv, h = stencil(
@@ -650,14 +654,14 @@
         send(right, "gy", 1), send(left, "gy", -1), left, right,
     )
     weights = remap_weights.reshape(NW * ABLK, PATCH * PATCH)
-    p = pressure_field(lab, press, weights)
+    p = pressure_field(summed_blocks(counts, press), weights)
     top, bottom, left, right = press_edges(p)
     hu, hv, fac = gradient(
         p, hu, hv, h,
         send(bottom, "gx", 1), send(top, "gx", -1),
         send(right, "gy", 1), send(left, "gy", -1),
     )
-    new_x, new_y = wind_field(lab, wind, weights, hu, hv, fac)
+    new_x, new_y = wind_field(summed_blocks(counts, wind), weights, hu, hv, fac)
     return (newh, new_x.reshape(newh.shape), new_y.reshape(newh.shape))
 
 

time: 146 us -> 184 us (1.26)
  waiting for transfers between devices: 4.34 us -> 39 us
  Pallas kernels: 79.7 us -> 101 us
  blocking collectives: 19.8 us -> 0 us
  between operations: 1.54 us -> 15 us
  starting transfers between devices: 34.7 us -> 24.7 us
  local copies, waits for them, and re-layouts: 4.75 us -> 2.09 us
    all_gather x0 -> x2, waiting for transfers between devices: none -> 38.3 us  [the longest x1 38.1 us: body(): press = lax.all_gather(press, both, axis=0, tiled=True)]
    pallas_call x2 -> x4, Pallas kernels: 4.64 us -> 26.1 us  [the longest x2 16.4 us: summed_blocks(): pl.pallas_call(sum_kernel, grid=(total // STEP,), out_shape=jax.ShapeDtyp...]
    all_to_all x1 -> x0, blocking collectives: 19.8 us -> none  [exchange(): got = lax.all_to_all(parts, both, split_axis=0, concat_axis=0, tiled=True)]
    all_to_all x2 -> x0, starting transfers between devices: 10.2 us -> none  [the longest x1 5.99 us: body(): asked = lax.all_to_all(want, both, split_axis=0, concat_axis=0, tiled=True)]
    all_to_all x2 -> x0, waiting for transfers between devices: 4.31 us -> none  [the longest x1 4.31 us: body(): asked = lax.all_to_all(want, both, split_axis=0, concat_axis=0, tiled=True)]
    reshape x2 -> x0, local copies, waits for them, and re-layouts: 2.01 us -> none  [the longest x1 1.33 us: body(): asked.reshape(devices * capacity, 1)]
  transfers between devices with their start and end apart: 10 -> 10, of which waited for: 1 -> 2; matrix products, arithmetic and copies ran while one was open for 0% -> 1% of each run, Pallas kernels for 43% -> 43%
where the time goes in v2:
time: 184 us; the launch traced here: 182 us
  Pallas kernels  101 us (55%)
  waiting for transfers between devices  39 us (21%)
  starting transfers between devices  24.7 us (13%)
  between operations  15 us (8%)
  local copies, waits for them, and re-layouts  2.09 us (1%)
    all_gather x1, waiting for transfers between devices, body(): press = lax.all_gather(press, both, axis=0, tiled=True)  38.1 us
    pallas_call x1, Pallas kernels, stencil(): pl.pallas_call(stencil_kernel, out_shape=(jax.ShapeDtypeStruct((rows, col...  34.3 us
    ppermute x8, starting transfers between devices, send(): return lax.ppermute(value, axis, pairs)  24.6 us
    pallas_call x2, Pallas kernels, summed_blocks(): pl.pallas_call(sum_kernel, grid=(total // STEP,), out_shape=jax.ShapeDtyp...  16.4 us
    pallas_call x1, Pallas kernels, gradient(): pl.pallas_call(gradient_kernel, out_shape=(grouped,) * 3, in_specs=[VMEM]...  12.6 us
    pallas_call x1, Pallas kernels, wind_field(): pl.pallas_call(wind_kernel, grid=(steps,), out_shape=(shape, shape), in_s...  11.9 us
    pallas_call x1, Pallas kernels, pressure_field(): pl.pallas_call(press_kernel, grid=(steps,), out_shape=jax.ShapeDtypeStruc...  8.57 us
    pallas_call x1, Pallas kernels, count_matrix(): pl.pallas_call(count_kernel, grid=(total // STEP,), out_shape=jax.ShapeDt...  7.72 us
  transfers between devices with their start and end apart: 10, of which 2 were waited for; matrix products, arithmetic and copies ran while one was open for 1% of the time, Pallas kernels for 43%

profile of v2, /device:TPU:12, one launch (start us, length us, event | category | flops | bytes accessed | tf_op | source)
XLA Modules:
  0.0 181.9 jit_solution(15284476485616119221)
XLA Ops:
  7.9 2.0 %mix.1 = (bf16[256,256]{1,0:T(8,128)(2,1)}, bf16[256,512]{1,0:T(8,128)(2,1)}) custom-call(f32[1]{0:T(128)} %bitcast.13.blend_ref, bf16[6,256,256]{2,1,0:T(8,128)(2,1)} %bitcast.16), custom_call_target="tpu_custom_call" | custom-call | tf_op jit(solution)/shard_map/mix/pallas_call | solution.py:58
  9.9 0.7 all-gather.3.cloned.1.call-update
  10.7 4.5 %edges.1 = (f32[8,512]{1,0:T(8,128)}, f32[8,512]{1,0:T(8,128)}, f32[8,1024]{1,0:T(8,128)}, f32[8,1024]{1,0:T(8,128)}) custom-call(f32[1024,512]{1,0:T(8,128)} %d_ref.1, s32[1024,512]{1,0:T(8,128)} %m_ref.1, f32[1024,512]{1,0:T(8,128)} %x_ref.1, f32[1024,512]{1,0:T(8,128)} %y_ref.1, f32[1024,512]{1,0:T(8,128)} %d_ref.1, s32[1024,512]{1,0:T(8,128)} %m_ref.1, ...), custom_call_target="tpu_custom_call" | custom-call | tf_op jit(solution)/shard_map/edges/pallas_call | solution.py:185
  15.1 3.5 %collective-permute-start = (f32[8,512]{1,0:T(8,128)}, f32[8,512]{1,0:T(8,128)S(1)}, u32[]{:S(2)}, u32[]{:S(2)}) collective-permute-start(f32[8,512]{1,0:T(8,128)} %get-tuple-element.22), channel_id=1, source_target_pairs={{0,8},{8,16},{16,24},{1,9},{9,17},{17,25},{2,10},{10,18},{18,26},{... | collective-permute-start | bytes 49160 | tf_op jit(solution)/shard_map/ppermute | solution.py:207
  18.6 2.4 %collective-permute-start.1 = (f32[8,512]{1,0:T(8,128)}, f32[8,512]{1,0:T(8,128)S(1)}, u32[]{:S(2)}, u32[]{:S(2)}) collective-permute-start(f32[8,512]{1,0:T(8,128)} %get-tuple-element.23), channel_id=1, source_target_pairs={{8,0},{16,8},{24,16},{9,1},{17,9},{25,17},{10,2},{18,10},{26,18},{... | collective-permute-start | bytes 49160 | tf_op jit(solution)/shard_map/ppermute | solution.py:207
  21.0 1.9 %collective-permute-start.2 = (f32[8,1024]{1,0:T(8,128)}, f32[8,1024]{1,0:T(8,128)S(1)}, u32[]{:S(2)}, u32[]{:S(2)}) collective-permute-start(f32[8,1024]{1,0:T(8,128)} %get-tuple-element.24.ro_ref), channel_id=1, source_target_pairs={{0,1},{1,2},{2,3},{3,4},{4,5},{5,6},{6,7},{8,9},{9,10},{10,11},{11... | collective-permute-start | bytes 98312 | tf_op jit(solution)/shard_map/ppermute | solution.py:207
  22.9 4.5 %collective-permute-start.3 = (f32[8,1024]{1,0:T(8,128)}, f32[8,1024]{1,0:T(8,128)S(1)}, u32[]{:S(2)}, u32[]{:S(2)}) collective-permute-start(f32[8,1024]{1,0:T(8,128)} %get-tuple-element.25.lo_ref), channel_id=1, source_target_pairs={{1,0},{2,1},{3,2},{4,3},{5,4},{6,5},{7,6},{9,8},{10,9},{11,10},{12... | collective-permute-start | bytes 98312 | tf_op jit(solution)/shard_map/ppermute | solution.py:207
  27.5 0.9 copy.16.block_ref
  28.3 0.6 add_bitcast_fusion.lab_ref
  28.9 7.7 %counts.1.s_ref = bf16[512,8192]{1,0:T(8,128)(2,1)} custom-call(s32[1,512]{1,0:T(1,128)} %add_bitcast_fusion.lab_ref, s32[512,1]{1,0:T(8,128)} %copy.16.block_ref), custom_call_target="tpu_custom_call" | custom-call | tf_op jit(solution)/shard_map/counts/pallas_call | solution.py:102
  36.7 38.1 %all-gather.5.cloned.1.call-done.tiles_ref = bf16[8192,256]{1,0:T(8,128)(2,1)} async-done(((bf16[256,256]{1,0:T(8,128)(2,1)}), bf16[8192,256]{1,0:T(8,128)(2,1)}) %all-gather.5.cloned.1.call-update) | async-done | bytes 4194320 | tf_op jit(solution)/shard_map/all_gather | solution.py:644
  74.8 7.1 %summed.3.summed_ref = bf16[512,256]{1,0:T(8,128)(2,1)} custom-call(bf16[512,8192]{1,0:T(8,128)(2,1)} %counts.1.s_ref, bf16[8192,256]{1,0:T(8,128)(2,1)} %all-gather.5.cloned.1.call-done.tiles_ref), custom_call_target="tpu_custom_call" | custom-call | tf_op jit(solution)/shard_map/summed/pallas_call | solution.py:130
  81.8 8.6 %pressure.1.p_ref = f32[4096,128]{1,0:T(8,128)} custom-call(bf16[512,256]{1,0:T(8,128)(2,1)} %summed.3.summed_ref, bf16[1024,4096]{1,0:T(8,128)(2,1)} %bitcast.14), custom_call_target="tpu_custom_call" | custom-call | flops 1073741824 | bytes 12582912 | tf_op jit(solution)/shard_map/pressure/pallas_call | solution.py:414
  90.4 2.6 %press_edges.1 = (f32[8,512]{1,0:T(8,128)}, f32[8,512]{1,0:T(8,128)}, f32[8,1024]{1,0:T(8,128)}, f32[8,1024]{1,0:T(8,128)}) custom-call(f32[4096,128]{1,0:T(8,128)} %pressure.1.p_ref), custom_call_target="tpu_custom_call" | custom-call | tf_op jit(solution)/shard_map/press_edges/pallas_call | solution.py:467
  93.0 2.1 %collective-permute-start.6 = (f32[8,1024]{1,0:T(8,128)}, f32[8,1024]{1,0:T(8,128)S(1)}, u32[]{:S(2)}, u32[]{:S(2)}) collective-permute-start(f32[8,1024]{1,0:T(8,128)} %get-tuple-element.34), channel_id=1, source_target_pairs={{0,1},{1,2},{2,3},{3,4},{4,5},{5,6},{6,7},{8,9},{9,10},{10,11},{11... | collective-permute-start | bytes 98312 | tf_op jit(solution)/shard_map/ppermute | solution.py:207
  95.1 4.3 %collective-permute-start.7 = (f32[8,1024]{1,0:T(8,128)}, f32[8,1024]{1,0:T(8,128)S(1)}, u32[]{:S(2)}, u32[]{:S(2)}) collective-permute-start(f32[8,1024]{1,0:T(8,128)} %get-tuple-element.35), channel_id=1, source_target_pairs={{1,0},{2,1},{3,2},{4,3},{5,4},{6,5},{7,6},{9,8},{10,9},{11,10},{12... | collective-permute-start | bytes 98312 | tf_op jit(solution)/shard_map/ppermute | solution.py:207
  99.5 2.7 %collective-permute-start.4 = (f32[8,512]{1,0:T(8,128)}, f32[8,512]{1,0:T(8,128)S(1)}, u32[]{:S(2)}, u32[]{:S(2)}) collective-permute-start(f32[8,512]{1,0:T(8,128)} %get-tuple-element.32), channel_id=1, source_target_pairs={{0,8},{8,16},{16,24},{1,9},{9,17},{17,25},{2,10},{10,18},{18,26},{... | collective-permute-start | bytes 49160 | tf_op jit(solution)/shard_map/ppermute | solution.py:207
  102.2 3.2 %collective-permute-start.5 = (f32[8,512]{1,0:T(8,128)}, f32[8,512]{1,0:T(8,128)S(1)}, u32[]{:S(2)}, u32[]{:S(2)}) collective-permute-start(f32[8,512]{1,0:T(8,128)} %get-tuple-element.33), channel_id=1, source_target_pairs={{8,0},{16,8},{24,16},{9,1},{17,9},{25,17},{10,2},{18,10},{26,18},{... | collective-permute-start | bytes 49160 | tf_op jit(solution)/shard_map/ppermute | solution.py:207
  105.4 0.6 copy-done.1
  106.0 34.3 %stencil.1 = (f32[1024,512]{1,0:T(8,128)}, f32[4096,128]{1,0:T(8,128)}, f32[4096,128]{1,0:T(8,128)}, f32[4096,128]{1,0:T(8,128)}) custom-call(f32[1024,512]{1,0:T(8,128)} %d_ref.1, s32[1024,512]{1,0:T(8,128)} %m_ref.1, f32[1024,512]{1,0:T(8,128)} %x_ref.1, f32[1024,512]{1,0:T(8,128)} %y_ref.1, f32[8,512]{1,0:T(8,128)} %copy-done.4, f32[8,512]{1,0:T(8,128)} %copy-done.5, ...), custom_call_target="tpu_custom_call" | custom-call | flops 104857600 | bytes 16777216 | tf_op jit(solution)/shard_map/stencil/pallas_call | solution.py:363
  140.4 0.5 copy-done.6
  141.0 12.6 %gradient.1 = (f32[4096,128]{1,0:T(8,128)}, f32[4096,128]{1,0:T(8,128)}, f32[4096,128]{1,0:T(8,128)}) custom-call(f32[4096,128]{1,0:T(8,128)} %pressure.1.p_ref, f32[4096,128]{1,0:T(8,128)} %get-tuple-element.29.hu_ref, f32[4096,128]{1,0:T(8,128)} %get-tuple-element.30.hv_ref, f32[4096,128]{1,0:T(8,128)} %get-tuple-element.31.h_ref, f32[8,512]{1,0:T(8,128)} %copy-done.6, ...), custom_call_target="tpu_custom_call" | custom-call | flops 10485760 | bytes 14680064 | tf_op jit(solution)/shard_map/gradient/pallas_call | solution.py:550
  153.8 9.4 %summed.2.summed_ref = bf16[512,512]{1,0:T(8,128)(2,1)} custom-call(bf16[512,8192]{1,0:T(8,128)(2,1)} %counts.1.s_ref, bf16[8192,512]{1,0:T(8,128)(2,1)} %all-gather.3.cloned.1.call-done.tiles_ref), custom_call_target="tpu_custom_call" | custom-call | tf_op jit(solution)/shard_map/summed/pallas_call | solution.py:130
  163.2 11.9 %wind.1 = (f32[16,64,512]{2,1,0:T(8,128)}, f32[16,64,512]{2,1,0:T(8,128)}) custom-call(bf16[512,512]{1,0:T(8,128)(2,1)} %summed.2.summed_ref, bf16[1024,4096]{1,0:T(8,128)(2,1)} %bitcast.15, f32[4096,128]{1,0:T(8,128)} %get-tuple-element.36.hu_ref, f32[4096,128]{1,0:T(8,128)} %get-tuple-element.37.hv_ref, f32[4096,128]{1,0:T(8,128)} %get-tuple-element.38.fac_ref), custom_call_target="tpu_custom_call" | custom-call | flops 2147483648 | bytes 20971520 | tf_op jit(solution)/shard_map/wind/pallas_call | solution.py:601
  (35 shorter events, 0.4 us)
Async XLA Ops:
  7.2 67.6 %all-gather.5.cloned.1.call-start = ((), (), s32[]{:S(2)}) async-start(), calls=%async_computation.1 | async-start | bytes 4325376 | tf_op jit(solution)/shard_map/all_gather | solution.py:644
  9.9 143.9 %all-gather.3.cloned.1.call-start = ((), (), s32[]{:S(2)}) async-start(), calls=%async_computation | async-start | bytes 8650752 | tf_op jit(solution)/shard_map/all_gather | solution.py:645
  10.6 16.8 %copy-start.8 = (s32[1,1,512]{2,1,0:T(1,128)S(1)}, s32[1,1,512]{2,1,0:T(1,128)}, u32[]{:S(2)}) copy-start(s32[1,1,512]{2,1,0:T(1,128)} %param.14) | copy-start | bytes 6148
  10.6 16.8 %copy-start.9 = (s32[1,1,512,1]{2,3,1,0:T(1,128)S(1)}, s32[1,1,512,1]{2,3,1,0:T(1,128)}, u32[]{:S(2)}) copy-start(s32[1,1,512,1]{2,3,1,0:T(1,128)} %param.13) | copy-start | bytes 6148
  10.6 17.7 %copy-start.10 = (s32[1,1,512]{2,1,0:T(1,128)S(1)}, s32[1,1,512]{2,1,0:T(1,128)}, u32[]{:S(2)}) copy-start(s32[1,1,512]{2,1,0:T(1,128)} %param.15) | copy-start | bytes 6148
  10.7 17.7 %copy-start.11 = (s32[1,1,512]{2,1,0:T(1,128)S(1)}, s32[1,1,512]{2,1,0:T(1,128)}, u32[]{:S(2)}) copy-start(s32[1,1,512]{2,1,0:T(1,128)} %param.16) | copy-start | bytes 6148
  15.1 80.0 %collective-permute-start = (f32[8,512]{1,0:T(8,128)}, f32[8,512]{1,0:T(8,128)S(1)}, u32[]{:S(2)}, u32[]{:S(2)}) collective-permute-start(f32[8,512]{1,0:T(8,128)} %get-tuple-element.22), channel_id=1, source_target_pairs={{0,8},{8,16},{16,24},{1,9},{9,17},{17,25},{2,10},{10,18},{18,26},{... | collective-permute-start | bytes 49160 | tf_op jit(solution)/shard_map/ppermute | solution.py:207
  18.6 80.8 %collective-permute-start.1 = (f32[8,512]{1,0:T(8,128)}, f32[8,512]{1,0:T(8,128)S(1)}, u32[]{:S(2)}, u32[]{:S(2)}) collective-permute-start(f32[8,512]{1,0:T(8,128)} %get-tuple-element.23), channel_id=1, source_target_pairs={{8,0},{16,8},{24,16},{9,1},{17,9},{25,17},{10,2},{18,10},{26,18},{... | collective-permute-start | bytes 49160 | tf_op jit(solution)/shard_map/ppermute | solution.py:207
  21.0 81.2 %collective-permute-start.2 = (f32[8,1024]{1,0:T(8,128)}, f32[8,1024]{1,0:T(8,128)S(1)}, u32[]{:S(2)}, u32[]{:S(2)}) collective-permute-start(f32[8,1024]{1,0:T(8,128)} %get-tuple-element.24.ro_ref), channel_id=1, source_target_pairs={{0,1},{1,2},{2,3},{3,4},{4,5},{5,6},{6,7},{8,9},{9,10},{10,11},{11... | collective-permute-start | bytes 98312 | tf_op jit(solution)/shard_map/ppermute | solution.py:207
  22.9 82.4 %collective-permute-start.3 = (f32[8,1024]{1,0:T(8,128)}, f32[8,1024]{1,0:T(8,128)S(1)}, u32[]{:S(2)}, u32[]{:S(2)}) collective-permute-start(f32[8,1024]{1,0:T(8,128)} %get-tuple-element.25.lo_ref), channel_id=1, source_target_pairs={{1,0},{2,1},{3,2},{4,3},{5,4},{6,5},{7,6},{9,8},{10,9},{11,10},{12... | collective-permute-start | bytes 98312 | tf_op jit(solution)/shard_map/ppermute | solution.py:207
  93.0 47.4 %collective-permute-start.6 = (f32[8,1024]{1,0:T(8,128)}, f32[8,1024]{1,0:T(8,128)S(1)}, u32[]{:S(2)}, u32[]{:S(2)}) collective-permute-start(f32[8,1024]{1,0:T(8,128)} %get-tuple-element.34), channel_id=1, source_target_pairs={{0,1},{1,2},{2,3},{3,4},{4,5},{5,6},{6,7},{8,9},{9,10},{10,11},{11... | collective-permute-start | bytes 98312 | tf_op jit(solution)/shard_map/ppermute | solution.py:207
  95.1 10.2 %copy-start.4 = (f32[8,512]{1,0:T(8,128)}, f32[8,512]{1,0:T(8,128)S(1)}, u32[]{:S(2)}) copy-start(f32[8,512]{1,0:T(8,128)S(1)} %collective-permute-done.up_ref) | copy-start | bytes 49156
  95.1 45.2 %collective-permute-start.7 = (f32[8,1024]{1,0:T(8,128)}, f32[8,1024]{1,0:T(8,128)S(1)}, u32[]{:S(2)}, u32[]{:S(2)}) collective-permute-start(f32[8,1024]{1,0:T(8,128)} %get-tuple-element.35), channel_id=1, source_target_pairs={{1,0},{2,1},{3,2},{4,3},{5,4},{6,5},{7,6},{9,8},{10,9},{11,10},{12... | collective-permute-start | bytes 98312 | tf_op jit(solution)/shard_map/ppermute | solution.py:207
  99.5 5.9 %copy-start.5 = (f32[8,512]{1,0:T(8,128)}, f32[8,512]{1,0:T(8,128)S(1)}, u32[]{:S(2)}) copy-start(f32[8,512]{1,0:T(8,128)S(1)} %collective-permute-done.1.dn_ref) | copy-start | bytes 49156
  99.5 40.8 %collective-permute-start.4 = (f32[8,512]{1,0:T(8,128)}, f32[8,512]{1,0:T(8,128)S(1)}, u32[]{:S(2)}, u32[]{:S(2)}) collective-permute-start(f32[8,512]{1,0:T(8,128)} %get-tuple-element.32), channel_id=1, source_target_pairs={{0,8},{8,16},{16,24},{1,9},{9,17},{17,25},{2,10},{10,18},{18,26},{... | collective-permute-start | bytes 49160 | tf_op jit(solution)/shard_map/ppermute | solution.py:207
  102.2 3.2 %copy-start = (f32[8,1024]{1,0:T(8,128)}, f32[8,1024]{1,0:T(8,128)S(1)}, u32[]{:S(2)}) copy-start(f32[8,1024]{1,0:T(8,128)S(1)} %collective-permute-done.2.lh_ref) | copy-start | bytes 98308
  102.2 38.1 %collective-permute-start.5 = (f32[8,512]{1,0:T(8,128)}, f32[8,512]{1,0:T(8,128)S(1)}, u32[]{:S(2)}, u32[]{:S(2)}) collective-permute-start(f32[8,512]{1,0:T(8,128)} %get-tuple-element.33), channel_id=1, source_target_pairs={{8,0},{16,8},{24,16},{9,1},{17,9},{25,17},{10,2},{18,10},{26,18},{... | collective-permute-start | bytes 49160 | tf_op jit(solution)/shard_map/ppermute | solution.py:207
  105.4 0.6 copy-start.1
  140.3 0.6 copy-start.6
  140.3 0.6 copy-start.7
  140.3 0.6 copy-start.2
  140.4 0.6 copy-start.3
Sparse Core Ops, SparseCore 0:
  11.4 63.2 all-gather.4
  77.6 76.1 all-gather.2

commit v3 on v1

v3 whole, which is shorter than its diff:
```python
import functools

import jax
import jax.numpy as jnp
from jax import lax
from jax.experimental import pallas as pl
from jax.experimental.pallas import tpu as pltpu
from jax.sharding import PartitionSpec as P

PATCH = 64
ABLK = 256
NW = 4
BPX = 16
BPY = 8
NPATCH = BPX * BPY

GRAV = 1.0
DT_DX = 0.2
TIME_STEP = 0.2
STRESS = 0.5
PRESS = 0.5

F32 = jnp.float32
BF16 = jnp.bfloat16
VMEM = pl.BlockSpec(memory_space=pltpu.VMEM)
SMEM = pl.BlockSpec(memory_space=pltpu.SMEM)
LANES = 128
TILE = 8
GROUPS = BPY * PATCH // LANES
HALVES = BPX // TILE
BAND = 128


def params(limit=56 << 20, **kw):
    return pltpu.CompilerParams(vmem_limit_bytes=limit, **kw)


def iota(shape, dim):
    return lax.broadcasted_iota(jnp.int32, shape, dim)


def rank_kernel(capacity, src_ref, blk_ref, pat_ref, wgt_ref, want_ref, lab_ref):
    devices = want_ref.shape[0]
    src = src_ref[...]
    ent = src.shape[1]
    hits = (iota((devices, ent), 0) == src).astype(F32)
    order = (iota((ent, ent), 0) <= iota((ent, ent), 1)).astype(BF16)
    ranks = jnp.dot(hits.astype(BF16), order, preferred_element_type=F32)
    mine = jnp.sum(hits * ranks, axis=0, keepdims=True).astype(jnp.int32) - 1
    place = iota((capacity, ent), 0) == mine
    pat = pat_ref[...]
    row_bits = BPX.bit_length() - 1
    col_bits = BPY.bit_length() - 1
    rows = jnp.zeros_like(pat)
    cols = jnp.zeros_like(pat)
    used_r = used_c = position = 0
    while used_r < row_bits or used_c < col_bits:
        value = jnp.bitwise_and(jnp.right_shift(pat, position), 1)
        if used_r < row_bits and (used_c >= col_bits or position % 2 == 0):
            rows = rows + value * (1 << used_r)
            used_r += 1
        else:
            cols = cols + value * (1 << used_c)
            used_c += 1
        position += 1

    def spread(row):
        picked = jnp.where(place, row.astype(F32), 0.0).astype(BF16)
        return lax.dot_general(
            hits.astype(BF16), picked, (((1,), (1,)), ((), ())),
            preferred_element_type=F32,
        ).astype(jnp.int32)

    want_ref[...] = spread(blk_ref[...])
    slot = spread(cols * BPX + rows)
    group = spread(wgt_ref[...] + 1)
    lab_ref[...] = jnp.where(group > 0, (group - 1) * NPATCH + slot, -1)


def make_requests(src, blk, pat, wgt, devices, capacity):
    shape = jax.ShapeDtypeStruct((devices, capacity), jnp.int32)
    return pl.pallas_call(
        functools.partial(rank_kernel, capacity),
        out_shape=(shape, shape),
        in_specs=[VMEM] * 4,
        out_specs=(VMEM, VMEM),
        compiler_params=params(16 << 20),
        name="requests",
    )(src, blk, pat, wgt)


def mix_kernel(blend_ref, atm_ref, press_ref, wind_ref):
    blend = blend_ref[0]
    keep = 1.0 - blend

    def mixed(k):
        first = atm_ref[k].astype(F32)
        second = atm_ref[3 + k].astype(F32)
        return (keep * first + blend * second).astype(BF16)

    press_ref[...] = mixed(2)
    for k in range(2):
        wind_ref[:, k * ABLK:(k + 1) * ABLK] = mixed(k)


def mix(blend, atm):
    blocks = atm.shape[1]
    return pl.pallas_call(
        mix_kernel,
        out_shape=(
            jax.ShapeDtypeStruct((blocks, ABLK), BF16),
            jax.ShapeDtypeStruct((blocks, 2 * ABLK), BF16),
        ),
        in_specs=[SMEM, VMEM],
        out_specs=(VMEM, VMEM),
        compiler_params=params(16 << 20),
        name="mix",
    )(blend, atm)


def serve_kernel(asked_ref, tiles_ref, out_ref):
    asked = asked_ref[...]
    pick = (asked == iota((asked.shape[0], tiles_ref.shape[0]), 1)).astype(BF16)
    out_ref[...] = jnp.dot(pick, tiles_ref[...], preferred_element_type=F32).astype(BF16)


def serve(asked, tiles):
    return pl.pallas_call(
        serve_kernel,
        out_shape=jax.ShapeDtypeStruct((asked.shape[0], tiles.shape[1]), BF16),
        in_specs=[VMEM, VMEM],
        out_specs=VMEM,
        compiler_params=params(32 << 20),
        name="serve",
    )(asked, tiles)


def edges_kernel(
    dl, ml, xl, yl, dr, mr, xr, yr, dt, mt, xt, yt, db, mb, xb, yb,
    top_ref, bottom_ref, left_ref, right_ref,
):
    def rows(d, m, x, y, at, out):
        wet = m[...] == 1
        for f, ref in enumerate((d, x, y)):
            out[f:f + 1, :] = jnp.where(wet, ref[...], 0.0)[at:at + 1]

    rows(dt, mt, xt, yt, 0, top_ref)
    rows(db, mb, xb, yb, TILE - 1, bottom_ref)
    lane = iota((LANES, LANES), 1)

    def step(b, carry):
        at = pl.ds(pl.multiple_of(b * LANES, LANES), LANES)
        wl = ml[at, :] == 1
        wr = mr[at, :] == 1
        packed = jnp.where(wl, dl[at, :], 0.0)
        packed = jnp.where(lane == 1, pltpu.roll(jnp.where(wl, xl[at, :], 0.0), 1, 1), packed)
        packed = jnp.where(lane == 2, pltpu.roll(jnp.where(wl, yl[at, :], 0.0), 2, 1), packed)
        packed = jnp.where(lane == 8, pltpu.roll(jnp.where(wr, dr[at, :], 0.0), 9, 1), packed)
        packed = jnp.where(lane == 9, pltpu.roll(jnp.where(wr, xr[at, :], 0.0), 10, 1), packed)
        packed = jnp.where(lane == 10, pltpu.roll(jnp.where(wr, yr[at, :], 0.0), 11, 1), packed)
        turned = packed.T
        left_ref[:, at] = turned[0:TILE]
        right_ref[:, at] = turned[TILE:2 * TILE]
        return carry

    lax.fori_loop(0, dl.shape[0] // LANES, step, 0)


def edge_cells(depth, mask, momx, momy):
    rows, cols = depth.shape
    fields = (depth, mask, momx, momy)
    left = pl.BlockSpec((rows, LANES), lambda i: (0, 0))
    right = pl.BlockSpec((rows, LANES), lambda i: (0, cols // LANES - 1))
    top = pl.BlockSpec((TILE, cols), lambda i: (0, 0))
    bottom = pl.BlockSpec((TILE, cols), lambda i: (rows // TILE - 1, 0))
    line = jax.ShapeDtypeStruct((TILE, cols), F32)
    column = jax.ShapeDtypeStruct((TILE, rows), F32)
    return pl.pallas_call(
        edges_kernel,
        grid=(1,),
        out_shape=(line, line, column, column),
        in_specs=[left] * 4 + [right] * 4 + [top] * 4 + [bottom] * 4,
        out_specs=(
            pl.BlockSpec((TILE, cols), lambda i: (0, 0)),
            pl.BlockSpec((TILE, cols), lambda i: (0, 0)),
            pl.BlockSpec((TILE, rows), lambda i: (0, 0)),
            pl.BlockSpec((TILE, rows), lambda i: (0, 0)),
        ),
        compiler_params=params(24 << 20),
        name="edges",
    )(*(fields * 4))


def send(value, axis, step):
    count = lax.axis_size(axis)
    if step > 0:
        pairs = [(i, i + 1) for i in range(count - 1)]
    else:
        pairs = [(i + 1, i) for i in range(count - 1)]
    return lax.ppermute(value, axis, pairs)


def derived(h, u, v):
    r = jnp.where(h > 0.0, lax.rsqrt(h), 0.0)
    s = h * r
    q = u * r
    p = v * r
    half = 0.5 * h * h
    return (h, u, v, s, q, p, q * q + half, p * p + half, q * p)


def along_x(c):
    return (c[0], c[1], c[2], c[3], c[4], c[5], c[6], c[8])


def along_y(c):
    return (c[0], c[2], c[1], c[3], c[5], c[4], c[7], c[8])


def flux(a, b):
    hl, nl, tl, sl, ql, pl_, fl, gl = a
    hr, nr, tr, sr, qr, pr, fr, gr = b
    both = jnp.minimum(hl, hr) > 0.0
    half = jnp.where(both, 0.5, 1.0)
    twice = half + half
    level = (hl + hr) * half
    rc = lax.rsqrt(level)
    c = level * rc
    total = sl + sr
    inv = pl.reciprocal(total, approx=True)
    inv = inv * (2.0 - total * inv)
    u = jnp.where(both, (ql + qr) * inv, 0.0)
    v = (pl_ + pr) * inv
    dh = jnp.where(both, hr - hl, 0.0)
    dn = (nr - nl) * twice
    dt = jnp.where(both, tr - tl, 0.0)
    mid = 0.5 * dh
    e = (0.5 * dn - u * mid) * rc
    s1 = u - c
    s3 = u + c
    b1 = jnp.abs(s1) * (mid - e)
    b3 = jnp.abs(s3) * (mid + e)
    b2 = jnp.abs(u) * (dt - v * dh)
    d = b1 + b3
    return (
        jnp.where(both, nl + nr, 0.0) - d,
        (fl + fr) * twice - (b1 * s1 + b3 * s3),
        jnp.where(both, gl + gr, 0.0) - (d * v + b2),
    )


CELL = 9


def stencil_kernel(
    d_ref, m_ref, x_ref, y_ref, up_ref, dn_ref, lh_ref, rh_ref, lo_ref,
    newh_ref, hu_ref, hv_ref, h_ref, *scratch,
):
    cell = scratch[:CELL]
    gx = scratch[CELL:CELL + 3]
    edge, ecol = scratch[CELL + 3:]
    step = pl.program_id(0)
    bands = pl.num_programs(0) - 1
    lane = iota((TILE, LANES), 1)

    @pl.when(step < bands)
    def _():
        def fill(t, carry):
            at = pl.ds(pl.multiple_of(t * TILE, TILE), TILE)
            to = pl.ds(pl.multiple_of(step * BAND + t * TILE + TILE, TILE), TILE)
            for g in range(GROUPS):
                cut = slice(g * LANES, (g + 1) * LANES)
                wet = m_ref[at, cut] == 1
                h = jnp.where(wet, d_ref[at, cut], 0.0)
                u = jnp.where(wet, x_ref[at, cut], 0.0)
                v = jnp.where(wet, y_ref[at, cut], 0.0)
                for dst, val in zip(cell, derived(h, u, v)):
                    dst[g, to, :] = val
            return carry

        lax.fori_loop(0, BAND // TILE, fill, 0, unroll=4)

    @pl.when(step == 0)
    def _():
        rows = bands * BAND
        for at, ref in ((0, up_ref), (rows + TILE, dn_ref)):
            for g in range(GROUPS):
                cut = slice(g * LANES, (g + 1) * LANES)
                line = [jnp.broadcast_to(ref[f:f + 1, cut], (TILE, LANES)) for f in range(3)]
                for dst, val in zip(cell, derived(*line)):
                    dst[g, pl.ds(at, TILE), :] = val
        outer = along_y(derived(lh_ref[0:1, :], lh_ref[1:2, :], lh_ref[2:3, :]))
        inner = along_y(derived(lo_ref[0:1, :], lo_ref[1:2, :], lo_ref[2:3, :]))
        edge[...] = jnp.zeros_like(edge)
        edge[0:3, :] = rh_ref[0:3, :]
        for f, val in enumerate(flux(outer, inner)):
            edge[3 + f:4 + f, :] = val

        def turn(b, carry):
            at = pl.ds(pl.multiple_of(b * LANES, LANES), LANES)
            ecol[at, :] = edge[:, at].T
            return carry

        lax.fori_loop(0, ecol.shape[0] // LANES, turn, 0)
        for g in range(GROUPS):
            now = along_x([ref[g, 0:TILE, :] for ref in cell])
            nxt = along_x([ref[g, 1:TILE + 1, :] for ref in cell])
            for dst, val in zip(gx, flux(now, nxt)):
                dst[g, 0:TILE, :] = val

    @pl.when(step > 0)
    def _():
        def body(t, carry):
            here = pl.multiple_of(t * TILE, TILE)
            mark = pl.multiple_of((step - 1) * BAND + t * TILE, TILE)
            base = pl.multiple_of(mark + TILE, TILE)
            sides = ecol[pl.ds(mark, TILE), :]
            now = [[ref[g, pl.ds(base, TILE), :] for ref in cell] for g in range(GROUPS)]
            back = [[pltpu.roll(val, LANES - 1, 1) for val in now[g][:3]] for g in range(GROUPS)]
            gy = []
            for g in range(GROUPS):
                if g < GROUPS - 1:
                    other = back[g + 1]
                else:
                    other = [sides[:, f:f + 1] for f in range(3)]
                right = [jnp.where(lane == LANES - 1, o, b) for o, b in zip(other, back[g])]
                gy.append(flux(along_y(now[g]), along_y(derived(*right))))
            moved = [[pltpu.roll(val, 1, 1) for val in gy[g]] for g in range(GROUPS)]
            for g in range(GROUPS):
                nxt = [ref[g, pl.ds(base + 1, TILE), :] for ref in cell]
                fx = flux(along_x(now[g]), along_x(nxt))
                for dst, val in zip(gx, fx):
                    dst[g, pl.ds(base, TILE), :] = val
                px = [src[g, pl.ds(base - 1, TILE), :] for src in gx]
                other = moved[g - 1] if g else [sides[:, 3 + f:4 + f] for f in range(3)]
                py = [jnp.where(lane == 0, o, b) for o, b in zip(other, moved[g])]
                fy = gy[g]
                h, u, v = now[g][:3]
                ch = (fx[0] - px[0]) + (fy[0] - py[0])
                cx = (fx[1] - px[1]) + (fy[2] - py[2])
                cy = (fx[2] - px[2]) + (fy[1] - py[1])
                at = pl.ds(here, TILE)
                newh_ref[at, g * LANES:(g + 1) * LANES] = jnp.where(
                    h > 0.0, h - (0.5 * DT_DX) * ch, 0.0
                )
                hu_ref[g, at, :] = u - (0.5 * DT_DX) * cx
                hv_ref[g, at, :] = v - (0.5 * DT_DX) * cy
                h_ref[g, at, :] = h
            return carry

        lax.fori_loop(0, BAND // TILE, body, 0, unroll=2)


def stencil(depth, mask, momx, momy, up, dn, lh, rh, lo):
    rows, cols = depth.shape
    bands = rows // BAND
    plane = jax.ShapeDtypeStruct((GROUPS, rows, LANES), F32)
    pad = pltpu.VMEM((GROUPS, rows + 2 * TILE, LANES), F32)
    band = pl.BlockSpec((BAND, cols), lambda i: (jnp.minimum(i, bands - 1), 0))
    line = pl.BlockSpec((TILE, cols), lambda i: (0, 0))
    column = pl.BlockSpec((TILE, rows), lambda i: (0, 0))
    part = pl.BlockSpec((GROUPS, BAND, LANES), lambda i: (0, jnp.maximum(i - 1, 0), 0))
    return pl.pallas_call(
        stencil_kernel,
        grid=(bands + 1,),
        out_shape=(jax.ShapeDtypeStruct((rows, cols), F32), plane, plane, plane),
        in_specs=[band] * 4 + [line] * 2 + [column] * 3,
        out_specs=(
            pl.BlockSpec((BAND, cols), lambda i: (jnp.maximum(i - 1, 0), 0)), part, part, part,
        ),
        scratch_shapes=[pad] * (CELL + 3)
        + [pltpu.VMEM((LANES, rows), F32), pltpu.VMEM((rows, LANES), F32)],
        compiler_params=params(48 << 20),
        cost_estimate=pl.CostEstimate(
            flops=200 * rows * cols, bytes_accessed=64 * rows * cols, transcendentals=0
        ),
        name="stencil",
    )(depth, mask, momx, momy, up, dn, lh, rh, lo)


def summed_of(lab, landed):
    select = (iota((NW * NPATCH, lab.shape[1]), 0) == lab).astype(BF16)
    return jnp.dot(select, landed, preferred_element_type=F32).astype(BF16)


def stack_left(left, summed, channels):
    for k in range(channels):
        for w in range(NW):
            left[k * NPATCH:(k + 1) * NPATCH, w * ABLK:(w + 1) * ABLK] = summed[
                w * NPATCH:(w + 1) * NPATCH, k * ABLK:(k + 1) * ABLK
            ]


PART = TILE * PATCH


def spread_rows(acc, field, k):
    low = iota((TILE, LANES), 1) < LANES // 2
    for t in range(TILE // 2):
        cut = slice(t * LANES, (t + 1) * LANES)
        for half in range(HALVES):
            for g in range(GROUPS):
                base = k * NPATCH + 2 * g * BPX + half * TILE
                even = acc[base:base + TILE, cut]
                odd = acc[base + BPX:base + BPX + TILE, cut]
                for i, val in (
                    (2 * t, jnp.where(low, even, pltpu.roll(odd, LANES // 2, 1))),
                    (2 * t + 1, jnp.where(low, pltpu.roll(even, LANES // 2, 1), odd)),
                ):
                    field[g, pl.ds(half * TILE * TILE + i, TILE, stride=TILE), :] = val


def press_kernel(
    lab_ref, landed_ref, w_ref, out_ref, top_ref, bottom_ref, left_ref, right_ref,
    left, acc, acc2, field, field2,
):
    step = pl.program_id(0)

    @pl.when(step == 0)
    def _():
        stack_left(left, summed_of(lab_ref[...], landed_ref[...]), 1)

    acc[...] = jnp.dot(left[...], w_ref[:, :PART], preferred_element_type=F32)
    acc2[...] = jnp.dot(left[...], w_ref[:, PART:], preferred_element_type=F32)
    for part, (src, mid) in enumerate(((acc, field), (acc2, field2))):
        spread_rows(src, mid, 0)
        for g in range(GROUPS):
            for r in range(BPX):
                to = pl.ds(pl.multiple_of(r * PATCH + (2 * step + part) * TILE, TILE), TILE)
                out_ref[g, to, :] = mid[g, r * TILE:(r + 1) * TILE, :]

    @pl.when(step == pl.num_programs(0) - 1)
    def _():
        rows = out_ref.shape[1]
        for g in range(GROUPS):
            cut = slice(g * LANES, (g + 1) * LANES)
            top_ref[:, cut] = out_ref[g, 0:TILE, :]
            bottom_ref[:, cut] = pltpu.roll(out_ref[g, rows - TILE:rows, :], 1, 0)
        lane = iota((LANES, LANES), 1)
        for b in range(rows // LANES):
            at = slice(b * LANES, (b + 1) * LANES)
            packed = jnp.where(
                lane == TILE,
                pltpu.roll(out_ref[GROUPS - 1, at, :], TILE + 1, 1),
                out_ref[0, at, :],
            )
            turned = packed.T
            left_ref[:, at] = turned[0:TILE]
            right_ref[:, at] = turned[TILE:2 * TILE]


def pressure_field(lab, landed, weights):
    steps = PATCH // (2 * TILE)
    rows = BPX * PATCH
    line = (TILE, BPY * PATCH)
    column = (TILE, rows)
    whole = (GROUPS, rows, LANES)

    def const(shape):
        return pl.BlockSpec(shape, lambda i: (0,) * len(shape))

    return pl.pallas_call(
        press_kernel,
        grid=(steps,),
        out_shape=tuple(jax.ShapeDtypeStruct(x, F32) for x in (whole, line, line, column, column)),
        in_specs=[
            const(lab.shape),
            const(landed.shape),
            pl.BlockSpec((NW * ABLK, 2 * PART), lambda i: (0, i)),
        ],
        out_specs=tuple(const(x) for x in (whole, line, line, column, column)),
        scratch_shapes=[
            pltpu.VMEM((NPATCH, NW * ABLK), BF16),
            pltpu.VMEM((NPATCH, PART), F32),
            pltpu.VMEM((NPATCH, PART), F32),
            pltpu.VMEM((GROUPS, BPX * TILE, LANES), F32),
            pltpu.VMEM((GROUPS, BPX * TILE, LANES), F32),
        ],
        compiler_params=params(32 << 20),
        cost_estimate=pl.CostEstimate(
            flops=2 * NPATCH * NW * ABLK * PATCH * PATCH, bytes_accessed=12 << 20, transcendentals=0
        ),
        name="pressure",
    )(lab, landed, weights)


def gradient_kernel(
    p_ref, hu_ref, hv_ref, h_ref, up_ref, dn_ref, lh_ref, rh_ref,
    ox_ref, oy_ref, fac_ref, padded, sides,
):
    step = pl.program_id(0)
    rows = p_ref.shape[1]

    @pl.when(step == 0)
    def _():
        stacked = jnp.concatenate([lh_ref[...], rh_ref[...]], axis=0)
        blank = jnp.zeros((LANES - 2 * TILE, LANES), F32)
        for b in range(rows // LANES):
            cut = slice(b * LANES, (b + 1) * LANES)
            sides[cut, :] = jnp.concatenate([stacked[:, cut], blank], axis=0).T
        for g in range(GROUPS):
            cut = slice(g * LANES, (g + 1) * LANES)
            padded[g, TILE:TILE + rows, :] = p_ref[g]
            padded[g, 0:TILE, :] = jnp.broadcast_to(up_ref[0:1, cut], (TILE, LANES))
            padded[g, rows + TILE:, :] = jnp.broadcast_to(dn_ref[0:1, cut], (TILE, LANES))

    lane = iota((TILE, LANES), 1)

    def body(t, carry):
        at = pl.ds(pl.multiple_of(t * TILE, TILE), TILE)
        mark = pl.multiple_of(step * BAND + t * TILE, TILE)
        base = pl.multiple_of(mark + TILE, TILE)
        ends = sides[pl.ds(mark, TILE), :]
        tiles = [padded[g, pl.ds(base, TILE), :] for g in range(GROUPS)]
        ups = [pltpu.roll(a, 1, 1) for a in tiles]
        downs = [pltpu.roll(a, LANES - 1, 1) for a in tiles]
        for g in range(GROUPS):
            before = ups[g - 1] if g else ends[:, 0:1]
            after = downs[g + 1] if g < GROUPS - 1 else ends[:, TILE:TILE + 1]
            prev = jnp.where(lane == 0, before, ups[g])
            nxt = jnp.where(lane == LANES - 1, after, downs[g])
            h = h_ref[g, at, :]
            wet = h > 0.0
            scale = (TIME_STEP * PRESS * 0.5) * h
            gx = padded[g, pl.ds(base + 1, TILE), :] - padded[g, pl.ds(base - 1, TILE), :]
            ox_ref[g, at, :] = jnp.where(wet, hu_ref[g, at, :] - scale * gx, 0.0)
            oy_ref[g, at, :] = jnp.where(wet, hv_ref[g, at, :] - scale * (nxt - prev), 0.0)
            fac_ref[g, at, :] = jnp.where(wet, TIME_STEP * STRESS, 0.0)
        return carry

    lax.fori_loop(0, BAND // TILE, body, 0, unroll=4)


def gradient(p, hu, hv, h, up, dn, lh, rh):
    rows = p.shape[1]
    plane = jax.ShapeDtypeStruct(p.shape, F32)
    part = pl.BlockSpec((GROUPS, BAND, LANES), lambda i: (0, i, 0))
    line = pl.BlockSpec(up.shape, lambda i: (0, 0))
    column = pl.BlockSpec(lh.shape, lambda i: (0, 0))
    return pl.pallas_call(
        gradient_kernel,
        grid=(rows // BAND,),
        out_shape=(plane,) * 3,
        in_specs=[pl.BlockSpec(p.shape, lambda i: (0, 0, 0))] + [part] * 3 + [line] * 2 + [column] * 2,
        out_specs=(part,) * 3,
        scratch_shapes=[
            pltpu.VMEM((GROUPS, rows + 2 * TILE, LANES), F32),
            pltpu.VMEM((rows, LANES), F32),
        ],
        compiler_params=params(24 << 20),
        cost_estimate=pl.CostEstimate(
            flops=20 * p.size, bytes_accessed=28 * p.size, transcendentals=0
        ),
        name="gradient",
    )(p, hu, hv, h, up, dn, lh, rh)


def wind_kernel(
    lab_ref, landed_ref, w_ref, hu_ref, hv_ref, fac_ref, ox_ref, oy_ref,
    left, acc, acc2, fx, fy, fx2, fy2,
):
    @pl.when(pl.program_id(0) == 0)
    def _():
        stack_left(left, summed_of(lab_ref[...], landed_ref[...]), 2)

    acc[...] = jnp.dot(left[...], w_ref[:, :PART], preferred_element_type=F32)
    acc2[...] = jnp.dot(left[...], w_ref[:, PART:], preferred_element_type=F32)
    for part, (src, mx, my) in enumerate(((acc, fx, fy), (acc2, fx2, fy2))):
        spread_rows(src, mx, 0)
        spread_rows(src, my, 1)
        cells = slice(part * TILE, (part + 1) * TILE)
        for g in range(GROUPS):
            for r in range(BPX):
                at = slice(r * TILE, (r + 1) * TILE)
                wx = mx[g, at, :]
                wy = my[g, at, :]
                speed = jnp.sqrt(wx * wx + wy * wy) * fac_ref[g, r, cells, :]
                cut = slice(g * LANES, (g + 1) * LANES)
                ox_ref[r, cells, cut] = hu_ref[g, r, cells, :] + speed * wx
                oy_ref[r, cells, cut] = hv_ref[g, r, cells, :] + speed * wy


def wind_field(lab, landed, weights, hu, hv, fac):
    deep = 2 * TILE
    steps = PATCH // deep
    cols = BPY * PATCH
    split = (GROUPS, BPX, PATCH, LANES)
    slab = pl.BlockSpec((GROUPS, BPX, deep, LANES), lambda i: (0, 0, i, 0))
    out = pl.BlockSpec((BPX, deep, cols), lambda i: (0, i, 0))
    shape = jax.ShapeDtypeStruct((BPX, PATCH, cols), F32)
    field = pltpu.VMEM((GROUPS, BPX * TILE, LANES), F32)
    return pl.pallas_call(
        wind_kernel,
        grid=(steps,),
        out_shape=(shape, shape),
        in_specs=[
            pl.BlockSpec(lab.shape, lambda i: (0, 0)),
            pl.BlockSpec(landed.shape, lambda i: (0, 0)),
            pl.BlockSpec((NW * ABLK, 2 * PART), lambda i: (0, i)),
            slab, slab, slab,
        ],
        out_specs=(out, out),
        scratch_shapes=[
            pltpu.VMEM((2 * NPATCH, NW * ABLK), BF16),
            pltpu.VMEM((2 * NPATCH, PART), F32),
            pltpu.VMEM((2 * NPATCH, PART), F32),
            field, field, field, field,
        ],
        compiler_params=params(40 << 20),
        cost_estimate=pl.CostEstimate(
            flops=4 * NPATCH * NW * ABLK * PATCH * PATCH, bytes_accessed=20 << 20, transcendentals=0
        ),
        name="wind",
    )(lab, landed, weights, hu.reshape(split), hv.reshape(split), fac.reshape(split))


def body(
    atm_blocks,
    remap_weights,
    ovl_source,
    ovl_block,
    ovl_patch,
    ovl_weight,
    depth_field,
    wet_mask,
    mom_x,
    mom_y,
    blend,
):
    count_x = lax.axis_size("gx")
    count_y = lax.axis_size("gy")
    devices = count_x * count_y
    entries = ovl_source.size
    capacity = 2 * entries // devices
    slots = devices * capacity
    atm = atm_blocks.reshape(atm_blocks.shape[2:]).transpose(1, 0, 2)
    blocks = atm.shape[1]
    press, wind = mix(blend.reshape(1), atm)
    press = lax.all_gather(press, "gx", axis=0, tiled=True)
    wind = lax.all_gather(wind, "gx", axis=0, tiled=True)

    source = ovl_source.reshape(1, entries)
    source = (source % count_y) * count_x + source // count_y
    want, lab = make_requests(
        source, ovl_block.reshape(1, entries),
        ovl_patch.reshape(1, entries), ovl_weight.reshape(1, entries), devices, capacity,
    )
    asked = lax.all_to_all(
        want.reshape(count_y, count_x, capacity), "gy", split_axis=0, concat_axis=0, tiled=True
    )
    asked = asked + blocks * jnp.arange(count_x, dtype=jnp.int32)[None, :, None]
    asked = asked.reshape(slots, 1)
    lab = lab.reshape(1, slots)

    def exchange(tiles):
        rows = serve(asked, tiles)
        parts = rows.reshape(count_y, slots // count_y, rows.shape[1])
        got = lax.all_to_all(parts, "gy", split_axis=0, concat_axis=0, tiled=True)
        return got.reshape(rows.shape)

    press = exchange(press)
    wind = exchange(wind)

    top, bottom, left, right = edge_cells(depth_field, wet_mask, mom_x, mom_y)
    newh, hu, hv, h = stencil(
        depth_field, wet_mask, mom_x, mom_y,
        send(bottom, "gx", 1), send(top, "gx", -1),
        send(right, "gy", 1), send(left, "gy", -1), left,
    )
    weights = remap_weights.reshape(NW * ABLK, PATCH * PATCH)
    p, top, bottom, left, right = pressure_field(lab, press, weights)
    hu, hv, fac = gradient(
        p, hu, hv, h,
        send(bottom, "gx", 1), send(top, "gx", -1),
        send(right, "gy", 1), send(left, "gy", -1),
    )
    new_x, new_y = wind_field(lab, wind, weights, hu, hv, fac)
    return (newh, new_x.reshape(newh.shape), new_y.reshape(newh.shape))


def solution(mesh):
    placed = (
        P("gx", "gy", None, None, None),
        P(),
        P("gx", "gy", None, None),
        P("gx", "gy", None),
        P("gx", "gy", None),
        P("gx", "gy", None),
        P("gx", "gy"),
        P("gx", "gy"),
        P("gx", "gy"),
        P("gx", "gy"),
        P(),
    )
    return jax.shard_map(
        body,
        mesh=mesh,
        in_specs=placed,
        out_specs=(P("gx", "gy"), P("gx", "gy"), P("gx", "gy")),
        check_vma=False,
    )
```

time: 146 us -> 151 us (1.034)
  Pallas kernels: 79.7 us -> 45.5 us
  local copies, waits for them, and re-layouts: 4.75 us -> 24.8 us
  between operations: 1.54 us -> 14.9 us
  blocking collectives: 19.8 us -> 22.2 us
  starting transfers between devices: 34.7 us -> 36.6 us
    pallas_call x5 -> x6, Pallas kernels: 61.1 us -> 34.4 us  [the longest x1 21.7 us: stencil(): pl.pallas_call(stencil_kernel, grid=(bands + 1,), out_shape=(jax.ShapeDty...]
    all_gather x0 -> x1, blocking collectives: none -> 22.2 us  [body(): press = lax.all_gather(press, 'gx', axis=0, tiled=True)]
    unnamed x20 -> x38, local copies, waits for them, and re-layouts: 2.24 us -> 23.7 us
    all_to_all x1 -> x0, blocking collectives: 19.8 us -> none  [exchange(): got = lax.all_to_all(parts, both, split_axis=0, concat_axis=0, tiled=True)]
    pallas_call x1, Pallas kernels: 12.4 us -> 8.7 us  [wind_field(): pl.pallas_call(wind_kernel, grid=(steps,), out_shape=(shape, shape), in_s...]
    all_to_all x2 -> x3, starting transfers between devices: 10.2 us -> 13.4 us  [the longest x2 9.14 us: exchange(): got = lax.all_to_all(parts, 'gy', split_axis=0, concat_axis=0, tiled=True)]
    pallas_call x1, Pallas kernels: 4.47 us -> 2.03 us  [edge_cells(): pl.pallas_call(edges_kernel, grid=(1,), out_shape=(line, line, column, co...]
    all_to_all x2 -> x3, waiting for transfers between devices: 4.31 us -> 4.64 us  [the longest x2 4.64 us: exchange(): got = lax.all_to_all(parts, 'gy', split_axis=0, concat_axis=0, tiled=True)]
  transfers between devices with their start and end apart: 10 -> 12, of which waited for: 1 -> 1; matrix products, arithmetic and copies ran while one was open for 0% -> 2% of each run, Pallas kernels for 43% -> 24%
where the time goes in v3:
time: 151 us; the launch traced here: 150 us
  Pallas kernels  45.5 us (30%)
  starting transfers between devices  36.6 us (24%)
  local copies, waits for them, and re-layouts  24.8 us (16%)
  blocking collectives  22.2 us (15%)
  between operations  14.9 us (10%)
  waiting for transfers between devices  4.68 us (3%)
    unnamed x38, local copies, waits for them, and re-layouts  23.7 us
    ppermute x8, starting transfers between devices, send(): return lax.ppermute(value, axis, pairs)  23.2 us
    all_gather x1, blocking collectives, body(): press = lax.all_gather(press, 'gx', axis=0, tiled=True)  22.2 us
    pallas_call x1, Pallas kernels, stencil(): pl.pallas_call(stencil_kernel, grid=(bands + 1,), out_shape=(jax.ShapeDty...  21.7 us
    all_to_all x2, starting transfers between devices, exchange(): got = lax.all_to_all(parts, 'gy', split_axis=0, concat_axis=0, tiled=True)  9.14 us
    pallas_call x1, Pallas kernels, wind_field(): pl.pallas_call(wind_kernel, grid=(steps,), out_shape=(shape, shape), in_s...  8.7 us
    pallas_call x1, Pallas kernels, gradient(): pl.pallas_call(gradient_kernel, grid=(rows // BAND,), out_shape=(plane,)...  5.24 us
    all_to_all x2, waiting for transfers between devices, exchange(): got = lax.all_to_all(parts, 'gy', split_axis=0, concat_axis=0, tiled=True)  4.64 us
  transfers between devices with their start and end apart: 12, of which 1 were waited for; matrix products, arithmetic and copies ran while one was open for 2% of the time, Pallas kernels for 24%

profile of v3, /device:TPU:12, one launch (start us, length us, event | category | flops | bytes accessed | tf_op | source)
XLA Modules:
  0.0 150.1 jit_solution(14544670656073381926)
XLA Ops:
  13.6 4.2 %all-to-all-start = ((s32[8,1,128]{2,1,0:T(1,128)}), s32[8,1,128]{2,1,0:T(1,128)S(1)}, u32[]{:S(2)}, u32[]{:S(2)}) async-start(s32[8,1,128]{2,1,0:T(1,128)} %reshape.230), calls=%async_computation | async-start | bytes 8192 | tf_op jit(solution)/shard_map/all_to_all | solution.py:648
  17.9 22.2 %all_gather.7.tiles_ref = bf16[1024,256]{1,0:T(8,128)(2,1)S(1)} all-gather(bf16[256,256]{1,0:T(8,128)(2,1)S(1)} %get-tuple-element.33), channel_id=1, replica_groups=mesh['gx'=4,'gy'=8] {'gx'}, dimensions={0}, use_global_device_ids=true | all-gather | bytes 655360 | tf_op jit(solution)/shard_map/all_gather | solution.py:639
  43.5 4.2 %all-to-all-start.2 = ((bf16[8,128,256]{2,1,0:T(8,128)(2,1)}), bf16[8,128,256]{2,1,0:T(8,128)(2,1)S(1)}, u32[]{:S(2)}, u32[]{:S(2)}) async-start(bf16[8,128,256]{2,1,0:T(8,128)(2,1)} %bitcast.11), calls=%async_computation.2 | async-start | bytes 1048576 | tf_op jit(solution)/shard_map/all_to_all | solution.py:658
  51.4 4.6 %all-to-all-done.2 = bf16[8,128,256]{2,1,0:T(8,128)(2,1)S(1)} async-done(((bf16[8,128,256]{2,1,0:T(8,128)(2,1)}), bf16[8,128,256]{2,1,0:T(8,128)(2,1)S(1)}, u32[]{:S(2)}, u32[]{:S(2)}) %all-to-all-start.2) | async-done | bytes 524320 | tf_op jit(solution)/shard_map/all_to_all | solution.py:658
  56.8 4.9 %all-to-all-start.1 = ((bf16[8,128,512]{2,1,0:T(8,128)(2,1)}), bf16[8,128,512]{2,1,0:T(8,128)(2,1)S(1)}, u32[]{:S(2)}, u32[]{:S(2)}) async-start(bf16[8,128,512]{2,1,0:T(8,128)(2,1)} %bitcast.35), calls=%async_computation.1 | async-start | bytes 2097152 | tf_op jit(solution)/shard_map/all_to_all | solution.py:658
  61.8 1.6 %copy-done.1 = s32[1024,512]{1,0:T(8,128)S(1)} copy-done((s32[1024,512]{1,0:T(8,128)S(1)}, s32[1024,512]{1,0:T(8,128)}, u32[]{:S(2)}) %copy-start.1) | copy-done | bytes 2097176
  63.3 1.6 %copy-done.2 = f32[1024,512]{1,0:T(8,128)S(1)} copy-done((f32[1024,512]{1,0:T(8,128)S(1)}, f32[1024,512]{1,0:T(8,128)}, u32[]{:S(2)}) %copy-start.2) | copy-done | bytes 2097176
  64.9 1.6 %copy-done.3 = f32[1024,512]{1,0:T(8,128)S(1)} copy-done((f32[1024,512]{1,0:T(8,128)S(1)}, f32[1024,512]{1,0:T(8,128)}, u32[]{:S(2)}) %copy-start.3) | copy-done | bytes 2097176
  66.5 2.0 %edges.1 = (f32[8,512]{1,0:T(8,128)S(1)}, f32[8,512]{1,0:T(8,128)S(1)}, f32[8,1024]{1,0:T(8,128)S(1)}, f32[8,1024]{1,0:T(8,128)S(1)}) custom-call(f32[1024,512]{1,0:T(8,128)S(1)} %copy-done, s32[1024,512]{1,0:T(8,128)S(1)} %copy-done.1, f32[1024,512]{1,0:T(8,128)S(1)} %copy-done.2, f32[1024,512]{1,0:T(8,128)S(1)} %copy-done.3, f32[1024,512]{1,0:T(8,128)S(1)} %copy-done, ...), custom_call_target="tpu_custom_call" | custom-call | tf_op jit(solution)/shard_map/edges/pallas_call | solution.py:178
  68.6 3.1 %collective-permute-start.3 = (f32[8,1024]{1,0:T(8,128)S(1)}, f32[8,1024]{1,0:T(8,128)S(1)}, u32[]{:S(2)}, u32[]{:S(2)}) collective-permute-start(f32[8,1024]{1,0:T(8,128)S(1)} %get-tuple-element.28.lo_ref), channel_id=1, source_target_pairs={{1,0},{2,1},{3,2},{4,3},{5,4},{6,5},{7,6},{9,8},{10,9},{11,10},{12... | collective-permute-start | bytes 98312 | tf_op jit(solution)/shard_map/ppermute | solution.py:200
  71.7 1.9 %collective-permute-start.2 = (f32[8,1024]{1,0:T(8,128)S(1)}, f32[8,1024]{1,0:T(8,128)S(1)}, u32[]{:S(2)}, u32[]{:S(2)}) collective-permute-start(f32[8,1024]{1,0:T(8,128)S(1)} %get-tuple-element.27), channel_id=1, source_target_pairs={{0,1},{1,2},{2,3},{3,4},{4,5},{5,6},{6,7},{8,9},{9,10},{10,11},{11... | collective-permute-start | bytes 98312 | tf_op jit(solution)/shard_map/ppermute | solution.py:200
  73.6 2.6 %collective-permute-start = (f32[8,512]{1,0:T(8,128)S(1)}, f32[8,512]{1,0:T(8,128)S(1)}, u32[]{:S(2)}, u32[]{:S(2)}) collective-permute-start(f32[8,512]{1,0:T(8,128)S(1)} %get-tuple-element.25), channel_id=1, source_target_pairs={{0,8},{8,16},{16,24},{1,9},{9,17},{17,25},{2,10},{10,18},{18,26},{... | collective-permute-start | bytes 49160 | tf_op jit(solution)/shard_map/ppermute | solution.py:200
  76.2 3.3 %collective-permute-start.1 = (f32[8,512]{1,0:T(8,128)S(1)}, f32[8,512]{1,0:T(8,128)S(1)}, u32[]{:S(2)}, u32[]{:S(2)}) collective-permute-start(f32[8,512]{1,0:T(8,128)S(1)} %get-tuple-element.26), channel_id=1, source_target_pairs={{8,0},{16,8},{24,16},{9,1},{17,9},{25,17},{10,2},{18,10},{26,18},{... | collective-permute-start | bytes 49160 | tf_op jit(solution)/shard_map/ppermute | solution.py:200
  79.5 3.4 %copy-done.4 = bf16[4,256,4096]{2,1,0:T(8,128)(2,1)S(1)} copy-done((bf16[4,256,4096]{2,1,0:T(8,128)(2,1)S(1)}, bf16[4,256,4096]{2,1,0:T(8,128)(2,1)}, u32[]{:S(2)}) %copy-start.4) | copy-done | bytes 8388632
  84.0 3.8 %pressure.1 = (f32[4,1024,128]{2,1,0:T(8,128)S(1)}, f32[8,512]{1,0:T(8,128)S(1)}, f32[8,512]{1,0:T(8,128)S(1)}, f32[8,1024]{1,0:T(8,128)S(1)}, f32[8,1024]{1,0:T(8,128)S(1)}) custom-call(s32[1,1024]{1,0:T(1,128)S(1)} %reshape.214.lab_ref, bf16[1024,256]{1,0:T(8,128)(2,1)S(1)} %bitcast.39, bf16[1024,4096]{1,0:T(8,128)(2,1)S(1)} %bitcast.33), custom_call_target="tpu_custom_call" | custom-call | flops 1073741824 | bytes 12582912 | tf_op jit(solution)/shard_map/pressure/pallas_call | solution.py:462
  87.7 2.1 %collective-permute-start.6 = (f32[8,1024]{1,0:T(8,128)S(1)}, f32[8,1024]{1,0:T(8,128)S(1)}, u32[]{:S(2)}, u32[]{:S(2)}) collective-permute-start(f32[8,1024]{1,0:T(8,128)S(1)} %get-tuple-element.40), channel_id=1, source_target_pairs={{0,1},{1,2},{2,3},{3,4},{4,5},{5,6},{6,7},{8,9},{9,10},{10,11},{11... | collective-permute-start | bytes 98312 | tf_op jit(solution)/shard_map/ppermute | solution.py:200
  89.8 4.4 %collective-permute-start.7 = (f32[8,1024]{1,0:T(8,128)S(1)}, f32[8,1024]{1,0:T(8,128)S(1)}, u32[]{:S(2)}, u32[]{:S(2)}) collective-permute-start(f32[8,1024]{1,0:T(8,128)S(1)} %get-tuple-element.41), channel_id=1, source_target_pairs={{1,0},{2,1},{3,2},{4,3},{5,4},{6,5},{7,6},{9,8},{10,9},{11,10},{12... | collective-permute-start | bytes 98312 | tf_op jit(solution)/shard_map/ppermute | solution.py:200
  94.2 3.4 %collective-permute-start.4 = (f32[8,512]{1,0:T(8,128)S(1)}, f32[8,512]{1,0:T(8,128)S(1)}, u32[]{:S(2)}, u32[]{:S(2)}) collective-permute-start(f32[8,512]{1,0:T(8,128)S(1)} %get-tuple-element.38), channel_id=1, source_target_pairs={{0,8},{8,16},{16,24},{1,9},{9,17},{17,25},{2,10},{10,18},{18,26},{... | collective-permute-start | bytes 49160 | tf_op jit(solution)/shard_map/ppermute | solution.py:200
  97.6 2.5 %collective-permute-start.5 = (f32[8,512]{1,0:T(8,128)S(1)}, f32[8,512]{1,0:T(8,128)S(1)}, u32[]{:S(2)}, u32[]{:S(2)}) collective-permute-start(f32[8,512]{1,0:T(8,128)S(1)} %get-tuple-element.39), channel_id=1, source_target_pairs={{8,0},{16,8},{24,16},{9,1},{17,9},{25,17},{10,2},{18,10},{26,18},{... | collective-permute-start | bytes 49160 | tf_op jit(solution)/shard_map/ppermute | solution.py:200
  100.1 21.7 %stencil.1 = (f32[1024,512]{1,0:T(8,128)}, f32[4,1024,128]{2,1,0:T(8,128)S(1)}, f32[4,1024,128]{2,1,0:T(8,128)S(1)}, f32[4,1024,128]{2,1,0:T(8,128)}) custom-call(f32[1024,512]{1,0:T(8,128)} %d_ref.1, s32[1024,512]{1,0:T(8,128)} %m_ref.1, f32[1024,512]{1,0:T(8,128)} %x_ref.1, f32[1024,512]{1,0:T(8,128)} %y_ref.1, f32[8,512]{1,0:T(8,128)S(1)} %collective-permute-done.up_ref, ...), custom_call_target="tpu_custom_call" | custom-call | flops 104857600 | bytes 33554432 | tf_op jit(solution)/shard_map/stencil/pallas_call | solution.py:363
  123.5 5.2 %gradient.1 = (f32[4,1024,128]{2,1,0:T(8,128)S(1)}, f32[4,1024,128]{2,1,0:T(8,128)S(1)}, f32[4,1024,128]{2,1,0:T(8,128)S(1)}) custom-call(f32[4,1024,128]{2,1,0:T(8,128)S(1)} %get-tuple-element.34.p_ref, f32[4,1024,128]{2,1,0:T(8,128)S(1)} %get-tuple-element.35.hu_ref, f32[4,1024,128]{2,1,0:T(8,128)S(1)} %get-tuple-element.36.hv_ref, ...), custom_call_target="tpu_custom_call" | custom-call | flops 10485760 | bytes 14680064 | tf_op jit(solution)/shard_map/gradient/pallas_call | solution.py:540
  131.4 1.6 %copy-done.7 = f32[4,1024,128]{2,1,0:T(8,128)S(1)} copy-done((f32[4,1024,128]{2,1,0:T(8,128)S(1)}, f32[4,1024,128]{2,1,0:T(8,128)}, u32[]{:S(2)}) %copy-start.7) | copy-done | bytes 2097176
  133.0 1.6 %copy-done.9 = f32[4,1024,128]{2,1,0:T(8,128)S(1)} copy-done((f32[4,1024,128]{2,1,0:T(8,128)S(1)}, f32[4,1024,128]{2,1,0:T(8,128)}, u32[]{:S(2)}) %copy-start.9) | copy-done | bytes 2097176
  134.6 8.7 %wind.1 = (f32[16,64,512]{2,1,0:T(8,128)}, f32[16,64,512]{2,1,0:T(8,128)}) custom-call(s32[1,1024]{1,0:T(1,128)S(1)} %reshape.214.lab_ref, bf16[1024,512]{1,0:T(8,128)(2,1)S(1)} %bitcast.34, bf16[1024,4096]{1,0:T(8,128)(2,1)} %bitcast.32, f32[4,16,64,128]{3,2,1,0:T(8,128)S(1)} %bitcast.36, f32[4,16,64,128]{3,2,1,0:T(8,128)S(1)} %bitcast.37, ...), custom_call_target="tpu_custom_call" | custom-call | flops 2147483648 | bytes 20971520 | tf_op jit(solution)/shard_map/wind/pallas_call | solution.py:592
  (56 shorter events, 19.0 us)
Async XLA Ops:
  7.2 40.6 %all-gather.2.cloned.1.call-start = ((), (), s32[]{:S(2)}) async-start(), calls=%async_computation.3 | async-start | bytes 1310720 | tf_op jit(solution)/shard_map/all_gather | solution.py:640
  7.9 1.1 copy-start.14
  13.6 26.5 %all-to-all-start = ((s32[8,1,128]{2,1,0:T(1,128)}), s32[8,1,128]{2,1,0:T(1,128)S(1)}, u32[]{:S(2)}, u32[]{:S(2)}) async-start(s32[8,1,128]{2,1,0:T(1,128)} %reshape.230), calls=%async_computation | async-start | bytes 8192 | tf_op jit(solution)/shard_map/all_to_all | solution.py:648
  43.5 12.5 %all-to-all-start.2 = ((bf16[8,128,256]{2,1,0:T(8,128)(2,1)}), bf16[8,128,256]{2,1,0:T(8,128)(2,1)S(1)}, u32[]{:S(2)}, u32[]{:S(2)}) async-start(bf16[8,128,256]{2,1,0:T(8,128)(2,1)} %bitcast.11), calls=%async_computation.2 | async-start | bytes 1048576 | tf_op jit(solution)/shard_map/all_to_all | solution.py:658
  47.7 14.0 %copy-start = (f32[1024,512]{1,0:T(8,128)S(1)}, f32[1024,512]{1,0:T(8,128)}, u32[]{:S(2)}) copy-start(f32[1024,512]{1,0:T(8,128)} %d_ref.1) | copy-start | bytes 6291460
  47.7 1.4 copy-start.13
  56.8 74.6 %all-to-all-start.1 = ((bf16[8,128,512]{2,1,0:T(8,128)(2,1)}), bf16[8,128,512]{2,1,0:T(8,128)(2,1)S(1)}, u32[]{:S(2)}, u32[]{:S(2)}) async-start(bf16[8,128,512]{2,1,0:T(8,128)(2,1)} %bitcast.35), calls=%async_computation.1 | async-start | bytes 2097152 | tf_op jit(solution)/shard_map/all_to_all | solution.py:658
  61.7 1.6 %copy-start.1 = (s32[1024,512]{1,0:T(8,128)S(1)}, s32[1024,512]{1,0:T(8,128)}, u32[]{:S(2)}) copy-start(s32[1024,512]{1,0:T(8,128)} %m_ref.1) | copy-start | bytes 6291460
  63.3 1.6 %copy-start.2 = (f32[1024,512]{1,0:T(8,128)S(1)}, f32[1024,512]{1,0:T(8,128)}, u32[]{:S(2)}) copy-start(f32[1024,512]{1,0:T(8,128)} %x_ref.1) | copy-start | bytes 6291460
  64.9 1.6 %copy-start.3 = (f32[1024,512]{1,0:T(8,128)S(1)}, f32[1024,512]{1,0:T(8,128)}, u32[]{:S(2)}) copy-start(f32[1024,512]{1,0:T(8,128)} %y_ref.1) | copy-start | bytes 6291460
  68.6 29.1 %collective-permute-start.3 = (f32[8,1024]{1,0:T(8,128)S(1)}, f32[8,1024]{1,0:T(8,128)S(1)}, u32[]{:S(2)}, u32[]{:S(2)}) collective-permute-start(f32[8,1024]{1,0:T(8,128)S(1)} %get-tuple-element.28.lo_ref), channel_id=1, source_target_pairs={{1,0},{2,1},{3,2},{4,3},{5,4},{6,5},{7,6},{9,8},{10,9},{11,10},{12... | collective-permute-start | bytes 98312 | tf_op jit(solution)/shard_map/ppermute | solution.py:200
  71.7 28.4 %collective-permute-start.2 = (f32[8,1024]{1,0:T(8,128)S(1)}, f32[8,1024]{1,0:T(8,128)S(1)}, u32[]{:S(2)}, u32[]{:S(2)}) collective-permute-start(f32[8,1024]{1,0:T(8,128)S(1)} %get-tuple-element.27), channel_id=1, source_target_pairs={{0,1},{1,2},{2,3},{3,4},{4,5},{5,6},{6,7},{8,9},{9,10},{10,11},{11... | collective-permute-start | bytes 98312 | tf_op jit(solution)/shard_map/ppermute | solution.py:200
  73.6 16.2 %collective-permute-start = (f32[8,512]{1,0:T(8,128)S(1)}, f32[8,512]{1,0:T(8,128)S(1)}, u32[]{:S(2)}, u32[]{:S(2)}) collective-permute-start(f32[8,512]{1,0:T(8,128)S(1)} %get-tuple-element.25), channel_id=1, source_target_pairs={{0,8},{8,16},{16,24},{1,9},{9,17},{17,25},{2,10},{10,18},{18,26},{... | collective-permute-start | bytes 49160 | tf_op jit(solution)/shard_map/ppermute | solution.py:200
  76.2 18.1 %collective-permute-start.1 = (f32[8,512]{1,0:T(8,128)S(1)}, f32[8,512]{1,0:T(8,128)S(1)}, u32[]{:S(2)}, u32[]{:S(2)}) collective-permute-start(f32[8,512]{1,0:T(8,128)S(1)} %get-tuple-element.26), channel_id=1, source_target_pairs={{8,0},{16,8},{24,16},{9,1},{17,9},{25,17},{10,2},{18,10},{26,18},{... | collective-permute-start | bytes 49160 | tf_op jit(solution)/shard_map/ppermute | solution.py:200
  79.5 3.4 %copy-start.4 = (bf16[4,256,4096]{2,1,0:T(8,128)(2,1)S(1)}, bf16[4,256,4096]{2,1,0:T(8,128)(2,1)}, u32[]{:S(2)}) copy-start(bf16[4,256,4096]{2,1,0:T(8,128)(2,1)} %param.12) | copy-start | bytes 25165828
  87.7 34.1 %collective-permute-start.6 = (f32[8,1024]{1,0:T(8,128)S(1)}, f32[8,1024]{1,0:T(8,128)S(1)}, u32[]{:S(2)}, u32[]{:S(2)}) collective-permute-start(f32[8,1024]{1,0:T(8,128)S(1)} %get-tuple-element.40), channel_id=1, source_target_pairs={{0,1},{1,2},{2,3},{3,4},{4,5},{5,6},{6,7},{8,9},{9,10},{10,11},{11... | collective-permute-start | bytes 98312 | tf_op jit(solution)/shard_map/ppermute | solution.py:200
  89.8 32.1 %collective-permute-start.7 = (f32[8,1024]{1,0:T(8,128)S(1)}, f32[8,1024]{1,0:T(8,128)S(1)}, u32[]{:S(2)}, u32[]{:S(2)}) collective-permute-start(f32[8,1024]{1,0:T(8,128)S(1)} %get-tuple-element.41), channel_id=1, source_target_pairs={{1,0},{2,1},{3,2},{4,3},{5,4},{6,5},{7,6},{9,8},{10,9},{11,10},{12... | collective-permute-start | bytes 98312 | tf_op jit(solution)/shard_map/ppermute | solution.py:200
  94.2 27.6 %collective-permute-start.4 = (f32[8,512]{1,0:T(8,128)S(1)}, f32[8,512]{1,0:T(8,128)S(1)}, u32[]{:S(2)}, u32[]{:S(2)}) collective-permute-start(f32[8,512]{1,0:T(8,128)S(1)} %get-tuple-element.38), channel_id=1, source_target_pairs={{0,8},{8,16},{16,24},{1,9},{9,17},{17,25},{2,10},{10,18},{18,26},{... | collective-permute-start | bytes 49160 | tf_op jit(solution)/shard_map/ppermute | solution.py:200
  97.6 24.3 %collective-permute-start.5 = (f32[8,512]{1,0:T(8,128)S(1)}, f32[8,512]{1,0:T(8,128)S(1)}, u32[]{:S(2)}, u32[]{:S(2)}) collective-permute-start(f32[8,512]{1,0:T(8,128)S(1)} %get-tuple-element.39), channel_id=1, source_target_pairs={{8,0},{16,8},{24,16},{9,1},{17,9},{25,17},{10,2},{18,10},{26,18},{... | collective-permute-start | bytes 49160 | tf_op jit(solution)/shard_map/ppermute | solution.py:200
  121.9 1.6 %copy-start.12 = (f32[4,1024,128]{2,1,0:T(8,128)S(1)}, f32[4,1024,128]{2,1,0:T(8,128)}, u32[]{:S(2)}) copy-start(f32[4,1024,128]{2,1,0:T(8,128)} %get-tuple-element.37.h_ref) | copy-start | bytes 6291460
  128.7 1.3 copy-start.6
  130.1 1.3 copy-start.8
  131.4 1.6 %copy-start.7 = (f32[4,1024,128]{2,1,0:T(8,128)S(1)}, f32[4,1024,128]{2,1,0:T(8,128)}, u32[]{:S(2)}) copy-start(f32[4,1024,128]{2,1,0:T(8,128)} %copy-done.6) | copy-start | bytes 6291460
  133.0 1.6 %copy-start.9 = (f32[4,1024,128]{2,1,0:T(8,128)S(1)}, f32[4,1024,128]{2,1,0:T(8,128)}, u32[]{:S(2)}) copy-start(f32[4,1024,128]{2,1,0:T(8,128)} %copy-done.8) | copy-start | bytes 6291460
  (6 other events, 4.9 us)
Sparse Core Ops, SparseCore 0:
  10.1 37.1 all-gather.1

commit v4 on v3

--- a/solution.py
+++ b/solution.py
@@ -118,21 +118,37 @@
     )(blend, atm)
 
 
-def serve_kernel(asked_ref, tiles_ref, out_ref):
-    asked = asked_ref[...]
-    pick = (asked == iota((asked.shape[0], tiles_ref.shape[0]), 1)).astype(BF16)
-    out_ref[...] = jnp.dot(pick, tiles_ref[...], preferred_element_type=F32).astype(BF16)
-
-
-def serve(asked, tiles):
+def serve_kernel(after_ref, asked_ref, tiles_ref, out_ref, turned, pick):
+    peers, _, capacity = asked_ref.shape
+    width = turned.shape[0]
+    turned[...] = jnp.zeros_like(turned)
+    turned[0:peers, 0:capacity] = asked_ref[:, 0, :]
+    columns = turned[...].T
+    blocks = tiles_ref.shape[0]
+    names = iota((capacity, blocks), 1)
+    for d in range(peers):
+        pick[d * capacity:(d + 1) * capacity, :] = (columns[0:capacity, d:d + 1] == names).astype(F32)
+    out_ref[...] = jnp.dot(
+        pick[...].astype(BF16), tiles_ref[...], preferred_element_type=F32
+    ).astype(BF16)
+
+
+def serve(after, asked, tiles):
+    peers, _, capacity = asked.shape
+    slots = peers * capacity
+    width = -(-max(peers, capacity) // LANES) * LANES
     return pl.pallas_call(
         serve_kernel,
-        out_shape=jax.ShapeDtypeStruct((asked.shape[0], tiles.shape[1]), BF16),
-        in_specs=[VMEM, VMEM],
+        out_shape=jax.ShapeDtypeStruct((slots, tiles.shape[1]), BF16),
+        in_specs=[pl.BlockSpec(memory_space=pl.ANY), VMEM, VMEM],
         out_specs=VMEM,
+        scratch_shapes=[
+            pltpu.VMEM((width, width), jnp.int32),
+            pltpu.VMEM((slots, tiles.shape[0]), F32),
+        ],
         compiler_params=params(32 << 20),
         name="serve",
-    )(asked, tiles)
+    )(after, asked, tiles)
 
 
 def edges_kernel(
@@ -186,7 +202,7 @@
             pl.BlockSpec((TILE, rows), lambda i: (0, 0)),
             pl.BlockSpec((TILE, rows), lambda i: (0, 0)),
         ),
-        compiler_params=params(24 << 20),
+        compiler_params=params(),
         name="edges",
     )(*(fields * 4))
 
@@ -310,36 +326,47 @@
 
     @pl.when(step > 0)
     def _():
+        start = pl.multiple_of((step - 1) * BAND, BAND)
+
+        def across(t, carry):
+            base = pl.multiple_of(start + t * TILE + TILE, TILE)
+            for g in range(GROUPS):
+                now = along_x([ref[g, pl.ds(base, TILE), :] for ref in cell])
+                nxt = along_x([ref[g, pl.ds(base + 1, TILE), :] for ref in cell])
+                for dst, val in zip(gx, flux(now, nxt)):
+                    dst[g, pl.ds(base, TILE), :] = val
+            return carry
+
+        lax.fori_loop(0, BAND // TILE, across, 0, unroll=2)
+
         def body(t, carry):
-            here = pl.multiple_of(t * TILE, TILE)
-            mark = pl.multiple_of((step - 1) * BAND + t * TILE, TILE)
+            mark = pl.multiple_of(start + t * TILE, TILE)
             base = pl.multiple_of(mark + TILE, TILE)
+            at = pl.ds(pl.multiple_of(t * TILE, TILE), TILE)
             sides = ecol[pl.ds(mark, TILE), :]
-            now = [[ref[g, pl.ds(base, TILE), :] for ref in cell] for g in range(GROUPS)]
-            back = [[pltpu.roll(val, LANES - 1, 1) for val in now[g][:3]] for g in range(GROUPS)]
-            gy = []
+            before = [pltpu.roll(sides, LANES - 4 - f, 1) for f in range(3)]
             for g in range(GROUPS):
+                now = [ref[g, pl.ds(base, TILE), :] for ref in cell]
                 if g < GROUPS - 1:
-                    other = back[g + 1]
+                    other = [ref[g + 1, pl.ds(base, TILE), :] for ref in cell[:3]]
                 else:
-                    other = [sides[:, f:f + 1] for f in range(3)]
-                right = [jnp.where(lane == LANES - 1, o, b) for o, b in zip(other, back[g])]
-                gy.append(flux(along_y(now[g]), along_y(derived(*right))))
-            moved = [[pltpu.roll(val, 1, 1) for val in gy[g]] for g in range(GROUPS)]
-            for g in range(GROUPS):
-                nxt = [ref[g, pl.ds(base + 1, TILE), :] for ref in cell]
-                fx = flux(along_x(now[g]), along_x(nxt))
-                for dst, val in zip(gx, fx):
-                    dst[g, pl.ds(base, TILE), :] = val
+                    other = [sides] + [pltpu.roll(sides, LANES - f, 1) for f in (1, 2)]
+                right = [
+                    pltpu.roll(jnp.where(lane == 0, o, c), LANES - 1, 1)
+                    for o, c in zip(other, now[:3])
+                ]
+                fy = flux(along_y(now), along_y(derived(*right)))
+                py = [
+                    pltpu.roll(jnp.where(lane == LANES - 1, o, c), 1, 1)
+                    for o, c in zip(before, fy)
+                ]
+                before = fy
+                fx = [src[g, pl.ds(base, TILE), :] for src in gx]
                 px = [src[g, pl.ds(base - 1, TILE), :] for src in gx]
-                other = moved[g - 1] if g else [sides[:, 3 + f:4 + f] for f in range(3)]
-                py = [jnp.where(lane == 0, o, b) for o, b in zip(other, moved[g])]
-                fy = gy[g]
-                h, u, v = now[g][:3]
+                h, u, v = now[:3]
                 ch = (fx[0] - px[0]) + (fy[0] - py[0])
                 cx = (fx[1] - px[1]) + (fy[2] - py[2])
                 cy = (fx[2] - px[2]) + (fy[1] - py[1])
-                at = pl.ds(here, TILE)
                 newh_ref[at, g * LANES:(g + 1) * LANES] = jnp.where(
                     h > 0.0, h - (0.5 * DT_DX) * ch, 0.0
                 )
@@ -370,7 +397,7 @@
         ),
         scratch_shapes=[pad] * (CELL + 3)
         + [pltpu.VMEM((LANES, rows), F32), pltpu.VMEM((rows, LANES), F32)],
-        compiler_params=params(48 << 20),
+        compiler_params=params(),
         cost_estimate=pl.CostEstimate(
             flops=200 * rows * cols, bytes_accessed=64 * rows * cols, transcendentals=0
         ),
@@ -634,39 +661,31 @@
     capacity = 2 * entries // devices
     slots = devices * capacity
     atm = atm_blocks.reshape(atm_blocks.shape[2:]).transpose(1, 0, 2)
-    blocks = atm.shape[1]
-    press, wind = mix(blend.reshape(1), atm)
-    press = lax.all_gather(press, "gx", axis=0, tiled=True)
-    wind = lax.all_gather(wind, "gx", axis=0, tiled=True)
-
-    source = ovl_source.reshape(1, entries)
-    source = (source % count_y) * count_x + source // count_y
+    both = ("gx", "gy")
     want, lab = make_requests(
-        source, ovl_block.reshape(1, entries),
+        ovl_source.reshape(1, entries), ovl_block.reshape(1, entries),
         ovl_patch.reshape(1, entries), ovl_weight.reshape(1, entries), devices, capacity,
     )
     asked = lax.all_to_all(
-        want.reshape(count_y, count_x, capacity), "gy", split_axis=0, concat_axis=0, tiled=True
+        want.reshape(devices, 1, capacity), both, split_axis=0, concat_axis=0, tiled=True
     )
-    asked = asked + blocks * jnp.arange(count_x, dtype=jnp.int32)[None, :, None]
-    asked = asked.reshape(slots, 1)
     lab = lab.reshape(1, slots)
-
-    def exchange(tiles):
-        rows = serve(asked, tiles)
-        parts = rows.reshape(count_y, slots // count_y, rows.shape[1])
-        got = lax.all_to_all(parts, "gy", split_axis=0, concat_axis=0, tiled=True)
+    press, wind = mix(blend.reshape(1), atm)
+    top, bottom, left, right = edge_cells(depth_field, wet_mask, mom_x, mom_y)
+
+    def exchange(after, tiles):
+        rows = serve(after, asked, tiles)
+        parts = rows.reshape(devices, capacity, rows.shape[1])
+        got = lax.all_to_all(parts, both, split_axis=0, concat_axis=0, tiled=True)
         return got.reshape(rows.shape)
 
-    press = exchange(press)
-    wind = exchange(wind)
-
-    top, bottom, left, right = edge_cells(depth_field, wet_mask, mom_x, mom_y)
+    press = exchange(top, press)
     newh, hu, hv, h = stencil(
         depth_field, wet_mask, mom_x, mom_y,
         send(bottom, "gx", 1), send(top, "gx", -1),
         send(right, "gy", 1), send(left, "gy", -1), left,
     )
+    wind = exchange(newh, wind)
     weights = remap_weights.reshape(NW * ABLK, PATCH * PATCH)
     p, top, bottom, left, right = pressure_field(lab, press, weights)
     hu, hv, fac = gradient(

time: 151 us -> 121 us (0.80)
  blocking collectives: 22.2 us -> 0 us
  between operations: 14.9 us -> 1.49 us
  local copies, waits for them, and re-layouts: 24.8 us -> 16.6 us
  Pallas kernels: 45.5 us -> 52.2 us
  waiting for transfers between devices: 4.68 us -> 9.18 us
  starting transfers between devices: 36.6 us -> 40.4 us
    all_gather x1 -> x0, blocking collectives: 22.2 us -> none  [body(): press = lax.all_gather(press, 'gx', axis=0, tiled=True)]
    ppermute x8, waiting for transfers between devices: 0.02 us -> 9.17 us  [send(): return lax.ppermute(value, axis, pairs)]
    unnamed x38, local copies, waits for them, and re-layouts: 23.7 us -> 16.6 us
    all_to_all x3, waiting for transfers between devices: 4.64 us -> 0.01 us  [the longest x2 0.01 us: exchange(): got = lax.all_to_all(parts, both, split_axis=0, concat_axis=0, tiled=True)]
    pallas_call x1, Pallas kernels: 21.7 us -> 26 us  [stencil(): pl.pallas_call(stencil_kernel, grid=(bands + 1,), out_shape=(jax.ShapeDty...]
    all_to_all x3, starting transfers between devices: 13.4 us -> 15.8 us  [the longest x2 9.84 us: exchange(): got = lax.all_to_all(parts, both, split_axis=0, concat_axis=0, tiled=True)]
    pallas_call x1, Pallas kernels: 2.03 us -> 4.46 us  [edge_cells(): pl.pallas_call(edges_kernel, grid=(1,), out_shape=(line, line, column, co...]
  transfers between devices with their start and end apart: 12 -> 11, of which waited for: 1 -> 3; matrix products, arithmetic and copies ran while one was open for 2% -> 0% of each run, Pallas kernels for 24% -> 34%
where the time goes in v4:
time: 121 us; the launch traced here: 120 us
  Pallas kernels  52.2 us (43%)
  starting transfers between devices  40.4 us (33%)
  local copies, waits for them, and re-layouts  16.6 us (14%)
  waiting for transfers between devices  9.18 us (8%)
  between operations  1.49 us (1%)
    pallas_call x1, Pallas kernels, stencil(): pl.pallas_call(stencil_kernel, grid=(bands + 1,), out_shape=(jax.ShapeDty...  26 us
    ppermute x8, starting transfers between devices, send(): return lax.ppermute(value, axis, pairs)  24.6 us
    unnamed x38, local copies, waits for them, and re-layouts  16.6 us
    all_to_all x2, starting transfers between devices, exchange(): got = lax.all_to_all(parts, both, split_axis=0, concat_axis=0, tiled=True)  9.84 us
    ppermute x8, waiting for transfers between devices, send(): return lax.ppermute(value, axis, pairs)  9.17 us
    pallas_call x1, Pallas kernels, wind_field(): pl.pallas_call(wind_kernel, grid=(steps,), out_shape=(shape, shape), in_s...  8.7 us
    all_to_all x1, starting transfers between devices, body(): lax.all_to_all(want.reshape(devices, 1, capacity), both, split_axis=0, co...  5.99 us
    pallas_call x1, Pallas kernels, gradient(): pl.pallas_call(gradient_kernel, grid=(rows // BAND,), out_shape=(plane,)...  5.26 us
  transfers between devices with their start and end apart: 11, of which 3 were waited for; matrix products, arithmetic and copies ran while one was open for 0% of the time, Pallas kernels for 34%

profile of v4, /device:TPU:12, one launch (start us, length us, event | category | flops | bytes accessed | tf_op | source)
XLA Modules:
  0.0 119.9 jit_solution(11604414643876255469)
XLA Ops:
  4.3 6.0 %all-to-all-start = ((s32[32,1,32]{2,1,0:T(1,128)}), s32[32,1,32]{2,1,0:T(1,128)S(1)}, u32[]{:S(2)}, u32[]{:S(2)}) async-start(s32[32,1,32]{2,1,0:T(1,128)} %bitcast.4), calls=%async_computation | async-start | bytes 32768 | tf_op jit(solution)/shard_map/all_to_all | solution.py:669
  12.2 4.5 %edges.1 = (f32[8,512]{1,0:T(8,128)}, f32[8,512]{1,0:T(8,128)}, f32[8,1024]{1,0:T(8,128)}, f32[8,1024]{1,0:T(8,128)}) custom-call(f32[1024,512]{1,0:T(8,128)} %d_ref.1, s32[1024,512]{1,0:T(8,128)} %m_ref.1, f32[1024,512]{1,0:T(8,128)} %x_ref.1, f32[1024,512]{1,0:T(8,128)} %y_ref.1, f32[1024,512]{1,0:T(8,128)} %d_ref.1, s32[1024,512]{1,0:T(8,128)} %m_ref.1, ...), custom_call_target="tpu_custom_call" | custom-call | tf_op jit(solution)/shard_map/edges/pallas_call | solution.py:194
  18.7 5.8 %all-to-all-start.2 = ((bf16[32,32,256]{2,1,0:T(8,128)(2,1)}), bf16[32,32,256]{2,1,0:T(8,128)(2,1)S(1)}, u32[]{:S(2)}, u32[]{:S(2)}) async-start(bf16[32,32,256]{2,1,0:T(8,128)(2,1)} %bitcast.11), calls=%async_computation.2 | async-start | bytes 1048576 | tf_op jit(solution)/shard_map/all_to_all | solution.py:679
  24.6 2.1 %collective-permute-start.2 = (f32[8,1024]{1,0:T(8,128)}, f32[8,1024]{1,0:T(8,128)S(1)}, u32[]{:S(2)}, u32[]{:S(2)}) collective-permute-start(f32[8,1024]{1,0:T(8,128)} %get-tuple-element.27), channel_id=1, source_target_pairs={{0,1},{1,2},{2,3},{3,4},{4,5},{5,6},{6,7},{8,9},{9,10},{10,11},{11... | collective-permute-start | bytes 98312 | tf_op jit(solution)/shard_map/ppermute | solution.py:216
  26.6 4.4 %collective-permute-start.3 = (f32[8,1024]{1,0:T(8,128)}, f32[8,1024]{1,0:T(8,128)S(1)}, u32[]{:S(2)}, u32[]{:S(2)}) collective-permute-start(f32[8,1024]{1,0:T(8,128)} %get-tuple-element.28.lo_ref), channel_id=1, source_target_pairs={{1,0},{2,1},{3,2},{4,3},{5,4},{6,5},{7,6},{9,8},{10,9},{11,10},{12... | collective-permute-start | bytes 98312 | tf_op jit(solution)/shard_map/ppermute | solution.py:216
  31.0 3.4 %collective-permute-start = (f32[8,512]{1,0:T(8,128)}, f32[8,512]{1,0:T(8,128)S(1)}, u32[]{:S(2)}, u32[]{:S(2)}) collective-permute-start(f32[8,512]{1,0:T(8,128)} %get-tuple-element.25), channel_id=1, source_target_pairs={{0,8},{8,16},{16,24},{1,9},{9,17},{17,25},{2,10},{10,18},{18,26},{... | collective-permute-start | bytes 49160 | tf_op jit(solution)/shard_map/ppermute | solution.py:216
  34.4 2.5 %collective-permute-start.1 = (f32[8,512]{1,0:T(8,128)}, f32[8,512]{1,0:T(8,128)S(1)}, u32[]{:S(2)}, u32[]{:S(2)}) collective-permute-start(f32[8,512]{1,0:T(8,128)} %get-tuple-element.26.after_ref), channel_id=1, source_target_pairs={{8,0},{16,8},{24,16},{9,1},{17,9},{25,17},{10,2},{18,10},{26,18},{... | collective-permute-start | bytes 49160 | tf_op jit(solution)/shard_map/ppermute | solution.py:216
  36.9 3.4 %collective-permute-done.1.dn_ref = f32[8,512]{1,0:T(8,128)S(1)} collective-permute-done((f32[8,512]{1,0:T(8,128)}, f32[8,512]{1,0:T(8,128)S(1)}, u32[]{:S(2)}, u32[]{:S(2)}) %collective-permute-start.1) | collective-permute-done | bytes 16416 | tf_op jit(solution)/shard_map/ppermute | solution.py:216
  41.5 26.0 %stencil.1 = (f32[1024,512]{1,0:T(8,128)}, f32[4,1024,128]{2,1,0:T(8,128)}, f32[4,1024,128]{2,1,0:T(8,128)}, f32[4,1024,128]{2,1,0:T(8,128)}) custom-call(f32[1024,512]{1,0:T(8,128)} %d_ref.1, s32[1024,512]{1,0:T(8,128)} %m_ref.1, f32[1024,512]{1,0:T(8,128)} %x_ref.1, f32[1024,512]{1,0:T(8,128)} %y_ref.1, f32[8,512]{1,0:T(8,128)} %copy-done.17, ...), custom_call_target="tpu_custom_call" | custom-call | flops 104857600 | bytes 33554432 | tf_op jit(solution)/shard_map/stencil/pallas_call | solution.py:390
  67.6 1.6 %copy-done.5 = f32[1024,512]{1,0:T(8,128)S(1)} copy-done((f32[1024,512]{1,0:T(8,128)S(1)}, f32[1024,512]{1,0:T(8,128)}, u32[]{:S(2)}) %copy-start.5) | copy-done | bytes 2097176
  69.1 1.6 %serve.2 = bf16[1024,512]{1,0:T(8,128)(2,1)} custom-call(f32[1024,512]{1,0:T(8,128)S(1)} %copy-done.5, s32[32,1,32]{2,1,0:T(1,128)S(1)} %all-to-all-done.asked_ref, bf16[256,512]{1,0:T(8,128)(2,1)S(1)} %get-tuple-element.32.tiles_ref), custom_call_target="tpu_custom_call" | custom-call | tf_op jit(solution)/shard_map/serve/pallas_call | solution.py:140
  70.7 4.0 %all-to-all-start.1 = ((bf16[32,32,512]{2,1,0:T(8,128)(2,1)}), bf16[32,32,512]{2,1,0:T(8,128)(2,1)S(1)}, u32[]{:S(2)}, u32[]{:S(2)}) async-start(bf16[32,32,512]{2,1,0:T(8,128)(2,1)} %bitcast.8), calls=%async_computation.1 | async-start | bytes 2097152 | tf_op jit(solution)/shard_map/all_to_all | solution.py:679
  74.8 3.4 %copy-done = bf16[4,256,4096]{2,1,0:T(8,128)(2,1)S(1)} copy-done((bf16[4,256,4096]{2,1,0:T(8,128)(2,1)S(1)}, bf16[4,256,4096]{2,1,0:T(8,128)(2,1)}, u32[]{:S(2)}) %copy-start) | copy-done | bytes 8388632
  78.2 3.8 %pressure.1 = (f32[4,1024,128]{2,1,0:T(8,128)S(1)}, f32[8,512]{1,0:T(8,128)S(1)}, f32[8,512]{1,0:T(8,128)S(1)}, f32[8,1024]{1,0:T(8,128)S(1)}, f32[8,1024]{1,0:T(8,128)S(1)}) custom-call(s32[1,1024]{1,0:T(1,128)S(1)} %reshape.64.lab_ref, bf16[1024,256]{1,0:T(8,128)(2,1)S(1)} %bitcast.26, bf16[1024,4096]{1,0:T(8,128)(2,1)S(1)} %bitcast.21), custom_call_target="tpu_custom_call" | custom-call | flops 1073741824 | bytes 12582912 | tf_op jit(solution)/shard_map/pressure/pallas_call | solution.py:489
  82.0 2.1 %collective-permute-start.6 = (f32[8,1024]{1,0:T(8,128)S(1)}, f32[8,1024]{1,0:T(8,128)S(1)}, u32[]{:S(2)}, u32[]{:S(2)}) collective-permute-start(f32[8,1024]{1,0:T(8,128)S(1)} %get-tuple-element.40), channel_id=1, source_target_pairs={{0,1},{1,2},{2,3},{3,4},{4,5},{5,6},{6,7},{8,9},{9,10},{10,11},{11... | collective-permute-start | bytes 98312 | tf_op jit(solution)/shard_map/ppermute | solution.py:216
  84.0 4.4 %collective-permute-start.7 = (f32[8,1024]{1,0:T(8,128)S(1)}, f32[8,1024]{1,0:T(8,128)S(1)}, u32[]{:S(2)}, u32[]{:S(2)}) collective-permute-start(f32[8,1024]{1,0:T(8,128)S(1)} %get-tuple-element.41), channel_id=1, source_target_pairs={{1,0},{2,1},{3,2},{4,3},{5,4},{6,5},{7,6},{9,8},{10,9},{11,10},{12... | collective-permute-start | bytes 98312 | tf_op jit(solution)/shard_map/ppermute | solution.py:216
  88.5 3.4 %collective-permute-start.4 = (f32[8,512]{1,0:T(8,128)S(1)}, f32[8,512]{1,0:T(8,128)S(1)}, u32[]{:S(2)}, u32[]{:S(2)}) collective-permute-start(f32[8,512]{1,0:T(8,128)S(1)} %get-tuple-element.38), channel_id=1, source_target_pairs={{0,8},{8,16},{16,24},{1,9},{9,17},{17,25},{2,10},{10,18},{18,26},{... | collective-permute-start | bytes 49160 | tf_op jit(solution)/shard_map/ppermute | solution.py:216
  91.8 2.5 %collective-permute-start.5 = (f32[8,512]{1,0:T(8,128)S(1)}, f32[8,512]{1,0:T(8,128)S(1)}, u32[]{:S(2)}, u32[]{:S(2)}) collective-permute-start(f32[8,512]{1,0:T(8,128)S(1)} %get-tuple-element.39), channel_id=1, source_target_pairs={{8,0},{16,8},{24,16},{9,1},{17,9},{25,17},{10,2},{18,10},{26,18},{... | collective-permute-start | bytes 49160 | tf_op jit(solution)/shard_map/ppermute | solution.py:216
  94.3 3.9 %collective-permute-done.4.up_ref = f32[8,512]{1,0:T(8,128)S(1)} collective-permute-done((f32[8,512]{1,0:T(8,128)S(1)}, f32[8,512]{1,0:T(8,128)S(1)}, u32[]{:S(2)}, u32[]{:S(2)}) %collective-permute-start.4) | collective-permute-done | bytes 16416 | tf_op jit(solution)/shard_map/ppermute | solution.py:216
  98.2 1.9 %collective-permute-done.5.dn_ref = f32[8,512]{1,0:T(8,128)S(1)} collective-permute-done((f32[8,512]{1,0:T(8,128)S(1)}, f32[8,512]{1,0:T(8,128)S(1)}, u32[]{:S(2)}, u32[]{:S(2)}) %collective-permute-start.5) | collective-permute-done | bytes 16416 | tf_op jit(solution)/shard_map/ppermute | solution.py:216
  100.1 5.3 %gradient.1 = (f32[4,1024,128]{2,1,0:T(8,128)S(1)}, f32[4,1024,128]{2,1,0:T(8,128)S(1)}, f32[4,1024,128]{2,1,0:T(8,128)S(1)}) custom-call(f32[4,1024,128]{2,1,0:T(8,128)S(1)} %get-tuple-element.34.p_ref, f32[4,1024,128]{2,1,0:T(8,128)S(1)} %copy-done.6, f32[4,1024,128]{2,1,0:T(8,128)S(1)} %copy-done.7, f32[4,1024,128]{2,1,0:T(8,128)S(1)} %copy-done.8, ...), custom_call_target="tpu_custom_call" | custom-call | flops 10485760 | bytes 14680064 | tf_op jit(solution)/shard_map/gradient/pallas_call | solution.py:567
  108.1 1.6 %copy-done.2 = f32[4,1024,128]{2,1,0:T(8,128)S(1)} copy-done((f32[4,1024,128]{2,1,0:T(8,128)S(1)}, f32[4,1024,128]{2,1,0:T(8,128)}, u32[]{:S(2)}) %copy-start.2) | copy-done | bytes 2097176
  109.6 1.6 %copy-done.4 = f32[4,1024,128]{2,1,0:T(8,128)S(1)} copy-done((f32[4,1024,128]{2,1,0:T(8,128)S(1)}, f32[4,1024,128]{2,1,0:T(8,128)}, u32[]{:S(2)}) %copy-start.4) | copy-done | bytes 2097176
  111.2 8.7 %wind.1 = (f32[16,64,512]{2,1,0:T(8,128)}, f32[16,64,512]{2,1,0:T(8,128)}) custom-call(s32[1,1024]{1,0:T(1,128)S(1)} %reshape.64.lab_ref, bf16[1024,512]{1,0:T(8,128)(2,1)S(1)} %bitcast.22, bf16[1024,4096]{1,0:T(8,128)(2,1)} %bitcast.20, f32[4,16,64,128]{3,2,1,0:T(8,128)S(1)} %bitcast.23, f32[4,16,64,128]{3,2,1,0:T(8,128)S(1)} %bitcast.24, ...), custom_call_target="tpu_custom_call" | custom-call | flops 2147483648 | bytes 20971520 | tf_op jit(solution)/shard_map/wind/pallas_call | solution.py:619
  (46 shorter events, 10.9 us)
Async XLA Ops:
  0.6 0.7 copy-start.11
  4.3 12.4 %all-to-all-start = ((s32[32,1,32]{2,1,0:T(1,128)}), s32[32,1,32]{2,1,0:T(1,128)S(1)}, u32[]{:S(2)}, u32[]{:S(2)}) async-start(s32[32,1,32]{2,1,0:T(1,128)} %bitcast.4), calls=%async_computation | async-start | bytes 32768 | tf_op jit(solution)/shard_map/all_to_all | solution.py:669
  10.9 1.1 copy-start.9
  16.7 0.7 copy-start.10
  18.7 52.0 %all-to-all-start.2 = ((bf16[32,32,256]{2,1,0:T(8,128)(2,1)}), bf16[32,32,256]{2,1,0:T(8,128)(2,1)S(1)}, u32[]{:S(2)}, u32[]{:S(2)}) async-start(bf16[32,32,256]{2,1,0:T(8,128)(2,1)} %bitcast.11), calls=%async_computation.2 | async-start | bytes 1048576 | tf_op jit(solution)/shard_map/all_to_all | solution.py:679
  24.6 15.7 %collective-permute-start.2 = (f32[8,1024]{1,0:T(8,128)}, f32[8,1024]{1,0:T(8,128)S(1)}, u32[]{:S(2)}, u32[]{:S(2)}) collective-permute-start(f32[8,1024]{1,0:T(8,128)} %get-tuple-element.27), channel_id=1, source_target_pairs={{0,1},{1,2},{2,3},{3,4},{4,5},{5,6},{6,7},{8,9},{9,10},{10,11},{11... | collective-permute-start | bytes 98312 | tf_op jit(solution)/shard_map/ppermute | solution.py:216
  26.6 13.7 %collective-permute-start.3 = (f32[8,1024]{1,0:T(8,128)}, f32[8,1024]{1,0:T(8,128)S(1)}, u32[]{:S(2)}, u32[]{:S(2)}) collective-permute-start(f32[8,1024]{1,0:T(8,128)} %get-tuple-element.28.lo_ref), channel_id=1, source_target_pairs={{1,0},{2,1},{3,2},{4,3},{5,4},{6,5},{7,6},{9,8},{10,9},{11,10},{12... | collective-permute-start | bytes 98312 | tf_op jit(solution)/shard_map/ppermute | solution.py:216
  31.0 5.9 %collective-permute-start = (f32[8,512]{1,0:T(8,128)}, f32[8,512]{1,0:T(8,128)S(1)}, u32[]{:S(2)}, u32[]{:S(2)}) collective-permute-start(f32[8,512]{1,0:T(8,128)} %get-tuple-element.25), channel_id=1, source_target_pairs={{0,8},{8,16},{16,24},{1,9},{9,17},{17,25},{2,10},{10,18},{18,26},{... | collective-permute-start | bytes 49160 | tf_op jit(solution)/shard_map/ppermute | solution.py:216
  34.4 5.8 %collective-permute-start.1 = (f32[8,512]{1,0:T(8,128)}, f32[8,512]{1,0:T(8,128)S(1)}, u32[]{:S(2)}, u32[]{:S(2)}) collective-permute-start(f32[8,512]{1,0:T(8,128)} %get-tuple-element.26.after_ref), channel_id=1, source_target_pairs={{8,0},{16,8},{24,16},{9,1},{17,9},{25,17},{10,2},{18,10},{26,18},{... | collective-permute-start | bytes 49160 | tf_op jit(solution)/shard_map/ppermute | solution.py:216
  36.9 3.4 %copy-start.17 = (f32[8,512]{1,0:T(8,128)}, f32[8,512]{1,0:T(8,128)S(1)}, u32[]{:S(2)}) copy-start(f32[8,512]{1,0:T(8,128)S(1)} %collective-permute-done.up_ref) | copy-start | bytes 49156
  67.5 1.6 %copy-start.5 = (f32[1024,512]{1,0:T(8,128)S(1)}, f32[1024,512]{1,0:T(8,128)}, u32[]{:S(2)}) copy-start(f32[1024,512]{1,0:T(8,128)} %get-tuple-element.22.after_ref) | copy-start | bytes 6291460
  70.7 37.4 %all-to-all-start.1 = ((bf16[32,32,512]{2,1,0:T(8,128)(2,1)}), bf16[32,32,512]{2,1,0:T(8,128)(2,1)S(1)}, u32[]{:S(2)}, u32[]{:S(2)}) async-start(bf16[32,32,512]{2,1,0:T(8,128)(2,1)} %bitcast.8), calls=%async_computation.1 | async-start | bytes 2097152 | tf_op jit(solution)/shard_map/all_to_all | solution.py:679
  74.8 3.4 %copy-start = (bf16[4,256,4096]{2,1,0:T(8,128)(2,1)S(1)}, bf16[4,256,4096]{2,1,0:T(8,128)(2,1)}, u32[]{:S(2)}) copy-start(bf16[4,256,4096]{2,1,0:T(8,128)(2,1)} %param.12) | copy-start | bytes 25165828
  78.2 21.9 %copy-start.6 = (f32[4,1024,128]{2,1,0:T(8,128)S(1)}, f32[4,1024,128]{2,1,0:T(8,128)}, u32[]{:S(2)}) copy-start(f32[4,1024,128]{2,1,0:T(8,128)} %get-tuple-element.35.hu_ref) | copy-start | bytes 6291460
  78.2 21.9 %copy-start.7 = (f32[4,1024,128]{2,1,0:T(8,128)S(1)}, f32[4,1024,128]{2,1,0:T(8,128)}, u32[]{:S(2)}) copy-start(f32[4,1024,128]{2,1,0:T(8,128)} %get-tuple-element.36.hv_ref) | copy-start | bytes 6291460
  78.2 21.9 %copy-start.8 = (f32[4,1024,128]{2,1,0:T(8,128)S(1)}, f32[4,1024,128]{2,1,0:T(8,128)}, u32[]{:S(2)}) copy-start(f32[4,1024,128]{2,1,0:T(8,128)} %get-tuple-element.37.h_ref) | copy-start | bytes 6291460
  82.0 18.1 %collective-permute-start.6 = (f32[8,1024]{1,0:T(8,128)S(1)}, f32[8,1024]{1,0:T(8,128)S(1)}, u32[]{:S(2)}, u32[]{:S(2)}) collective-permute-start(f32[8,1024]{1,0:T(8,128)S(1)} %get-tuple-element.40), channel_id=1, source_target_pairs={{0,1},{1,2},{2,3},{3,4},{4,5},{5,6},{6,7},{8,9},{9,10},{10,11},{11... | collective-permute-start | bytes 98312 | tf_op jit(solution)/shard_map/ppermute | solution.py:216
  84.0 16.1 %collective-permute-start.7 = (f32[8,1024]{1,0:T(8,128)S(1)}, f32[8,1024]{1,0:T(8,128)S(1)}, u32[]{:S(2)}, u32[]{:S(2)}) collective-permute-start(f32[8,1024]{1,0:T(8,128)S(1)} %get-tuple-element.41), channel_id=1, source_target_pairs={{1,0},{2,1},{3,2},{4,3},{5,4},{6,5},{7,6},{9,8},{10,9},{11,10},{12... | collective-permute-start | bytes 98312 | tf_op jit(solution)/shard_map/ppermute | solution.py:216
  88.5 9.8 %collective-permute-start.4 = (f32[8,512]{1,0:T(8,128)S(1)}, f32[8,512]{1,0:T(8,128)S(1)}, u32[]{:S(2)}, u32[]{:S(2)}) collective-permute-start(f32[8,512]{1,0:T(8,128)S(1)} %get-tuple-element.38), channel_id=1, source_target_pairs={{0,8},{8,16},{16,24},{1,9},{9,17},{17,25},{2,10},{10,18},{18,26},{... | collective-permute-start | bytes 49160 | tf_op jit(solution)/shard_map/ppermute | solution.py:216
  91.8 8.3 %collective-permute-start.5 = (f32[8,512]{1,0:T(8,128)S(1)}, f32[8,512]{1,0:T(8,128)S(1)}, u32[]{:S(2)}, u32[]{:S(2)}) collective-permute-start(f32[8,512]{1,0:T(8,128)S(1)} %get-tuple-element.39), channel_id=1, source_target_pairs={{8,0},{16,8},{24,16},{9,1},{17,9},{25,17},{10,2},{18,10},{26,18},{... | collective-permute-start | bytes 49160 | tf_op jit(solution)/shard_map/ppermute | solution.py:216
  105.4 1.3 %copy-start.1 = (f32[4,1024,128]{2,1,0:T(8,128)}, f32[4,1024,128]{2,1,0:T(8,128)S(1)}, u32[]{:S(2)}) copy-start(f32[4,1024,128]{2,1,0:T(8,128)S(1)} %get-tuple-element.43) | copy-start | bytes 6291460
  106.7 1.3 %copy-start.3 = (f32[4,1024,128]{2,1,0:T(8,128)}, f32[4,1024,128]{2,1,0:T(8,128)S(1)}, u32[]{:S(2)}) copy-start(f32[4,1024,128]{2,1,0:T(8,128)S(1)} %get-tuple-element.44) | copy-start | bytes 6291460
  108.1 1.6 %copy-start.2 = (f32[4,1024,128]{2,1,0:T(8,128)S(1)}, f32[4,1024,128]{2,1,0:T(8,128)}, u32[]{:S(2)}) copy-start(f32[4,1024,128]{2,1,0:T(8,128)} %copy-done.1) | copy-start | bytes 6291460
  109.6 1.6 %copy-start.4 = (f32[4,1024,128]{2,1,0:T(8,128)S(1)}, f32[4,1024,128]{2,1,0:T(8,128)}, u32[]{:S(2)}) copy-start(f32[4,1024,128]{2,1,0:T(8,128)} %copy-done.3) | copy-start | bytes 6291460
  (6 other events, 3.9 us)

commit v5 on v4

--- a/solution.py
+++ b/solution.py
@@ -84,7 +84,7 @@
         out_shape=(shape, shape),
         in_specs=[VMEM] * 4,
         out_specs=(VMEM, VMEM),
-        compiler_params=params(16 << 20),
+        compiler_params=params(),
         name="requests",
     )(src, blk, pat, wgt)
 
@@ -113,7 +113,7 @@
         ),
         in_specs=[SMEM, VMEM],
         out_specs=(VMEM, VMEM),
-        compiler_params=params(16 << 20),
+        compiler_params=params(),
         name="mix",
     )(blend, atm)
 
@@ -269,12 +269,10 @@
 
 
 def stencil_kernel(
-    d_ref, m_ref, x_ref, y_ref, up_ref, dn_ref, lh_ref, rh_ref, lo_ref,
-    newh_ref, hu_ref, hv_ref, h_ref, *scratch,
+    d_ref, m_ref, x_ref, y_ref, newh_ref, hu_ref, hv_ref, h_ref, *scratch,
 ):
     cell = scratch[:CELL]
-    gx = scratch[CELL:CELL + 3]
-    edge, ecol = scratch[CELL + 3:]
+    gx = scratch[CELL:]
     step = pl.program_id(0)
     bands = pl.num_programs(0) - 1
     lane = iota((TILE, LANES), 1)
@@ -296,33 +294,14 @@
 
         lax.fori_loop(0, BAND // TILE, fill, 0, unroll=4)
 
+    rows = bands * BAND
+
     @pl.when(step == 0)
     def _():
-        rows = bands * BAND
-        for at, ref in ((0, up_ref), (rows + TILE, dn_ref)):
-            for g in range(GROUPS):
-                cut = slice(g * LANES, (g + 1) * LANES)
-                line = [jnp.broadcast_to(ref[f:f + 1, cut], (TILE, LANES)) for f in range(3)]
-                for dst, val in zip(cell, derived(*line)):
-                    dst[g, pl.ds(at, TILE), :] = val
-        outer = along_y(derived(lh_ref[0:1, :], lh_ref[1:2, :], lh_ref[2:3, :]))
-        inner = along_y(derived(lo_ref[0:1, :], lo_ref[1:2, :], lo_ref[2:3, :]))
-        edge[...] = jnp.zeros_like(edge)
-        edge[0:3, :] = rh_ref[0:3, :]
-        for f, val in enumerate(flux(outer, inner)):
-            edge[3 + f:4 + f, :] = val
-
-        def turn(b, carry):
-            at = pl.ds(pl.multiple_of(b * LANES, LANES), LANES)
-            ecol[at, :] = edge[:, at].T
-            return carry
-
-        lax.fori_loop(0, ecol.shape[0] // LANES, turn, 0)
-        for g in range(GROUPS):
-            now = along_x([ref[g, 0:TILE, :] for ref in cell])
-            nxt = along_x([ref[g, 1:TILE + 1, :] for ref in cell])
-            for dst, val in zip(gx, flux(now, nxt)):
-                dst[g, 0:TILE, :] = val
+        for dst in cell:
+            dst[:, rows + TILE:, :] = jnp.zeros((GROUPS, TILE, LANES), F32)
+        for dst in gx:
+            dst[:, 0:TILE, :] = jnp.zeros((GROUPS, TILE, LANES), F32)
 
     @pl.when(step > 0)
     def _():
@@ -337,25 +316,31 @@
                     dst[g, pl.ds(base, TILE), :] = val
             return carry
 
-        lax.fori_loop(0, BAND // TILE, across, 0, unroll=2)
+        lax.fori_loop(0, BAND // TILE, across, 0, unroll=4)
+
+        @pl.when(step == bands)
+        def _():
+            for dst in gx:
+                dst[:, rows + TILE - 1:rows + TILE, :] = jnp.zeros((GROUPS, 1, LANES), F32)
 
         def body(t, carry):
             mark = pl.multiple_of(start + t * TILE, TILE)
             base = pl.multiple_of(mark + TILE, TILE)
             at = pl.ds(pl.multiple_of(t * TILE, TILE), TILE)
-            sides = ecol[pl.ds(mark, TILE), :]
-            before = [pltpu.roll(sides, LANES - 4 - f, 1) for f in range(3)]
+            before = [jnp.zeros((TILE, LANES), F32)] * 3
             for g in range(GROUPS):
                 now = [ref[g, pl.ds(base, TILE), :] for ref in cell]
                 if g < GROUPS - 1:
                     other = [ref[g + 1, pl.ds(base, TILE), :] for ref in cell[:3]]
                 else:
-                    other = [sides] + [pltpu.roll(sides, LANES - f, 1) for f in (1, 2)]
+                    other = now[:3]
                 right = [
                     pltpu.roll(jnp.where(lane == 0, o, c), LANES - 1, 1)
                     for o, c in zip(other, now[:3])
                 ]
                 fy = flux(along_y(now), along_y(derived(*right)))
+                if g == GROUPS - 1:
+                    fy = [jnp.where(lane == LANES - 1, 0.0, val) for val in fy]
                 py = [
                     pltpu.roll(jnp.where(lane == LANES - 1, o, c), 1, 1)
                     for o, c in zip(before, fy)
@@ -367,42 +352,35 @@
                 ch = (fx[0] - px[0]) + (fy[0] - py[0])
                 cx = (fx[1] - px[1]) + (fy[2] - py[2])
                 cy = (fx[2] - px[2]) + (fy[1] - py[1])
-                newh_ref[at, g * LANES:(g + 1) * LANES] = jnp.where(
-                    h > 0.0, h - (0.5 * DT_DX) * ch, 0.0
-                )
+                newh_ref[g, at, :] = h - (0.5 * DT_DX) * ch
                 hu_ref[g, at, :] = u - (0.5 * DT_DX) * cx
                 hv_ref[g, at, :] = v - (0.5 * DT_DX) * cy
                 h_ref[g, at, :] = h
             return carry
 
-        lax.fori_loop(0, BAND // TILE, body, 0, unroll=2)
-
-
-def stencil(depth, mask, momx, momy, up, dn, lh, rh, lo):
+        lax.fori_loop(0, BAND // TILE, body, 0, unroll=4)
+
+
+def stencil(depth, mask, momx, momy):
     rows, cols = depth.shape
     bands = rows // BAND
     plane = jax.ShapeDtypeStruct((GROUPS, rows, LANES), F32)
     pad = pltpu.VMEM((GROUPS, rows + 2 * TILE, LANES), F32)
     band = pl.BlockSpec((BAND, cols), lambda i: (jnp.minimum(i, bands - 1), 0))
-    line = pl.BlockSpec((TILE, cols), lambda i: (0, 0))
-    column = pl.BlockSpec((TILE, rows), lambda i: (0, 0))
     part = pl.BlockSpec((GROUPS, BAND, LANES), lambda i: (0, jnp.maximum(i - 1, 0), 0))
     return pl.pallas_call(
         stencil_kernel,
         grid=(bands + 1,),
-        out_shape=(jax.ShapeDtypeStruct((rows, cols), F32), plane, plane, plane),
-        in_specs=[band] * 4 + [line] * 2 + [column] * 3,
-        out_specs=(
-            pl.BlockSpec((BAND, cols), lambda i: (jnp.maximum(i - 1, 0), 0)), part, part, part,
-        ),
-        scratch_shapes=[pad] * (CELL + 3)
-        + [pltpu.VMEM((LANES, rows), F32), pltpu.VMEM((rows, LANES), F32)],
+        out_shape=(plane,) * 4,
+        in_specs=[band] * 4,
+        out_specs=(part,) * 4,
+        scratch_shapes=[pad] * (CELL + 3),
         compiler_params=params(),
         cost_estimate=pl.CostEstimate(
             flops=200 * rows * cols, bytes_accessed=64 * rows * cols, transcendentals=0
         ),
         name="stencil",
-    )(depth, mask, momx, momy, up, dn, lh, rh, lo)
+    )(depth, mask, momx, momy)
 
 
 def summed_of(lab, landed):
@@ -438,7 +416,8 @@
 
 
 def press_kernel(
-    lab_ref, landed_ref, w_ref, out_ref, top_ref, bottom_ref, left_ref, right_ref,
+    lab_ref, landed_ref, w_ref, top0_ref, bottom0_ref, left0_ref, right0_ref,
+    out_ref, top_ref, bottom_ref, left_ref, right_ref,
     left, acc, acc2, field, field2,
 ):
     step = pl.program_id(0)
@@ -459,24 +438,27 @@
     @pl.when(step == pl.num_programs(0) - 1)
     def _():
         rows = out_ref.shape[1]
+        mine = iota((TILE, LANES), 0) == 3
         for g in range(GROUPS):
             cut = slice(g * LANES, (g + 1) * LANES)
-            top_ref[:, cut] = out_ref[g, 0:TILE, :]
-            bottom_ref[:, cut] = pltpu.roll(out_ref[g, rows - TILE:rows, :], 1, 0)
+            head = pltpu.roll(out_ref[g, 0:TILE, :], 3, 0)
+            tail = pltpu.roll(out_ref[g, rows - TILE:rows, :], 4, 0)
+            top_ref[:, cut] = jnp.where(mine, head, top0_ref[:, cut])
+            bottom_ref[:, cut] = jnp.where(mine, tail, bottom0_ref[:, cut])
         lane = iota((LANES, LANES), 1)
         for b in range(rows // LANES):
             at = slice(b * LANES, (b + 1) * LANES)
             packed = jnp.where(
-                lane == TILE,
-                pltpu.roll(out_ref[GROUPS - 1, at, :], TILE + 1, 1),
-                out_ref[0, at, :],
+                lane == TILE + 3,
+                pltpu.roll(out_ref[GROUPS - 1, at, :], TILE + 4, 1),
+                pltpu.roll(out_ref[0, at, :], 3, 1),
             )
             turned = packed.T
-            left_ref[:, at] = turned[0:TILE]
-            right_ref[:, at] = turned[TILE:2 * TILE]
-
-
-def pressure_field(lab, landed, weights):
+            left_ref[:, at] = jnp.where(mine, turned[0:TILE], left0_ref[:, at])
+            right_ref[:, at] = jnp.where(mine, turned[TILE:2 * TILE], right0_ref[:, at])
+
+
+def pressure_field(lab, landed, weights, edges):
     steps = PATCH // (2 * TILE)
     rows = BPX * PATCH
     line = (TILE, BPY * PATCH)
@@ -494,7 +476,7 @@
             const(lab.shape),
             const(landed.shape),
             pl.BlockSpec((NW * ABLK, 2 * PART), lambda i: (0, i)),
-        ],
+        ] + [const(x) for x in (line, line, column, column)],
         out_specs=tuple(const(x) for x in (whole, line, line, column, column)),
         scratch_shapes=[
             pltpu.VMEM((NPATCH, NW * ABLK), BF16),
@@ -503,33 +485,52 @@
             pltpu.VMEM((GROUPS, BPX * TILE, LANES), F32),
             pltpu.VMEM((GROUPS, BPX * TILE, LANES), F32),
         ],
-        compiler_params=params(32 << 20),
+        compiler_params=params(),
         cost_estimate=pl.CostEstimate(
             flops=2 * NPATCH * NW * ABLK * PATCH * PATCH, bytes_accessed=12 << 20, transcendentals=0
         ),
         name="pressure",
-    )(lab, landed, weights)
-
-
-def gradient_kernel(
-    p_ref, hu_ref, hv_ref, h_ref, up_ref, dn_ref, lh_ref, rh_ref,
-    ox_ref, oy_ref, fac_ref, padded, sides,
+    )(lab, landed, weights, *edges)
+
+
+def settle_kernel(
+    p_ref, newh_ref, hu_ref, hv_ref, h_ref, up_ref, dn_ref, lh_ref, rh_ref,
+    top_ref, bottom_ref, left_ref, right_ref,
+    oh_ref, ox_ref, oy_ref, fac_ref, padded, edge, sides,
 ):
     step = pl.program_id(0)
     rows = p_ref.shape[1]
 
+    def cells(ref):
+        return derived(ref[0:1, :], ref[1:2, :], ref[2:3, :])
+
+    def add_row(before, after, at, own_ref, sign):
+        gh, gn, gt = flux(along_x(cells(before)), along_x(cells(after)))
+        wet = own_ref[0:1, :] > 0.0
+        fix = [jnp.where(wet, (sign * 0.5 * DT_DX) * val, 0.0) for val in (gh, gn, gt)]
+        oh_ref[at:at + 1, :] += fix[0]
+        for g in range(GROUPS):
+            cut = slice(g * LANES, (g + 1) * LANES)
+            ox_ref[g, at:at + 1, :] += fix[1][:, cut]
+            oy_ref[g, at:at + 1, :] += fix[2][:, cut]
+
     @pl.when(step == 0)
     def _():
-        stacked = jnp.concatenate([lh_ref[...], rh_ref[...]], axis=0)
-        blank = jnp.zeros((LANES - 2 * TILE, LANES), F32)
+        edge[0:1, :] = lh_ref[3:4, :]
+        edge[1:2, :] = rh_ref[3:4, :]
+        for at, before, after, sign in ((2, lh_ref, left_ref, 1.0), (5, right_ref, rh_ref, -1.0)):
+            gh, gn, gt = flux(along_y(cells(before)), along_y(cells(after)))
+            for f, val in enumerate((gh, gt, gn)):
+                edge[at + f:at + f + 1, :] = (sign * 0.5 * DT_DX) * val
+        blank = jnp.zeros((LANES - TILE, LANES), F32)
         for b in range(rows // LANES):
             cut = slice(b * LANES, (b + 1) * LANES)
-            sides[cut, :] = jnp.concatenate([stacked[:, cut], blank], axis=0).T
+            sides[cut, :] = jnp.concatenate([edge[:, cut], blank], axis=0).T
         for g in range(GROUPS):
             cut = slice(g * LANES, (g + 1) * LANES)
             padded[g, TILE:TILE + rows, :] = p_ref[g]
-            padded[g, 0:TILE, :] = jnp.broadcast_to(up_ref[0:1, cut], (TILE, LANES))
-            padded[g, rows + TILE:, :] = jnp.broadcast_to(dn_ref[0:1, cut], (TILE, LANES))
+            padded[g, 0:TILE, :] = jnp.broadcast_to(up_ref[3:4, cut], (TILE, LANES))
+            padded[g, rows + TILE:, :] = jnp.broadcast_to(dn_ref[3:4, cut], (TILE, LANES))
 
     lane = iota((TILE, LANES), 1)
 
@@ -543,43 +544,67 @@
         downs = [pltpu.roll(a, LANES - 1, 1) for a in tiles]
         for g in range(GROUPS):
             before = ups[g - 1] if g else ends[:, 0:1]
-            after = downs[g + 1] if g < GROUPS - 1 else ends[:, TILE:TILE + 1]
+            after = downs[g + 1] if g < GROUPS - 1 else ends[:, 1:2]
             prev = jnp.where(lane == 0, before, ups[g])
             nxt = jnp.where(lane == LANES - 1, after, downs[g])
             h = h_ref[g, at, :]
             wet = h > 0.0
             scale = (TIME_STEP * PRESS * 0.5) * h
             gx = padded[g, pl.ds(base + 1, TILE), :] - padded[g, pl.ds(base - 1, TILE), :]
-            ox_ref[g, at, :] = jnp.where(wet, hu_ref[g, at, :] - scale * gx, 0.0)
-            oy_ref[g, at, :] = jnp.where(wet, hv_ref[g, at, :] - scale * (nxt - prev), 0.0)
+            new = [
+                newh_ref[g, at, :],
+                hu_ref[g, at, :] - scale * gx,
+                hv_ref[g, at, :] - scale * (nxt - prev),
+            ]
+            if g == 0:
+                new = [jnp.where(lane == 0, a + ends[:, 2 + f:3 + f], a) for f, a in enumerate(new)]
+            if g == GROUPS - 1:
+                new = [
+                    jnp.where(lane == LANES - 1, a + ends[:, 5 + f:6 + f], a)
+                    for f, a in enumerate(new)
+                ]
+            oh_ref[at, g * LANES:(g + 1) * LANES] = jnp.where(wet, new[0], 0.0)
+            ox_ref[g, at, :] = jnp.where(wet, new[1], 0.0)
+            oy_ref[g, at, :] = jnp.where(wet, new[2], 0.0)
             fac_ref[g, at, :] = jnp.where(wet, TIME_STEP * STRESS, 0.0)
         return carry
 
     lax.fori_loop(0, BAND // TILE, body, 0, unroll=4)
 
-
-def gradient(p, hu, hv, h, up, dn, lh, rh):
+    @pl.when(step == 0)
+    def _():
+        add_row(up_ref, top_ref, 0, top_ref, 1.0)
+
+    @pl.when(step == pl.num_programs(0) - 1)
+    def _():
+        add_row(bottom_ref, dn_ref, BAND - 1, bottom_ref, -1.0)
+
+
+def settle(p, newh, hu, hv, h, halos, edges):
     rows = p.shape[1]
+    cols = GROUPS * LANES
     plane = jax.ShapeDtypeStruct(p.shape, F32)
     part = pl.BlockSpec((GROUPS, BAND, LANES), lambda i: (0, i, 0))
-    line = pl.BlockSpec(up.shape, lambda i: (0, 0))
-    column = pl.BlockSpec(lh.shape, lambda i: (0, 0))
+    line = pl.BlockSpec((TILE, cols), lambda i: (0, 0))
+    column = pl.BlockSpec((TILE, rows), lambda i: (0, 0))
     return pl.pallas_call(
-        gradient_kernel,
+        settle_kernel,
         grid=(rows // BAND,),
-        out_shape=(plane,) * 3,
-        in_specs=[pl.BlockSpec(p.shape, lambda i: (0, 0, 0))] + [part] * 3 + [line] * 2 + [column] * 2,
-        out_specs=(part,) * 3,
+        out_shape=(jax.ShapeDtypeStruct((rows, cols), F32),) + (plane,) * 3,
+        in_specs=[pl.BlockSpec(p.shape, lambda i: (0, 0, 0))] + [part] * 4
+        + [line, line, column, column] * 2,
+        out_specs=(pl.BlockSpec((BAND, cols), lambda i: (i, 0)),) + (part,) * 3,
         scratch_shapes=[
             pltpu.VMEM((GROUPS, rows + 2 * TILE, LANES), F32),
+            pltpu.VMEM((TILE, rows), F32),
             pltpu.VMEM((rows, LANES), F32),
         ],
-        compiler_params=params(24 << 20),
+        compiler_params=params(),
         cost_estimate=pl.CostEstimate(
-            flops=20 * p.size, bytes_accessed=28 * p.size, transcendentals=0
+            flops=20 * p.size, bytes_accessed=36 * p.size, transcendentals=0
         ),
-        name="gradient",
-    )(p, hu, hv, h, up, dn, lh, rh)
+        name="settle",
+    )(p, newh, hu, hv, h, *halos, *edges)
 
 
 def wind_kernel(
@@ -633,7 +658,7 @@
             pltpu.VMEM((2 * NPATCH, PART), F32),
             field, field, field, field,
         ],
-        compiler_params=params(40 << 20),
+        compiler_params=params(),
         cost_estimate=pl.CostEstimate(
             flops=4 * NPATCH * NW * ABLK * PATCH * PATCH, bytes_accessed=20 << 20, transcendentals=0
         ),
@@ -680,19 +705,14 @@
         return got.reshape(rows.shape)
 
     press = exchange(top, press)
-    newh, hu, hv, h = stencil(
-        depth_field, wet_mask, mom_x, mom_y,
-        send(bottom, "gx", 1), send(top, "gx", -1),
-        send(right, "gy", 1), send(left, "gy", -1), left,
-    )
+    newh, hu, hv, h = stencil(depth_field, wet_mask, mom_x, mom_y)
     wind = exchange(newh, wind)
     weights = remap_weights.reshape(NW * ABLK, PATCH * PATCH)
-    p, top, bottom, left, right = pressure_field(lab, press, weights)
-    hu, hv, fac = gradient(
-        p, hu, hv, h,
-        send(bottom, "gx", 1), send(top, "gx", -1),
-        send(right, "gy", 1), send(left, "gy", -1),
+    p, top, bottom, left, right = pressure_field(lab, press, weights, (top, bottom, left, right))
+    halos = (
+        send(bottom, "gx", 1), send(top, "gx", -1), send(right, "gy", 1), send(left, "gy", -1),
     )
+    newh, hu, hv, fac = settle(p, newh, hu, hv, h, halos, (top, bottom, left, right))
     new_x, new_y = wind_field(lab, wind, weights, hu, hv, fac)
     return (newh, new_x.reshape(newh.shape), new_y.reshape(newh.shape))
 

time: 121 us -> 101 us (0.83)
  local copies, waits for them, and re-layouts: 16.6 us -> 4.58 us
  starting transfers between devices: 40.4 us -> 30 us
  Pallas kernels: 52.2 us -> 59.6 us
  waiting for transfers between devices: 9.18 us -> 4.74 us
    unnamed x38 -> x22, local copies, waits for them, and re-layouts: 16.6 us -> 3.91 us
    ppermute x8 -> x4, starting transfers between devices: 24.6 us -> 12.3 us  [send(): return lax.ppermute(value, axis, pairs)]
    ppermute x8 -> x4, waiting for transfers between devices: 9.17 us -> 4.73 us  [send(): return lax.ppermute(value, axis, pairs)]
    pallas_call x1, Pallas kernels: 3.79 us -> 7.66 us  [pressure_field(): pl.pallas_call(press_kernel, grid=(steps,), out_shape=tuple((jax.ShapeDty...]
    pallas_call x1, Pallas kernels: 0.14 us -> 1.98 us  [mix(): pl.pallas_call(mix_kernel, out_shape=(jax.ShapeDtypeStruct((blocks, ABLK)...]
    all_to_all x2, starting transfers between devices: 9.84 us -> 11.7 us  [exchange(): got = lax.all_to_all(parts, both, split_axis=0, concat_axis=0, tiled=True)]
    pallas_call x1, Pallas kernels: 8.7 us -> 10.2 us  [wind_field(): pl.pallas_call(wind_kernel, grid=(steps,), out_shape=(shape, shape), in_s...]
  transfers between devices with their start and end apart: 11 -> 7, of which waited for: 3 -> 2; matrix products, arithmetic and copies ran while one was open for 0% -> 1% of each run, Pallas kernels for 34% -> 46%
where the time goes in v5:
time: 101 us; the launch traced here: 100 us
  Pallas kernels  59.6 us (59%)
  starting transfers between devices  30 us (30%)
  waiting for transfers between devices  4.74 us (5%)
  local copies, waits for them, and re-layouts  4.58 us (5%)
  between operations  1.43 us (1%)
    pallas_call x1, Pallas kernels, stencil(): pl.pallas_call(stencil_kernel, grid=(bands + 1,), out_shape=(plane,) * 4,...  18.9 us
    ppermute x4, starting transfers between devices, send(): return lax.ppermute(value, axis, pairs)  12.3 us
    pallas_call x1, Pallas kernels, settle(): pl.pallas_call(settle_kernel, grid=(rows // BAND,), out_shape=(jax.ShapeD...  11.8 us
    all_to_all x2, starting transfers between devices, exchange(): got = lax.all_to_all(parts, both, split_axis=0, concat_axis=0, tiled=True)  11.7 us
    pallas_call x1, Pallas kernels, wind_field(): pl.pallas_call(wind_kernel, grid=(steps,), out_shape=(shape, shape), in_s...  10.2 us
    pallas_call x1, Pallas kernels, pressure_field(): pl.pallas_call(press_kernel, grid=(steps,), out_shape=tuple((jax.ShapeDty...  7.66 us
    all_to_all x1, starting transfers between devices, body(): lax.all_to_all(want.reshape(devices, 1, capacity), both, split_axis=0, co...  5.99 us
    ppermute x4, waiting for transfers between devices, send(): return lax.ppermute(value, axis, pairs)  4.73 us
  transfers between devices with their start and end apart: 7, of which 2 were waited for; matrix products, arithmetic and copies ran while one was open for 1% of the time, Pallas kernels for 46%

profile of v5, /device:TPU:12, one launch (start us, length us, event | category | flops | bytes accessed | tf_op | source)
XLA Modules:
  0.0 100.3 jit_solution(11773403953770005723)
XLA Ops:
  0.6 1.7 %requests.1 = (s32[32,32]{1,0:T(8,128)}, s32[32,32]{1,0:T(8,128)}) custom-call(s32[1,512]{1,0:T(1,128)} %bitcast.29, s32[1,512]{1,0:T(1,128)} %bitcast.30, s32[1,512]{1,0:T(1,128)} %bitcast.31, s32[1,512]{1,0:T(1,128)} %bitcast.32), custom_call_target="tpu_custom_call" | custom-call | tf_op jit(solution)/shard_map/requests/pallas_call | solution.py:82
  2.3 6.0 %all-to-all-start = ((s32[32,1,32]{2,1,0:T(1,128)}), s32[32,1,32]{2,1,0:T(1,128)S(1)}, u32[]{:S(2)}, u32[]{:S(2)}) async-start(s32[32,1,32]{2,1,0:T(1,128)} %bitcast.28), calls=%async_computation | async-start | bytes 32768 | tf_op jit(solution)/shard_map/all_to_all | solution.py:694
  9.0 2.0 %mix.1 = (bf16[256,256]{1,0:T(8,128)(2,1)}, bf16[256,512]{1,0:T(8,128)(2,1)}) custom-call(f32[1]{0:T(128)} %bitcast.19.blend_ref, bf16[6,256,256]{2,1,0:T(8,128)(2,1)} %bitcast.27), custom_call_target="tpu_custom_call" | custom-call | tf_op jit(solution)/shard_map/mix/pallas_call | solution.py:108
  11.0 4.5 %edges.1 = (f32[8,512]{1,0:T(8,128)}, f32[8,512]{1,0:T(8,128)}, f32[8,1024]{1,0:T(8,128)}, f32[8,1024]{1,0:T(8,128)}) custom-call(f32[1024,512]{1,0:T(8,128)} %d_ref.1, s32[1024,512]{1,0:T(8,128)} %m_ref.1, f32[1024,512]{1,0:T(8,128)} %x_ref.1, f32[1024,512]{1,0:T(8,128)} %y_ref.1, f32[1024,512]{1,0:T(8,128)} %d_ref.1, s32[1024,512]{1,0:T(8,128)} %m_ref.1, ...), custom_call_target="tpu_custom_call" | custom-call | tf_op jit(solution)/shard_map/edges/pallas_call | solution.py:194
  15.5 0.7 copy-done.3
  16.2 1.3 %serve.2 = bf16[1024,256]{1,0:T(8,128)(2,1)} custom-call(f32[8,512]{1,0:T(8,128)S(1)} %copy-done.3, s32[32,1,32]{2,1,0:T(1,128)S(1)} %all-to-all-done.asked_ref, bf16[256,256]{1,0:T(8,128)(2,1)S(1)} %copy-done.2), custom_call_target="tpu_custom_call" | custom-call | tf_op jit(solution)/shard_map/serve/pallas_call | solution.py:140
  17.5 5.8 %all-to-all-start.1 = ((bf16[32,32,256]{2,1,0:T(8,128)(2,1)}), bf16[32,32,256]{2,1,0:T(8,128)(2,1)S(1)}, u32[]{:S(2)}, u32[]{:S(2)}) async-start(bf16[32,32,256]{2,1,0:T(8,128)(2,1)} %bitcast.8), calls=%async_computation.1 | async-start | bytes 1048576 | tf_op jit(solution)/shard_map/all_to_all | solution.py:704
  23.3 18.9 %stencil.1 = (f32[4,1024,128]{2,1,0:T(8,128)}, f32[4,1024,128]{2,1,0:T(8,128)}, f32[4,1024,128]{2,1,0:T(8,128)}, f32[4,1024,128]{2,1,0:T(8,128)}) custom-call(f32[1024,512]{1,0:T(8,128)} %d_ref.1, s32[1024,512]{1,0:T(8,128)} %m_ref.1, f32[1024,512]{1,0:T(8,128)} %x_ref.1, f32[1024,512]{1,0:T(8,128)} %y_ref.1), custom_call_target="tpu_custom_call" | custom-call | flops 104857600 | bytes 33554432 | tf_op jit(solution)/shard_map/stencil/pallas_call | solution.py:371
  42.3 1.6 %copy-done = f32[4,1024,128]{2,1,0:T(8,128)S(1)} copy-done((f32[4,1024,128]{2,1,0:T(8,128)S(1)}, f32[4,1024,128]{2,1,0:T(8,128)}, u32[]{:S(2)}) %copy-start) | copy-done | bytes 2097176
  43.9 1.6 %serve.3 = bf16[1024,512]{1,0:T(8,128)(2,1)} custom-call(f32[4,1024,128]{2,1,0:T(8,128)S(1)} %copy-done, s32[32,1,32]{2,1,0:T(1,128)S(1)} %all-to-all-done.asked_ref, bf16[256,512]{1,0:T(8,128)(2,1)S(1)} %copy-done.1), custom_call_target="tpu_custom_call" | custom-call | tf_op jit(solution)/shard_map/serve/pallas_call | solution.py:140
  45.5 5.8 %all-to-all-start.2 = ((bf16[32,32,512]{2,1,0:T(8,128)(2,1)}), bf16[32,32,512]{2,1,0:T(8,128)(2,1)S(1)}, u32[]{:S(2)}, u32[]{:S(2)}) async-start(bf16[32,32,512]{2,1,0:T(8,128)(2,1)} %bitcast.11), calls=%async_computation.2 | async-start | bytes 2097152 | tf_op jit(solution)/shard_map/all_to_all | solution.py:704
  51.3 0.7 reshape.64.lab_ref
  52.0 7.7 %pressure.1 = (f32[4,1024,128]{2,1,0:T(8,128)}, f32[8,512]{1,0:T(8,128)}, f32[8,512]{1,0:T(8,128)}, f32[8,1024]{1,0:T(8,128)}, f32[8,1024]{1,0:T(8,128)}) custom-call(s32[1,1024]{1,0:T(1,128)} %reshape.64.lab_ref, bf16[1024,256]{1,0:T(8,128)(2,1)} %bitcast.26, bf16[1024,4096]{1,0:T(8,128)(2,1)} %bitcast.20, f32[8,512]{1,0:T(8,128)} %get-tuple-element.27.after_ref.top0_ref, ...), custom_call_target="tpu_custom_call" | custom-call | flops 1073741824 | bytes 12582912 | tf_op jit(solution)/shard_map/pressure/pallas_call | solution.py:471
  59.6 2.1 %collective-permute-start.2 = (f32[8,1024]{1,0:T(8,128)}, f32[8,1024]{1,0:T(8,128)S(1)}, u32[]{:S(2)}, u32[]{:S(2)}) collective-permute-start(f32[8,1024]{1,0:T(8,128)} %get-tuple-element.40.right_ref), channel_id=1, source_target_pairs={{0,1},{1,2},{2,3},{3,4},{4,5},{5,6},{6,7},{8,9},{9,10},{10,11},{11... | collective-permute-start | bytes 98312 | tf_op jit(solution)/shard_map/ppermute | solution.py:216
  61.7 4.4 %collective-permute-start.3 = (f32[8,1024]{1,0:T(8,128)}, f32[8,1024]{1,0:T(8,128)S(1)}, u32[]{:S(2)}, u32[]{:S(2)}) collective-permute-start(f32[8,1024]{1,0:T(8,128)} %get-tuple-element.41.left_ref), channel_id=1, source_target_pairs={{1,0},{2,1},{3,2},{4,3},{5,4},{6,5},{7,6},{9,8},{10,9},{11,10},{12... | collective-permute-start | bytes 98312 | tf_op jit(solution)/shard_map/ppermute | solution.py:216
  66.1 3.4 %collective-permute-start = (f32[8,512]{1,0:T(8,128)}, f32[8,512]{1,0:T(8,128)S(1)}, u32[]{:S(2)}, u32[]{:S(2)}) collective-permute-start(f32[8,512]{1,0:T(8,128)} %get-tuple-element.38.bottom_ref), channel_id=1, source_target_pairs={{0,8},{8,16},{16,24},{1,9},{9,17},{17,25},{2,10},{10,18},{18,26},{... | collective-permute-start | bytes 49160 | tf_op jit(solution)/shard_map/ppermute | solution.py:216
  69.5 2.5 %collective-permute-start.1 = (f32[8,512]{1,0:T(8,128)}, f32[8,512]{1,0:T(8,128)S(1)}, u32[]{:S(2)}, u32[]{:S(2)}) collective-permute-start(f32[8,512]{1,0:T(8,128)} %get-tuple-element.39.top_ref), channel_id=1, source_target_pairs={{8,0},{16,8},{24,16},{9,1},{17,9},{25,17},{10,2},{18,10},{26,18},{... | collective-permute-start | bytes 49160 | tf_op jit(solution)/shard_map/ppermute | solution.py:216
  72.0 2.9 %collective-permute-done.up_ref = f32[8,512]{1,0:T(8,128)S(1)} collective-permute-done((f32[8,512]{1,0:T(8,128)}, f32[8,512]{1,0:T(8,128)S(1)}, u32[]{:S(2)}, u32[]{:S(2)}) %collective-permute-start) | collective-permute-done | bytes 16416 | tf_op jit(solution)/shard_map/ppermute | solution.py:216
  74.8 1.9 %collective-permute-done.1.dn_ref = f32[8,512]{1,0:T(8,128)S(1)} collective-permute-done((f32[8,512]{1,0:T(8,128)}, f32[8,512]{1,0:T(8,128)S(1)}, u32[]{:S(2)}, u32[]{:S(2)}) %collective-permute-start.1) | collective-permute-done | bytes 16416 | tf_op jit(solution)/shard_map/ppermute | solution.py:216
  76.7 0.6 copy-done.9
  77.3 0.0 copy-done.7
  77.3 11.8 %settle.1 = (f32[1024,512]{1,0:T(8,128)}, f32[4,1024,128]{2,1,0:T(8,128)}, f32[4,1024,128]{2,1,0:T(8,128)}, f32[4,1024,128]{2,1,0:T(8,128)}) custom-call(f32[4,1024,128]{2,1,0:T(8,128)} %get-tuple-element.33.p_ref, f32[4,1024,128]{2,1,0:T(8,128)} %get-tuple-element.34.newh_ref.after_ref, f32[4,1024,128]{2,1,0:T(8,128)} %get-tuple-element.35.hu_ref, ...), custom_call_target="tpu_custom_call" | custom-call | flops 10485760 | bytes 18874368 | tf_op jit(solution)/shard_map/settle/pallas_call | solution.py:590
  89.2 1.0 copy-done.4
  90.2 10.2 %wind.1 = (f32[16,64,512]{2,1,0:T(8,128)}, f32[16,64,512]{2,1,0:T(8,128)}) custom-call(s32[1,1024]{1,0:T(1,128)} %reshape.64.lab_ref, bf16[1024,512]{1,0:T(8,128)(2,1)} %bitcast.22, bf16[1024,4096]{1,0:T(8,128)(2,1)} %bitcast.21, f32[4,16,64,128]{3,2,1,0:T(8,128)} %bitcast.23, f32[4,16,64,128]{3,2,1,0:T(8,128)} %bitcast.24, f32[4,16,64,128]{3,2,1,0:T(8,128)} %bitcast.25), custom_call_target="tpu_custom_call" | custom-call | flops 2147483648 | bytes 20971520 | tf_op jit(solution)/shard_map/wind/pallas_call | solution.py:644
  (22 shorter events, 0.1 us)
Async XLA Ops:
  2.3 13.1 %all-to-all-start = ((s32[32,1,32]{2,1,0:T(1,128)}), s32[32,1,32]{2,1,0:T(1,128)S(1)}, u32[]{:S(2)}, u32[]{:S(2)}) async-start(s32[32,1,32]{2,1,0:T(1,128)} %bitcast.28), calls=%async_computation | async-start | bytes 32768 | tf_op jit(solution)/shard_map/all_to_all | solution.py:694
  11.0 4.5 %copy-start.2 = (bf16[256,256]{1,0:T(8,128)(2,1)S(1)}, bf16[256,256]{1,0:T(8,128)(2,1)}, u32[]{:S(2)}) copy-start(bf16[256,256]{1,0:T(8,128)(2,1)} %get-tuple-element.29.tiles_ref) | copy-start | bytes 393220
  15.4 0.7 copy-start.3
  17.5 28.0 %all-to-all-start.1 = ((bf16[32,32,256]{2,1,0:T(8,128)(2,1)}), bf16[32,32,256]{2,1,0:T(8,128)(2,1)S(1)}, u32[]{:S(2)}, u32[]{:S(2)}) async-start(bf16[32,32,256]{2,1,0:T(8,128)(2,1)} %bitcast.8), calls=%async_computation.1 | async-start | bytes 1048576 | tf_op jit(solution)/shard_map/all_to_all | solution.py:704
  23.3 18.9 %copy-start.1 = (bf16[256,512]{1,0:T(8,128)(2,1)S(1)}, bf16[256,512]{1,0:T(8,128)(2,1)}, u32[]{:S(2)}) copy-start(bf16[256,512]{1,0:T(8,128)(2,1)} %get-tuple-element.43.tiles_ref) | copy-start | bytes 786436
  42.3 1.6 %copy-start = (f32[4,1024,128]{2,1,0:T(8,128)S(1)}, f32[4,1024,128]{2,1,0:T(8,128)}, u32[]{:S(2)}) copy-start(f32[4,1024,128]{2,1,0:T(8,128)} %get-tuple-element.34.newh_ref.after_ref) | copy-start | bytes 6291460
  43.9 7.4 %copy-start.10 = (s32[32,32]{1,0:T(8,128)S(1)}, s32[32,32]{1,0:T(8,128)}, u32[]{:S(2)}) copy-start(s32[32,32]{1,0:T(8,128)} %get-tuple-element.26) | copy-start | bytes 12292
  45.5 6.5 %copy-start.5 = (bf16[32,32,256]{2,1,0:T(8,128)(2,1)}, bf16[32,32,256]{2,1,0:T(8,128)(2,1)S(1)}, u32[]{:S(2)}) copy-start(bf16[32,32,256]{2,1,0:T(8,128)(2,1)S(1)} %all-to-all-done.1) | copy-start | bytes 1572868
  45.5 43.7 %all-to-all-start.2 = ((bf16[32,32,512]{2,1,0:T(8,128)(2,1)}), bf16[32,32,512]{2,1,0:T(8,128)(2,1)S(1)}, u32[]{:S(2)}, u32[]{:S(2)}) async-start(bf16[32,32,512]{2,1,0:T(8,128)(2,1)} %bitcast.11), calls=%async_computation.2 | async-start | bytes 2097152 | tf_op jit(solution)/shard_map/all_to_all | solution.py:704
  59.6 17.1 %collective-permute-start.2 = (f32[8,1024]{1,0:T(8,128)}, f32[8,1024]{1,0:T(8,128)S(1)}, u32[]{:S(2)}, u32[]{:S(2)}) collective-permute-start(f32[8,1024]{1,0:T(8,128)} %get-tuple-element.40.right_ref), channel_id=1, source_target_pairs={{0,1},{1,2},{2,3},{3,4},{4,5},{5,6},{6,7},{8,9},{9,10},{10,11},{11... | collective-permute-start | bytes 98312 | tf_op jit(solution)/shard_map/ppermute | solution.py:216
  61.7 15.0 %collective-permute-start.3 = (f32[8,1024]{1,0:T(8,128)}, f32[8,1024]{1,0:T(8,128)S(1)}, u32[]{:S(2)}, u32[]{:S(2)}) collective-permute-start(f32[8,1024]{1,0:T(8,128)} %get-tuple-element.41.left_ref), channel_id=1, source_target_pairs={{1,0},{2,1},{3,2},{4,3},{5,4},{6,5},{7,6},{9,8},{10,9},{11,10},{12... | collective-permute-start | bytes 98312 | tf_op jit(solution)/shard_map/ppermute | solution.py:216
  66.1 8.7 %collective-permute-start = (f32[8,512]{1,0:T(8,128)}, f32[8,512]{1,0:T(8,128)S(1)}, u32[]{:S(2)}, u32[]{:S(2)}) collective-permute-start(f32[8,512]{1,0:T(8,128)} %get-tuple-element.38.bottom_ref), channel_id=1, source_target_pairs={{0,8},{8,16},{16,24},{1,9},{9,17},{17,25},{2,10},{10,18},{18,26},{... | collective-permute-start | bytes 49160 | tf_op jit(solution)/shard_map/ppermute | solution.py:216
  69.5 7.2 %collective-permute-start.1 = (f32[8,512]{1,0:T(8,128)}, f32[8,512]{1,0:T(8,128)S(1)}, u32[]{:S(2)}, u32[]{:S(2)}) collective-permute-start(f32[8,512]{1,0:T(8,128)} %get-tuple-element.39.top_ref), channel_id=1, source_target_pairs={{8,0},{16,8},{24,16},{9,1},{17,9},{25,17},{10,2},{18,10},{26,18},{... | collective-permute-start | bytes 49160 | tf_op jit(solution)/shard_map/ppermute | solution.py:216
  74.8 1.9 %copy-start.8 = (f32[8,512]{1,0:T(8,128)}, f32[8,512]{1,0:T(8,128)S(1)}, u32[]{:S(2)}) copy-start(f32[8,512]{1,0:T(8,128)S(1)} %collective-permute-done.up_ref) | copy-start | bytes 49156
  76.7 0.6 copy-start.9
  76.7 0.6 copy-start.6
  76.7 0.6 copy-start.7
  89.2 1.0 %copy-start.4 = (bf16[32,32,512]{2,1,0:T(8,128)(2,1)}, bf16[32,32,512]{2,1,0:T(8,128)(2,1)S(1)}, u32[]{:S(2)}) copy-start(bf16[32,32,512]{2,1,0:T(8,128)(2,1)S(1)} %all-to-all-done.2) | copy-start | bytes 3145732

commit v6 on v5

--- a/solution.py
+++ b/solution.py
@@ -269,7 +269,7 @@
 
 
 def stencil_kernel(
-    d_ref, m_ref, x_ref, y_ref, newh_ref, hu_ref, hv_ref, h_ref, *scratch,
+    d_ref, m_ref, x_ref, y_ref, newh_ref, hu_ref, hv_ref, h_ref, token_ref, *scratch,
 ):
     cell = scratch[:CELL]
     gx = scratch[CELL:]
@@ -298,6 +298,7 @@
 
     @pl.when(step == 0)
     def _():
+        token_ref[...] = jnp.zeros_like(token_ref)
         for dst in cell:
             dst[:, rows + TILE:, :] = jnp.zeros((GROUPS, TILE, LANES), F32)
         for dst in gx:
@@ -352,7 +353,9 @@
                 ch = (fx[0] - px[0]) + (fy[0] - py[0])
                 cx = (fx[1] - px[1]) + (fy[2] - py[2])
                 cy = (fx[2] - px[2]) + (fy[1] - py[1])
-                newh_ref[g, at, :] = h - (0.5 * DT_DX) * ch
+                newh_ref[at, g * LANES:(g + 1) * LANES] = jnp.where(
+                    h > 0.0, h - (0.5 * DT_DX) * ch, 0.0
+                )
                 hu_ref[g, at, :] = u - (0.5 * DT_DX) * cx
                 hv_ref[g, at, :] = v - (0.5 * DT_DX) * cy
                 h_ref[g, at, :] = h
@@ -371,9 +374,15 @@
     return pl.pallas_call(
         stencil_kernel,
         grid=(bands + 1,),
-        out_shape=(plane,) * 4,
+        out_shape=(
+            jax.ShapeDtypeStruct((rows, cols), F32), plane, plane, plane,
+            jax.ShapeDtypeStruct((TILE, LANES), F32),
+        ),
         in_specs=[band] * 4,
-        out_specs=(part,) * 4,
+        out_specs=(
+            pl.BlockSpec((BAND, cols), lambda i: (jnp.maximum(i - 1, 0), 0)), part, part, part,
+            pl.BlockSpec((TILE, LANES), lambda i: (0, 0)),
+        ),
         scratch_shapes=[pad] * (CELL + 3),
         compiler_params=params(),
         cost_estimate=pl.CostEstimate(
@@ -493,162 +502,193 @@
     )(lab, landed, weights, *edges)
 
 
-def settle_kernel(
-    p_ref, newh_ref, hu_ref, hv_ref, h_ref, up_ref, dn_ref, lh_ref, rh_ref,
-    top_ref, bottom_ref, left_ref, right_ref,
-    oh_ref, ox_ref, oy_ref, fac_ref, padded, edge, sides,
+def border_kernel(
+    up_ref, dn_ref, lh_ref, rh_ref, top_ref, bottom_ref, left_ref, right_ref, old_ref,
+    new_ref, sides_ref, ends_ref, edge, first, last, head, tail, load, save,
+):
+    rows, cols = old_ref.shape
+    middle = pl.ds(LANES, cols - 2 * LANES)
+    places = (
+        (slice(None), pl.ds(0, LANES)),
+        (slice(None), pl.ds(cols - LANES, LANES)),
+        (pl.ds(0, TILE), middle),
+        (pl.ds(rows - TILE, TILE), middle),
+    )
+    parts = (first, last, head, tail)
+    loads = [
+        pltpu.make_async_copy(old_ref.at[at], part, load.at[n])
+        for n, (at, part) in enumerate(zip(places, parts))
+    ]
+    for copy in loads:
+        copy.start()
+
+    def cells(ref):
+        return derived(ref[0:1, :], ref[1:2, :], ref[2:3, :])
+
+    edge[0:1, :] = lh_ref[3:4, :]
+    edge[1:2, :] = rh_ref[3:4, :]
+    for at, before, after, own, sign in (
+        (2, lh_ref, left_ref, left_ref, 1.0), (5, right_ref, rh_ref, right_ref, -1.0),
+    ):
+        gh, gn, gt = flux(along_y(cells(before)), along_y(cells(after)))
+        wet = own[0:1, :] > 0.0
+        for f, val in enumerate((gh, gt, gn)):
+            edge[at + f:at + f + 1, :] = jnp.where(wet, (sign * 0.5 * DT_DX) * val, 0.0)
+    blank = jnp.zeros((LANES - TILE, LANES), F32)
+    for b in range(rows // LANES):
+        cut = slice(b * LANES, (b + 1) * LANES)
+        sides_ref[cut, :] = jnp.concatenate([edge[:, cut], blank], axis=0).T
+    ends_ref[...] = jnp.zeros_like(ends_ref)
+    for at, before, after, own, sign in (
+        (0, up_ref, top_ref, top_ref, 1.0), (3, bottom_ref, dn_ref, bottom_ref, -1.0),
+    ):
+        fluxes = flux(along_x(cells(before)), along_x(cells(after)))
+        wet = own[0:1, :] > 0.0
+        for f, val in enumerate(fluxes):
+            ends_ref[at + f:at + f + 1, :] = jnp.where(wet, (sign * 0.5 * DT_DX) * val, 0.0)
+
+    for copy in loads:
+        copy.wait()
+    lane = iota((rows, LANES), 1)
+    sides = sides_ref[...]
+    first[...] += jnp.where(lane == 0, pltpu.roll(sides, LANES - 2, 1), 0.0)
+    last[...] += jnp.where(lane == LANES - 1, pltpu.roll(sides, LANES - 6, 1), 0.0)
+    for at, line in ((0, 0), (rows - 1, 3)):
+        first[at:at + 1, :] += ends_ref[line:line + 1, 0:LANES]
+        last[at:at + 1, :] += ends_ref[line:line + 1, cols - LANES:cols]
+    head[0:1, :] += ends_ref[0:1, LANES:cols - LANES]
+    tail[TILE - 1:TILE, :] += ends_ref[3:4, LANES:cols - LANES]
+    saves = [
+        pltpu.make_async_copy(part, new_ref.at[at], save.at[n])
+        for n, (at, part) in enumerate(zip(places, parts))
+    ]
+    for copy in saves:
+        copy.start()
+    for copy in saves:
+        copy.wait()
+
+
+def border(halos, edges, newh):
+    rows, cols = newh.shape
+    whole = pl.BlockSpec(memory_space=pl.ANY)
+    return pl.pallas_call(
+        border_kernel,
+        out_shape=(
+            jax.ShapeDtypeStruct((rows, cols), F32),
+            jax.ShapeDtypeStruct((rows, LANES), F32),
+            jax.ShapeDtypeStruct((TILE, cols), F32),
+        ),
+        in_specs=[VMEM] * 8 + [whole],
+        out_specs=(whole, VMEM, VMEM),
+        input_output_aliases={8: 0},
+        scratch_shapes=[
+            pltpu.VMEM((TILE, rows), F32),
+            pltpu.VMEM((rows, LANES), F32),
+            pltpu.VMEM((rows, LANES), F32),
+            pltpu.VMEM((TILE, cols - 2 * LANES), F32),
+            pltpu.VMEM((TILE, cols - 2 * LANES), F32),
+            pltpu.SemaphoreType.DMA((4,)),
+            pltpu.SemaphoreType.DMA((4,)),
+        ],
+        compiler_params=params(),
+        name="border",
+    )(*halos, *edges, newh)
+
+
+def finish_kernel(
+    lab_ref, landed_ref, w_ref, p_ref, up_ref, dn_ref, sides_ref, ends_ref,
+    hu_ref, hv_ref, h_ref, ox_ref, oy_ref,
+    left, acc, acc2, fx, fy, fx2, fy2, padded,
 ):
     step = pl.program_id(0)
     rows = p_ref.shape[1]
 
-    def cells(ref):
-        return derived(ref[0:1, :], ref[1:2, :], ref[2:3, :])
-
-    def add_row(before, after, at, own_ref, sign):
-        gh, gn, gt = flux(along_x(cells(before)), along_x(cells(after)))
-        wet = own_ref[0:1, :] > 0.0
-        fix = [jnp.where(wet, (sign * 0.5 * DT_DX) * val, 0.0) for val in (gh, gn, gt)]
-        oh_ref[at:at + 1, :] += fix[0]
-        for g in range(GROUPS):
-            cut = slice(g * LANES, (g + 1) * LANES)
-            ox_ref[g, at:at + 1, :] += fix[1][:, cut]
-            oy_ref[g, at:at + 1, :] += fix[2][:, cut]
-
     @pl.when(step == 0)
     def _():
-        edge[0:1, :] = lh_ref[3:4, :]
-        edge[1:2, :] = rh_ref[3:4, :]
-        for at, before, after, sign in ((2, lh_ref, left_ref, 1.0), (5, right_ref, rh_ref, -1.0)):
-            gh, gn, gt = flux(along_y(cells(before)), along_y(cells(after)))
-            for f, val in enumerate((gh, gt, gn)):
-                edge[at + f:at + f + 1, :] = (sign * 0.5 * DT_DX) * val
-        blank = jnp.zeros((LANES - TILE, LANES), F32)
-        for b in range(rows // LANES):
-            cut = slice(b * LANES, (b + 1) * LANES)
-            sides[cut, :] = jnp.concatenate([edge[:, cut], blank], axis=0).T
+        stack_left(left, summed_of(lab_ref[...], landed_ref[...]), 2)
         for g in range(GROUPS):
             cut = slice(g * LANES, (g + 1) * LANES)
             padded[g, TILE:TILE + rows, :] = p_ref[g]
             padded[g, 0:TILE, :] = jnp.broadcast_to(up_ref[3:4, cut], (TILE, LANES))
             padded[g, rows + TILE:, :] = jnp.broadcast_to(dn_ref[3:4, cut], (TILE, LANES))
 
-    lane = iota((TILE, LANES), 1)
-
-    def body(t, carry):
-        at = pl.ds(pl.multiple_of(t * TILE, TILE), TILE)
-        mark = pl.multiple_of(step * BAND + t * TILE, TILE)
-        base = pl.multiple_of(mark + TILE, TILE)
-        ends = sides[pl.ds(mark, TILE), :]
-        tiles = [padded[g, pl.ds(base, TILE), :] for g in range(GROUPS)]
-        ups = [pltpu.roll(a, 1, 1) for a in tiles]
-        downs = [pltpu.roll(a, LANES - 1, 1) for a in tiles]
-        for g in range(GROUPS):
-            before = ups[g - 1] if g else ends[:, 0:1]
-            after = downs[g + 1] if g < GROUPS - 1 else ends[:, 1:2]
-            prev = jnp.where(lane == 0, before, ups[g])
-            nxt = jnp.where(lane == LANES - 1, after, downs[g])
-            h = h_ref[g, at, :]
-            wet = h > 0.0
-            scale = (TIME_STEP * PRESS * 0.5) * h
-            gx = padded[g, pl.ds(base + 1, TILE), :] - padded[g, pl.ds(base - 1, TILE), :]
-            new = [
-                newh_ref[g, at, :],
-                hu_ref[g, at, :] - scale * gx,
-                hv_ref[g, at, :] - scale * (nxt - prev),
-            ]
-            if g == 0:
-                new = [jnp.where(lane == 0, a + ends[:, 2 + f:3 + f], a) for f, a in enumerate(new)]
-            if g == GROUPS - 1:
-                new = [
-                    jnp.where(lane == LANES - 1, a + ends[:, 5 + f:6 + f], a)
-                    for f, a in enumerate(new)
-                ]
-            oh_ref[at, g * LANES:(g + 1) * LANES] = jnp.where(wet, new[0], 0.0)
-            ox_ref[g, at, :] = jnp.where(wet, new[1], 0.0)
-            oy_ref[g, at, :] = jnp.where(wet, new[2], 0.0)
-            fac_ref[g, at, :] = jnp.where(wet, TIME_STEP * STRESS, 0.0)
-        return carry
-
-    lax.fori_loop(0, BAND // TILE, body, 0, unroll=4)
-
-    @pl.when(step == 0)
-    def _():
-        add_row(up_ref, top_ref, 0, top_ref, 1.0)
-
-    @pl.when(step == pl.num_programs(0) - 1)
-    def _():
-        add_row(bottom_ref, dn_ref, BAND - 1, bottom_ref, -1.0)
-
-
-def settle(p, newh, hu, hv, h, halos, edges):
-    rows = p.shape[1]
-    cols = GROUPS * LANES
-    plane = jax.ShapeDtypeStruct(p.shape, F32)
-    part = pl.BlockSpec((GROUPS, BAND, LANES), lambda i: (0, i, 0))
-    line = pl.BlockSpec((TILE, cols), lambda i: (0, 0))
-    column = pl.BlockSpec((TILE, rows), lambda i: (0, 0))
-    return pl.pallas_call(
-        settle_kernel,
-        grid=(rows // BAND,),
-        out_shape=(jax.ShapeDtypeStruct((rows, cols), F32),) + (plane,) * 3,
-        in_specs=[pl.BlockSpec(p.shape, lambda i: (0, 0, 0))] + [part] * 4
-        + [line, line, column, column] * 2,
-        out_specs=(pl.BlockSpec((BAND, cols), lambda i: (i, 0)),) + (part,) * 3,
-        scratch_shapes=[
-            pltpu.VMEM((GROUPS, rows + 2 * TILE, LANES), F32),
-            pltpu.VMEM((TILE, rows), F32),
-            pltpu.VMEM((rows, LANES), F32),
-        ],
-        compiler_params=params(),
-        cost_estimate=pl.CostEstimate(
-            flops=20 * p.size, bytes_accessed=36 * p.size, transcendentals=0
-        ),
-        name="settle",
-    )(p, newh, hu, hv, h, *halos, *edges)
-
-
-def wind_kernel(
-    lab_ref, landed_ref, w_ref, hu_ref, hv_ref, fac_ref, ox_ref, oy_ref,
-    left, acc, acc2, fx, fy, fx2, fy2,
-):
-    @pl.when(pl.program_id(0) == 0)
-    def _():
-        stack_left(left, summed_of(lab_ref[...], landed_ref[...]), 2)
-
     acc[...] = jnp.dot(left[...], w_ref[:, :PART], preferred_element_type=F32)
     acc2[...] = jnp.dot(left[...], w_ref[:, PART:], preferred_element_type=F32)
+    lane = iota((TILE, LANES), 1)
     for part, (src, mx, my) in enumerate(((acc, fx, fy), (acc2, fx2, fy2))):
         spread_rows(src, mx, 0)
         spread_rows(src, my, 1)
         cells = slice(part * TILE, (part + 1) * TILE)
-        for g in range(GROUPS):
-            for r in range(BPX):
-                at = slice(r * TILE, (r + 1) * TILE)
+        for r in range(BPX):
+            at = slice(r * TILE, (r + 1) * TILE)
+            mark = pl.multiple_of(r * PATCH + (2 * step + part) * TILE, TILE)
+            base = pl.multiple_of(mark + TILE, TILE)
+            ends = sides_ref[pl.ds(mark, TILE), :]
+            tiles = [padded[g, pl.ds(base, TILE), :] for g in range(GROUPS)]
+            for g in range(GROUPS):
+                before = tiles[g - 1] if g else pltpu.roll(ends, LANES - 1, 1)
+                after = tiles[g + 1] if g < GROUPS - 1 else pltpu.roll(ends, LANES - 1, 1)
+                prev = pltpu.roll(jnp.where(lane == LANES - 1, before, tiles[g]), 1, 1)
+                nxt = pltpu.roll(jnp.where(lane == 0, after, tiles[g]), LANES - 1, 1)
+                h = h_ref[g, r, cells, :]
+                wet = h > 0.0
+                scale = (TIME_STEP * PRESS * 0.5) * h
+                gx = padded[g, pl.ds(base + 1, TILE), :] - padded[g, pl.ds(base - 1, TILE), :]
                 wx = mx[g, at, :]
                 wy = my[g, at, :]
-                speed = jnp.sqrt(wx * wx + wy * wy) * fac_ref[g, r, cells, :]
+                speed = (TIME_STEP * STRESS) * jnp.sqrt(wx * wx + wy * wy)
+                new = [
+                    hu_ref[g, r, cells, :] - scale * gx + speed * wx,
+                    hv_ref[g, r, cells, :] - scale * (nxt - prev) + speed * wy,
+                ]
+                for own, edge, shift in ((0, 0, 3), (GROUPS - 1, LANES - 1, 6)):
+                    if g == own:
+                        new = [
+                            jnp.where(
+                                lane == edge,
+                                a + pltpu.roll(ends, (edge - shift - f) % LANES, 1),
+                                a,
+                            )
+                            for f, a in enumerate(new)
+                        ]
                 cut = slice(g * LANES, (g + 1) * LANES)
-                ox_ref[r, cells, cut] = hu_ref[g, r, cells, :] + speed * wx
-                oy_ref[r, cells, cut] = hv_ref[g, r, cells, :] + speed * wy
-
-
-def wind_field(lab, landed, weights, hu, hv, fac):
+                ox_ref[r, cells, cut] = jnp.where(wet, new[0], 0.0)
+                oy_ref[r, cells, cut] = jnp.where(wet, new[1], 0.0)
+
+    @pl.when(step == 0)
+    def _():
+        ox_ref[0, 0:1, :] += ends_ref[1:2, :]
+        oy_ref[0, 0:1, :] += ends_ref[2:3, :]
+
+    @pl.when(step == pl.num_programs(0) - 1)
+    def _():
+        deep = ox_ref.shape[1]
+        ox_ref[BPX - 1, deep - 1:deep, :] += ends_ref[4:5, :]
+        oy_ref[BPX - 1, deep - 1:deep, :] += ends_ref[5:6, :]
+
+
+def finish(lab, landed, weights, p, up, dn, sides, ends, hu, hv, h):
     deep = 2 * TILE
     steps = PATCH // deep
     cols = BPY * PATCH
+    rows = p.shape[1]
     split = (GROUPS, BPX, PATCH, LANES)
     slab = pl.BlockSpec((GROUPS, BPX, deep, LANES), lambda i: (0, 0, i, 0))
     out = pl.BlockSpec((BPX, deep, cols), lambda i: (0, i, 0))
     shape = jax.ShapeDtypeStruct((BPX, PATCH, cols), F32)
     field = pltpu.VMEM((GROUPS, BPX * TILE, LANES), F32)
+
+    def const(x):
+        return pl.BlockSpec(x.shape, lambda i: (0,) * x.ndim)
+
     return pl.pallas_call(
-        wind_kernel,
+        finish_kernel,
         grid=(steps,),
         out_shape=(shape, shape),
         in_specs=[
-            pl.BlockSpec(lab.shape, lambda i: (0, 0)),
-            pl.BlockSpec(landed.shape, lambda i: (0, 0)),
+            const(lab), const(landed),
             pl.BlockSpec((NW * ABLK, 2 * PART), lambda i: (0, i)),
+            const(p), const(up), const(dn), const(sides), const(ends),
             slab, slab, slab,
         ],
         out_specs=(out, out),
@@ -657,13 +697,17 @@
             pltpu.VMEM((2 * NPATCH, PART), F32),
             pltpu.VMEM((2 * NPATCH, PART), F32),
             field, field, field, field,
+            pltpu.VMEM((GROUPS, rows + 2 * TILE, LANES), F32),
         ],
         compiler_params=params(),
         cost_estimate=pl.CostEstimate(
             flops=4 * NPATCH * NW * ABLK * PATCH * PATCH, bytes_accessed=20 << 20, transcendentals=0
         ),
-        name="wind",
-    )(lab, landed, weights, hu.reshape(split), hv.reshape(split), fac.reshape(split))
+        name="finish",
+    )(
+        lab, landed, weights, p, up, dn, sides, ends,
+        hu.reshape(split), hv.reshape(split), h.reshape(split),
+    )
 
 
 def body(
@@ -705,15 +749,16 @@
         return got.reshape(rows.shape)
 
     press = exchange(top, press)
-    newh, hu, hv, h = stencil(depth_field, wet_mask, mom_x, mom_y)
-    wind = exchange(newh, wind)
+    newh, hu, hv, h, token = stencil(depth_field, wet_mask, mom_x, mom_y)
+    wind = exchange(token, wind)
     weights = remap_weights.reshape(NW * ABLK, PATCH * PATCH)
-    p, top, bottom, left, right = pressure_field(lab, press, weights, (top, bottom, left, right))
+    p, *edges = pressure_field(lab, press, weights, (top, bottom, left, right))
+    top, bottom, left, right = edges
     halos = (
         send(bottom, "gx", 1), send(top, "gx", -1), send(right, "gy", 1), send(left, "gy", -1),
     )
-    newh, hu, hv, fac = settle(p, newh, hu, hv, h, halos, (top, bottom, left, right))
-    new_x, new_y = wind_field(lab, wind, weights, hu, hv, fac)
+    newh, sides, ends = border(halos, edges, newh)
+    new_x, new_y = finish(lab, wind, weights, p, halos[0], halos[1], sides, ends, hu, hv, h)
     return (newh, new_x.reshape(newh.shape), new_y.reshape(newh.shape))
 
 

time: 101 us -> 98.7 us (0.977)
  Pallas kernels: 59.6 us -> 58.2 us
    pallas_call x3, Pallas kernels: 40.9 us -> 39.4 us  [the longest x1 18.9 us: stencil(): pl.pallas_call(stencil_kernel, grid=(bands + 1,), out_shape=(jax.ShapeDty...]
  transfers between devices with their start and end apart: 7 -> 7, of which waited for: 2 -> 2; matrix products, arithmetic and copies ran while one was open for 1% -> 1% of each run, Pallas kernels for 46% -> 40%
where the time goes in v6:
time: 98.7 us; the launch traced here: 97.9 us
  Pallas kernels  58.2 us (59%)
  starting transfers between devices  29.9 us (30%)
  waiting for transfers between devices  4.66 us (5%)
  local copies, waits for them, and re-layouts  3.73 us (4%)
  between operations  1.44 us (1%)
    pallas_call x1, Pallas kernels, stencil(): pl.pallas_call(stencil_kernel, grid=(bands + 1,), out_shape=(jax.ShapeDty...  18.9 us
    pallas_call x1, Pallas kernels, finish(): pl.pallas_call(finish_kernel, grid=(steps,), out_shape=(shape, shape), in...  16.4 us
    ppermute x4, starting transfers between devices, send(): return lax.ppermute(value, axis, pairs)  12.3 us
    all_to_all x2, starting transfers between devices, exchange(): got = lax.all_to_all(parts, both, split_axis=0, concat_axis=0, tiled=True)  11.7 us
    pallas_call x1, Pallas kernels, pressure_field(): pl.pallas_call(press_kernel, grid=(steps,), out_shape=tuple((jax.ShapeDty...  7.74 us
    all_to_all x1, starting transfers between devices, body(): lax.all_to_all(want.reshape(devices, 1, capacity), both, split_axis=0, co...  5.99 us
    ppermute x4, waiting for transfers between devices, send(): return lax.ppermute(value, axis, pairs)  4.65 us
    pallas_call x1, Pallas kernels, edge_cells(): pl.pallas_call(edges_kernel, grid=(1,), out_shape=(line, line, column, co...  4.46 us
  transfers between devices with their start and end apart: 7, of which 2 were waited for; matrix products, arithmetic and copies ran while one was open for 1% of the time, Pallas kernels for 40%

profile of v6, /device:TPU:12, one launch (start us, length us, event | category | flops | bytes accessed | tf_op | source)
XLA Modules:
  0.0 97.9 jit_solution(3465515729331644035)
XLA Ops:
  0.6 1.7 %requests.1 = (s32[32,32]{1,0:T(8,128)}, s32[32,32]{1,0:T(8,128)}) custom-call(s32[1,512]{1,0:T(1,128)} %bitcast.29, s32[1,512]{1,0:T(1,128)} %bitcast.30, s32[1,512]{1,0:T(1,128)} %bitcast.31, s32[1,512]{1,0:T(1,128)} %bitcast.32), custom_call_target="tpu_custom_call" | custom-call | tf_op jit(solution)/shard_map/requests/pallas_call | solution.py:82
  2.3 6.0 %all-to-all-start = ((s32[32,1,32]{2,1,0:T(1,128)}), s32[32,1,32]{2,1,0:T(1,128)S(1)}, u32[]{:S(2)}, u32[]{:S(2)}) async-start(s32[32,1,32]{2,1,0:T(1,128)} %bitcast.28), calls=%async_computation | async-start | bytes 32768 | tf_op jit(solution)/shard_map/all_to_all | solution.py:738
  9.0 2.0 %mix.1 = (bf16[256,256]{1,0:T(8,128)(2,1)}, bf16[256,512]{1,0:T(8,128)(2,1)}) custom-call(f32[1]{0:T(128)} %bitcast.19.blend_ref, bf16[6,256,256]{2,1,0:T(8,128)(2,1)} %bitcast.27), custom_call_target="tpu_custom_call" | custom-call | tf_op jit(solution)/shard_map/mix/pallas_call | solution.py:108
  11.0 4.5 %edges.1 = (f32[8,512]{1,0:T(8,128)}, f32[8,512]{1,0:T(8,128)}, f32[8,1024]{1,0:T(8,128)}, f32[8,1024]{1,0:T(8,128)}) custom-call(f32[1024,512]{1,0:T(8,128)} %d_ref.1, s32[1024,512]{1,0:T(8,128)} %m_ref.1, f32[1024,512]{1,0:T(8,128)} %x_ref.1, f32[1024,512]{1,0:T(8,128)} %y_ref.1, f32[1024,512]{1,0:T(8,128)} %d_ref.1, s32[1024,512]{1,0:T(8,128)} %m_ref.1, ...), custom_call_target="tpu_custom_call" | custom-call | tf_op jit(solution)/shard_map/edges/pallas_call | solution.py:194
  15.5 0.7 copy-done.2
  16.2 1.3 %serve.2 = bf16[1024,256]{1,0:T(8,128)(2,1)} custom-call(f32[8,512]{1,0:T(8,128)S(1)} %copy-done.2, s32[32,1,32]{2,1,0:T(1,128)S(1)} %all-to-all-done.asked_ref, bf16[256,256]{1,0:T(8,128)(2,1)S(1)} %copy-done.1), custom_call_target="tpu_custom_call" | custom-call | tf_op jit(solution)/shard_map/serve/pallas_call | solution.py:140
  17.5 5.8 %all-to-all-start.1 = ((bf16[32,32,256]{2,1,0:T(8,128)(2,1)}), bf16[32,32,256]{2,1,0:T(8,128)(2,1)S(1)}, u32[]{:S(2)}, u32[]{:S(2)}) async-start(bf16[32,32,256]{2,1,0:T(8,128)(2,1)} %bitcast.8), calls=%async_computation.1 | async-start | bytes 1048576 | tf_op jit(solution)/shard_map/all_to_all | solution.py:748
  23.3 18.9 %stencil.1 = (f32[1024,512]{1,0:T(8,128)}, f32[4,1024,128]{2,1,0:T(8,128)}, f32[4,1024,128]{2,1,0:T(8,128)}, f32[4,1024,128]{2,1,0:T(8,128)}, f32[8,128]{1,0:T(8,128)}) custom-call(f32[1024,512]{1,0:T(8,128)} %d_ref.1, s32[1024,512]{1,0:T(8,128)} %m_ref.1, f32[1024,512]{1,0:T(8,128)} %x_ref.1, f32[1024,512]{1,0:T(8,128)} %y_ref.1), custom_call_target="tpu_custom_call" | custom-call | flops 104857600 | bytes 33554432 | tf_op jit(solution)/shard_map/stencil/pallas_call | solution.py:374
  42.3 0.7 copy-done.3
  42.9 1.5 %serve.3 = bf16[1024,512]{1,0:T(8,128)(2,1)} custom-call(f32[8,128]{1,0:T(8,128)S(1)} %copy-done.3, s32[32,1,32]{2,1,0:T(1,128)S(1)} %all-to-all-done.asked_ref, bf16[256,512]{1,0:T(8,128)(2,1)S(1)} %copy-done), custom_call_target="tpu_custom_call" | custom-call | tf_op jit(solution)/shard_map/serve/pallas_call | solution.py:140
  44.5 5.8 %all-to-all-start.2 = ((bf16[32,32,512]{2,1,0:T(8,128)(2,1)}), bf16[32,32,512]{2,1,0:T(8,128)(2,1)S(1)}, u32[]{:S(2)}, u32[]{:S(2)}) async-start(bf16[32,32,512]{2,1,0:T(8,128)(2,1)} %bitcast.11), calls=%async_computation.2 | async-start | bytes 2097152 | tf_op jit(solution)/shard_map/all_to_all | solution.py:748
  50.3 0.7 reshape.64.lab_ref
  51.0 7.7 %pressure.1 = (f32[4,1024,128]{2,1,0:T(8,128)}, f32[8,512]{1,0:T(8,128)}, f32[8,512]{1,0:T(8,128)}, f32[8,1024]{1,0:T(8,128)}, f32[8,1024]{1,0:T(8,128)}) custom-call(s32[1,1024]{1,0:T(1,128)} %reshape.64.lab_ref, bf16[1024,256]{1,0:T(8,128)(2,1)} %bitcast.26, bf16[1024,4096]{1,0:T(8,128)(2,1)} %bitcast.20, f32[8,512]{1,0:T(8,128)} %get-tuple-element.27.after_ref.top0_ref, ...), custom_call_target="tpu_custom_call" | custom-call | flops 1073741824 | bytes 12582912 | tf_op jit(solution)/shard_map/pressure/pallas_call | solution.py:480
  58.7 2.0 %collective-permute-start.2 = (f32[8,1024]{1,0:T(8,128)}, f32[8,1024]{1,0:T(8,128)S(1)}, u32[]{:S(2)}, u32[]{:S(2)}) collective-permute-start(f32[8,1024]{1,0:T(8,128)} %get-tuple-element.35.right_ref), channel_id=1, source_target_pairs={{0,1},{1,2},{2,3},{3,4},{4,5},{5,6},{6,7},{8,9},{9,10},{10,11},{11... | collective-permute-start | bytes 98312 | tf_op jit(solution)/shard_map/ppermute | solution.py:216
  60.8 4.4 %collective-permute-start.3 = (f32[8,1024]{1,0:T(8,128)}, f32[8,1024]{1,0:T(8,128)S(1)}, u32[]{:S(2)}, u32[]{:S(2)}) collective-permute-start(f32[8,1024]{1,0:T(8,128)} %get-tuple-element.36.left_ref), channel_id=1, source_target_pairs={{1,0},{2,1},{3,2},{4,3},{5,4},{6,5},{7,6},{9,8},{10,9},{11,10},{12... | collective-permute-start | bytes 98312 | tf_op jit(solution)/shard_map/ppermute | solution.py:216
  65.2 3.4 %collective-permute-start = (f32[8,512]{1,0:T(8,128)}, f32[8,512]{1,0:T(8,128)S(1)}, u32[]{:S(2)}, u32[]{:S(2)}) collective-permute-start(f32[8,512]{1,0:T(8,128)} %get-tuple-element.33.bottom_ref), channel_id=1, source_target_pairs={{0,8},{8,16},{16,24},{1,9},{9,17},{17,25},{2,10},{10,18},{18,26},{... | collective-permute-start | bytes 49160 | tf_op jit(solution)/shard_map/ppermute | solution.py:216
  68.6 2.5 %collective-permute-start.1 = (f32[8,512]{1,0:T(8,128)}, f32[8,512]{1,0:T(8,128)S(1)}, u32[]{:S(2)}, u32[]{:S(2)}) collective-permute-start(f32[8,512]{1,0:T(8,128)} %get-tuple-element.34.top_ref), channel_id=1, source_target_pairs={{8,0},{16,8},{24,16},{9,1},{17,9},{25,17},{10,2},{18,10},{26,18},{... | collective-permute-start | bytes 49160 | tf_op jit(solution)/shard_map/ppermute | solution.py:216
  71.1 2.8 %collective-permute-done.up_ref = f32[8,512]{1,0:T(8,128)S(1)} collective-permute-done((f32[8,512]{1,0:T(8,128)}, f32[8,512]{1,0:T(8,128)S(1)}, u32[]{:S(2)}, u32[]{:S(2)}) %collective-permute-start) | collective-permute-done | bytes 16416 | tf_op jit(solution)/shard_map/ppermute | solution.py:216
  73.8 1.9 %collective-permute-done.1.dn_ref = f32[8,512]{1,0:T(8,128)S(1)} collective-permute-done((f32[8,512]{1,0:T(8,128)}, f32[8,512]{1,0:T(8,128)S(1)}, u32[]{:S(2)}, u32[]{:S(2)}) %collective-permute-start.1) | collective-permute-done | bytes 16416 | tf_op jit(solution)/shard_map/ppermute | solution.py:216
  75.7 0.6 copy-done.7
  76.3 0.0 copy-done.8
  76.3 4.2 %border.1 = (f32[1024,512]{1,0:T(8,128)}, f32[1024,128]{1,0:T(8,128)}, f32[8,512]{1,0:T(8,128)}) custom-call(f32[8,512]{1,0:T(8,128)} %copy-done.6, f32[8,512]{1,0:T(8,128)} %copy-done.7, f32[8,1024]{1,0:T(8,128)} %copy-done.8, f32[8,1024]{1,0:T(8,128)} %copy-done.9, f32[8,512]{1,0:T(8,128)} %get-tuple-element.34.top_ref, ...), custom_call_target="tpu_custom_call", output_to_operand_aliasing={{0}: (8, {})} | custom-call | tf_op jit(solution)/shard_map/border/pallas_call | solution.py:574
  80.5 1.1 %copy-done.4 = bf16[32,32,512]{2,1,0:T(8,128)(2,1)} copy-done((bf16[32,32,512]{2,1,0:T(8,128)(2,1)}, bf16[32,32,512]{2,1,0:T(8,128)(2,1)S(1)}, u32[]{:S(2)}) %copy-start.4) | copy-done | bytes 1048600
  81.6 16.4 %finish.1 = (f32[16,64,512]{2,1,0:T(8,128)}, f32[16,64,512]{2,1,0:T(8,128)}) custom-call(s32[1,1024]{1,0:T(1,128)} %reshape.64.lab_ref, bf16[1024,512]{1,0:T(8,128)(2,1)} %bitcast.22, bf16[1024,4096]{1,0:T(8,128)(2,1)} %bitcast.21, f32[4,1024,128]{2,1,0:T(8,128)} %get-tuple-element.41.p_ref, f32[8,512]{1,0:T(8,128)} %copy-done.6, f32[8,512]{1,0:T(8,128)} %copy-done.7, ...), custom_call_target="tpu_custom_call" | custom-call | flops 2147483648 | bytes 20971520 | tf_op jit(solution)/shard_map/finish/pallas_call | solution.py:684
  (22 shorter events, 0.0 us)
Async XLA Ops:
  2.3 13.1 %all-to-all-start = ((s32[32,1,32]{2,1,0:T(1,128)}), s32[32,1,32]{2,1,0:T(1,128)S(1)}, u32[]{:S(2)}, u32[]{:S(2)}) async-start(s32[32,1,32]{2,1,0:T(1,128)} %bitcast.28), calls=%async_computation | async-start | bytes 32768 | tf_op jit(solution)/shard_map/all_to_all | solution.py:738
  11.0 4.5 %copy-start.1 = (bf16[256,256]{1,0:T(8,128)(2,1)S(1)}, bf16[256,256]{1,0:T(8,128)(2,1)}, u32[]{:S(2)}) copy-start(bf16[256,256]{1,0:T(8,128)(2,1)} %get-tuple-element.29.tiles_ref) | copy-start | bytes 393220
  15.4 0.7 copy-start.2
  17.5 27.0 %all-to-all-start.1 = ((bf16[32,32,256]{2,1,0:T(8,128)(2,1)}), bf16[32,32,256]{2,1,0:T(8,128)(2,1)S(1)}, u32[]{:S(2)}, u32[]{:S(2)}) async-start(bf16[32,32,256]{2,1,0:T(8,128)(2,1)} %bitcast.8), calls=%async_computation.1 | async-start | bytes 1048576 | tf_op jit(solution)/shard_map/all_to_all | solution.py:748
  23.3 18.9 %copy-start = (bf16[256,512]{1,0:T(8,128)(2,1)S(1)}, bf16[256,512]{1,0:T(8,128)(2,1)}, u32[]{:S(2)}) copy-start(bf16[256,512]{1,0:T(8,128)(2,1)} %get-tuple-element.40.tiles_ref) | copy-start | bytes 786436
  23.3 27.0 %copy-start.10 = (s32[32,32]{1,0:T(8,128)S(1)}, s32[32,32]{1,0:T(8,128)}, u32[]{:S(2)}) copy-start(s32[32,32]{1,0:T(8,128)} %get-tuple-element.26) | copy-start | bytes 12292
  42.3 0.7 copy-start.3
  44.5 6.5 %copy-start.5 = (bf16[32,32,256]{2,1,0:T(8,128)(2,1)}, bf16[32,32,256]{2,1,0:T(8,128)(2,1)S(1)}, u32[]{:S(2)}) copy-start(bf16[32,32,256]{2,1,0:T(8,128)(2,1)S(1)} %all-to-all-done.1) | copy-start | bytes 1572868
  44.5 36.0 %all-to-all-start.2 = ((bf16[32,32,512]{2,1,0:T(8,128)(2,1)}), bf16[32,32,512]{2,1,0:T(8,128)(2,1)S(1)}, u32[]{:S(2)}, u32[]{:S(2)}) async-start(bf16[32,32,512]{2,1,0:T(8,128)(2,1)} %bitcast.11), calls=%async_computation.2 | async-start | bytes 2097152 | tf_op jit(solution)/shard_map/all_to_all | solution.py:748
  58.7 17.0 %collective-permute-start.2 = (f32[8,1024]{1,0:T(8,128)}, f32[8,1024]{1,0:T(8,128)S(1)}, u32[]{:S(2)}, u32[]{:S(2)}) collective-permute-start(f32[8,1024]{1,0:T(8,128)} %get-tuple-element.35.right_ref), channel_id=1, source_target_pairs={{0,1},{1,2},{2,3},{3,4},{4,5},{5,6},{6,7},{8,9},{9,10},{10,11},{11... | collective-permute-start | bytes 98312 | tf_op jit(solution)/shard_map/ppermute | solution.py:216
  60.8 14.9 %collective-permute-start.3 = (f32[8,1024]{1,0:T(8,128)}, f32[8,1024]{1,0:T(8,128)S(1)}, u32[]{:S(2)}, u32[]{:S(2)}) collective-permute-start(f32[8,1024]{1,0:T(8,128)} %get-tuple-element.36.left_ref), channel_id=1, source_target_pairs={{1,0},{2,1},{3,2},{4,3},{5,4},{6,5},{7,6},{9,8},{10,9},{11,10},{12... | collective-permute-start | bytes 98312 | tf_op jit(solution)/shard_map/ppermute | solution.py:216
  65.2 8.6 %collective-permute-start = (f32[8,512]{1,0:T(8,128)}, f32[8,512]{1,0:T(8,128)S(1)}, u32[]{:S(2)}, u32[]{:S(2)}) collective-permute-start(f32[8,512]{1,0:T(8,128)} %get-tuple-element.33.bottom_ref), channel_id=1, source_target_pairs={{0,8},{8,16},{16,24},{1,9},{9,17},{17,25},{2,10},{10,18},{18,26},{... | collective-permute-start | bytes 49160 | tf_op jit(solution)/shard_map/ppermute | solution.py:216
  68.6 7.1 %collective-permute-start.1 = (f32[8,512]{1,0:T(8,128)}, f32[8,512]{1,0:T(8,128)S(1)}, u32[]{:S(2)}, u32[]{:S(2)}) collective-permute-start(f32[8,512]{1,0:T(8,128)} %get-tuple-element.34.top_ref), channel_id=1, source_target_pairs={{8,0},{16,8},{24,16},{9,1},{17,9},{25,17},{10,2},{18,10},{26,18},{... | collective-permute-start | bytes 49160 | tf_op jit(solution)/shard_map/ppermute | solution.py:216
  73.8 1.9 %copy-start.6 = (f32[8,512]{1,0:T(8,128)}, f32[8,512]{1,0:T(8,128)S(1)}, u32[]{:S(2)}) copy-start(f32[8,512]{1,0:T(8,128)S(1)} %collective-permute-done.up_ref) | copy-start | bytes 49156
  75.7 0.6 copy-start.7
  75.7 0.6 copy-start.8
  75.7 0.6 copy-start.9
  80.5 1.1 %copy-start.4 = (bf16[32,32,512]{2,1,0:T(8,128)(2,1)}, bf16[32,32,512]{2,1,0:T(8,128)(2,1)S(1)}, u32[]{:S(2)}) copy-start(bf16[32,32,512]{2,1,0:T(8,128)(2,1)S(1)} %all-to-all-done.2) | copy-start | bytes 3145732

commit v7 on v6

--- a/solution.py
+++ b/solution.py
@@ -202,7 +202,8 @@
             pl.BlockSpec((TILE, rows), lambda i: (0, 0)),
             pl.BlockSpec((TILE, rows), lambda i: (0, 0)),
         ),
-        compiler_params=params(),
+        compiler_params=params(56 << 20),
+        cost_estimate=pl.CostEstimate(flops=0, bytes_accessed=8 << 20, transcendentals=0),
         name="edges",
     )(*(fields * 4))
 
@@ -384,7 +385,7 @@
             pl.BlockSpec((TILE, LANES), lambda i: (0, 0)),
         ),
         scratch_shapes=[pad] * (CELL + 3),
-        compiler_params=params(),
+        compiler_params=params(36 << 20),
         cost_estimate=pl.CostEstimate(
             flops=200 * rows * cols, bytes_accessed=64 * rows * cols, transcendentals=0
         ),
@@ -494,7 +495,7 @@
             pltpu.VMEM((GROUPS, BPX * TILE, LANES), F32),
             pltpu.VMEM((GROUPS, BPX * TILE, LANES), F32),
         ],
-        compiler_params=params(),
+        compiler_params=params(24 << 20),
         cost_estimate=pl.CostEstimate(
             flops=2 * NPATCH * NW * ABLK * PATCH * PATCH, bytes_accessed=12 << 20, transcendentals=0
         ),
@@ -590,7 +591,8 @@
             pltpu.SemaphoreType.DMA((4,)),
             pltpu.SemaphoreType.DMA((4,)),
         ],
-        compiler_params=params(),
+        compiler_params=params(16 << 20),
+        cost_estimate=pl.CostEstimate(flops=0, bytes_accessed=6 << 20, transcendentals=0),
         name="border",
     )(*halos, *edges, newh)
 
@@ -699,7 +701,7 @@
             field, field, field, field,
             pltpu.VMEM((GROUPS, rows + 2 * TILE, LANES), F32),
         ],
-        compiler_params=params(),
+        compiler_params=params(34 << 20),
         cost_estimate=pl.CostEstimate(
             flops=4 * NPATCH * NW * ABLK * PATCH * PATCH, bytes_accessed=20 << 20, transcendentals=0
         ),

time: 98.7 us -> 110 us (1.11)
  local copies, waits for them, and re-layouts: 3.73 us -> 24.3 us
  Pallas kernels: 58.2 us -> 49 us
    unnamed x22 -> x48, local copies, waits for them, and re-layouts: 3.06 us -> 24.2 us
    pallas_call x1, Pallas kernels: 7.74 us -> 3.94 us  [pressure_field(): pl.pallas_call(press_kernel, grid=(steps,), out_shape=tuple((jax.ShapeDty...]
    pallas_call x1, Pallas kernels: 16.4 us -> 14 us  [finish(): pl.pallas_call(finish_kernel, grid=(steps,), out_shape=(shape, shape), in...]
    pallas_call x1, Pallas kernels: 4.16 us -> 2.47 us  [border(): pl.pallas_call(border_kernel, out_shape=(jax.ShapeDtypeStruct((rows, cols...]
    pallas_call x1, Pallas kernels: 18.9 us -> 17.4 us  [stencil(): pl.pallas_call(stencil_kernel, grid=(bands + 1,), out_shape=(jax.ShapeDty...]
  transfers between devices with their start and end apart: 7 -> 7, of which waited for: 2 -> 2; matrix products, arithmetic and copies ran while one was open for 1% -> 0% of each run, Pallas kernels for 40% -> 29%
where the time goes in v7:
time: 110 us; the launch traced here: 109 us
  Pallas kernels  49 us (45%)
  starting transfers between devices  30.1 us (27%)
  local copies, waits for them, and re-layouts  24.3 us (22%)
  waiting for transfers between devices  4.16 us (4%)
  between operations  1.46 us (1%)
    unnamed x48, local copies, waits for them, and re-layouts  24.2 us
    pallas_call x1, Pallas kernels, stencil(): pl.pallas_call(stencil_kernel, grid=(bands + 1,), out_shape=(jax.ShapeDty...  17.4 us
    pallas_call x1, Pallas kernels, finish(): pl.pallas_call(finish_kernel, grid=(steps,), out_shape=(shape, shape), in...  14 us
    ppermute x4, starting transfers between devices, send(): return lax.ppermute(value, axis, pairs)  12.4 us
    all_to_all x2, starting transfers between devices, exchange(): got = lax.all_to_all(parts, both, split_axis=0, concat_axis=0, tiled=True)  11.7 us
    all_to_all x1, starting transfers between devices, body(): lax.all_to_all(want.reshape(devices, 1, capacity), both, split_axis=0, co...  5.99 us
    pallas_call x1, Pallas kernels, edge_cells(): pl.pallas_call(edges_kernel, grid=(1,), out_shape=(line, line, column, co...  4.57 us
    ppermute x4, waiting for transfers between devices, send(): return lax.ppermute(value, axis, pairs)  4.15 us
  transfers between devices with their start and end apart: 7, of which 2 were waited for; matrix products, arithmetic and copies ran while one was open for 0% of the time, Pallas kernels for 29%

profile of v7, /device:TPU:12, one launch (start us, length us, event | category | flops | bytes accessed | tf_op | source)
XLA Modules:
  0.0 109.0 jit_solution(9763521856889114171)
XLA Ops:
  0.6 1.7 %requests.1 = (s32[32,32]{1,0:T(8,128)}, s32[32,32]{1,0:T(8,128)}) custom-call(s32[1,512]{1,0:T(1,128)} %bitcast.29, s32[1,512]{1,0:T(1,128)} %bitcast.30, s32[1,512]{1,0:T(1,128)} %bitcast.31, s32[1,512]{1,0:T(1,128)} %bitcast.32), custom_call_target="tpu_custom_call" | custom-call | tf_op jit(solution)/shard_map/requests/pallas_call | solution.py:82
  2.3 6.0 %all-to-all-start = ((s32[32,1,32]{2,1,0:T(1,128)}), s32[32,1,32]{2,1,0:T(1,128)S(1)}, u32[]{:S(2)}, u32[]{:S(2)}) async-start(s32[32,1,32]{2,1,0:T(1,128)} %bitcast.28), calls=%async_computation | async-start | bytes 32768 | tf_op jit(solution)/shard_map/all_to_all | solution.py:740
  9.0 2.0 %mix.1 = (bf16[256,256]{1,0:T(8,128)(2,1)}, bf16[256,512]{1,0:T(8,128)(2,1)}) custom-call(f32[1]{0:T(128)} %bitcast.19.blend_ref, bf16[6,256,256]{2,1,0:T(8,128)(2,1)} %bitcast.27), custom_call_target="tpu_custom_call" | custom-call | tf_op jit(solution)/shard_map/mix/pallas_call | solution.py:108
  11.0 4.6 %edges.1 = (f32[8,512]{1,0:T(8,128)}, f32[8,512]{1,0:T(8,128)}, f32[8,1024]{1,0:T(8,128)}, f32[8,1024]{1,0:T(8,128)}) custom-call(f32[1024,512]{1,0:T(8,128)} %d_ref.1, s32[1024,512]{1,0:T(8,128)} %m_ref.1, f32[1024,512]{1,0:T(8,128)} %x_ref.1, f32[1024,512]{1,0:T(8,128)} %y_ref.1, f32[1024,512]{1,0:T(8,128)} %d_ref.1, s32[1024,512]{1,0:T(8,128)} %m_ref.1, ...), custom_call_target="tpu_custom_call" | custom-call | bytes 8388608 | tf_op jit(solution)/shard_map/edges/pallas_call | solution.py:194
  17.6 5.8 %all-to-all-start.1 = ((bf16[32,32,256]{2,1,0:T(8,128)(2,1)}), bf16[32,32,256]{2,1,0:T(8,128)(2,1)S(1)}, u32[]{:S(2)}, u32[]{:S(2)}) async-start(bf16[32,32,256]{2,1,0:T(8,128)(2,1)} %bitcast.8), calls=%async_computation.1 | async-start | bytes 1048576 | tf_op jit(solution)/shard_map/all_to_all | solution.py:750
  23.5 1.6 %copy-done.1 = s32[1024,512]{1,0:T(8,128)S(1)} copy-done((s32[1024,512]{1,0:T(8,128)S(1)}, s32[1024,512]{1,0:T(8,128)}, u32[]{:S(2)}) %copy-start.1) | copy-done | bytes 2097176
  25.1 1.6 %copy-done.2 = f32[1024,512]{1,0:T(8,128)S(1)} copy-done((f32[1024,512]{1,0:T(8,128)S(1)}, f32[1024,512]{1,0:T(8,128)}, u32[]{:S(2)}) %copy-start.2) | copy-done | bytes 2097176
  26.7 1.6 %copy-done.3 = f32[1024,512]{1,0:T(8,128)S(1)} copy-done((f32[1024,512]{1,0:T(8,128)S(1)}, f32[1024,512]{1,0:T(8,128)}, u32[]{:S(2)}) %copy-start.3) | copy-done | bytes 2097176
  28.2 17.4 %stencil.1 = (f32[1024,512]{1,0:T(8,128)}, f32[4,1024,128]{2,1,0:T(8,128)S(1)}, f32[4,1024,128]{2,1,0:T(8,128)S(1)}, f32[4,1024,128]{2,1,0:T(8,128)S(1)}, f32[8,128]{1,0:T(8,128)S(1)}) custom-call(f32[1024,512]{1,0:T(8,128)S(1)} %copy-done, s32[1024,512]{1,0:T(8,128)S(1)} %copy-done.1, f32[1024,512]{1,0:T(8,128)S(1)} %copy-done.2, f32[1024,512]{1,0:T(8,128)S(1)} %copy-done.3), custom_call_target="tpu_custom_call" | custom-call | flops 104857600 | bytes 33554432 | tf_op jit(solution)/shard_map/stencil/pallas_call | solution.py:375
  51.3 5.8 %all-to-all-start.2 = ((bf16[32,32,512]{2,1,0:T(8,128)(2,1)}), bf16[32,32,512]{2,1,0:T(8,128)(2,1)S(1)}, u32[]{:S(2)}, u32[]{:S(2)}) async-start(bf16[32,32,512]{2,1,0:T(8,128)(2,1)} %bitcast.11), calls=%async_computation.2 | async-start | bytes 2097152 | tf_op jit(solution)/shard_map/all_to_all | solution.py:750
  57.2 3.4 %copy-done.4 = bf16[4,256,4096]{2,1,0:T(8,128)(2,1)S(1)} copy-done((bf16[4,256,4096]{2,1,0:T(8,128)(2,1)S(1)}, bf16[4,256,4096]{2,1,0:T(8,128)(2,1)}, u32[]{:S(2)}) %copy-start.4) | copy-done | bytes 8388632
  60.6 3.9 %pressure.1 = (f32[4,1024,128]{2,1,0:T(8,128)S(1)}, f32[8,512]{1,0:T(8,128)S(1)}, f32[8,512]{1,0:T(8,128)S(1)}, f32[8,1024]{1,0:T(8,128)S(1)}, f32[8,1024]{1,0:T(8,128)S(1)}) custom-call(s32[1,1024]{1,0:T(1,128)S(1)} %reshape.64.lab_ref, bf16[1024,256]{1,0:T(8,128)(2,1)S(1)} %bitcast.26, bf16[1024,4096]{1,0:T(8,128)(2,1)S(1)} %bitcast.20, ...), custom_call_target="tpu_custom_call" | custom-call | flops 1073741824 | bytes 12582912 | tf_op jit(solution)/shard_map/pressure/pallas_call | solution.py:481
  65.9 2.2 %collective-permute-start.2 = (f32[8,1024]{1,0:T(8,128)S(1)}, f32[8,1024]{1,0:T(8,128)S(1)}, u32[]{:S(2)}, u32[]{:S(2)}) collective-permute-start(f32[8,1024]{1,0:T(8,128)S(1)} %get-tuple-element.35.right_ref), channel_id=1, source_target_pairs={{0,1},{1,2},{2,3},{3,4},{4,5},{5,6},{6,7},{8,9},{9,10},{10,11},{11... | collective-permute-start | bytes 98312 | tf_op jit(solution)/shard_map/ppermute | solution.py:217
  68.1 4.4 %collective-permute-start.3 = (f32[8,1024]{1,0:T(8,128)S(1)}, f32[8,1024]{1,0:T(8,128)S(1)}, u32[]{:S(2)}, u32[]{:S(2)}) collective-permute-start(f32[8,1024]{1,0:T(8,128)S(1)} %get-tuple-element.36.left_ref), channel_id=1, source_target_pairs={{1,0},{2,1},{3,2},{4,3},{5,4},{6,5},{7,6},{9,8},{10,9},{11,10},{12... | collective-permute-start | bytes 98312 | tf_op jit(solution)/shard_map/ppermute | solution.py:217
  72.5 3.4 %collective-permute-start = (f32[8,512]{1,0:T(8,128)S(1)}, f32[8,512]{1,0:T(8,128)S(1)}, u32[]{:S(2)}, u32[]{:S(2)}) collective-permute-start(f32[8,512]{1,0:T(8,128)S(1)} %get-tuple-element.33.bottom_ref), channel_id=1, source_target_pairs={{0,8},{8,16},{16,24},{1,9},{9,17},{17,25},{2,10},{10,18},{18,26},{... | collective-permute-start | bytes 49160 | tf_op jit(solution)/shard_map/ppermute | solution.py:217
  75.9 2.4 %collective-permute-start.1 = (f32[8,512]{1,0:T(8,128)S(1)}, f32[8,512]{1,0:T(8,128)S(1)}, u32[]{:S(2)}, u32[]{:S(2)}) collective-permute-start(f32[8,512]{1,0:T(8,128)S(1)} %get-tuple-element.34.top_ref), channel_id=1, source_target_pairs={{8,0},{16,8},{24,16},{9,1},{17,9},{25,17},{10,2},{18,10},{26,18},{... | collective-permute-start | bytes 49160 | tf_op jit(solution)/shard_map/ppermute | solution.py:217
  78.3 2.3 %collective-permute-done.up_ref = f32[8,512]{1,0:T(8,128)S(1)} collective-permute-done((f32[8,512]{1,0:T(8,128)S(1)}, f32[8,512]{1,0:T(8,128)S(1)}, u32[]{:S(2)}, u32[]{:S(2)}) %collective-permute-start) | collective-permute-done | bytes 16416 | tf_op jit(solution)/shard_map/ppermute | solution.py:217
  80.6 1.9 %collective-permute-done.1.dn_ref = f32[8,512]{1,0:T(8,128)S(1)} collective-permute-done((f32[8,512]{1,0:T(8,128)S(1)}, f32[8,512]{1,0:T(8,128)S(1)}, u32[]{:S(2)}, u32[]{:S(2)}) %collective-permute-start.1) | collective-permute-done | bytes 16416 | tf_op jit(solution)/shard_map/ppermute | solution.py:217
  82.5 2.5 %border.1 = (f32[1024,512]{1,0:T(8,128)}, f32[1024,128]{1,0:T(8,128)S(1)}, f32[8,512]{1,0:T(8,128)S(1)}) custom-call(f32[8,512]{1,0:T(8,128)S(1)} %collective-permute-done.up_ref, f32[8,512]{1,0:T(8,128)S(1)} %collective-permute-done.1.dn_ref, f32[8,1024]{1,0:T(8,128)S(1)} %collective-permute-done.2.lh_ref, ...), custom_call_target="tpu_custom_call", output_to_operand_aliasing={{0}: (8, {})} | custom-call | bytes 6291456 | tf_op jit(solution)/shard_map/border/pallas_call | solution.py:575
  85.8 3.4 %copy-done.5 = bf16[4,256,4096]{2,1,0:T(8,128)(2,1)S(1)} copy-done((bf16[4,256,4096]{2,1,0:T(8,128)(2,1)S(1)}, bf16[4,256,4096]{2,1,0:T(8,128)(2,1)}, u32[]{:S(2)}) %copy-start.5) | copy-done | bytes 8388632
  89.1 1.6 %copy-done.9 = f32[4,1024,128]{2,1,0:T(8,128)S(1)} copy-done((f32[4,1024,128]{2,1,0:T(8,128)S(1)}, f32[4,1024,128]{2,1,0:T(8,128)}, u32[]{:S(2)}) %copy-start.9) | copy-done | bytes 2097176
  90.7 1.6 %copy-done.11 = f32[4,1024,128]{2,1,0:T(8,128)S(1)} copy-done((f32[4,1024,128]{2,1,0:T(8,128)S(1)}, f32[4,1024,128]{2,1,0:T(8,128)}, u32[]{:S(2)}) %copy-start.11) | copy-done | bytes 2097176
  92.3 1.6 %copy-done.13 = f32[4,1024,128]{2,1,0:T(8,128)S(1)} copy-done((f32[4,1024,128]{2,1,0:T(8,128)S(1)}, f32[4,1024,128]{2,1,0:T(8,128)}, u32[]{:S(2)}) %copy-start.13) | copy-done | bytes 2097176
  95.0 14.0 %finish.1 = (f32[16,64,512]{2,1,0:T(8,128)}, f32[16,64,512]{2,1,0:T(8,128)}) custom-call(s32[1,1024]{1,0:T(1,128)S(1)} %reshape.64.lab_ref, bf16[1024,512]{1,0:T(8,128)(2,1)S(1)} %bitcast.22, bf16[1024,4096]{1,0:T(8,128)(2,1)S(1)} %bitcast.21, f32[4,1024,128]{2,1,0:T(8,128)S(1)} %copy-done.13, f32[8,512]{1,0:T(8,128)S(1)} %collective-permute-done.up_ref, ...), custom_call_target="tpu_custom_call" | custom-call | flops 2147483648 | bytes 20971520 | tf_op jit(solution)/shard_map/finish/pallas_call | solution.py:686
  (48 shorter events, 10.9 us)
Async XLA Ops:
  2.3 13.2 %all-to-all-start = ((s32[32,1,32]{2,1,0:T(1,128)}), s32[32,1,32]{2,1,0:T(1,128)S(1)}, u32[]{:S(2)}, u32[]{:S(2)}) async-start(s32[32,1,32]{2,1,0:T(1,128)} %bitcast.28), calls=%async_computation | async-start | bytes 32768 | tf_op jit(solution)/shard_map/all_to_all | solution.py:740
  11.0 4.6 %copy-start.17 = (bf16[256,256]{1,0:T(8,128)(2,1)S(1)}, bf16[256,256]{1,0:T(8,128)(2,1)}, u32[]{:S(2)}) copy-start(bf16[256,256]{1,0:T(8,128)(2,1)} %get-tuple-element.29.tiles_ref) | copy-start | bytes 393220
  11.0 12.5 %copy-start = (f32[1024,512]{1,0:T(8,128)S(1)}, f32[1024,512]{1,0:T(8,128)}, u32[]{:S(2)}) copy-start(f32[1024,512]{1,0:T(8,128)} %d_ref.1) | copy-start | bytes 6291460
  17.6 33.6 %all-to-all-start.1 = ((bf16[32,32,256]{2,1,0:T(8,128)(2,1)}), bf16[32,32,256]{2,1,0:T(8,128)(2,1)S(1)}, u32[]{:S(2)}, u32[]{:S(2)}) async-start(bf16[32,32,256]{2,1,0:T(8,128)(2,1)} %bitcast.8), calls=%async_computation.1 | async-start | bytes 1048576 | tf_op jit(solution)/shard_map/all_to_all | solution.py:750
  23.5 1.6 %copy-start.1 = (s32[1024,512]{1,0:T(8,128)S(1)}, s32[1024,512]{1,0:T(8,128)}, u32[]{:S(2)}) copy-start(s32[1024,512]{1,0:T(8,128)} %m_ref.1) | copy-start | bytes 6291460
  25.1 1.6 %copy-start.2 = (f32[1024,512]{1,0:T(8,128)S(1)}, f32[1024,512]{1,0:T(8,128)}, u32[]{:S(2)}) copy-start(f32[1024,512]{1,0:T(8,128)} %x_ref.1) | copy-start | bytes 6291460
  26.7 1.6 %copy-start.3 = (f32[1024,512]{1,0:T(8,128)S(1)}, f32[1024,512]{1,0:T(8,128)}, u32[]{:S(2)}) copy-start(f32[1024,512]{1,0:T(8,128)} %y_ref.1) | copy-start | bytes 6291460
  28.2 21.4 %copy-start.16 = (bf16[256,512]{1,0:T(8,128)(2,1)S(1)}, bf16[256,512]{1,0:T(8,128)(2,1)}, u32[]{:S(2)}) copy-start(bf16[256,512]{1,0:T(8,128)(2,1)} %get-tuple-element.40.tiles_ref) | copy-start | bytes 786436
  49.6 7.5 %copy-start.23 = (s32[32,32]{1,0:T(8,128)S(1)}, s32[32,32]{1,0:T(8,128)}, u32[]{:S(2)}) copy-start(s32[32,32]{1,0:T(8,128)} %get-tuple-element.26) | copy-start | bytes 12292
  49.6 7.5 %copy-start.19 = (f32[8,512]{1,0:T(8,128)S(1)}, f32[8,512]{1,0:T(8,128)}, u32[]{:S(2)}) copy-start(f32[8,512]{1,0:T(8,128)} %get-tuple-element.27.after_ref.top0_ref) | copy-start | bytes 49156
  49.6 7.5 %copy-start.20 = (f32[8,1024]{1,0:T(8,128)S(1)}, f32[8,1024]{1,0:T(8,128)}, u32[]{:S(2)}) copy-start(f32[8,1024]{1,0:T(8,128)} %get-tuple-element.31.left0_ref) | copy-start | bytes 98308
  49.6 7.5 %copy-start.21 = (f32[8,1024]{1,0:T(8,128)S(1)}, f32[8,1024]{1,0:T(8,128)}, u32[]{:S(2)}) copy-start(f32[8,1024]{1,0:T(8,128)} %get-tuple-element.32.right0_ref) | copy-start | bytes 98308
  49.6 7.5 %copy-start.22 = (f32[8,512]{1,0:T(8,128)S(1)}, f32[8,512]{1,0:T(8,128)}, u32[]{:S(2)}) copy-start(f32[8,512]{1,0:T(8,128)} %get-tuple-element.30.bottom0_ref) | copy-start | bytes 49156
  51.3 34.5 %all-to-all-start.2 = ((bf16[32,32,512]{2,1,0:T(8,128)(2,1)}), bf16[32,32,512]{2,1,0:T(8,128)(2,1)S(1)}, u32[]{:S(2)}, u32[]{:S(2)}) async-start(bf16[32,32,512]{2,1,0:T(8,128)(2,1)} %bitcast.11), calls=%async_computation.2 | async-start | bytes 2097152 | tf_op jit(solution)/shard_map/all_to_all | solution.py:750
  57.2 3.4 %copy-start.4 = (bf16[4,256,4096]{2,1,0:T(8,128)(2,1)S(1)}, bf16[4,256,4096]{2,1,0:T(8,128)(2,1)}, u32[]{:S(2)}) copy-start(bf16[4,256,4096]{2,1,0:T(8,128)(2,1)} %param.12) | copy-start | bytes 25165828
  65.9 19.9 %copy-start.7 = (f32[4,1024,128]{2,1,0:T(8,128)S(1)}, f32[4,1024,128]{2,1,0:T(8,128)}, u32[]{:S(2)}) copy-start(f32[4,1024,128]{2,1,0:T(8,128)} %copy-done.6) | copy-start | bytes 6291460
  65.9 16.6 %collective-permute-start.2 = (f32[8,1024]{1,0:T(8,128)S(1)}, f32[8,1024]{1,0:T(8,128)S(1)}, u32[]{:S(2)}, u32[]{:S(2)}) collective-permute-start(f32[8,1024]{1,0:T(8,128)S(1)} %get-tuple-element.35.right_ref), channel_id=1, source_target_pairs={{0,1},{1,2},{2,3},{3,4},{4,5},{5,6},{6,7},{8,9},{9,10},{10,11},{11... | collective-permute-start | bytes 98312 | tf_op jit(solution)/shard_map/ppermute | solution.py:217
  68.1 14.4 %collective-permute-start.3 = (f32[8,1024]{1,0:T(8,128)S(1)}, f32[8,1024]{1,0:T(8,128)S(1)}, u32[]{:S(2)}, u32[]{:S(2)}) collective-permute-start(f32[8,1024]{1,0:T(8,128)S(1)} %get-tuple-element.36.left_ref), channel_id=1, source_target_pairs={{1,0},{2,1},{3,2},{4,3},{5,4},{6,5},{7,6},{9,8},{10,9},{11,10},{12... | collective-permute-start | bytes 98312 | tf_op jit(solution)/shard_map/ppermute | solution.py:217
  72.5 8.1 %collective-permute-start = (f32[8,512]{1,0:T(8,128)S(1)}, f32[8,512]{1,0:T(8,128)S(1)}, u32[]{:S(2)}, u32[]{:S(2)}) collective-permute-start(f32[8,512]{1,0:T(8,128)S(1)} %get-tuple-element.33.bottom_ref), channel_id=1, source_target_pairs={{0,8},{8,16},{16,24},{1,9},{9,17},{17,25},{2,10},{10,18},{18,26},{... | collective-permute-start | bytes 49160 | tf_op jit(solution)/shard_map/ppermute | solution.py:217
  75.9 6.6 %collective-permute-start.1 = (f32[8,512]{1,0:T(8,128)S(1)}, f32[8,512]{1,0:T(8,128)S(1)}, u32[]{:S(2)}, u32[]{:S(2)}) collective-permute-start(f32[8,512]{1,0:T(8,128)S(1)} %get-tuple-element.34.top_ref), channel_id=1, source_target_pairs={{8,0},{16,8},{24,16},{9,1},{17,9},{25,17},{10,2},{18,10},{26,18},{... | collective-permute-start | bytes 49160 | tf_op jit(solution)/shard_map/ppermute | solution.py:217
  85.8 3.4 %copy-start.5 = (bf16[4,256,4096]{2,1,0:T(8,128)(2,1)S(1)}, bf16[4,256,4096]{2,1,0:T(8,128)(2,1)}, u32[]{:S(2)}) copy-start(bf16[4,256,4096]{2,1,0:T(8,128)(2,1)} %param.12) | copy-start | bytes 25165828
  89.1 1.6 %copy-start.9 = (f32[4,1024,128]{2,1,0:T(8,128)S(1)}, f32[4,1024,128]{2,1,0:T(8,128)}, u32[]{:S(2)}) copy-start(f32[4,1024,128]{2,1,0:T(8,128)} %copy-done.8) | copy-start | bytes 6291460
  90.7 1.6 %copy-start.11 = (f32[4,1024,128]{2,1,0:T(8,128)S(1)}, f32[4,1024,128]{2,1,0:T(8,128)}, u32[]{:S(2)}) copy-start(f32[4,1024,128]{2,1,0:T(8,128)} %copy-done.10) | copy-start | bytes 6291460
  92.3 1.6 %copy-start.13 = (f32[4,1024,128]{2,1,0:T(8,128)S(1)}, f32[4,1024,128]{2,1,0:T(8,128)}, u32[]{:S(2)}) copy-start(f32[4,1024,128]{2,1,0:T(8,128)} %copy-done.12) | copy-start | bytes 6291460
  (7 other events, 7.9 us)

commit v8 on v6

--- a/solution.py
+++ b/solution.py
@@ -292,7 +292,7 @@
                     dst[g, to, :] = val
             return carry
 
-        lax.fori_loop(0, BAND // TILE, fill, 0, unroll=4)
+        lax.fori_loop(0, BAND // TILE, fill, 0, unroll=8)
 
     rows = bands * BAND
 
@@ -317,7 +317,7 @@
                     dst[g, pl.ds(base, TILE), :] = val
             return carry
 
-        lax.fori_loop(0, BAND // TILE, across, 0, unroll=4)
+        lax.fori_loop(0, BAND // TILE, across, 0, unroll=8)
 
         @pl.when(step == bands)
         def _():
@@ -361,7 +361,7 @@
                 h_ref[g, at, :] = h
             return carry
 
-        lax.fori_loop(0, BAND // TILE, body, 0, unroll=4)
+        lax.fori_loop(0, BAND // TILE, body, 0, unroll=8)
 
 
 def stencil(depth, mask, momx, momy):
@@ -441,26 +441,30 @@
         spread_rows(src, mid, 0)
         for g in range(GROUPS):
             for r in range(BPX):
-                to = pl.ds(pl.multiple_of(r * PATCH + (2 * step + part) * TILE, TILE), TILE)
+                to = pl.ds(pl.multiple_of(TILE + r * PATCH + (2 * step + part) * TILE, TILE), TILE)
                 out_ref[g, to, :] = mid[g, r * TILE:(r + 1) * TILE, :]
 
     @pl.when(step == pl.num_programs(0) - 1)
     def _():
-        rows = out_ref.shape[1]
+        rows = out_ref.shape[1] - 2 * TILE
         mine = iota((TILE, LANES), 0) == 3
+        blank = jnp.zeros((TILE, LANES), F32)
         for g in range(GROUPS):
             cut = slice(g * LANES, (g + 1) * LANES)
-            head = pltpu.roll(out_ref[g, 0:TILE, :], 3, 0)
-            tail = pltpu.roll(out_ref[g, rows - TILE:rows, :], 4, 0)
+            head = pltpu.roll(out_ref[g, TILE:2 * TILE, :], 3, 0)
+            tail = pltpu.roll(out_ref[g, rows:rows + TILE, :], 4, 0)
+            out_ref[g, 0:TILE, :] = blank
+            out_ref[g, rows + TILE:, :] = blank
             top_ref[:, cut] = jnp.where(mine, head, top0_ref[:, cut])
             bottom_ref[:, cut] = jnp.where(mine, tail, bottom0_ref[:, cut])
         lane = iota((LANES, LANES), 1)
         for b in range(rows // LANES):
             at = slice(b * LANES, (b + 1) * LANES)
+            inner = slice(TILE + b * LANES, TILE + (b + 1) * LANES)
             packed = jnp.where(
                 lane == TILE + 3,
-                pltpu.roll(out_ref[GROUPS - 1, at, :], TILE + 4, 1),
-                pltpu.roll(out_ref[0, at, :], 3, 1),
+                pltpu.roll(out_ref[GROUPS - 1, inner, :], TILE + 4, 1),
+                pltpu.roll(out_ref[0, inner, :], 3, 1),
             )
             turned = packed.T
             left_ref[:, at] = jnp.where(mine, turned[0:TILE], left0_ref[:, at])
@@ -472,7 +476,7 @@
     rows = BPX * PATCH
     line = (TILE, BPY * PATCH)
     column = (TILE, rows)
-    whole = (GROUPS, rows, LANES)
+    whole = (GROUPS, rows + 2 * TILE, LANES)
 
     def const(shape):
         return pl.BlockSpec(shape, lambda i: (0,) * len(shape))
@@ -525,34 +529,38 @@
     def cells(ref):
         return derived(ref[0:1, :], ref[1:2, :], ref[2:3, :])
 
-    edge[0:1, :] = lh_ref[3:4, :]
-    edge[1:2, :] = rh_ref[3:4, :]
-    for at, before, after, own, sign in (
-        (2, lh_ref, left_ref, left_ref, 1.0), (5, right_ref, rh_ref, right_ref, -1.0),
+    pull = TIME_STEP * PRESS * 0.5
+    edge[...] = jnp.zeros_like(edge)
+    for at, before, after, own, far, sign in (
+        (0, lh_ref, left_ref, left_ref, lh_ref, 1.0),
+        (3, right_ref, rh_ref, right_ref, rh_ref, -1.0),
     ):
         gh, gn, gt = flux(along_y(cells(before)), along_y(cells(after)))
         wet = own[0:1, :] > 0.0
-        for f, val in enumerate((gh, gt, gn)):
-            edge[at + f:at + f + 1, :] = jnp.where(wet, (sign * 0.5 * DT_DX) * val, 0.0)
+        press = (pull * own[0:1, :]) * far[3:4, :]
+        for f, val in enumerate((gh * (0.5 * DT_DX), gt * (0.5 * DT_DX), gn * (0.5 * DT_DX) + press)):
+            edge[at + f:at + f + 1, :] = jnp.where(wet, sign * val, 0.0)
     blank = jnp.zeros((LANES - TILE, LANES), F32)
     for b in range(rows // LANES):
         cut = slice(b * LANES, (b + 1) * LANES)
         sides_ref[cut, :] = jnp.concatenate([edge[:, cut], blank], axis=0).T
     ends_ref[...] = jnp.zeros_like(ends_ref)
-    for at, before, after, own, sign in (
-        (0, up_ref, top_ref, top_ref, 1.0), (3, bottom_ref, dn_ref, bottom_ref, -1.0),
+    for at, before, after, own, far, sign in (
+        (0, up_ref, top_ref, top_ref, up_ref, 1.0),
+        (3, bottom_ref, dn_ref, bottom_ref, dn_ref, -1.0),
     ):
-        fluxes = flux(along_x(cells(before)), along_x(cells(after)))
+        gh, gn, gt = flux(along_x(cells(before)), along_x(cells(after)))
         wet = own[0:1, :] > 0.0
-        for f, val in enumerate(fluxes):
-            ends_ref[at + f:at + f + 1, :] = jnp.where(wet, (sign * 0.5 * DT_DX) * val, 0.0)
+        press = (pull * own[0:1, :]) * far[3:4, :]
+        for f, val in enumerate((gh * (0.5 * DT_DX), gn * (0.5 * DT_DX) + press, gt * (0.5 * DT_DX))):
+            ends_ref[at + f:at + f + 1, :] = jnp.where(wet, sign * val, 0.0)
 
     for copy in loads:
         copy.wait()
     lane = iota((rows, LANES), 1)
     sides = sides_ref[...]
-    first[...] += jnp.where(lane == 0, pltpu.roll(sides, LANES - 2, 1), 0.0)
-    last[...] += jnp.where(lane == LANES - 1, pltpu.roll(sides, LANES - 6, 1), 0.0)
+    first[...] += jnp.where(lane == 0, sides, 0.0)
+    last[...] += jnp.where(lane == LANES - 1, pltpu.roll(sides, LANES - 4, 1), 0.0)
     for at, line in ((0, 0), (rows - 1, 3)):
         first[at:at + 1, :] += ends_ref[line:line + 1, 0:LANES]
         last[at:at + 1, :] += ends_ref[line:line + 1, cols - LANES:cols]
@@ -596,21 +604,15 @@
 
 
 def finish_kernel(
-    lab_ref, landed_ref, w_ref, p_ref, up_ref, dn_ref, sides_ref, ends_ref,
+    lab_ref, landed_ref, w_ref, p_ref, sides_ref, ends_ref,
     hu_ref, hv_ref, h_ref, ox_ref, oy_ref,
-    left, acc, acc2, fx, fy, fx2, fy2, padded,
+    left, acc, acc2, fx, fy, fx2, fy2,
 ):
     step = pl.program_id(0)
-    rows = p_ref.shape[1]
 
     @pl.when(step == 0)
     def _():
         stack_left(left, summed_of(lab_ref[...], landed_ref[...]), 2)
-        for g in range(GROUPS):
-            cut = slice(g * LANES, (g + 1) * LANES)
-            padded[g, TILE:TILE + rows, :] = p_ref[g]
-            padded[g, 0:TILE, :] = jnp.broadcast_to(up_ref[3:4, cut], (TILE, LANES))
-            padded[g, rows + TILE:, :] = jnp.broadcast_to(dn_ref[3:4, cut], (TILE, LANES))
 
     acc[...] = jnp.dot(left[...], w_ref[:, :PART], preferred_element_type=F32)
     acc2[...] = jnp.dot(left[...], w_ref[:, PART:], preferred_element_type=F32)
@@ -624,24 +626,25 @@
             mark = pl.multiple_of(r * PATCH + (2 * step + part) * TILE, TILE)
             base = pl.multiple_of(mark + TILE, TILE)
             ends = sides_ref[pl.ds(mark, TILE), :]
-            tiles = [padded[g, pl.ds(base, TILE), :] for g in range(GROUPS)]
+            tiles = [p_ref[g, pl.ds(base, TILE), :] for g in range(GROUPS)]
             for g in range(GROUPS):
-                before = tiles[g - 1] if g else pltpu.roll(ends, LANES - 1, 1)
-                after = tiles[g + 1] if g < GROUPS - 1 else pltpu.roll(ends, LANES - 1, 1)
+                before = tiles[g - 1] if g else 0.0
+                after = tiles[g + 1] if g < GROUPS - 1 else 0.0
                 prev = pltpu.roll(jnp.where(lane == LANES - 1, before, tiles[g]), 1, 1)
                 nxt = pltpu.roll(jnp.where(lane == 0, after, tiles[g]), LANES - 1, 1)
                 h = h_ref[g, r, cells, :]
                 wet = h > 0.0
                 scale = (TIME_STEP * PRESS * 0.5) * h
-                gx = padded[g, pl.ds(base + 1, TILE), :] - padded[g, pl.ds(base - 1, TILE), :]
+                gx = p_ref[g, pl.ds(base + 1, TILE), :] - p_ref[g, pl.ds(base - 1, TILE), :]
                 wx = mx[g, at, :]
                 wy = my[g, at, :]
-                speed = (TIME_STEP * STRESS) * jnp.sqrt(wx * wx + wy * wy)
+                power = wx * wx + wy * wy
+                speed = jnp.where(power > 0.0, power * lax.rsqrt(power), 0.0) * (TIME_STEP * STRESS)
                 new = [
                     hu_ref[g, r, cells, :] - scale * gx + speed * wx,
                     hv_ref[g, r, cells, :] - scale * (nxt - prev) + speed * wy,
                 ]
-                for own, edge, shift in ((0, 0, 3), (GROUPS - 1, LANES - 1, 6)):
+                for own, edge, shift in ((0, 0, 1), (GROUPS - 1, LANES - 1, 4)):
                     if g == own:
                         new = [
                             jnp.where(
@@ -667,11 +670,10 @@
         oy_ref[BPX - 1, deep - 1:deep, :] += ends_ref[5:6, :]
 
 
-def finish(lab, landed, weights, p, up, dn, sides, ends, hu, hv, h):
+def finish(lab, landed, weights, p, sides, ends, hu, hv, h):
     deep = 2 * TILE
     steps = PATCH // deep
     cols = BPY * PATCH
-    rows = p.shape[1]
     split = (GROUPS, BPX, PATCH, LANES)
     slab = pl.BlockSpec((GROUPS, BPX, deep, LANES), lambda i: (0, 0, i, 0))
     out = pl.BlockSpec((BPX, deep, cols), lambda i: (0, i, 0))
@@ -688,7 +690,7 @@
         in_specs=[
             const(lab), const(landed),
             pl.BlockSpec((NW * ABLK, 2 * PART), lambda i: (0, i)),
-            const(p), const(up), const(dn), const(sides), const(ends),
+            const(p), const(sides), const(ends),
             slab, slab, slab,
         ],
         out_specs=(out, out),
@@ -697,7 +699,6 @@
             pltpu.VMEM((2 * NPATCH, PART), F32),
             pltpu.VMEM((2 * NPATCH, PART), F32),
             field, field, field, field,
-            pltpu.VMEM((GROUPS, rows + 2 * TILE, LANES), F32),
         ],
         compiler_params=params(),
         cost_estimate=pl.CostEstimate(
@@ -705,7 +706,7 @@
         ),
         name="finish",
     )(
-        lab, landed, weights, p, up, dn, sides, ends,
+        lab, landed, weights, p, sides, ends,
         hu.reshape(split), hv.reshape(split), h.reshape(split),
     )
 
@@ -758,7 +759,7 @@
         send(bottom, "gx", 1), send(top, "gx", -1), send(right, "gy", 1), send(left, "gy", -1),
     )
     newh, sides, ends = border(halos, edges, newh)
-    new_x, new_y = finish(lab, wind, weights, p, halos[0], halos[1], sides, ends, hu, hv, h)
+    new_x, new_y = finish(lab, wind, weights, p, sides, ends, hu, hv, h)
     return (newh, new_x.reshape(newh.shape), new_y.reshape(newh.shape))
 
 

time: 98.7 us -> 92.4 us (0.936)
  Pallas kernels: 58.2 us -> 51.8 us
    pallas_call x1, Pallas kernels: 16.4 us -> 11.8 us  [finish(): pl.pallas_call(finish_kernel, grid=(steps,), out_shape=(shape, shape), in...]
    pallas_call x1, Pallas kernels: 18.9 us -> 17.3 us  [stencil(): pl.pallas_call(stencil_kernel, grid=(bands + 1,), out_shape=(jax.ShapeDty...]
where the time goes in v8:
time: 92.4 us; the launch traced here: 91.6 us
  Pallas kernels  51.8 us (56%)
  starting transfers between devices  29.9 us (32%)
  waiting for transfers between devices  4.71 us (5%)
  local copies, waits for them, and re-layouts  3.71 us (4%)
  between operations  1.44 us (2%)
    pallas_call x1, Pallas kernels, stencil(): pl.pallas_call(stencil_kernel, grid=(bands + 1,), out_shape=(jax.ShapeDty...  17.3 us
    ppermute x4, starting transfers between devices, send(): return lax.ppermute(value, axis, pairs)  12.3 us
    pallas_call x1, Pallas kernels, finish(): pl.pallas_call(finish_kernel, grid=(steps,), out_shape=(shape, shape), in...  11.8 us
    all_to_all x2, starting transfers between devices, exchange(): got = lax.all_to_all(parts, both, split_axis=0, concat_axis=0, tiled=True)  11.7 us
    pallas_call x1, Pallas kernels, pressure_field(): pl.pallas_call(press_kernel, grid=(steps,), out_shape=tuple((jax.ShapeDty...  7.69 us
    all_to_all x1, starting transfers between devices, body(): lax.all_to_all(want.reshape(devices, 1, capacity), both, split_axis=0, co...  5.99 us
    ppermute x4, waiting for transfers between devices, send(): return lax.ppermute(value, axis, pairs)  4.7 us
    pallas_call x1, Pallas kernels, edge_cells(): pl.pallas_call(edges_kernel, grid=(1,), out_shape=(line, line, column, co...  4.46 us
  transfers between devices with their start and end apart: 7, of which 2 were waited for; matrix products, arithmetic and copies ran while one was open for 1% of the time, Pallas kernels for 40%

profile of v8, /device:TPU:12, one launch (start us, length us, event | category | flops | bytes accessed | tf_op | source)
XLA Modules:
  0.0 91.6 jit_solution(2504145452556460225)
XLA Ops:
  0.6 1.7 %requests.1 = (s32[32,32]{1,0:T(8,128)}, s32[32,32]{1,0:T(8,128)}) custom-call(s32[1,512]{1,0:T(1,128)} %bitcast.29, s32[1,512]{1,0:T(1,128)} %bitcast.30, s32[1,512]{1,0:T(1,128)} %bitcast.31, s32[1,512]{1,0:T(1,128)} %bitcast.32), custom_call_target="tpu_custom_call" | custom-call | tf_op jit(solution)/shard_map/requests/pallas_call | solution.py:82
  2.3 6.0 %all-to-all-start = ((s32[32,1,32]{2,1,0:T(1,128)}), s32[32,1,32]{2,1,0:T(1,128)S(1)}, u32[]{:S(2)}, u32[]{:S(2)}) async-start(s32[32,1,32]{2,1,0:T(1,128)} %bitcast.28), calls=%async_computation | async-start | bytes 32768 | tf_op jit(solution)/shard_map/all_to_all | solution.py:739
  9.0 2.0 %mix.1 = (bf16[256,256]{1,0:T(8,128)(2,1)}, bf16[256,512]{1,0:T(8,128)(2,1)}) custom-call(f32[1]{0:T(128)} %bitcast.19.blend_ref, bf16[6,256,256]{2,1,0:T(8,128)(2,1)} %bitcast.27), custom_call_target="tpu_custom_call" | custom-call | tf_op jit(solution)/shard_map/mix/pallas_call | solution.py:108
  11.0 4.5 %edges.1 = (f32[8,512]{1,0:T(8,128)}, f32[8,512]{1,0:T(8,128)}, f32[8,1024]{1,0:T(8,128)}, f32[8,1024]{1,0:T(8,128)}) custom-call(f32[1024,512]{1,0:T(8,128)} %d_ref.1, s32[1024,512]{1,0:T(8,128)} %m_ref.1, f32[1024,512]{1,0:T(8,128)} %x_ref.1, f32[1024,512]{1,0:T(8,128)} %y_ref.1, f32[1024,512]{1,0:T(8,128)} %d_ref.1, s32[1024,512]{1,0:T(8,128)} %m_ref.1, ...), custom_call_target="tpu_custom_call" | custom-call | tf_op jit(solution)/shard_map/edges/pallas_call | solution.py:194
  15.5 0.7 copy-done.2
  16.2 1.3 %serve.2 = bf16[1024,256]{1,0:T(8,128)(2,1)} custom-call(f32[8,512]{1,0:T(8,128)S(1)} %copy-done.2, s32[32,1,32]{2,1,0:T(1,128)S(1)} %all-to-all-done.asked_ref, bf16[256,256]{1,0:T(8,128)(2,1)S(1)} %copy-done.1), custom_call_target="tpu_custom_call" | custom-call | tf_op jit(solution)/shard_map/serve/pallas_call | solution.py:140
  17.5 5.8 %all-to-all-start.1 = ((bf16[32,32,256]{2,1,0:T(8,128)(2,1)}), bf16[32,32,256]{2,1,0:T(8,128)(2,1)S(1)}, u32[]{:S(2)}, u32[]{:S(2)}) async-start(bf16[32,32,256]{2,1,0:T(8,128)(2,1)} %bitcast.8), calls=%async_computation.1 | async-start | bytes 1048576 | tf_op jit(solution)/shard_map/all_to_all | solution.py:749
  23.3 17.3 %stencil.1 = (f32[1024,512]{1,0:T(8,128)}, f32[4,1024,128]{2,1,0:T(8,128)}, f32[4,1024,128]{2,1,0:T(8,128)}, f32[4,1024,128]{2,1,0:T(8,128)}, f32[8,128]{1,0:T(8,128)}) custom-call(f32[1024,512]{1,0:T(8,128)} %d_ref.1, s32[1024,512]{1,0:T(8,128)} %m_ref.1, f32[1024,512]{1,0:T(8,128)} %x_ref.1, f32[1024,512]{1,0:T(8,128)} %y_ref.1), custom_call_target="tpu_custom_call" | custom-call | flops 104857600 | bytes 33554432 | tf_op jit(solution)/shard_map/stencil/pallas_call | solution.py:374
  40.7 0.7 copy-done.3
  41.4 1.5 %serve.3 = bf16[1024,512]{1,0:T(8,128)(2,1)} custom-call(f32[8,128]{1,0:T(8,128)S(1)} %copy-done.3, s32[32,1,32]{2,1,0:T(1,128)S(1)} %all-to-all-done.asked_ref, bf16[256,512]{1,0:T(8,128)(2,1)S(1)} %copy-done), custom_call_target="tpu_custom_call" | custom-call | tf_op jit(solution)/shard_map/serve/pallas_call | solution.py:140
  42.9 5.8 %all-to-all-start.2 = ((bf16[32,32,512]{2,1,0:T(8,128)(2,1)}), bf16[32,32,512]{2,1,0:T(8,128)(2,1)S(1)}, u32[]{:S(2)}, u32[]{:S(2)}) async-start(bf16[32,32,512]{2,1,0:T(8,128)(2,1)} %bitcast.11), calls=%async_computation.2 | async-start | bytes 2097152 | tf_op jit(solution)/shard_map/all_to_all | solution.py:749
  48.7 0.7 reshape.64.lab_ref
  49.4 7.7 %pressure.1 = (f32[4,1040,128]{2,1,0:T(8,128)}, f32[8,512]{1,0:T(8,128)}, f32[8,512]{1,0:T(8,128)}, f32[8,1024]{1,0:T(8,128)}, f32[8,1024]{1,0:T(8,128)}) custom-call(s32[1,1024]{1,0:T(1,128)} %reshape.64.lab_ref, bf16[1024,256]{1,0:T(8,128)(2,1)} %bitcast.26, bf16[1024,4096]{1,0:T(8,128)(2,1)} %bitcast.20, f32[8,512]{1,0:T(8,128)} %get-tuple-element.27.after_ref.top0_ref, ...), custom_call_target="tpu_custom_call" | custom-call | flops 1073741824 | bytes 12582912 | tf_op jit(solution)/shard_map/pressure/pallas_call | solution.py:484
  57.1 2.0 %collective-permute-start.2 = (f32[8,1024]{1,0:T(8,128)}, f32[8,1024]{1,0:T(8,128)S(1)}, u32[]{:S(2)}, u32[]{:S(2)}) collective-permute-start(f32[8,1024]{1,0:T(8,128)} %get-tuple-element.35.right_ref), channel_id=1, source_target_pairs={{0,1},{1,2},{2,3},{3,4},{4,5},{5,6},{6,7},{8,9},{9,10},{10,11},{11... | collective-permute-start | bytes 98312 | tf_op jit(solution)/shard_map/ppermute | solution.py:216
  59.2 4.4 %collective-permute-start.3 = (f32[8,1024]{1,0:T(8,128)}, f32[8,1024]{1,0:T(8,128)S(1)}, u32[]{:S(2)}, u32[]{:S(2)}) collective-permute-start(f32[8,1024]{1,0:T(8,128)} %get-tuple-element.36.left_ref), channel_id=1, source_target_pairs={{1,0},{2,1},{3,2},{4,3},{5,4},{6,5},{7,6},{9,8},{10,9},{11,10},{12... | collective-permute-start | bytes 98312 | tf_op jit(solution)/shard_map/ppermute | solution.py:216
  63.6 3.4 %collective-permute-start = (f32[8,512]{1,0:T(8,128)}, f32[8,512]{1,0:T(8,128)S(1)}, u32[]{:S(2)}, u32[]{:S(2)}) collective-permute-start(f32[8,512]{1,0:T(8,128)} %get-tuple-element.33.bottom_ref), channel_id=1, source_target_pairs={{0,8},{8,16},{16,24},{1,9},{9,17},{17,25},{2,10},{10,18},{18,26},{... | collective-permute-start | bytes 49160 | tf_op jit(solution)/shard_map/ppermute | solution.py:216
  67.0 2.5 %collective-permute-start.1 = (f32[8,512]{1,0:T(8,128)}, f32[8,512]{1,0:T(8,128)S(1)}, u32[]{:S(2)}, u32[]{:S(2)}) collective-permute-start(f32[8,512]{1,0:T(8,128)} %get-tuple-element.34.top_ref), channel_id=1, source_target_pairs={{8,0},{16,8},{24,16},{9,1},{17,9},{25,17},{10,2},{18,10},{26,18},{... | collective-permute-start | bytes 49160 | tf_op jit(solution)/shard_map/ppermute | solution.py:216
  69.4 2.8 %collective-permute-done.up_ref = f32[8,512]{1,0:T(8,128)S(1)} collective-permute-done((f32[8,512]{1,0:T(8,128)}, f32[8,512]{1,0:T(8,128)S(1)}, u32[]{:S(2)}, u32[]{:S(2)}) %collective-permute-start) | collective-permute-done | bytes 16416 | tf_op jit(solution)/shard_map/ppermute | solution.py:216
  72.3 1.9 %collective-permute-done.1.dn_ref = f32[8,512]{1,0:T(8,128)S(1)} collective-permute-done((f32[8,512]{1,0:T(8,128)}, f32[8,512]{1,0:T(8,128)S(1)}, u32[]{:S(2)}, u32[]{:S(2)}) %collective-permute-start.1) | collective-permute-done | bytes 16416 | tf_op jit(solution)/shard_map/ppermute | solution.py:216
  74.2 0.6 copy-done.9
  74.7 0.0 copy-done.6
  74.8 4.0 %border.1 = (f32[1024,512]{1,0:T(8,128)}, f32[1024,128]{1,0:T(8,128)}, f32[8,512]{1,0:T(8,128)}) custom-call(f32[8,512]{1,0:T(8,128)} %copy-done.8, f32[8,512]{1,0:T(8,128)} %copy-done.9, f32[8,1024]{1,0:T(8,128)} %copy-done.6, f32[8,1024]{1,0:T(8,128)} %copy-done.7, f32[8,512]{1,0:T(8,128)} %get-tuple-element.34.top_ref, ...), custom_call_target="tpu_custom_call", output_to_operand_aliasing={{0}: (8, {})} | custom-call | tf_op jit(solution)/shard_map/border/pallas_call | solution.py:582
  78.8 1.0 %copy-done.4 = bf16[32,32,512]{2,1,0:T(8,128)(2,1)} copy-done((bf16[32,32,512]{2,1,0:T(8,128)(2,1)}, bf16[32,32,512]{2,1,0:T(8,128)(2,1)S(1)}, u32[]{:S(2)}) %copy-start.4) | copy-done | bytes 1048600
  79.8 11.8 %finish.1 = (f32[16,64,512]{2,1,0:T(8,128)}, f32[16,64,512]{2,1,0:T(8,128)}) custom-call(s32[1,1024]{1,0:T(1,128)} %reshape.64.lab_ref, bf16[1024,512]{1,0:T(8,128)(2,1)} %bitcast.22, bf16[1024,4096]{1,0:T(8,128)(2,1)} %bitcast.21, f32[4,1040,128]{2,1,0:T(8,128)} %get-tuple-element.41.p_ref, f32[1024,128]{1,0:T(8,128)} %get-tuple-element.42.sides_ref, ...), custom_call_target="tpu_custom_call" | custom-call | flops 2147483648 | bytes 20971520 | tf_op jit(solution)/shard_map/finish/pallas_call | solution.py:686
  (22 shorter events, 0.0 us)
Async XLA Ops:
  2.3 13.1 %all-to-all-start = ((s32[32,1,32]{2,1,0:T(1,128)}), s32[32,1,32]{2,1,0:T(1,128)S(1)}, u32[]{:S(2)}, u32[]{:S(2)}) async-start(s32[32,1,32]{2,1,0:T(1,128)} %bitcast.28), calls=%async_computation | async-start | bytes 32768 | tf_op jit(solution)/shard_map/all_to_all | solution.py:739
  11.0 4.5 %copy-start.1 = (bf16[256,256]{1,0:T(8,128)(2,1)S(1)}, bf16[256,256]{1,0:T(8,128)(2,1)}, u32[]{:S(2)}) copy-start(bf16[256,256]{1,0:T(8,128)(2,1)} %get-tuple-element.29.tiles_ref) | copy-start | bytes 393220
  15.4 0.7 copy-start.2
  17.5 25.4 %all-to-all-start.1 = ((bf16[32,32,256]{2,1,0:T(8,128)(2,1)}), bf16[32,32,256]{2,1,0:T(8,128)(2,1)S(1)}, u32[]{:S(2)}, u32[]{:S(2)}) async-start(bf16[32,32,256]{2,1,0:T(8,128)(2,1)} %bitcast.8), calls=%async_computation.1 | async-start | bytes 1048576 | tf_op jit(solution)/shard_map/all_to_all | solution.py:749
  23.3 17.3 %copy-start = (bf16[256,512]{1,0:T(8,128)(2,1)S(1)}, bf16[256,512]{1,0:T(8,128)(2,1)}, u32[]{:S(2)}) copy-start(bf16[256,512]{1,0:T(8,128)(2,1)} %get-tuple-element.40.tiles_ref) | copy-start | bytes 786436
  23.3 25.4 %copy-start.10 = (s32[32,32]{1,0:T(8,128)S(1)}, s32[32,32]{1,0:T(8,128)}, u32[]{:S(2)}) copy-start(s32[32,32]{1,0:T(8,128)} %get-tuple-element.26) | copy-start | bytes 12292
  40.7 0.7 copy-start.3
  42.9 6.5 %copy-start.5 = (bf16[32,32,256]{2,1,0:T(8,128)(2,1)}, bf16[32,32,256]{2,1,0:T(8,128)(2,1)S(1)}, u32[]{:S(2)}) copy-start(bf16[32,32,256]{2,1,0:T(8,128)(2,1)S(1)} %all-to-all-done.1) | copy-start | bytes 1572868
  42.9 35.9 %all-to-all-start.2 = ((bf16[32,32,512]{2,1,0:T(8,128)(2,1)}), bf16[32,32,512]{2,1,0:T(8,128)(2,1)S(1)}, u32[]{:S(2)}, u32[]{:S(2)}) async-start(bf16[32,32,512]{2,1,0:T(8,128)(2,1)} %bitcast.11), calls=%async_computation.2 | async-start | bytes 2097152 | tf_op jit(solution)/shard_map/all_to_all | solution.py:749
  57.1 17.0 %collective-permute-start.2 = (f32[8,1024]{1,0:T(8,128)}, f32[8,1024]{1,0:T(8,128)S(1)}, u32[]{:S(2)}, u32[]{:S(2)}) collective-permute-start(f32[8,1024]{1,0:T(8,128)} %get-tuple-element.35.right_ref), channel_id=1, source_target_pairs={{0,1},{1,2},{2,3},{3,4},{4,5},{5,6},{6,7},{8,9},{9,10},{10,11},{11... | collective-permute-start | bytes 98312 | tf_op jit(solution)/shard_map/ppermute | solution.py:216
  59.2 15.0 %collective-permute-start.3 = (f32[8,1024]{1,0:T(8,128)}, f32[8,1024]{1,0:T(8,128)S(1)}, u32[]{:S(2)}, u32[]{:S(2)}) collective-permute-start(f32[8,1024]{1,0:T(8,128)} %get-tuple-element.36.left_ref), channel_id=1, source_target_pairs={{1,0},{2,1},{3,2},{4,3},{5,4},{6,5},{7,6},{9,8},{10,9},{11,10},{12... | collective-permute-start | bytes 98312 | tf_op jit(solution)/shard_map/ppermute | solution.py:216
  63.6 8.7 %collective-permute-start = (f32[8,512]{1,0:T(8,128)}, f32[8,512]{1,0:T(8,128)S(1)}, u32[]{:S(2)}, u32[]{:S(2)}) collective-permute-start(f32[8,512]{1,0:T(8,128)} %get-tuple-element.33.bottom_ref), channel_id=1, source_target_pairs={{0,8},{8,16},{16,24},{1,9},{9,17},{17,25},{2,10},{10,18},{18,26},{... | collective-permute-start | bytes 49160 | tf_op jit(solution)/shard_map/ppermute | solution.py:216
  67.0 7.2 %collective-permute-start.1 = (f32[8,512]{1,0:T(8,128)}, f32[8,512]{1,0:T(8,128)S(1)}, u32[]{:S(2)}, u32[]{:S(2)}) collective-permute-start(f32[8,512]{1,0:T(8,128)} %get-tuple-element.34.top_ref), channel_id=1, source_target_pairs={{8,0},{16,8},{24,16},{9,1},{17,9},{25,17},{10,2},{18,10},{26,18},{... | collective-permute-start | bytes 49160 | tf_op jit(solution)/shard_map/ppermute | solution.py:216
  72.3 1.9 %copy-start.8 = (f32[8,512]{1,0:T(8,128)}, f32[8,512]{1,0:T(8,128)S(1)}, u32[]{:S(2)}) copy-start(f32[8,512]{1,0:T(8,128)S(1)} %collective-permute-done.up_ref) | copy-start | bytes 49156
  74.1 0.6 copy-start.9
  74.1 0.6 copy-start.6
  74.1 0.6 copy-start.7
  78.8 1.1 %copy-start.4 = (bf16[32,32,512]{2,1,0:T(8,128)(2,1)}, bf16[32,32,512]{2,1,0:T(8,128)(2,1)S(1)}, u32[]{:S(2)}) copy-start(bf16[32,32,512]{2,1,0:T(8,128)(2,1)S(1)} %all-to-all-done.2) | copy-start | bytes 3145732

commit v9 on v8

--- a/solution.py
+++ b/solution.py
@@ -268,41 +268,60 @@
 CELL = 9
 
 
-def stencil_kernel(
-    d_ref, m_ref, x_ref, y_ref, newh_ref, hu_ref, hv_ref, h_ref, token_ref, *scratch,
-):
-    cell = scratch[:CELL]
-    gx = scratch[CELL:]
+def stencil_kernel(opening, closing, *refs):
+    fields = refs[:4]
+    refs = refs[5:]
+    above = () if opening else refs[:4]
+    if not opening:
+        refs = refs[8:]
+    newh_ref, hu_ref, hv_ref, h_ref, token_ref = refs[:5]
+    cell = refs[5:5 + CELL]
+    gx = refs[5 + CELL:]
     step = pl.program_id(0)
     bands = pl.num_programs(0) - 1
     lane = iota((TILE, LANES), 1)
 
-    @pl.when(step < bands)
-    def _():
+    def masked(d, m, x, y, at, cut):
+        wet = m[at, cut] == 1
+        return derived(*[jnp.where(wet, ref[at, cut], 0.0) for ref in (d, x, y)])
+
+    def fill_band():
         def fill(t, carry):
             at = pl.ds(pl.multiple_of(t * TILE, TILE), TILE)
             to = pl.ds(pl.multiple_of(step * BAND + t * TILE + TILE, TILE), TILE)
             for g in range(GROUPS):
                 cut = slice(g * LANES, (g + 1) * LANES)
-                wet = m_ref[at, cut] == 1
-                h = jnp.where(wet, d_ref[at, cut], 0.0)
-                u = jnp.where(wet, x_ref[at, cut], 0.0)
-                v = jnp.where(wet, y_ref[at, cut], 0.0)
-                for dst, val in zip(cell, derived(h, u, v)):
+                for dst, val in zip(cell, masked(*fields, at, cut)):
                     dst[g, to, :] = val
             return carry
 
         lax.fori_loop(0, BAND // TILE, fill, 0, unroll=8)
 
-    rows = bands * BAND
+    if closing:
+        pl.when(step < bands)(fill_band)
+    else:
+        fill_band()
 
     @pl.when(step == 0)
     def _():
         token_ref[...] = jnp.zeros_like(token_ref)
-        for dst in cell:
-            dst[:, rows + TILE:, :] = jnp.zeros((GROUPS, TILE, LANES), F32)
-        for dst in gx:
-            dst[:, 0:TILE, :] = jnp.zeros((GROUPS, TILE, LANES), F32)
+        if closing:
+            for dst in cell:
+                dst[:, dst.shape[1] - BAND:dst.shape[1] - BAND + TILE, :] = jnp.zeros(
+                    (GROUPS, TILE, LANES), F32
+                )
+        if opening:
+            for dst in gx:
+                dst[:, 0:TILE, :] = jnp.zeros((GROUPS, TILE, LANES), F32)
+        else:
+            for g in range(GROUPS):
+                cut = slice(g * LANES, (g + 1) * LANES)
+                for dst, val in zip(cell, masked(*above, slice(None), cut)):
+                    dst[g, 0:TILE, :] = val
+                now = along_x([ref[g, 0:TILE, :] for ref in cell])
+                nxt = along_x([ref[g, 1:TILE + 1, :] for ref in cell])
+                for dst, val in zip(gx, flux(now, nxt)):
+                    dst[g, 0:TILE, :] = val
 
     @pl.when(step > 0)
     def _():
@@ -319,10 +338,12 @@
 
         lax.fori_loop(0, BAND // TILE, across, 0, unroll=8)
 
-        @pl.when(step == bands)
-        def _():
-            for dst in gx:
-                dst[:, rows + TILE - 1:rows + TILE, :] = jnp.zeros((GROUPS, 1, LANES), F32)
+        if closing:
+            @pl.when(step == bands)
+            def _():
+                for dst in gx:
+                    at = dst.shape[1] - BAND - 1
+                    dst[:, at:at + 1, :] = jnp.zeros((GROUPS, 1, LANES), F32)
 
         def body(t, carry):
             mark = pl.multiple_of(start + t * TILE, TILE)
@@ -364,32 +385,39 @@
         lax.fori_loop(0, BAND // TILE, body, 0, unroll=8)
 
 
-def stencil(depth, mask, momx, momy):
-    rows, cols = depth.shape
+def stencil(fields, after, first, count, old=()):
+    rows, cols = fields[0].shape
     bands = rows // BAND
+    opening = first == 0
+    closing = first + count == bands
     plane = jax.ShapeDtypeStruct((GROUPS, rows, LANES), F32)
-    pad = pltpu.VMEM((GROUPS, rows + 2 * TILE, LANES), F32)
-    band = pl.BlockSpec((BAND, cols), lambda i: (jnp.minimum(i, bands - 1), 0))
-    part = pl.BlockSpec((GROUPS, BAND, LANES), lambda i: (0, jnp.maximum(i - 1, 0), 0))
+    scratch = pltpu.VMEM((GROUPS, (count + 1) * BAND + TILE, LANES), F32)
+    band = pl.BlockSpec((BAND, cols), lambda i: (jnp.minimum(first + i, bands - 1), 0))
+    above = pl.BlockSpec((TILE, cols), lambda i: (first * BAND // TILE - 1, 0))
+    whole = pl.BlockSpec(memory_space=pl.ANY)
+    part = pl.BlockSpec((GROUPS, BAND, LANES), lambda i: (0, first + jnp.maximum(i - 1, 0), 0))
     return pl.pallas_call(
-        stencil_kernel,
-        grid=(bands + 1,),
+        functools.partial(stencil_kernel, opening, closing),
+        grid=(count + 1,),
         out_shape=(
             jax.ShapeDtypeStruct((rows, cols), F32), plane, plane, plane,
             jax.ShapeDtypeStruct((TILE, LANES), F32),
         ),
-        in_specs=[band] * 4,
+        in_specs=[band] * 4 + [whole] + ([] if opening else [above] * 4 + [whole] * 4),
         out_specs=(
-            pl.BlockSpec((BAND, cols), lambda i: (jnp.maximum(i - 1, 0), 0)), part, part, part,
+            pl.BlockSpec((BAND, cols), lambda i: (first + jnp.maximum(i - 1, 0), 0)),
+            part, part, part,
             pl.BlockSpec((TILE, LANES), lambda i: (0, 0)),
         ),
-        scratch_shapes=[pad] * (CELL + 3),
+        scratch_shapes=[scratch] * (CELL + 3),
+        input_output_aliases={} if opening else {9 + n: n for n in range(4)},
         compiler_params=params(),
         cost_estimate=pl.CostEstimate(
-            flops=200 * rows * cols, bytes_accessed=64 * rows * cols, transcendentals=0
+            flops=200 * count * BAND * cols, bytes_accessed=64 * count * BAND * cols,
+            transcendentals=0,
         ),
         name="stencil",
-    )(depth, mask, momx, momy)
+    )(*fields, after, *(() if opening else fields), *old)
 
 
 def summed_of(lab, landed):
@@ -750,7 +778,10 @@
         return got.reshape(rows.shape)
 
     press = exchange(top, press)
-    newh, hu, hv, h, token = stencil(depth_field, wet_mask, mom_x, mom_y)
+    fields = (depth_field, wet_mask, mom_x, mom_y)
+    bands = depth_field.shape[0] // BAND
+    ahead = bands * 5 // 8
+    *planes, token = stencil(fields, lab, 0, ahead)
     wind = exchange(token, wind)
     weights = remap_weights.reshape(NW * ABLK, PATCH * PATCH)
     p, *edges = pressure_field(lab, press, weights, (top, bottom, left, right))
@@ -758,6 +789,7 @@
     halos = (
         send(bottom, "gx", 1), send(top, "gx", -1), send(right, "gy", 1), send(left, "gy", -1),
     )
+    newh, hu, hv, h, _ = stencil(fields, top, ahead, bands - ahead, planes)
     newh, sides, ends = border(halos, edges, newh)
     new_x, new_y = finish(lab, wind, weights, p, sides, ends, hu, hv, h)
     return (newh, new_x.reshape(newh.shape), new_y.reshape(newh.shape))

time: 92.4 us -> 90.3 us (0.977)
  waiting for transfers between devices: 4.71 us -> 0.02 us
  Pallas kernels: 51.8 us -> 54.3 us
    ppermute x4, waiting for transfers between devices: 4.7 us -> 0.01 us  [send(): return lax.ppermute(value, axis, pairs)]
    pallas_call x1 -> x2, Pallas kernels: 17.3 us -> 19.8 us  [stencil(): pl.pallas_call(functools.partial(stencil_kernel, opening, closing), grid=...]
  transfers between devices with their start and end apart: 7 -> 7, of which waited for: 2 -> 0; matrix products, arithmetic and copies ran while one was open for 1% -> 1% of each run, Pallas kernels for 40% -> 44%
where the time goes in v9:
time: 90.3 us; the launch traced here: 89.4 us
  Pallas kernels  54.3 us (60%)
  starting transfers between devices  29.9 us (33%)
  local copies, waits for them, and re-layouts  3.72 us (4%)
  between operations  1.47 us (2%)
    pallas_call x2, Pallas kernels, stencil(): pl.pallas_call(functools.partial(stencil_kernel, opening, closing), grid=...  19.8 us
    ppermute x4, starting transfers between devices, send(): return lax.ppermute(value, axis, pairs)  12.3 us
    pallas_call x1, Pallas kernels, finish(): pl.pallas_call(finish_kernel, grid=(steps,), out_shape=(shape, shape), in...  11.8 us
    all_to_all x2, starting transfers between devices, exchange(): got = lax.all_to_all(parts, both, split_axis=0, concat_axis=0, tiled=True)  11.7 us
    pallas_call x1, Pallas kernels, pressure_field(): pl.pallas_call(press_kernel, grid=(steps,), out_shape=tuple((jax.ShapeDty...  7.73 us
    all_to_all x1, starting transfers between devices, body(): lax.all_to_all(want.reshape(devices, 1, capacity), both, split_axis=0, co...  5.99 us
    pallas_call x1, Pallas kernels, edge_cells(): pl.pallas_call(edges_kernel, grid=(1,), out_shape=(line, line, column, co...  4.47 us
    pallas_call x1, Pallas kernels, border(): pl.pallas_call(border_kernel, out_shape=(jax.ShapeDtypeStruct((rows, cols...  4 us
  transfers between devices with their start and end apart: 7, of which 0 were waited for; matrix products, arithmetic and copies ran while one was open for 1% of the time, Pallas kernels for 44%

profile of v9, /device:TPU:12, one launch (start us, length us, event | category | flops | bytes accessed | tf_op | source)
XLA Modules:
  0.0 89.4 jit_solution(6014759245119641367)
XLA Ops:
  0.6 1.7 %requests.1 = (s32[32,32]{1,0:T(8,128)}, s32[32,32]{1,0:T(8,128)}) custom-call(s32[1,512]{1,0:T(1,128)} %bitcast.29, s32[1,512]{1,0:T(1,128)} %bitcast.30, s32[1,512]{1,0:T(1,128)} %bitcast.31, s32[1,512]{1,0:T(1,128)} %bitcast.32), custom_call_target="tpu_custom_call" | custom-call | tf_op jit(solution)/shard_map/requests/pallas_call | solution.py:82
  2.3 6.0 %all-to-all-start = ((s32[32,1,32]{2,1,0:T(1,128)}), s32[32,1,32]{2,1,0:T(1,128)S(1)}, u32[]{:S(2)}, u32[]{:S(2)}) async-start(s32[32,1,32]{2,1,0:T(1,128)} %bitcast.28), calls=%async_computation | async-start | bytes 32768 | tf_op jit(solution)/shard_map/all_to_all | solution.py:767
  9.0 2.0 %mix.1 = (bf16[256,256]{1,0:T(8,128)(2,1)}, bf16[256,512]{1,0:T(8,128)(2,1)}) custom-call(f32[1]{0:T(128)} %bitcast.19.blend_ref, bf16[6,256,256]{2,1,0:T(8,128)(2,1)} %bitcast.27), custom_call_target="tpu_custom_call" | custom-call | tf_op jit(solution)/shard_map/mix/pallas_call | solution.py:108
  11.0 4.5 %edges.1 = (f32[8,512]{1,0:T(8,128)}, f32[8,512]{1,0:T(8,128)}, f32[8,1024]{1,0:T(8,128)}, f32[8,1024]{1,0:T(8,128)}) custom-call(f32[1024,512]{1,0:T(8,128)} %refs_5_.1, s32[1024,512]{1,0:T(8,128)} %refs_6_.1, f32[1024,512]{1,0:T(8,128)} %refs_7_.1, f32[1024,512]{1,0:T(8,128)} %refs_8_.1, f32[1024,512]{1,0:T(8,128)} %refs_5_.1, s32[1024,512]{1,0:T(8,128)} %refs_6_.1, ...), custom_call_target="tpu_custom_call" | custom-call | tf_op jit(solution)/shard_map/edges/pallas_call | solution.py:194
  15.5 0.7 copy-done.2
  16.2 1.3 %serve.2 = bf16[1024,256]{1,0:T(8,128)(2,1)} custom-call(f32[8,512]{1,0:T(8,128)S(1)} %copy-done.2, s32[32,1,32]{2,1,0:T(1,128)S(1)} %all-to-all-done.asked_ref, bf16[256,256]{1,0:T(8,128)(2,1)S(1)} %copy-done.1), custom_call_target="tpu_custom_call" | custom-call | tf_op jit(solution)/shard_map/serve/pallas_call | solution.py:140
  17.5 5.8 %all-to-all-start.1 = ((bf16[32,32,256]{2,1,0:T(8,128)(2,1)}), bf16[32,32,256]{2,1,0:T(8,128)(2,1)S(1)}, u32[]{:S(2)}, u32[]{:S(2)}) async-start(bf16[32,32,256]{2,1,0:T(8,128)(2,1)} %bitcast.8), calls=%async_computation.1 | async-start | bytes 1048576 | tf_op jit(solution)/shard_map/all_to_all | solution.py:777
  23.3 0.7 reshape.64.lab_ref.refs_4_
  24.0 11.8 %stencil.2 = (f32[1024,512]{1,0:T(8,128)}, f32[4,1024,128]{2,1,0:T(8,128)}, f32[4,1024,128]{2,1,0:T(8,128)}, f32[4,1024,128]{2,1,0:T(8,128)}, f32[8,128]{1,0:T(8,128)}) custom-call(f32[1024,512]{1,0:T(8,128)} %refs_5_.1, s32[1024,512]{1,0:T(8,128)} %refs_6_.1, f32[1024,512]{1,0:T(8,128)} %refs_7_.1, f32[1024,512]{1,0:T(8,128)} %refs_8_.1, ...), custom_call_target="tpu_custom_call" | custom-call | flops 65536000 | bytes 20971520 | tf_op jit(solution)/shard_map/stencil/pallas_call | solution.py:399
  35.8 0.7 copy-done.3
  36.5 1.5 %serve.3 = bf16[1024,512]{1,0:T(8,128)(2,1)} custom-call(f32[8,128]{1,0:T(8,128)S(1)} %copy-done.3, s32[32,1,32]{2,1,0:T(1,128)S(1)} %all-to-all-done.asked_ref, bf16[256,512]{1,0:T(8,128)(2,1)S(1)} %copy-done), custom_call_target="tpu_custom_call" | custom-call | tf_op jit(solution)/shard_map/serve/pallas_call | solution.py:140
  38.0 5.8 %all-to-all-start.2 = ((bf16[32,32,512]{2,1,0:T(8,128)(2,1)}), bf16[32,32,512]{2,1,0:T(8,128)(2,1)S(1)}, u32[]{:S(2)}, u32[]{:S(2)}) async-start(bf16[32,32,512]{2,1,0:T(8,128)(2,1)} %bitcast.11), calls=%async_computation.2 | async-start | bytes 2097152 | tf_op jit(solution)/shard_map/all_to_all | solution.py:777
  43.9 7.7 %pressure.1 = (f32[4,1040,128]{2,1,0:T(8,128)}, f32[8,512]{1,0:T(8,128)}, f32[8,512]{1,0:T(8,128)}, f32[8,1024]{1,0:T(8,128)}, f32[8,1024]{1,0:T(8,128)}) custom-call(s32[1,1024]{1,0:T(1,128)} %reshape.64.lab_ref.refs_4_, bf16[1024,256]{1,0:T(8,128)(2,1)} %bitcast.26, bf16[1024,4096]{1,0:T(8,128)(2,1)} %bitcast.20, ...), custom_call_target="tpu_custom_call" | custom-call | flops 1073741824 | bytes 12582912 | tf_op jit(solution)/shard_map/pressure/pallas_call | solution.py:512
  51.6 2.1 %collective-permute-start.2 = (f32[8,1024]{1,0:T(8,128)}, f32[8,1024]{1,0:T(8,128)S(1)}, u32[]{:S(2)}, u32[]{:S(2)}) collective-permute-start(f32[8,1024]{1,0:T(8,128)} %get-tuple-element.39.right_ref), channel_id=1, source_target_pairs={{0,1},{1,2},{2,3},{3,4},{4,5},{5,6},{6,7},{8,9},{9,10},{10,11},{11... | collective-permute-start | bytes 98312 | tf_op jit(solution)/shard_map/ppermute | solution.py:216
  53.7 4.4 %collective-permute-start.3 = (f32[8,1024]{1,0:T(8,128)}, f32[8,1024]{1,0:T(8,128)S(1)}, u32[]{:S(2)}, u32[]{:S(2)}) collective-permute-start(f32[8,1024]{1,0:T(8,128)} %get-tuple-element.40.left_ref), channel_id=1, source_target_pairs={{1,0},{2,1},{3,2},{4,3},{5,4},{6,5},{7,6},{9,8},{10,9},{11,10},{12... | collective-permute-start | bytes 98312 | tf_op jit(solution)/shard_map/ppermute | solution.py:216
  58.1 2.5 %collective-permute-start.1 = (f32[8,512]{1,0:T(8,128)}, f32[8,512]{1,0:T(8,128)S(1)}, u32[]{:S(2)}, u32[]{:S(2)}) collective-permute-start(f32[8,512]{1,0:T(8,128)} %get-tuple-element.38.refs_4_.top_ref), channel_id=1, source_target_pairs={{8,0},{16,8},{24,16},{9,1},{17,9},{25,17},{10,2},{18,10},{26,18},{... | collective-permute-start | bytes 49160 | tf_op jit(solution)/shard_map/ppermute | solution.py:216
  60.6 3.4 %collective-permute-start = (f32[8,512]{1,0:T(8,128)}, f32[8,512]{1,0:T(8,128)S(1)}, u32[]{:S(2)}, u32[]{:S(2)}) collective-permute-start(f32[8,512]{1,0:T(8,128)} %get-tuple-element.37.bottom_ref), channel_id=1, source_target_pairs={{0,8},{8,16},{16,24},{1,9},{9,17},{17,25},{2,10},{10,18},{18,26},{... | collective-permute-start | bytes 49160 | tf_op jit(solution)/shard_map/ppermute | solution.py:216
  63.9 8.0 %stencil.3 = (f32[1024,512]{1,0:T(8,128)}, f32[4,1024,128]{2,1,0:T(8,128)}, f32[4,1024,128]{2,1,0:T(8,128)}, f32[4,1024,128]{2,1,0:T(8,128)}, f32[8,128]{1,0:T(8,128)}) custom-call(f32[1024,512]{1,0:T(8,128)} %refs_5_.1, s32[1024,512]{1,0:T(8,128)} %refs_6_.1, ...), custom_call_target="tpu_custom_call", output_to_operand_aliasing={{0}: (9, {}), {1}: (10, {}), {2}: (11, {}), {3}: (12, {})} | custom-call | flops 39321600 | bytes 12582912 | tf_op jit(solution)/shard_map/stencil/pallas_call | solution.py:399
  72.0 0.5 copy-done.8
  72.5 0.0 copy-done.6
  72.6 0.0 copy-done.7
  72.6 4.0 %border.1 = (f32[1024,512]{1,0:T(8,128)}, f32[1024,128]{1,0:T(8,128)}, f32[8,512]{1,0:T(8,128)}) custom-call(f32[8,512]{1,0:T(8,128)} %copy-done.9, f32[8,512]{1,0:T(8,128)} %copy-done.8, f32[8,1024]{1,0:T(8,128)} %copy-done.6, f32[8,1024]{1,0:T(8,128)} %copy-done.7, f32[8,512]{1,0:T(8,128)} %get-tuple-element.38.refs_4_.top_ref, ...), custom_call_target="tpu_custom_call", output_to_operand_aliasing={{0}: (8, {})} | custom-call | tf_op jit(solution)/shard_map/border/pallas_call | solution.py:610
  76.6 1.0 %copy-done.4 = bf16[32,32,512]{2,1,0:T(8,128)(2,1)} copy-done((bf16[32,32,512]{2,1,0:T(8,128)(2,1)}, bf16[32,32,512]{2,1,0:T(8,128)(2,1)S(1)}, u32[]{:S(2)}) %copy-start.4) | copy-done | bytes 1048600
  77.7 11.8 %finish.1 = (f32[16,64,512]{2,1,0:T(8,128)}, f32[16,64,512]{2,1,0:T(8,128)}) custom-call(s32[1,1024]{1,0:T(1,128)} %reshape.64.lab_ref.refs_4_, bf16[1024,512]{1,0:T(8,128)(2,1)} %bitcast.25, bf16[1024,4096]{1,0:T(8,128)(2,1)} %bitcast.21, f32[4,1040,128]{2,1,0:T(8,128)} %get-tuple-element.49.p_ref, f32[1024,128]{1,0:T(8,128)} %get-tuple-element.50.sides_ref, ...), custom_call_target="tpu_custom_call" | custom-call | flops 2147483648 | bytes 20971520 | tf_op jit(solution)/shard_map/finish/pallas_call | solution.py:714
  (23 shorter events, 0.1 us)
Async XLA Ops:
  2.3 13.1 %all-to-all-start = ((s32[32,1,32]{2,1,0:T(1,128)}), s32[32,1,32]{2,1,0:T(1,128)S(1)}, u32[]{:S(2)}, u32[]{:S(2)}) async-start(s32[32,1,32]{2,1,0:T(1,128)} %bitcast.28), calls=%async_computation | async-start | bytes 32768 | tf_op jit(solution)/shard_map/all_to_all | solution.py:767
  11.0 4.5 %copy-start.1 = (bf16[256,256]{1,0:T(8,128)(2,1)S(1)}, bf16[256,256]{1,0:T(8,128)(2,1)}, u32[]{:S(2)}) copy-start(bf16[256,256]{1,0:T(8,128)(2,1)} %get-tuple-element.33.tiles_ref) | copy-start | bytes 393220
  11.0 12.4 %copy-start.10 = (s32[32,32]{1,0:T(8,128)S(1)}, s32[32,32]{1,0:T(8,128)}, u32[]{:S(2)}) copy-start(s32[32,32]{1,0:T(8,128)} %get-tuple-element.30) | copy-start | bytes 12292
  15.5 0.7 copy-start.2
  17.5 20.5 %all-to-all-start.1 = ((bf16[32,32,256]{2,1,0:T(8,128)(2,1)}), bf16[32,32,256]{2,1,0:T(8,128)(2,1)S(1)}, u32[]{:S(2)}, u32[]{:S(2)}) async-start(bf16[32,32,256]{2,1,0:T(8,128)(2,1)} %bitcast.8), calls=%async_computation.1 | async-start | bytes 1048576 | tf_op jit(solution)/shard_map/all_to_all | solution.py:777
  24.0 11.8 %copy-start = (bf16[256,512]{1,0:T(8,128)(2,1)S(1)}, bf16[256,512]{1,0:T(8,128)(2,1)}, u32[]{:S(2)}) copy-start(bf16[256,512]{1,0:T(8,128)(2,1)} %get-tuple-element.48.tiles_ref) | copy-start | bytes 786436
  35.8 0.7 copy-start.3
  38.0 5.8 %copy-start.5 = (bf16[32,32,256]{2,1,0:T(8,128)(2,1)}, bf16[32,32,256]{2,1,0:T(8,128)(2,1)S(1)}, u32[]{:S(2)}) copy-start(bf16[32,32,256]{2,1,0:T(8,128)(2,1)S(1)} %all-to-all-done.1) | copy-start | bytes 1572868
  38.0 38.6 %all-to-all-start.2 = ((bf16[32,32,512]{2,1,0:T(8,128)(2,1)}), bf16[32,32,512]{2,1,0:T(8,128)(2,1)S(1)}, u32[]{:S(2)}, u32[]{:S(2)}) async-start(bf16[32,32,512]{2,1,0:T(8,128)(2,1)} %bitcast.11), calls=%async_computation.2 | async-start | bytes 2097152 | tf_op jit(solution)/shard_map/all_to_all | solution.py:777
  51.6 20.4 %collective-permute-start.2 = (f32[8,1024]{1,0:T(8,128)}, f32[8,1024]{1,0:T(8,128)S(1)}, u32[]{:S(2)}, u32[]{:S(2)}) collective-permute-start(f32[8,1024]{1,0:T(8,128)} %get-tuple-element.39.right_ref), channel_id=1, source_target_pairs={{0,1},{1,2},{2,3},{3,4},{4,5},{5,6},{6,7},{8,9},{9,10},{10,11},{11... | collective-permute-start | bytes 98312 | tf_op jit(solution)/shard_map/ppermute | solution.py:216
  53.7 18.3 %collective-permute-start.3 = (f32[8,1024]{1,0:T(8,128)}, f32[8,1024]{1,0:T(8,128)S(1)}, u32[]{:S(2)}, u32[]{:S(2)}) collective-permute-start(f32[8,1024]{1,0:T(8,128)} %get-tuple-element.40.left_ref), channel_id=1, source_target_pairs={{1,0},{2,1},{3,2},{4,3},{5,4},{6,5},{7,6},{9,8},{10,9},{11,10},{12... | collective-permute-start | bytes 98312 | tf_op jit(solution)/shard_map/ppermute | solution.py:216
  58.1 13.9 %collective-permute-start.1 = (f32[8,512]{1,0:T(8,128)}, f32[8,512]{1,0:T(8,128)S(1)}, u32[]{:S(2)}, u32[]{:S(2)}) collective-permute-start(f32[8,512]{1,0:T(8,128)} %get-tuple-element.38.refs_4_.top_ref), channel_id=1, source_target_pairs={{8,0},{16,8},{24,16},{9,1},{17,9},{25,17},{10,2},{18,10},{26,18},{... | collective-permute-start | bytes 49160 | tf_op jit(solution)/shard_map/ppermute | solution.py:216
  60.6 11.4 %collective-permute-start = (f32[8,512]{1,0:T(8,128)}, f32[8,512]{1,0:T(8,128)S(1)}, u32[]{:S(2)}, u32[]{:S(2)}) collective-permute-start(f32[8,512]{1,0:T(8,128)} %get-tuple-element.37.bottom_ref), channel_id=1, source_target_pairs={{0,8},{8,16},{16,24},{1,9},{9,17},{17,25},{2,10},{10,18},{18,26},{... | collective-permute-start | bytes 49160 | tf_op jit(solution)/shard_map/ppermute | solution.py:216
  71.9 0.6 copy-start.8
  71.9 0.6 copy-start.9
  72.0 0.6 copy-start.6
  72.0 0.6 copy-start.7
  76.6 1.0 %copy-start.4 = (bf16[32,32,512]{2,1,0:T(8,128)(2,1)}, bf16[32,32,512]{2,1,0:T(8,128)(2,1)S(1)}, u32[]{:S(2)}) copy-start(bf16[32,32,512]{2,1,0:T(8,128)(2,1)S(1)} %all-to-all-done.2) | copy-start | bytes 3145732

commit v10 on v9

--- a/solution.py
+++ b/solution.py
@@ -146,7 +146,7 @@
             pltpu.VMEM((width, width), jnp.int32),
             pltpu.VMEM((slots, tiles.shape[0]), F32),
         ],
-        compiler_params=params(32 << 20),
+        compiler_params=params(56 << 20),
         name="serve",
     )(after, asked, tiles)
 
@@ -336,7 +336,7 @@
                     dst[g, pl.ds(base, TILE), :] = val
             return carry
 
-        lax.fori_loop(0, BAND // TILE, across, 0, unroll=8)
+        lax.fori_loop(0, BAND // TILE, across, 0, unroll=16)
 
         if closing:
             @pl.when(step == bands)
@@ -382,7 +382,7 @@
                 h_ref[g, at, :] = h
             return carry
 
-        lax.fori_loop(0, BAND // TILE, body, 0, unroll=8)
+        lax.fori_loop(0, BAND // TILE, body, 0, unroll=16)
 
 
 def stencil(fields, after, first, count, old=()):
@@ -436,6 +436,21 @@
 PART = TILE * PATCH
 
 
+def weight_parts(step, w_ref, held, arrived):
+    width = held.shape[2]
+
+    def copy(n):
+        at = pl.ds(pl.multiple_of(n * width, width), width)
+        return pltpu.make_async_copy(w_ref.at[:, at], held.at[n], arrived.at[n])
+
+    @pl.when(step == 0)
+    def _():
+        for n in range(held.shape[0]):
+            copy(n).start()
+
+    return copy(step).wait
+
+
 def spread_rows(acc, field, k):
     low = iota((TILE, LANES), 1) < LANES // 2
     for t in range(TILE // 2):
@@ -454,17 +469,22 @@
 
 def press_kernel(
     lab_ref, landed_ref, w_ref, top0_ref, bottom0_ref, left0_ref, right0_ref,
-    out_ref, top_ref, bottom_ref, left_ref, right_ref,
-    left, acc, acc2, field, field2,
+    out_ref, top_ref, bottom_ref, left_ref, right_ref, row_ref,
+    held, arrived, left, acc, acc2, field, field2,
 ):
     step = pl.program_id(0)
+    take = weight_parts(step, w_ref, held, arrived)
 
     @pl.when(step == 0)
     def _():
-        stack_left(left, summed_of(lab_ref[...], landed_ref[...]), 1)
-
-    acc[...] = jnp.dot(left[...], w_ref[:, :PART], preferred_element_type=F32)
-    acc2[...] = jnp.dot(left[...], w_ref[:, PART:], preferred_element_type=F32)
+        peers, capacity = lab_ref.shape
+        for d in range(peers):
+            row_ref[:, d * capacity:(d + 1) * capacity] = lab_ref[d:d + 1, :]
+        stack_left(left, summed_of(row_ref[...], landed_ref[...]), 1)
+
+    take()
+    acc[...] = jnp.dot(left[...], held[step, :, :PART], preferred_element_type=F32)
+    acc2[...] = jnp.dot(left[...], held[step, :, PART:], preferred_element_type=F32)
     for part, (src, mid) in enumerate(((acc, field), (acc2, field2))):
         spread_rows(src, mid, 0)
         for g in range(GROUPS):
@@ -512,14 +532,17 @@
     return pl.pallas_call(
         press_kernel,
         grid=(steps,),
-        out_shape=tuple(jax.ShapeDtypeStruct(x, F32) for x in (whole, line, line, column, column)),
+        out_shape=tuple(jax.ShapeDtypeStruct(x, F32) for x in (whole, line, line, column, column))
+        + (jax.ShapeDtypeStruct((1, lab.size), jnp.int32),),
         in_specs=[
             const(lab.shape),
             const(landed.shape),
-            pl.BlockSpec((NW * ABLK, 2 * PART), lambda i: (0, i)),
+            pl.BlockSpec(memory_space=pl.ANY),
         ] + [const(x) for x in (line, line, column, column)],
-        out_specs=tuple(const(x) for x in (whole, line, line, column, column)),
+        out_specs=tuple(const(x) for x in (whole, line, line, column, column, (1, lab.size))),
         scratch_shapes=[
+            pltpu.VMEM((steps, NW * ABLK, 2 * PART), BF16),
+            pltpu.SemaphoreType.DMA((steps,)),
             pltpu.VMEM((NPATCH, NW * ABLK), BF16),
             pltpu.VMEM((NPATCH, PART), F32),
             pltpu.VMEM((NPATCH, PART), F32),
@@ -634,16 +657,19 @@
 def finish_kernel(
     lab_ref, landed_ref, w_ref, p_ref, sides_ref, ends_ref,
     hu_ref, hv_ref, h_ref, ox_ref, oy_ref,
-    left, acc, acc2, fx, fy, fx2, fy2,
+    held, arrived, left, acc, acc2, fx, fy, fx2, fy2,
 ):
     step = pl.program_id(0)
+
+    take = weight_parts(step, w_ref, held, arrived)
 
     @pl.when(step == 0)
     def _():
         stack_left(left, summed_of(lab_ref[...], landed_ref[...]), 2)
 
-    acc[...] = jnp.dot(left[...], w_ref[:, :PART], preferred_element_type=F32)
-    acc2[...] = jnp.dot(left[...], w_ref[:, PART:], preferred_element_type=F32)
+    take()
+    acc[...] = jnp.dot(left[...], held[step, :, :PART], preferred_element_type=F32)
+    acc2[...] = jnp.dot(left[...], held[step, :, PART:], preferred_element_type=F32)
     lane = iota((TILE, LANES), 1)
     for part, (src, mx, my) in enumerate(((acc, fx, fy), (acc2, fx2, fy2))):
         spread_rows(src, mx, 0)
@@ -717,12 +743,14 @@
         out_shape=(shape, shape),
         in_specs=[
             const(lab), const(landed),
-            pl.BlockSpec((NW * ABLK, 2 * PART), lambda i: (0, i)),
+            pl.BlockSpec(memory_space=pl.ANY),
             const(p), const(sides), const(ends),
             slab, slab, slab,
         ],
         out_specs=(out, out),
         scratch_shapes=[
+            pltpu.VMEM((steps, NW * ABLK, 2 * PART), BF16),
+            pltpu.SemaphoreType.DMA((steps,)),
             pltpu.VMEM((2 * NPATCH, NW * ABLK), BF16),
             pltpu.VMEM((2 * NPATCH, PART), F32),
             pltpu.VMEM((2 * NPATCH, PART), F32),
@@ -767,7 +795,6 @@
     asked = lax.all_to_all(
         want.reshape(devices, 1, capacity), both, split_axis=0, concat_axis=0, tiled=True
     )
-    lab = lab.reshape(1, slots)
     press, wind = mix(blend.reshape(1), atm)
     top, bottom, left, right = edge_cells(depth_field, wet_mask, mom_x, mom_y)
 
@@ -784,7 +811,7 @@
     *planes, token = stencil(fields, lab, 0, ahead)
     wind = exchange(token, wind)
     weights = remap_weights.reshape(NW * ABLK, PATCH * PATCH)
-    p, *edges = pressure_field(lab, press, weights, (top, bottom, left, right))
+    p, *edges, lab = pressure_field(lab, press, weights, (top, bottom, left, right))
     top, bottom, left, right = edges
     halos = (
         send(bottom, "gx", 1), send(top, "gx", -1), send(right, "gy", 1), send(left, "gy", -1),

time: 90.3 us -> 109 us (1.21)
  Pallas kernels: 54.3 us -> 74.4 us
  local copies, waits for them, and re-layouts: 3.72 us -> 2.28 us
    pallas_call x2, Pallas kernels: 19.8 us -> 38.9 us  [stencil(): pl.pallas_call(functools.partial(stencil_kernel, opening, closing), grid=...]
    pallas_call x2, Pallas kernels: 2.86 us -> 4.75 us  [serve(): pl.pallas_call(serve_kernel, out_shape=jax.ShapeDtypeStruct((slots, tiles...]
    unnamed x22 -> x14, local copies, waits for them, and re-layouts: 3.05 us -> 2.28 us
  transfers between devices with their start and end apart: 7 -> 7, of which waited for: 0 -> 0; matrix products, arithmetic and copies ran while one was open for 1% -> 0% of each run, Pallas kernels for 44% -> 55%
where the time goes in v10:
time: 109 us; the launch traced here: 108 us
  Pallas kernels  74.4 us (68%)
  starting transfers between devices  30 us (28%)
  local copies, waits for them, and re-layouts  2.28 us (2%)
  between operations  1.45 us (1%)
    pallas_call x2, Pallas kernels, stencil(): pl.pallas_call(functools.partial(stencil_kernel, opening, closing), grid=...  38.9 us
    ppermute x4, starting transfers between devices, send(): return lax.ppermute(value, axis, pairs)  12.3 us
    all_to_all x2, starting transfers between devices, exchange(): got = lax.all_to_all(parts, both, split_axis=0, concat_axis=0, tiled=True)  11.7 us
    pallas_call x1, Pallas kernels, finish(): pl.pallas_call(finish_kernel, grid=(steps,), out_shape=(shape, shape), in...  11.4 us
    pallas_call x1, Pallas kernels, pressure_field(): pl.pallas_call(press_kernel, grid=(steps,), out_shape=tuple((jax.ShapeDty...  7.13 us
    all_to_all x1, starting transfers between devices, body(): lax.all_to_all(want.reshape(devices, 1, capacity), both, split_axis=0, co...  5.99 us
    pallas_call x2, Pallas kernels, serve(): pl.pallas_call(serve_kernel, out_shape=jax.ShapeDtypeStruct((slots, tiles...  4.75 us
    pallas_call x1, Pallas kernels, edge_cells(): pl.pallas_call(edges_kernel, grid=(1,), out_shape=(line, line, column, co...  4.45 us
  transfers between devices with their start and end apart: 7, of which 0 were waited for; matrix products, arithmetic and copies ran while one was open for 0% of the time, Pallas kernels for 55%

profile of v10, /device:TPU:12, one launch (start us, length us, event | category | flops | bytes accessed | tf_op | source)
XLA Modules:
  0.0 108.1 jit_solution(13922079608470861917)
XLA Ops:
  0.6 1.7 %requests.1 = (s32[32,32]{1,0:T(8,128)}, s32[32,32]{1,0:T(8,128)}) custom-call(s32[1,512]{1,0:T(1,128)} %bitcast.31, s32[1,512]{1,0:T(1,128)} %bitcast.32, s32[1,512]{1,0:T(1,128)} %bitcast.33, s32[1,512]{1,0:T(1,128)} %bitcast.34), custom_call_target="tpu_custom_call" | custom-call | tf_op jit(solution)/shard_map/requests/pallas_call | solution.py:82
  2.3 6.0 %all-to-all-start = ((s32[32,1,32]{2,1,0:T(1,128)}), s32[32,1,32]{2,1,0:T(1,128)S(1)}, u32[]{:S(2)}, u32[]{:S(2)}) async-start(s32[32,1,32]{2,1,0:T(1,128)} %bitcast.30), calls=%async_computation | async-start | bytes 32768 | tf_op jit(solution)/shard_map/all_to_all | solution.py:795
  9.0 2.0 %mix.1 = (bf16[256,256]{1,0:T(8,128)(2,1)}, bf16[256,512]{1,0:T(8,128)(2,1)}) custom-call(f32[1]{0:T(128)} %bitcast.19.blend_ref, bf16[6,256,256]{2,1,0:T(8,128)(2,1)} %bitcast.29), custom_call_target="tpu_custom_call" | custom-call | tf_op jit(solution)/shard_map/mix/pallas_call | solution.py:108
  11.0 4.4 %edges.1 = (f32[8,512]{1,0:T(8,128)}, f32[8,512]{1,0:T(8,128)}, f32[8,1024]{1,0:T(8,128)}, f32[8,1024]{1,0:T(8,128)}) custom-call(f32[1024,512]{1,0:T(8,128)} %refs_5_.1, s32[1024,512]{1,0:T(8,128)} %refs_6_.1, f32[1024,512]{1,0:T(8,128)} %refs_7_.1, f32[1024,512]{1,0:T(8,128)} %refs_8_.1, f32[1024,512]{1,0:T(8,128)} %refs_5_.1, s32[1024,512]{1,0:T(8,128)} %refs_6_.1, ...), custom_call_target="tpu_custom_call" | custom-call | tf_op jit(solution)/shard_map/edges/pallas_call | solution.py:194
  15.4 0.6 copy-done.2
  16.0 2.2 %serve.2 = bf16[1024,256]{1,0:T(8,128)(2,1)} custom-call(f32[8,512]{1,0:T(8,128)} %get-tuple-element.32.after_ref.top0_ref, s32[32,1,32]{2,1,0:T(1,128)} %copy-done.2, bf16[256,256]{1,0:T(8,128)(2,1)} %get-tuple-element.34.tiles_ref), custom_call_target="tpu_custom_call" | custom-call | tf_op jit(solution)/shard_map/serve/pallas_call | solution.py:140
  18.3 5.8 %all-to-all-start.1 = ((bf16[32,32,256]{2,1,0:T(8,128)(2,1)}), bf16[32,32,256]{2,1,0:T(8,128)(2,1)S(1)}, u32[]{:S(2)}, u32[]{:S(2)}) async-start(bf16[32,32,256]{2,1,0:T(8,128)(2,1)} %bitcast.28), calls=%async_computation.1 | async-start | bytes 1048576 | tf_op jit(solution)/shard_map/all_to_all | solution.py:804
  24.1 23.2 %stencil.2 = (f32[1024,512]{1,0:T(8,128)}, f32[4,1024,128]{2,1,0:T(8,128)}, f32[4,1024,128]{2,1,0:T(8,128)}, f32[4,1024,128]{2,1,0:T(8,128)}, f32[8,128]{1,0:T(8,128)}) custom-call(f32[1024,512]{1,0:T(8,128)} %refs_5_.1, s32[1024,512]{1,0:T(8,128)} %refs_6_.1, f32[1024,512]{1,0:T(8,128)} %refs_7_.1, f32[1024,512]{1,0:T(8,128)} %refs_8_.1, ...), custom_call_target="tpu_custom_call" | custom-call | flops 65536000 | bytes 20971520 | tf_op jit(solution)/shard_map/stencil/pallas_call | solution.py:399
  47.3 2.5 %serve.3 = bf16[1024,512]{1,0:T(8,128)(2,1)} custom-call(f32[8,128]{1,0:T(8,128)} %get-tuple-element.49.after_ref, s32[32,1,32]{2,1,0:T(1,128)} %copy-done.2, bf16[256,512]{1,0:T(8,128)(2,1)} %get-tuple-element.50.tiles_ref), custom_call_target="tpu_custom_call" | custom-call | tf_op jit(solution)/shard_map/serve/pallas_call | solution.py:140
  49.8 5.8 %all-to-all-start.2 = ((bf16[32,32,512]{2,1,0:T(8,128)(2,1)}), bf16[32,32,512]{2,1,0:T(8,128)(2,1)S(1)}, u32[]{:S(2)}, u32[]{:S(2)}) async-start(bf16[32,32,512]{2,1,0:T(8,128)(2,1)} %bitcast.26), calls=%async_computation.2 | async-start | bytes 2097152 | tf_op jit(solution)/shard_map/all_to_all | solution.py:804
  55.7 7.1 %pressure.1 = (f32[4,1040,128]{2,1,0:T(8,128)}, f32[8,512]{1,0:T(8,128)}, f32[8,512]{1,0:T(8,128)}, f32[8,1024]{1,0:T(8,128)}, f32[8,1024]{1,0:T(8,128)}, /*index=5*/s32[1,1024]{1,0:T(1,128)}) custom-call(s32[32,32]{1,0:T(8,128)} %get-tuple-element.31.lab_ref.refs_4_, bf16[1024,256]{1,0:T(8,128)(2,1)} %bitcast.27, bf16[1024,4096]{1,0:T(8,128)(2,1)} %bitcast.20, ...), custom_call_target="tpu_custom_call" | custom-call | flops 1073741824 | bytes 12582912 | tf_op jit(solution)/shard_map/pressure/pallas_call | solution.py:532
  62.8 2.1 %collective-permute-start.2 = (f32[8,1024]{1,0:T(8,128)}, f32[8,1024]{1,0:T(8,128)S(1)}, u32[]{:S(2)}, u32[]{:S(2)}) collective-permute-start(f32[8,1024]{1,0:T(8,128)} %get-tuple-element.40.right_ref), channel_id=1, source_target_pairs={{0,1},{1,2},{2,3},{3,4},{4,5},{5,6},{6,7},{8,9},{9,10},{10,11},{11... | collective-permute-start | bytes 98312 | tf_op jit(solution)/shard_map/ppermute | solution.py:216
  64.9 4.4 %collective-permute-start.3 = (f32[8,1024]{1,0:T(8,128)}, f32[8,1024]{1,0:T(8,128)S(1)}, u32[]{:S(2)}, u32[]{:S(2)}) collective-permute-start(f32[8,1024]{1,0:T(8,128)} %get-tuple-element.41.left_ref), channel_id=1, source_target_pairs={{1,0},{2,1},{3,2},{4,3},{5,4},{6,5},{7,6},{9,8},{10,9},{11,10},{12... | collective-permute-start | bytes 98312 | tf_op jit(solution)/shard_map/ppermute | solution.py:216
  69.3 2.5 %collective-permute-start.1 = (f32[8,512]{1,0:T(8,128)}, f32[8,512]{1,0:T(8,128)S(1)}, u32[]{:S(2)}, u32[]{:S(2)}) collective-permute-start(f32[8,512]{1,0:T(8,128)} %get-tuple-element.39.refs_4_.top_ref), channel_id=1, source_target_pairs={{8,0},{16,8},{24,16},{9,1},{17,9},{25,17},{10,2},{18,10},{26,18},{... | collective-permute-start | bytes 49160 | tf_op jit(solution)/shard_map/ppermute | solution.py:216
  71.8 3.4 %collective-permute-start = (f32[8,512]{1,0:T(8,128)}, f32[8,512]{1,0:T(8,128)S(1)}, u32[]{:S(2)}, u32[]{:S(2)}) collective-permute-start(f32[8,512]{1,0:T(8,128)} %get-tuple-element.38.bottom_ref), channel_id=1, source_target_pairs={{0,8},{8,16},{16,24},{1,9},{9,17},{17,25},{2,10},{10,18},{18,26},{... | collective-permute-start | bytes 49160 | tf_op jit(solution)/shard_map/ppermute | solution.py:216
  75.1 15.7 %stencil.3 = (f32[1024,512]{1,0:T(8,128)}, f32[4,1024,128]{2,1,0:T(8,128)}, f32[4,1024,128]{2,1,0:T(8,128)}, f32[4,1024,128]{2,1,0:T(8,128)}, f32[8,128]{1,0:T(8,128)}) custom-call(f32[1024,512]{1,0:T(8,128)} %refs_5_.1, s32[1024,512]{1,0:T(8,128)} %refs_6_.1, ...), custom_call_target="tpu_custom_call", output_to_operand_aliasing={{0}: (9, {}), {1}: (10, {}), {2}: (11, {}), {3}: (12, {})} | custom-call | flops 39321600 | bytes 12582912 | tf_op jit(solution)/shard_map/stencil/pallas_call | solution.py:399
  90.9 0.0 copy-start.3
  90.9 0.5 copy-done.5
  91.5 0.0 copy-done.6
  91.5 0.0 copy-done.3
  91.5 0.0 copy-done.4
  91.5 4.0 %border.1 = (f32[1024,512]{1,0:T(8,128)}, f32[1024,128]{1,0:T(8,128)}, f32[8,512]{1,0:T(8,128)}) custom-call(f32[8,512]{1,0:T(8,128)} %copy-done.6, f32[8,512]{1,0:T(8,128)} %copy-done.5, f32[8,1024]{1,0:T(8,128)} %copy-done.3, f32[8,1024]{1,0:T(8,128)} %copy-done.4, f32[8,512]{1,0:T(8,128)} %get-tuple-element.39.refs_4_.top_ref, ...), custom_call_target="tpu_custom_call", output_to_operand_aliasing={{0}: (8, {})} | custom-call | tf_op jit(solution)/shard_map/border/pallas_call | solution.py:633
  95.6 1.1 copy-done
  96.6 11.4 %finish.1 = (f32[16,64,512]{2,1,0:T(8,128)}, f32[16,64,512]{2,1,0:T(8,128)}) custom-call(s32[1,1024]{1,0:T(1,128)} %get-tuple-element.48.lab_ref, bf16[1024,512]{1,0:T(8,128)(2,1)} %bitcast.25, bf16[1024,4096]{1,0:T(8,128)(2,1)} %bitcast.21, f32[4,1040,128]{2,1,0:T(8,128)} %get-tuple-element.51.p_ref, f32[1024,128]{1,0:T(8,128)} %get-tuple-element.52.sides_ref, ...), custom_call_target="tpu_custom_call" | custom-call | flops 2147483648 | bytes 20971520 | tf_op jit(solution)/shard_map/finish/pallas_call | solution.py:740
  (14 shorter events, 0.0 us)
Async XLA Ops:
  2.3 13.1 %all-to-all-start = ((s32[32,1,32]{2,1,0:T(1,128)}), s32[32,1,32]{2,1,0:T(1,128)S(1)}, u32[]{:S(2)}, u32[]{:S(2)}) async-start(s32[32,1,32]{2,1,0:T(1,128)} %bitcast.30), calls=%async_computation | async-start | bytes 32768 | tf_op jit(solution)/shard_map/all_to_all | solution.py:795
  15.4 0.6 copy-start.2
  18.3 31.6 %all-to-all-start.1 = ((bf16[32,32,256]{2,1,0:T(8,128)(2,1)}), bf16[32,32,256]{2,1,0:T(8,128)(2,1)S(1)}, u32[]{:S(2)}, u32[]{:S(2)}) async-start(bf16[32,32,256]{2,1,0:T(8,128)(2,1)} %bitcast.28), calls=%async_computation.1 | async-start | bytes 1048576 | tf_op jit(solution)/shard_map/all_to_all | solution.py:804
  49.8 5.8 %copy-start.1 = (bf16[32,32,256]{2,1,0:T(8,128)(2,1)}, bf16[32,32,256]{2,1,0:T(8,128)(2,1)S(1)}, u32[]{:S(2)}) copy-start(bf16[32,32,256]{2,1,0:T(8,128)(2,1)S(1)} %all-to-all-done.1) | copy-start | bytes 1572868
  49.8 45.7 %all-to-all-start.2 = ((bf16[32,32,512]{2,1,0:T(8,128)(2,1)}), bf16[32,32,512]{2,1,0:T(8,128)(2,1)S(1)}, u32[]{:S(2)}, u32[]{:S(2)}) async-start(bf16[32,32,512]{2,1,0:T(8,128)(2,1)} %bitcast.26), calls=%async_computation.2 | async-start | bytes 2097152 | tf_op jit(solution)/shard_map/all_to_all | solution.py:804
  62.8 28.1 %collective-permute-start.2 = (f32[8,1024]{1,0:T(8,128)}, f32[8,1024]{1,0:T(8,128)S(1)}, u32[]{:S(2)}, u32[]{:S(2)}) collective-permute-start(f32[8,1024]{1,0:T(8,128)} %get-tuple-element.40.right_ref), channel_id=1, source_target_pairs={{0,1},{1,2},{2,3},{3,4},{4,5},{5,6},{6,7},{8,9},{9,10},{10,11},{11... | collective-permute-start | bytes 98312 | tf_op jit(solution)/shard_map/ppermute | solution.py:216
  64.9 26.1 %collective-permute-start.3 = (f32[8,1024]{1,0:T(8,128)}, f32[8,1024]{1,0:T(8,128)S(1)}, u32[]{:S(2)}, u32[]{:S(2)}) collective-permute-start(f32[8,1024]{1,0:T(8,128)} %get-tuple-element.41.left_ref), channel_id=1, source_target_pairs={{1,0},{2,1},{3,2},{4,3},{5,4},{6,5},{7,6},{9,8},{10,9},{11,10},{12... | collective-permute-start | bytes 98312 | tf_op jit(solution)/shard_map/ppermute | solution.py:216
  69.3 21.6 %collective-permute-start.1 = (f32[8,512]{1,0:T(8,128)}, f32[8,512]{1,0:T(8,128)S(1)}, u32[]{:S(2)}, u32[]{:S(2)}) collective-permute-start(f32[8,512]{1,0:T(8,128)} %get-tuple-element.39.refs_4_.top_ref), channel_id=1, source_target_pairs={{8,0},{16,8},{24,16},{9,1},{17,9},{25,17},{10,2},{18,10},{26,18},{... | collective-permute-start | bytes 49160 | tf_op jit(solution)/shard_map/ppermute | solution.py:216
  71.8 19.1 %collective-permute-start = (f32[8,512]{1,0:T(8,128)}, f32[8,512]{1,0:T(8,128)S(1)}, u32[]{:S(2)}, u32[]{:S(2)}) collective-permute-start(f32[8,512]{1,0:T(8,128)} %get-tuple-element.38.bottom_ref), channel_id=1, source_target_pairs={{0,8},{8,16},{16,24},{1,9},{9,17},{17,25},{2,10},{10,18},{18,26},{... | collective-permute-start | bytes 49160 | tf_op jit(solution)/shard_map/ppermute | solution.py:216
  90.9 0.6 copy-start.5
  90.9 0.6 copy-start.6
  90.9 0.6 copy-start.3
  90.9 0.6 copy-start.4
  95.6 1.1 copy-start

commit v11 on v10

--- a/solution.py
+++ b/solution.py
@@ -146,7 +146,7 @@
             pltpu.VMEM((width, width), jnp.int32),
             pltpu.VMEM((slots, tiles.shape[0]), F32),
         ],
-        compiler_params=params(56 << 20),
+        compiler_params=params(32 << 20),
         name="serve",
     )(after, asked, tiles)
 
@@ -336,7 +336,7 @@
                     dst[g, pl.ds(base, TILE), :] = val
             return carry
 
-        lax.fori_loop(0, BAND // TILE, across, 0, unroll=16)
+        lax.fori_loop(0, BAND // TILE, across, 0, unroll=8)
 
         if closing:
             @pl.when(step == bands)
@@ -382,7 +382,7 @@
                 h_ref[g, at, :] = h
             return carry
 
-        lax.fori_loop(0, BAND // TILE, body, 0, unroll=16)
+        lax.fori_loop(0, BAND // TILE, body, 0, unroll=8)
 
 
 def stencil(fields, after, first, count, old=()):
@@ -557,114 +557,90 @@
     )(lab, landed, weights, *edges)
 
 
-def border_kernel(
-    up_ref, dn_ref, lh_ref, rh_ref, top_ref, bottom_ref, left_ref, right_ref, old_ref,
-    new_ref, sides_ref, ends_ref, edge, first, last, head, tail, load, save,
-):
-    rows, cols = old_ref.shape
+def border_places(rows, cols):
     middle = pl.ds(LANES, cols - 2 * LANES)
-    places = (
+    return (
         (slice(None), pl.ds(0, LANES)),
         (slice(None), pl.ds(cols - LANES, LANES)),
         (pl.ds(0, TILE), middle),
         (pl.ds(rows - TILE, TILE), middle),
     )
+
+
+def border_additions(halos, edges, edge, sides, ends):
+    up_ref, dn_ref, lh_ref, rh_ref = halos
+    top_ref, bottom_ref, left_ref, right_ref = edges
+
+    def cells(ref):
+        return derived(ref[0:1, :], ref[1:2, :], ref[2:3, :])
+
+    pull = TIME_STEP * PRESS * 0.5
+    step = 0.5 * DT_DX
+    for out, turned in ((edge, along_y), (ends, along_x)):
+        out[...] = jnp.zeros_like(out)
+        far_low, far_high, own_low, own_high = (
+            (lh_ref, rh_ref, left_ref, right_ref) if out is edge
+            else (up_ref, dn_ref, top_ref, bottom_ref)
+        )
+        for at, before, after, own, far, sign in (
+            (0, far_low, own_low, own_low, far_low, 1.0),
+            (3, own_high, far_high, own_high, far_high, -1.0),
+        ):
+            gh, gn, gt = flux(turned(cells(before)), turned(cells(after)))
+            wet = own[0:1, :] > 0.0
+            normal = gn * step + (pull * own[0:1, :]) * far[3:4, :]
+            pair = (gt * step, normal) if out is edge else (normal, gt * step)
+            for f, val in enumerate((gh * step,) + pair):
+                out[at + f:at + f + 1, :] = jnp.where(wet, sign * val, 0.0)
+    blank = jnp.zeros((LANES - TILE, LANES), F32)
+    for b in range(sides.shape[0] // LANES):
+        cut = slice(b * LANES, (b + 1) * LANES)
+        sides[cut, :] = jnp.concatenate([edge[:, cut], blank], axis=0).T
+
+
+def patch_border(parts, sides, ends):
+    first, last, head, tail = parts
+    rows = first.shape[0]
+    cols = ends.shape[1]
+    lane = iota((rows, LANES), 1)
+    values = sides[...]
+    first[...] += jnp.where(lane == 0, values, 0.0)
+    last[...] += jnp.where(lane == LANES - 1, pltpu.roll(values, LANES - 4, 1), 0.0)
+    for at, line in ((0, 0), (rows - 1, 3)):
+        first[at:at + 1, :] += ends[line:line + 1, 0:LANES]
+        last[at:at + 1, :] += ends[line:line + 1, cols - LANES:cols]
+    head[0:1, :] += ends[0:1, LANES:cols - LANES]
+    tail[TILE - 1:TILE, :] += ends[3:4, LANES:cols - LANES]
+
+
+def finish_kernel(
+    lab_ref, landed_ref, w_ref, p_ref, up_ref, dn_ref, lh_ref, rh_ref,
+    top_ref, bottom_ref, left_ref, right_ref, old_ref,
+    hu_ref, hv_ref, h_ref, ox_ref, oy_ref, new_ref,
+    held, arrived, left, acc, acc2, fx, fy, fx2, fy2,
+    edge, sides_ref, ends_ref, first, last, head, tail, loaded, saved,
+):
+    step = pl.program_id(0)
+    take = weight_parts(step, w_ref, held, arrived)
     parts = (first, last, head, tail)
+    places = border_places(*old_ref.shape)
     loads = [
-        pltpu.make_async_copy(old_ref.at[at], part, load.at[n])
+        pltpu.make_async_copy(old_ref.at[at], part, loaded.at[n])
         for n, (at, part) in enumerate(zip(places, parts))
     ]
-    for copy in loads:
-        copy.start()
-
-    def cells(ref):
-        return derived(ref[0:1, :], ref[1:2, :], ref[2:3, :])
-
-    pull = TIME_STEP * PRESS * 0.5
-    edge[...] = jnp.zeros_like(edge)
-    for at, before, after, own, far, sign in (
-        (0, lh_ref, left_ref, left_ref, lh_ref, 1.0),
-        (3, right_ref, rh_ref, right_ref, rh_ref, -1.0),
-    ):
-        gh, gn, gt = flux(along_y(cells(before)), along_y(cells(after)))
-        wet = own[0:1, :] > 0.0
-        press = (pull * own[0:1, :]) * far[3:4, :]
-        for f, val in enumerate((gh * (0.5 * DT_DX), gt * (0.5 * DT_DX), gn * (0.5 * DT_DX) + press)):
-            edge[at + f:at + f + 1, :] = jnp.where(wet, sign * val, 0.0)
-    blank = jnp.zeros((LANES - TILE, LANES), F32)
-    for b in range(rows // LANES):
-        cut = slice(b * LANES, (b + 1) * LANES)
-        sides_ref[cut, :] = jnp.concatenate([edge[:, cut], blank], axis=0).T
-    ends_ref[...] = jnp.zeros_like(ends_ref)
-    for at, before, after, own, far, sign in (
-        (0, up_ref, top_ref, top_ref, up_ref, 1.0),
-        (3, bottom_ref, dn_ref, bottom_ref, dn_ref, -1.0),
-    ):
-        gh, gn, gt = flux(along_x(cells(before)), along_x(cells(after)))
-        wet = own[0:1, :] > 0.0
-        press = (pull * own[0:1, :]) * far[3:4, :]
-        for f, val in enumerate((gh * (0.5 * DT_DX), gn * (0.5 * DT_DX) + press, gt * (0.5 * DT_DX))):
-            ends_ref[at + f:at + f + 1, :] = jnp.where(wet, sign * val, 0.0)
-
-    for copy in loads:
-        copy.wait()
-    lane = iota((rows, LANES), 1)
-    sides = sides_ref[...]
-    first[...] += jnp.where(lane == 0, sides, 0.0)
-    last[...] += jnp.where(lane == LANES - 1, pltpu.roll(sides, LANES - 4, 1), 0.0)
-    for at, line in ((0, 0), (rows - 1, 3)):
-        first[at:at + 1, :] += ends_ref[line:line + 1, 0:LANES]
-        last[at:at + 1, :] += ends_ref[line:line + 1, cols - LANES:cols]
-    head[0:1, :] += ends_ref[0:1, LANES:cols - LANES]
-    tail[TILE - 1:TILE, :] += ends_ref[3:4, LANES:cols - LANES]
     saves = [
-        pltpu.make_async_copy(part, new_ref.at[at], save.at[n])
+        pltpu.make_async_copy(part, new_ref.at[at], saved.at[n])
         for n, (at, part) in enumerate(zip(places, parts))
     ]
-    for copy in saves:
-        copy.start()
-    for copy in saves:
-        copy.wait()
-
-
-def border(halos, edges, newh):
-    rows, cols = newh.shape
-    whole = pl.BlockSpec(memory_space=pl.ANY)
-    return pl.pallas_call(
-        border_kernel,
-        out_shape=(
-            jax.ShapeDtypeStruct((rows, cols), F32),
-            jax.ShapeDtypeStruct((rows, LANES), F32),
-            jax.ShapeDtypeStruct((TILE, cols), F32),
-        ),
-        in_specs=[VMEM] * 8 + [whole],
-        out_specs=(whole, VMEM, VMEM),
-        input_output_aliases={8: 0},
-        scratch_shapes=[
-            pltpu.VMEM((TILE, rows), F32),
-            pltpu.VMEM((rows, LANES), F32),
-            pltpu.VMEM((rows, LANES), F32),
-            pltpu.VMEM((TILE, cols - 2 * LANES), F32),
-            pltpu.VMEM((TILE, cols - 2 * LANES), F32),
-            pltpu.SemaphoreType.DMA((4,)),
-            pltpu.SemaphoreType.DMA((4,)),
-        ],
-        compiler_params=params(),
-        name="border",
-    )(*halos, *edges, newh)
-
-
-def finish_kernel(
-    lab_ref, landed_ref, w_ref, p_ref, sides_ref, ends_ref,
-    hu_ref, hv_ref, h_ref, ox_ref, oy_ref,
-    held, arrived, left, acc, acc2, fx, fy, fx2, fy2,
-):
-    step = pl.program_id(0)
-
-    take = weight_parts(step, w_ref, held, arrived)
 
     @pl.when(step == 0)
     def _():
+        for copy in loads:
+            copy.start()
+        border_additions(
+            (up_ref, dn_ref, lh_ref, rh_ref), (top_ref, bottom_ref, left_ref, right_ref),
+            edge, sides_ref, ends_ref,
+        )
         stack_left(left, summed_of(lab_ref[...], landed_ref[...]), 2)
 
     take()
@@ -712,6 +688,14 @@
                 ox_ref[r, cells, cut] = jnp.where(wet, new[0], 0.0)
                 oy_ref[r, cells, cut] = jnp.where(wet, new[1], 0.0)
 
+    @pl.when(step == 1)
+    def _():
+        for copy in loads:
+            copy.wait()
+        patch_border(parts, sides_ref, ends_ref)
+        for copy in saves:
+            copy.start()
+
     @pl.when(step == 0)
     def _():
         ox_ref[0, 0:1, :] += ends_ref[1:2, :]
@@ -722,9 +706,11 @@
         deep = ox_ref.shape[1]
         ox_ref[BPX - 1, deep - 1:deep, :] += ends_ref[4:5, :]
         oy_ref[BPX - 1, deep - 1:deep, :] += ends_ref[5:6, :]
-
-
-def finish(lab, landed, weights, p, sides, ends, hu, hv, h):
+        for copy in saves:
+            copy.wait()
+
+
+def finish(lab, landed, weights, p, halos, edges, newh, hu, hv, h):
     deep = 2 * TILE
     steps = PATCH // deep
     cols = BPY * PATCH
@@ -732,6 +718,8 @@
     slab = pl.BlockSpec((GROUPS, BPX, deep, LANES), lambda i: (0, 0, i, 0))
     out = pl.BlockSpec((BPX, deep, cols), lambda i: (0, i, 0))
     shape = jax.ShapeDtypeStruct((BPX, PATCH, cols), F32)
+    rows = newh.shape[0]
+    whole = pl.BlockSpec(memory_space=pl.ANY)
     field = pltpu.VMEM((GROUPS, BPX * TILE, LANES), F32)
 
     def const(x):
@@ -740,14 +728,15 @@
     return pl.pallas_call(
         finish_kernel,
         grid=(steps,),
-        out_shape=(shape, shape),
+        out_shape=(shape, shape, jax.ShapeDtypeStruct(newh.shape, F32)),
         in_specs=[
             const(lab), const(landed),
-            pl.BlockSpec(memory_space=pl.ANY),
-            const(p), const(sides), const(ends),
+            whole,
+            const(p), *[const(x) for x in (*halos, *edges)], whole,
             slab, slab, slab,
         ],
-        out_specs=(out, out),
+        out_specs=(out, out, whole),
+        input_output_aliases={12: 2},
         scratch_shapes=[
             pltpu.VMEM((steps, NW * ABLK, 2 * PART), BF16),
             pltpu.SemaphoreType.DMA((steps,)),
@@ -755,6 +744,15 @@
             pltpu.VMEM((2 * NPATCH, PART), F32),
             pltpu.VMEM((2 * NPATCH, PART), F32),
             field, field, field, field,
+            pltpu.VMEM((TILE, rows), F32),
+            pltpu.VMEM((rows, LANES), F32),
+            pltpu.VMEM((TILE, cols), F32),
+            pltpu.VMEM((rows, LANES), F32),
+            pltpu.VMEM((rows, LANES), F32),
+            pltpu.VMEM((TILE, cols - 2 * LANES), F32),
+            pltpu.VMEM((TILE, cols - 2 * LANES), F32),
+            pltpu.SemaphoreType.DMA((4,)),
+            pltpu.SemaphoreType.DMA((4,)),
         ],
         compiler_params=params(),
         cost_estimate=pl.CostEstimate(
@@ -762,7 +760,7 @@
         ),
         name="finish",
     )(
-        lab, landed, weights, p, sides, ends,
+        lab, landed, weights, p, *halos, *edges, newh,
         hu.reshape(split), hv.reshape(split), h.reshape(split),
     )
 
@@ -817,8 +815,7 @@
         send(bottom, "gx", 1), send(top, "gx", -1), send(right, "gy", 1), send(left, "gy", -1),
     )
     newh, hu, hv, h, _ = stencil(fields, top, ahead, bands - ahead, planes)
-    newh, sides, ends = border(halos, edges, newh)
-    new_x, new_y = finish(lab, wind, weights, p, sides, ends, hu, hv, h)
+    new_x, new_y, newh = finish(lab, wind, weights, p, halos, edges, newh, hu, hv, h)
     return (newh, new_x.reshape(newh.shape), new_y.reshape(newh.shape))
 
 

time: 109 us -> 84.6 us (0.78)
  Pallas kernels: 74.4 us -> 49.8 us
    pallas_call x2, Pallas kernels: 38.9 us -> 19.8 us  [stencil(): pl.pallas_call(functools.partial(stencil_kernel, opening, closing), grid=...]
    pallas_call x2 -> x1, Pallas kernels: 15.4 us -> 11.9 us  [finish(): pl.pallas_call(finish_kernel, grid=(steps,), out_shape=(shape, shape, jax...]
    pallas_call x2, Pallas kernels: 4.75 us -> 2.85 us  [serve(): pl.pallas_call(serve_kernel, out_shape=jax.ShapeDtypeStruct((slots, tiles...]
    unnamed x14 -> x20, local copies, waits for them, and re-layouts: 2.28 us -> 2.46 us
  transfers between devices with their start and end apart: 7 -> 7, of which waited for: 0 -> 1; matrix products, arithmetic and copies ran while one was open for 0% -> 0% of each run, Pallas kernels for 55% -> 42%
where the time goes in v11:
time: 84.6 us; the launch traced here: 83.7 us
  Pallas kernels  49.8 us (59%)
  starting transfers between devices  29.6 us (35%)
  local copies, waits for them, and re-layouts  2.46 us (3%)
  between operations  1.47 us (2%)
    pallas_call x2, Pallas kernels, stencil(): pl.pallas_call(functools.partial(stencil_kernel, opening, closing), grid=...  19.8 us
    ppermute x4, starting transfers between devices, send(): return lax.ppermute(value, axis, pairs)  12.3 us
    pallas_call x1, Pallas kernels, finish(): pl.pallas_call(finish_kernel, grid=(steps,), out_shape=(shape, shape, jax...  11.9 us
    all_to_all x2, starting transfers between devices, exchange(): got = lax.all_to_all(parts, both, split_axis=0, concat_axis=0, tiled=True)  11.4 us
    pallas_call x1, Pallas kernels, pressure_field(): pl.pallas_call(press_kernel, grid=(steps,), out_shape=tuple((jax.ShapeDty...  7.13 us
    all_to_all x1, starting transfers between devices, body(): lax.all_to_all(want.reshape(devices, 1, capacity), both, split_axis=0, co...  5.99 us
    pallas_call x1, Pallas kernels, edge_cells(): pl.pallas_call(edges_kernel, grid=(1,), out_shape=(line, line, column, co...  4.47 us
    pallas_call x2, Pallas kernels, serve(): pl.pallas_call(serve_kernel, out_shape=jax.ShapeDtypeStruct((slots, tiles...  2.85 us
  transfers between devices with their start and end apart: 7, of which 1 were waited for; matrix products, arithmetic and copies ran while one was open for 0% of the time, Pallas kernels for 42%

profile of v11, /device:TPU:12, one launch (start us, length us, event | category | flops | bytes accessed | tf_op | source)
XLA Modules:
  0.0 83.7 jit_solution(6476268542940728445)
XLA Ops:
  0.6 1.7 %requests.1 = (s32[32,32]{1,0:T(8,128)}, s32[32,32]{1,0:T(8,128)}) custom-call(s32[1,512]{1,0:T(1,128)} %bitcast.29, s32[1,512]{1,0:T(1,128)} %bitcast.30, s32[1,512]{1,0:T(1,128)} %bitcast.31, s32[1,512]{1,0:T(1,128)} %bitcast.32), custom_call_target="tpu_custom_call" | custom-call | tf_op jit(solution)/shard_map/requests/pallas_call | solution.py:82
  2.3 6.0 %all-to-all-start = ((s32[32,1,32]{2,1,0:T(1,128)}), s32[32,1,32]{2,1,0:T(1,128)S(1)}, u32[]{:S(2)}, u32[]{:S(2)}) async-start(s32[32,1,32]{2,1,0:T(1,128)} %bitcast.28), calls=%async_computation | async-start | bytes 32768 | tf_op jit(solution)/shard_map/all_to_all | solution.py:793
  9.0 2.0 %mix.1 = (bf16[256,256]{1,0:T(8,128)(2,1)}, bf16[256,512]{1,0:T(8,128)(2,1)}) custom-call(f32[1]{0:T(128)} %bitcast.19.blend_ref, bf16[6,256,256]{2,1,0:T(8,128)(2,1)} %bitcast.27), custom_call_target="tpu_custom_call" | custom-call | tf_op jit(solution)/shard_map/mix/pallas_call | solution.py:108
  11.0 4.5 %edges.1 = (f32[8,512]{1,0:T(8,128)}, f32[8,512]{1,0:T(8,128)}, f32[8,1024]{1,0:T(8,128)}, f32[8,1024]{1,0:T(8,128)}) custom-call(f32[1024,512]{1,0:T(8,128)} %refs_5_.1, s32[1024,512]{1,0:T(8,128)} %refs_6_.1, f32[1024,512]{1,0:T(8,128)} %refs_7_.1, f32[1024,512]{1,0:T(8,128)} %refs_8_.1, f32[1024,512]{1,0:T(8,128)} %refs_5_.1, s32[1024,512]{1,0:T(8,128)} %refs_6_.1, ...), custom_call_target="tpu_custom_call" | custom-call | tf_op jit(solution)/shard_map/edges/pallas_call | solution.py:194
  15.5 0.7 copy-done.2
  16.2 1.3 %serve.2 = bf16[1024,256]{1,0:T(8,128)(2,1)} custom-call(f32[8,512]{1,0:T(8,128)S(1)} %copy-done.2, s32[32,1,32]{2,1,0:T(1,128)S(1)} %all-to-all-done.asked_ref, bf16[256,256]{1,0:T(8,128)(2,1)S(1)} %copy-done.1), custom_call_target="tpu_custom_call" | custom-call | tf_op jit(solution)/shard_map/serve/pallas_call | solution.py:140
  17.5 5.8 %all-to-all-start.1 = ((bf16[32,32,256]{2,1,0:T(8,128)(2,1)}), bf16[32,32,256]{2,1,0:T(8,128)(2,1)S(1)}, u32[]{:S(2)}, u32[]{:S(2)}) async-start(bf16[32,32,256]{2,1,0:T(8,128)(2,1)} %bitcast.8), calls=%async_computation.1 | async-start | bytes 1048576 | tf_op jit(solution)/shard_map/all_to_all | solution.py:802
  23.4 11.8 %stencil.2 = (f32[1024,512]{1,0:T(8,128)}, f32[4,1024,128]{2,1,0:T(8,128)}, f32[4,1024,128]{2,1,0:T(8,128)}, f32[4,1024,128]{2,1,0:T(8,128)}, f32[8,128]{1,0:T(8,128)}) custom-call(f32[1024,512]{1,0:T(8,128)} %refs_5_.1, s32[1024,512]{1,0:T(8,128)} %refs_6_.1, f32[1024,512]{1,0:T(8,128)} %refs_7_.1, f32[1024,512]{1,0:T(8,128)} %refs_8_.1, ...), custom_call_target="tpu_custom_call" | custom-call | flops 65536000 | bytes 20971520 | tf_op jit(solution)/shard_map/stencil/pallas_call | solution.py:399
  35.2 0.7 copy-done.3
  35.8 1.5 %serve.3 = bf16[1024,512]{1,0:T(8,128)(2,1)} custom-call(f32[8,128]{1,0:T(8,128)S(1)} %copy-done.3, s32[32,1,32]{2,1,0:T(1,128)S(1)} %all-to-all-done.asked_ref, bf16[256,512]{1,0:T(8,128)(2,1)S(1)} %copy-done), custom_call_target="tpu_custom_call" | custom-call | tf_op jit(solution)/shard_map/serve/pallas_call | solution.py:140
  37.4 0.3 all-to-all-done.1
  37.7 5.5 %all-to-all-start.2 = ((bf16[32,32,512]{2,1,0:T(8,128)(2,1)}), bf16[32,32,512]{2,1,0:T(8,128)(2,1)S(1)}, u32[]{:S(2)}, u32[]{:S(2)}) async-start(bf16[32,32,512]{2,1,0:T(8,128)(2,1)} %bitcast.11), calls=%async_computation.2 | async-start | bytes 2097152 | tf_op jit(solution)/shard_map/all_to_all | solution.py:802
  43.2 7.1 %pressure.1 = (f32[4,1040,128]{2,1,0:T(8,128)}, f32[8,512]{1,0:T(8,128)}, f32[8,512]{1,0:T(8,128)}, f32[8,1024]{1,0:T(8,128)}, f32[8,1024]{1,0:T(8,128)}, /*index=5*/s32[1,1024]{1,0:T(1,128)}) custom-call(s32[32,32]{1,0:T(8,128)} %get-tuple-element.29.lab_ref.refs_4_, bf16[1024,256]{1,0:T(8,128)(2,1)} %bitcast.26, bf16[1024,4096]{1,0:T(8,128)(2,1)} %bitcast.20, ...), custom_call_target="tpu_custom_call" | custom-call | flops 1073741824 | bytes 12582912 | tf_op jit(solution)/shard_map/pressure/pallas_call | solution.py:532
  50.4 2.1 %collective-permute-start.2 = (f32[8,1024]{1,0:T(8,128)}, f32[8,1024]{1,0:T(8,128)S(1)}, u32[]{:S(2)}, u32[]{:S(2)}) collective-permute-start(f32[8,1024]{1,0:T(8,128)} %get-tuple-element.42.right_ref), channel_id=1, source_target_pairs={{0,1},{1,2},{2,3},{3,4},{4,5},{5,6},{6,7},{8,9},{9,10},{10,11},{11... | collective-permute-start | bytes 98312 | tf_op jit(solution)/shard_map/ppermute | solution.py:216
  52.4 4.4 %collective-permute-start.3 = (f32[8,1024]{1,0:T(8,128)}, f32[8,1024]{1,0:T(8,128)S(1)}, u32[]{:S(2)}, u32[]{:S(2)}) collective-permute-start(f32[8,1024]{1,0:T(8,128)} %get-tuple-element.43.left_ref), channel_id=1, source_target_pairs={{1,0},{2,1},{3,2},{4,3},{5,4},{6,5},{7,6},{9,8},{10,9},{11,10},{12... | collective-permute-start | bytes 98312 | tf_op jit(solution)/shard_map/ppermute | solution.py:216
  56.8 2.5 %collective-permute-start.1 = (f32[8,512]{1,0:T(8,128)}, f32[8,512]{1,0:T(8,128)S(1)}, u32[]{:S(2)}, u32[]{:S(2)}) collective-permute-start(f32[8,512]{1,0:T(8,128)} %get-tuple-element.41.refs_4_.top_ref), channel_id=1, source_target_pairs={{8,0},{16,8},{24,16},{9,1},{17,9},{25,17},{10,2},{18,10},{26,18},{... | collective-permute-start | bytes 49160 | tf_op jit(solution)/shard_map/ppermute | solution.py:216
  59.3 3.4 %collective-permute-start = (f32[8,512]{1,0:T(8,128)}, f32[8,512]{1,0:T(8,128)S(1)}, u32[]{:S(2)}, u32[]{:S(2)}) collective-permute-start(f32[8,512]{1,0:T(8,128)} %get-tuple-element.40.bottom_ref), channel_id=1, source_target_pairs={{0,8},{8,16},{16,24},{1,9},{9,17},{17,25},{2,10},{10,18},{18,26},{... | collective-permute-start | bytes 49160 | tf_op jit(solution)/shard_map/ppermute | solution.py:216
  62.7 8.0 %stencil.3 = (f32[1024,512]{1,0:T(8,128)}, f32[4,1024,128]{2,1,0:T(8,128)}, f32[4,1024,128]{2,1,0:T(8,128)}, f32[4,1024,128]{2,1,0:T(8,128)}, f32[8,128]{1,0:T(8,128)}) custom-call(f32[1024,512]{1,0:T(8,128)} %refs_5_.1, s32[1024,512]{1,0:T(8,128)} %refs_6_.1, ...), custom_call_target="tpu_custom_call", output_to_operand_aliasing={{0}: (9, {}), {1}: (10, {}), {2}: (11, {}), {3}: (12, {})} | custom-call | flops 39321600 | bytes 12582912 | tf_op jit(solution)/shard_map/stencil/pallas_call | solution.py:399
  70.8 0.5 copy-done.8
  71.3 0.0 copy-done.9
  71.3 0.0 copy-done.6
  71.3 0.0 copy-done.7
  71.4 0.5 copy-done.4
  71.8 11.9 %finish.1 = (f32[16,64,512]{2,1,0:T(8,128)}, f32[16,64,512]{2,1,0:T(8,128)}, f32[1024,512]{1,0:T(8,128)}) custom-call(s32[1,1024]{1,0:T(1,128)} %get-tuple-element.36.lab_ref, bf16[1024,512]{1,0:T(8,128)(2,1)} %bitcast.25, bf16[1024,4096]{1,0:T(8,128)(2,1)} %bitcast.21, f32[4,1040,128]{2,1,0:T(8,128)} %get-tuple-element.39.p_ref, ...), custom_call_target="tpu_custom_call", output_to_operand_aliasing={{2}: (12, {})} | custom-call | flops 2147483648 | bytes 20971520 | tf_op jit(solution)/shard_map/finish/pallas_call | solution.py:728
  (19 shorter events, 0.0 us)
Async XLA Ops:
  2.3 13.1 %all-to-all-start = ((s32[32,1,32]{2,1,0:T(1,128)}), s32[32,1,32]{2,1,0:T(1,128)S(1)}, u32[]{:S(2)}, u32[]{:S(2)}) async-start(s32[32,1,32]{2,1,0:T(1,128)} %bitcast.28), calls=%async_computation | async-start | bytes 32768 | tf_op jit(solution)/shard_map/all_to_all | solution.py:793
  11.0 4.5 %copy-start.1 = (bf16[256,256]{1,0:T(8,128)(2,1)S(1)}, bf16[256,256]{1,0:T(8,128)(2,1)}, u32[]{:S(2)}) copy-start(bf16[256,256]{1,0:T(8,128)(2,1)} %get-tuple-element.32.tiles_ref) | copy-start | bytes 393220
  15.5 0.7 copy-start.2
  17.5 20.2 %all-to-all-start.1 = ((bf16[32,32,256]{2,1,0:T(8,128)(2,1)}), bf16[32,32,256]{2,1,0:T(8,128)(2,1)S(1)}, u32[]{:S(2)}, u32[]{:S(2)}) async-start(bf16[32,32,256]{2,1,0:T(8,128)(2,1)} %bitcast.8), calls=%async_computation.1 | async-start | bytes 1048576 | tf_op jit(solution)/shard_map/all_to_all | solution.py:802
  23.3 11.8 %copy-start = (bf16[256,512]{1,0:T(8,128)(2,1)S(1)}, bf16[256,512]{1,0:T(8,128)(2,1)}, u32[]{:S(2)}) copy-start(bf16[256,512]{1,0:T(8,128)(2,1)} %get-tuple-element.38.tiles_ref) | copy-start | bytes 786436
  35.2 0.7 copy-start.3
  37.7 5.5 %copy-start.5 = (bf16[32,32,256]{2,1,0:T(8,128)(2,1)}, bf16[32,32,256]{2,1,0:T(8,128)(2,1)S(1)}, u32[]{:S(2)}) copy-start(bf16[32,32,256]{2,1,0:T(8,128)(2,1)S(1)} %all-to-all-done.1) | copy-start | bytes 1572868
  37.7 33.1 %all-to-all-start.2 = ((bf16[32,32,512]{2,1,0:T(8,128)(2,1)}), bf16[32,32,512]{2,1,0:T(8,128)(2,1)S(1)}, u32[]{:S(2)}, u32[]{:S(2)}) async-start(bf16[32,32,512]{2,1,0:T(8,128)(2,1)} %bitcast.11), calls=%async_computation.2 | async-start | bytes 2097152 | tf_op jit(solution)/shard_map/all_to_all | solution.py:802
  50.4 20.4 %collective-permute-start.2 = (f32[8,1024]{1,0:T(8,128)}, f32[8,1024]{1,0:T(8,128)S(1)}, u32[]{:S(2)}, u32[]{:S(2)}) collective-permute-start(f32[8,1024]{1,0:T(8,128)} %get-tuple-element.42.right_ref), channel_id=1, source_target_pairs={{0,1},{1,2},{2,3},{3,4},{4,5},{5,6},{6,7},{8,9},{9,10},{10,11},{11... | collective-permute-start | bytes 98312 | tf_op jit(solution)/shard_map/ppermute | solution.py:216
  52.4 18.3 %collective-permute-start.3 = (f32[8,1024]{1,0:T(8,128)}, f32[8,1024]{1,0:T(8,128)S(1)}, u32[]{:S(2)}, u32[]{:S(2)}) collective-permute-start(f32[8,1024]{1,0:T(8,128)} %get-tuple-element.43.left_ref), channel_id=1, source_target_pairs={{1,0},{2,1},{3,2},{4,3},{5,4},{6,5},{7,6},{9,8},{10,9},{11,10},{12... | collective-permute-start | bytes 98312 | tf_op jit(solution)/shard_map/ppermute | solution.py:216
  56.8 13.9 %collective-permute-start.1 = (f32[8,512]{1,0:T(8,128)}, f32[8,512]{1,0:T(8,128)S(1)}, u32[]{:S(2)}, u32[]{:S(2)}) collective-permute-start(f32[8,512]{1,0:T(8,128)} %get-tuple-element.41.refs_4_.top_ref), channel_id=1, source_target_pairs={{8,0},{16,8},{24,16},{9,1},{17,9},{25,17},{10,2},{18,10},{26,18},{... | collective-permute-start | bytes 49160 | tf_op jit(solution)/shard_map/ppermute | solution.py:216
  59.3 11.4 %collective-permute-start = (f32[8,512]{1,0:T(8,128)}, f32[8,512]{1,0:T(8,128)S(1)}, u32[]{:S(2)}, u32[]{:S(2)}) collective-permute-start(f32[8,512]{1,0:T(8,128)} %get-tuple-element.40.bottom_ref), channel_id=1, source_target_pairs={{0,8},{8,16},{16,24},{1,9},{9,17},{17,25},{2,10},{10,18},{18,26},{... | collective-permute-start | bytes 49160 | tf_op jit(solution)/shard_map/ppermute | solution.py:216
  70.7 0.6 copy-start.8
  70.7 0.6 copy-start.9
  70.7 0.6 copy-start.6
  70.8 0.6 copy-start.7
  70.8 1.1 %copy-start.4 = (bf16[32,32,512]{2,1,0:T(8,128)(2,1)}, bf16[32,32,512]{2,1,0:T(8,128)(2,1)S(1)}, u32[]{:S(2)}) copy-start(bf16[32,32,512]{2,1,0:T(8,128)(2,1)S(1)} %all-to-all-done.2) | copy-start | bytes 3145732

commit v12 on v11

--- a/solution.py
+++ b/solution.py
@@ -89,7 +89,7 @@
     )(src, blk, pat, wgt)
 
 
-def mix_kernel(blend_ref, atm_ref, press_ref, wind_ref):
+def mix_kernel(after_ref, blend_ref, atm_ref, press_ref, wind_ref):
     blend = blend_ref[0]
     keep = 1.0 - blend
 
@@ -103,7 +103,7 @@
         wind_ref[:, k * ABLK:(k + 1) * ABLK] = mixed(k)
 
 
-def mix(blend, atm):
+def mix(after, blend, atm):
     blocks = atm.shape[1]
     return pl.pallas_call(
         mix_kernel,
@@ -111,14 +111,15 @@
             jax.ShapeDtypeStruct((blocks, ABLK), BF16),
             jax.ShapeDtypeStruct((blocks, 2 * ABLK), BF16),
         ),
-        in_specs=[SMEM, VMEM],
+        in_specs=[pl.BlockSpec(memory_space=pl.ANY), SMEM, VMEM],
         out_specs=(VMEM, VMEM),
         compiler_params=params(),
         name="mix",
-    )(blend, atm)
-
-
-def serve_kernel(after_ref, asked_ref, tiles_ref, out_ref, turned, pick):
+    )(after, blend, atm)
+
+
+def serve_kernel(*refs):
+    asked_ref, tiles_ref, out_ref, turned, pick = refs[-5:]
     peers, _, capacity = asked_ref.shape
     width = turned.shape[0]
     turned[...] = jnp.zeros_like(turned)
@@ -140,7 +141,7 @@
     return pl.pallas_call(
         serve_kernel,
         out_shape=jax.ShapeDtypeStruct((slots, tiles.shape[1]), BF16),
-        in_specs=[pl.BlockSpec(memory_space=pl.ANY), VMEM, VMEM],
+        in_specs=[pl.BlockSpec(memory_space=pl.ANY)] * len(after) + [VMEM, VMEM],
         out_specs=VMEM,
         scratch_shapes=[
             pltpu.VMEM((width, width), jnp.int32),
@@ -148,7 +149,7 @@
         ],
         compiler_params=params(32 << 20),
         name="serve",
-    )(after, asked, tiles)
+    )(*after, asked, tiles)
 
 
 def edges_kernel(
@@ -616,12 +617,36 @@
 def finish_kernel(
     lab_ref, landed_ref, w_ref, p_ref, up_ref, dn_ref, lh_ref, rh_ref,
     top_ref, bottom_ref, left_ref, right_ref, old_ref,
-    hu_ref, hv_ref, h_ref, ox_ref, oy_ref, new_ref,
+    hu_hbm, hv_hbm, h_hbm, ox_ref, oy_ref, new_ref,
     held, arrived, left, acc, acc2, fx, fy, fx2, fy2,
     edge, sides_ref, ends_ref, first, last, head, tail, loaded, saved,
+    press, got_press, hus, hvs, hs, got,
 ):
     step = pl.program_id(0)
+    deep = hus.shape[3]
+    take_press = pltpu.make_async_copy(p_ref, press, got_press)
+
+    def state(n):
+        at = pl.ds(pl.multiple_of(n * deep, deep), deep)
+        return [
+            pltpu.make_async_copy(src.at[:, :, at, :], dst.at[n], got.at[f, n])
+            for f, (src, dst) in enumerate(((hu_hbm, hus), (hv_hbm, hvs), (h_hbm, hs)))
+        ]
+
+    @pl.when(step == 0)
+    def _():
+        for copy in state(0):
+            copy.start()
+        take_press.start()
+
     take = weight_parts(step, w_ref, held, arrived)
+
+    @pl.when(step == 0)
+    def _():
+        for n in range(1, hus.shape[0]):
+            for copy in state(n):
+                copy.start()
+
     parts = (first, last, head, tail)
     places = border_places(*old_ref.shape)
     loads = [
@@ -646,6 +671,9 @@
     take()
     acc[...] = jnp.dot(left[...], held[step, :, :PART], preferred_element_type=F32)
     acc2[...] = jnp.dot(left[...], held[step, :, PART:], preferred_element_type=F32)
+    pl.when(step == 0)(take_press.wait)
+    for copy in state(step):
+        copy.wait()
     lane = iota((TILE, LANES), 1)
     for part, (src, mx, my) in enumerate(((acc, fx, fy), (acc2, fx2, fy2))):
         spread_rows(src, mx, 0)
@@ -656,23 +684,23 @@
             mark = pl.multiple_of(r * PATCH + (2 * step + part) * TILE, TILE)
             base = pl.multiple_of(mark + TILE, TILE)
             ends = sides_ref[pl.ds(mark, TILE), :]
-            tiles = [p_ref[g, pl.ds(base, TILE), :] for g in range(GROUPS)]
+            tiles = [press[g, pl.ds(base, TILE), :] for g in range(GROUPS)]
             for g in range(GROUPS):
                 before = tiles[g - 1] if g else 0.0
                 after = tiles[g + 1] if g < GROUPS - 1 else 0.0
                 prev = pltpu.roll(jnp.where(lane == LANES - 1, before, tiles[g]), 1, 1)
                 nxt = pltpu.roll(jnp.where(lane == 0, after, tiles[g]), LANES - 1, 1)
-                h = h_ref[g, r, cells, :]
+                h = hs[step, g, r, cells, :]
                 wet = h > 0.0
                 scale = (TIME_STEP * PRESS * 0.5) * h
-                gx = p_ref[g, pl.ds(base + 1, TILE), :] - p_ref[g, pl.ds(base - 1, TILE), :]
+                gx = press[g, pl.ds(base + 1, TILE), :] - press[g, pl.ds(base - 1, TILE), :]
                 wx = mx[g, at, :]
                 wy = my[g, at, :]
                 power = wx * wx + wy * wy
                 speed = jnp.where(power > 0.0, power * lax.rsqrt(power), 0.0) * (TIME_STEP * STRESS)
                 new = [
-                    hu_ref[g, r, cells, :] - scale * gx + speed * wx,
-                    hv_ref[g, r, cells, :] - scale * (nxt - prev) + speed * wy,
+                    hus[step, g, r, cells, :] - scale * gx + speed * wx,
+                    hvs[step, g, r, cells, :] - scale * (nxt - prev) + speed * wy,
                 ]
                 for own, edge, shift in ((0, 0, 1), (GROUPS - 1, LANES - 1, 4)):
                     if g == own:
@@ -703,7 +731,6 @@
 
     @pl.when(step == pl.num_programs(0) - 1)
     def _():
-        deep = ox_ref.shape[1]
         ox_ref[BPX - 1, deep - 1:deep, :] += ends_ref[4:5, :]
         oy_ref[BPX - 1, deep - 1:deep, :] += ends_ref[5:6, :]
         for copy in saves:
@@ -715,7 +742,7 @@
     steps = PATCH // deep
     cols = BPY * PATCH
     split = (GROUPS, BPX, PATCH, LANES)
-    slab = pl.BlockSpec((GROUPS, BPX, deep, LANES), lambda i: (0, 0, i, 0))
+    slab = pltpu.VMEM((steps, GROUPS, BPX, deep, LANES), F32)
     out = pl.BlockSpec((BPX, deep, cols), lambda i: (0, i, 0))
     shape = jax.ShapeDtypeStruct((BPX, PATCH, cols), F32)
     rows = newh.shape[0]
@@ -732,8 +759,8 @@
         in_specs=[
             const(lab), const(landed),
             whole,
-            const(p), *[const(x) for x in (*halos, *edges)], whole,
-            slab, slab, slab,
+            whole, *[const(x) for x in (*halos, *edges)], whole,
+            whole, whole, whole,
         ],
         out_specs=(out, out, whole),
         input_output_aliases={12: 2},
@@ -753,6 +780,10 @@
             pltpu.VMEM((TILE, cols - 2 * LANES), F32),
             pltpu.SemaphoreType.DMA((4,)),
             pltpu.SemaphoreType.DMA((4,)),
+            pltpu.VMEM(p.shape, F32),
+            pltpu.SemaphoreType.DMA(()),
+            slab, slab, slab,
+            pltpu.SemaphoreType.DMA((3, steps)),
         ],
         compiler_params=params(),
         cost_estimate=pl.CostEstimate(
@@ -793,8 +824,8 @@
     asked = lax.all_to_all(
         want.reshape(devices, 1, capacity), both, split_axis=0, concat_axis=0, tiled=True
     )
-    press, wind = mix(blend.reshape(1), atm)
     top, bottom, left, right = edge_cells(depth_field, wet_mask, mom_x, mom_y)
+    press, wind = mix(top, blend.reshape(1), atm)
 
     def exchange(after, tiles):
         rows = serve(after, asked, tiles)
@@ -802,12 +833,12 @@
         got = lax.all_to_all(parts, both, split_axis=0, concat_axis=0, tiled=True)
         return got.reshape(rows.shape)
 
-    press = exchange(top, press)
+    press = exchange((), press)
     fields = (depth_field, wet_mask, mom_x, mom_y)
     bands = depth_field.shape[0] // BAND
     ahead = bands * 5 // 8
     *planes, token = stencil(fields, lab, 0, ahead)
-    wind = exchange(token, wind)
+    wind = exchange((token,), wind)
     weights = remap_weights.reshape(NW * ABLK, PATCH * PATCH)
     p, *edges, lab = pressure_field(lab, press, weights, (top, bottom, left, right))
     top, bottom, left, right = edges

time: 84.6 us -> 85.2 us (level)
    unnamed x20 -> x18, local copies, waits for them, and re-layouts: 2.46 us -> 2.66 us
  transfers between devices with their start and end apart: 7 -> 7, of which waited for: 1 -> 1; matrix products, arithmetic and copies ran while one was open for 0% -> 0% of each run, Pallas kernels for 42% -> 41%
where the time goes in v12:
time: 85.2 us; the launch traced here: 84.3 us
  Pallas kernels  50.2 us (59%)
  starting transfers between devices  29.6 us (35%)
  local copies, waits for them, and re-layouts  2.66 us (3%)
  between operations  1.46 us (2%)
    pallas_call x2, Pallas kernels, stencil(): pl.pallas_call(functools.partial(stencil_kernel, opening, closing), grid=...  19.7 us
    pallas_call x1, Pallas kernels, finish(): pl.pallas_call(finish_kernel, grid=(steps,), out_shape=(shape, shape, jax...  12.4 us
    ppermute x4, starting transfers between devices, send(): return lax.ppermute(value, axis, pairs)  12.3 us
    all_to_all x2, starting transfers between devices, exchange(): got = lax.all_to_all(parts, both, split_axis=0, concat_axis=0, tiled=True)  11.3 us
    pallas_call x1, Pallas kernels, pressure_field(): pl.pallas_call(press_kernel, grid=(steps,), out_shape=tuple((jax.ShapeDty...  7.12 us
    all_to_all x1, starting transfers between devices, body(): lax.all_to_all(want.reshape(devices, 1, capacity), both, split_axis=0, co...  5.99 us
    pallas_call x1, Pallas kernels, edge_cells(): pl.pallas_call(edges_kernel, grid=(1,), out_shape=(line, line, column, co...  4.46 us
    pallas_call x2, Pallas kernels, serve(): pl.pallas_call(serve_kernel, out_shape=jax.ShapeDtypeStruct((slots, tiles...  2.85 us
  transfers between devices with their start and end apart: 7, of which 1 were waited for; matrix products, arithmetic and copies ran while one was open for 0% of the time, Pallas kernels for 41%

profile of v12, /device:TPU:12, one launch (start us, length us, event | category | flops | bytes accessed | tf_op | source)
XLA Modules:
  0.0 84.3 jit_solution(13700069078724091222)
XLA Ops:
  0.6 1.7 %requests.1 = (s32[32,32]{1,0:T(8,128)}, s32[32,32]{1,0:T(8,128)}) custom-call(s32[1,512]{1,0:T(1,128)} %bitcast.29, s32[1,512]{1,0:T(1,128)} %bitcast.30, s32[1,512]{1,0:T(1,128)} %bitcast.31, s32[1,512]{1,0:T(1,128)} %bitcast.32), custom_call_target="tpu_custom_call" | custom-call | tf_op jit(solution)/shard_map/requests/pallas_call | solution.py:82
  2.3 6.0 %all-to-all-start = ((s32[32,1,32]{2,1,0:T(1,128)}), s32[32,1,32]{2,1,0:T(1,128)S(1)}, u32[]{:S(2)}, u32[]{:S(2)}) async-start(s32[32,1,32]{2,1,0:T(1,128)} %bitcast.28), calls=%async_computation | async-start | bytes 32768 | tf_op jit(solution)/shard_map/all_to_all | solution.py:824
  9.0 4.5 %edges.1 = (f32[8,512]{1,0:T(8,128)}, f32[8,512]{1,0:T(8,128)}, f32[8,1024]{1,0:T(8,128)}, f32[8,1024]{1,0:T(8,128)}) custom-call(f32[1024,512]{1,0:T(8,128)} %refs_5_.1, s32[1024,512]{1,0:T(8,128)} %refs_6_.1, f32[1024,512]{1,0:T(8,128)} %refs_7_.1, f32[1024,512]{1,0:T(8,128)} %refs_8_.1, f32[1024,512]{1,0:T(8,128)} %refs_5_.1, s32[1024,512]{1,0:T(8,128)} %refs_6_.1, ...), custom_call_target="tpu_custom_call" | custom-call | tf_op jit(solution)/shard_map/edges/pallas_call | solution.py:195
  13.4 2.0 %mix.1 = (bf16[256,256]{1,0:T(8,128)(2,1)}, bf16[256,512]{1,0:T(8,128)(2,1)}) custom-call(f32[8,512]{1,0:T(8,128)} %get-tuple-element.31.after_ref.top0_ref, f32[1]{0:T(128)} %bitcast.19.blend_ref, bf16[6,256,256]{2,1,0:T(8,128)(2,1)} %bitcast.27), custom_call_target="tpu_custom_call" | custom-call | tf_op jit(solution)/shard_map/mix/pallas_call | solution.py:108
  15.4 0.9 %copy-done.1 = bf16[256,256]{1,0:T(8,128)(2,1)S(1)} copy-done((bf16[256,256]{1,0:T(8,128)(2,1)S(1)}, bf16[256,256]{1,0:T(8,128)(2,1)}, u32[]{:S(2)}) %copy-start.1) | copy-done | bytes 131096
  16.3 1.3 %serve.2 = bf16[1024,256]{1,0:T(8,128)(2,1)} custom-call(s32[32,1,32]{2,1,0:T(1,128)S(1)} %all-to-all-done.refs_0_.refs_1_, bf16[256,256]{1,0:T(8,128)(2,1)S(1)} %copy-done.1), custom_call_target="tpu_custom_call" | custom-call | tf_op jit(solution)/shard_map/serve/pallas_call | solution.py:141
  17.7 5.8 %all-to-all-start.1 = ((bf16[32,32,256]{2,1,0:T(8,128)(2,1)}), bf16[32,32,256]{2,1,0:T(8,128)(2,1)S(1)}, u32[]{:S(2)}, u32[]{:S(2)}) async-start(bf16[32,32,256]{2,1,0:T(8,128)(2,1)} %bitcast.8), calls=%async_computation.1 | async-start | bytes 1048576 | tf_op jit(solution)/shard_map/all_to_all | solution.py:833
  23.5 11.8 %stencil.2 = (f32[1024,512]{1,0:T(8,128)}, f32[4,1024,128]{2,1,0:T(8,128)}, f32[4,1024,128]{2,1,0:T(8,128)}, f32[4,1024,128]{2,1,0:T(8,128)}, f32[8,128]{1,0:T(8,128)}) custom-call(f32[1024,512]{1,0:T(8,128)} %refs_5_.1, s32[1024,512]{1,0:T(8,128)} %refs_6_.1, f32[1024,512]{1,0:T(8,128)} %refs_7_.1, f32[1024,512]{1,0:T(8,128)} %refs_8_.1, ...), custom_call_target="tpu_custom_call" | custom-call | flops 65536000 | bytes 20971520 | tf_op jit(solution)/shard_map/stencil/pallas_call | solution.py:400
  35.3 0.7 copy-done.2
  36.0 1.5 %serve.3 = bf16[1024,512]{1,0:T(8,128)(2,1)} custom-call(f32[8,128]{1,0:T(8,128)S(1)} %copy-done.2, s32[32,1,32]{2,1,0:T(1,128)S(1)} %all-to-all-done.refs_0_.refs_1_, bf16[256,512]{1,0:T(8,128)(2,1)S(1)} %copy-done), custom_call_target="tpu_custom_call" | custom-call | tf_op jit(solution)/shard_map/serve/pallas_call | solution.py:141
  37.5 0.3 all-to-all-done.1
  37.8 5.5 %all-to-all-start.2 = ((bf16[32,32,512]{2,1,0:T(8,128)(2,1)}), bf16[32,32,512]{2,1,0:T(8,128)(2,1)S(1)}, u32[]{:S(2)}, u32[]{:S(2)}) async-start(bf16[32,32,512]{2,1,0:T(8,128)(2,1)} %bitcast.11), calls=%async_computation.2 | async-start | bytes 2097152 | tf_op jit(solution)/shard_map/all_to_all | solution.py:833
  43.4 7.1 %pressure.1 = (f32[4,1040,128]{2,1,0:T(8,128)}, f32[8,512]{1,0:T(8,128)}, f32[8,512]{1,0:T(8,128)}, f32[8,1024]{1,0:T(8,128)}, f32[8,1024]{1,0:T(8,128)}, /*index=5*/s32[1,1024]{1,0:T(1,128)}) custom-call(s32[32,32]{1,0:T(8,128)} %get-tuple-element.29.lab_ref.refs_4_, bf16[1024,256]{1,0:T(8,128)(2,1)} %bitcast.26, bf16[1024,4096]{1,0:T(8,128)(2,1)} %bitcast.20, ...), custom_call_target="tpu_custom_call" | custom-call | flops 1073741824 | bytes 12582912 | tf_op jit(solution)/shard_map/pressure/pallas_call | solution.py:533
  50.5 2.1 %collective-permute-start.2 = (f32[8,1024]{1,0:T(8,128)}, f32[8,1024]{1,0:T(8,128)S(1)}, u32[]{:S(2)}, u32[]{:S(2)}) collective-permute-start(f32[8,1024]{1,0:T(8,128)} %get-tuple-element.42.right_ref), channel_id=1, source_target_pairs={{0,1},{1,2},{2,3},{3,4},{4,5},{5,6},{6,7},{8,9},{9,10},{10,11},{11... | collective-permute-start | bytes 98312 | tf_op jit(solution)/shard_map/ppermute | solution.py:217
  52.6 4.4 %collective-permute-start.3 = (f32[8,1024]{1,0:T(8,128)}, f32[8,1024]{1,0:T(8,128)S(1)}, u32[]{:S(2)}, u32[]{:S(2)}) collective-permute-start(f32[8,1024]{1,0:T(8,128)} %get-tuple-element.43.left_ref), channel_id=1, source_target_pairs={{1,0},{2,1},{3,2},{4,3},{5,4},{6,5},{7,6},{9,8},{10,9},{11,10},{12... | collective-permute-start | bytes 98312 | tf_op jit(solution)/shard_map/ppermute | solution.py:217
  57.0 2.5 %collective-permute-start.1 = (f32[8,512]{1,0:T(8,128)}, f32[8,512]{1,0:T(8,128)S(1)}, u32[]{:S(2)}, u32[]{:S(2)}) collective-permute-start(f32[8,512]{1,0:T(8,128)} %get-tuple-element.41.refs_4_.top_ref), channel_id=1, source_target_pairs={{8,0},{16,8},{24,16},{9,1},{17,9},{25,17},{10,2},{18,10},{26,18},{... | collective-permute-start | bytes 49160 | tf_op jit(solution)/shard_map/ppermute | solution.py:217
  59.4 3.4 %collective-permute-start = (f32[8,512]{1,0:T(8,128)}, f32[8,512]{1,0:T(8,128)S(1)}, u32[]{:S(2)}, u32[]{:S(2)}) collective-permute-start(f32[8,512]{1,0:T(8,128)} %get-tuple-element.40.bottom_ref), channel_id=1, source_target_pairs={{0,8},{8,16},{16,24},{1,9},{9,17},{17,25},{2,10},{10,18},{18,26},{... | collective-permute-start | bytes 49160 | tf_op jit(solution)/shard_map/ppermute | solution.py:217
  62.8 8.0 %stencil.3 = (f32[1024,512]{1,0:T(8,128)}, f32[4,1024,128]{2,1,0:T(8,128)}, f32[4,1024,128]{2,1,0:T(8,128)}, f32[4,1024,128]{2,1,0:T(8,128)}, f32[8,128]{1,0:T(8,128)}) custom-call(f32[1024,512]{1,0:T(8,128)} %refs_5_.1, s32[1024,512]{1,0:T(8,128)} %refs_6_.1, ...), custom_call_target="tpu_custom_call", output_to_operand_aliasing={{0}: (9, {}), {1}: (10, {}), {2}: (11, {}), {3}: (12, {})} | custom-call | flops 39321600 | bytes 12582912 | tf_op jit(solution)/shard_map/stencil/pallas_call | solution.py:400
  70.9 0.5 copy-done.7
  71.4 0.0 copy-done.8
  71.4 0.0 copy-done.5
  71.5 0.0 copy-done.6
  71.5 0.5 copy-done.3
  72.0 12.4 %finish.1 = (f32[16,64,512]{2,1,0:T(8,128)}, f32[16,64,512]{2,1,0:T(8,128)}, f32[1024,512]{1,0:T(8,128)}) custom-call(s32[1,1024]{1,0:T(1,128)} %get-tuple-element.36.lab_ref, bf16[1024,512]{1,0:T(8,128)(2,1)} %bitcast.25, bf16[1024,4096]{1,0:T(8,128)(2,1)} %bitcast.21, f32[4,1040,128]{2,1,0:T(8,128)} %get-tuple-element.39.p_ref, ...), custom_call_target="tpu_custom_call", output_to_operand_aliasing={{2}: (12, {})} | custom-call | flops 2147483648 | bytes 20971520 | tf_op jit(solution)/shard_map/finish/pallas_call | solution.py:755
  (17 shorter events, 0.0 us)
Async XLA Ops:
  2.3 13.1 %all-to-all-start = ((s32[32,1,32]{2,1,0:T(1,128)}), s32[32,1,32]{2,1,0:T(1,128)S(1)}, u32[]{:S(2)}, u32[]{:S(2)}) async-start(s32[32,1,32]{2,1,0:T(1,128)} %bitcast.28), calls=%async_computation | async-start | bytes 32768 | tf_op jit(solution)/shard_map/all_to_all | solution.py:824
  15.4 0.9 %copy-start.1 = (bf16[256,256]{1,0:T(8,128)(2,1)S(1)}, bf16[256,256]{1,0:T(8,128)(2,1)}, u32[]{:S(2)}) copy-start(bf16[256,256]{1,0:T(8,128)(2,1)} %get-tuple-element.32.refs_1_) | copy-start | bytes 393220
  17.7 20.2 %all-to-all-start.1 = ((bf16[32,32,256]{2,1,0:T(8,128)(2,1)}), bf16[32,32,256]{2,1,0:T(8,128)(2,1)S(1)}, u32[]{:S(2)}, u32[]{:S(2)}) async-start(bf16[32,32,256]{2,1,0:T(8,128)(2,1)} %bitcast.8), calls=%async_computation.1 | async-start | bytes 1048576 | tf_op jit(solution)/shard_map/all_to_all | solution.py:833
  23.5 11.8 %copy-start = (bf16[256,512]{1,0:T(8,128)(2,1)S(1)}, bf16[256,512]{1,0:T(8,128)(2,1)}, u32[]{:S(2)}) copy-start(bf16[256,512]{1,0:T(8,128)(2,1)} %get-tuple-element.38.refs_2_) | copy-start | bytes 786436
  35.3 0.7 copy-start.2
  37.8 5.5 %copy-start.4 = (bf16[32,32,256]{2,1,0:T(8,128)(2,1)}, bf16[32,32,256]{2,1,0:T(8,128)(2,1)S(1)}, u32[]{:S(2)}) copy-start(bf16[32,32,256]{2,1,0:T(8,128)(2,1)S(1)} %all-to-all-done.1) | copy-start | bytes 1572868
  37.8 33.0 %all-to-all-start.2 = ((bf16[32,32,512]{2,1,0:T(8,128)(2,1)}), bf16[32,32,512]{2,1,0:T(8,128)(2,1)S(1)}, u32[]{:S(2)}, u32[]{:S(2)}) async-start(bf16[32,32,512]{2,1,0:T(8,128)(2,1)} %bitcast.11), calls=%async_computation.2 | async-start | bytes 2097152 | tf_op jit(solution)/shard_map/all_to_all | solution.py:833
  50.5 20.3 %collective-permute-start.2 = (f32[8,1024]{1,0:T(8,128)}, f32[8,1024]{1,0:T(8,128)S(1)}, u32[]{:S(2)}, u32[]{:S(2)}) collective-permute-start(f32[8,1024]{1,0:T(8,128)} %get-tuple-element.42.right_ref), channel_id=1, source_target_pairs={{0,1},{1,2},{2,3},{3,4},{4,5},{5,6},{6,7},{8,9},{9,10},{10,11},{11... | collective-permute-start | bytes 98312 | tf_op jit(solution)/shard_map/ppermute | solution.py:217
  52.6 18.3 %collective-permute-start.3 = (f32[8,1024]{1,0:T(8,128)}, f32[8,1024]{1,0:T(8,128)S(1)}, u32[]{:S(2)}, u32[]{:S(2)}) collective-permute-start(f32[8,1024]{1,0:T(8,128)} %get-tuple-element.43.left_ref), channel_id=1, source_target_pairs={{1,0},{2,1},{3,2},{4,3},{5,4},{6,5},{7,6},{9,8},{10,9},{11,10},{12... | collective-permute-start | bytes 98312 | tf_op jit(solution)/shard_map/ppermute | solution.py:217
  57.0 13.8 %collective-permute-start.1 = (f32[8,512]{1,0:T(8,128)}, f32[8,512]{1,0:T(8,128)S(1)}, u32[]{:S(2)}, u32[]{:S(2)}) collective-permute-start(f32[8,512]{1,0:T(8,128)} %get-tuple-element.41.refs_4_.top_ref), channel_id=1, source_target_pairs={{8,0},{16,8},{24,16},{9,1},{17,9},{25,17},{10,2},{18,10},{26,18},{... | collective-permute-start | bytes 49160 | tf_op jit(solution)/shard_map/ppermute | solution.py:217
  59.4 11.4 %collective-permute-start = (f32[8,512]{1,0:T(8,128)}, f32[8,512]{1,0:T(8,128)S(1)}, u32[]{:S(2)}, u32[]{:S(2)}) collective-permute-start(f32[8,512]{1,0:T(8,128)} %get-tuple-element.40.bottom_ref), channel_id=1, source_target_pairs={{0,8},{8,16},{16,24},{1,9},{9,17},{17,25},{2,10},{10,18},{18,26},{... | collective-permute-start | bytes 49160 | tf_op jit(solution)/shard_map/ppermute | solution.py:217
  70.8 0.6 copy-start.7
  70.8 0.6 copy-start.8
  70.8 0.6 copy-start.5
  70.9 0.6 copy-start.6
  70.9 1.1 %copy-start.3 = (bf16[32,32,512]{2,1,0:T(8,128)(2,1)}, bf16[32,32,512]{2,1,0:T(8,128)(2,1)S(1)}, u32[]{:S(2)}) copy-start(bf16[32,32,512]{2,1,0:T(8,128)(2,1)S(1)} %all-to-all-done.2) | copy-start | bytes 3145732

commit v13 on v11

--- a/solution.py
+++ b/solution.py
@@ -617,7 +617,7 @@
     lab_ref, landed_ref, w_ref, p_ref, up_ref, dn_ref, lh_ref, rh_ref,
     top_ref, bottom_ref, left_ref, right_ref, old_ref,
     hu_ref, hv_ref, h_ref, ox_ref, oy_ref, new_ref,
-    held, arrived, left, acc, acc2, fx, fy, fx2, fy2,
+    held, arrived, left, acc, mx, my,
     edge, sides_ref, ends_ref, first, last, head, tail, loaded, saved,
 ):
     step = pl.program_id(0)
@@ -644,15 +644,17 @@
         stack_left(left, summed_of(lab_ref[...], landed_ref[...]), 2)
 
     take()
-    acc[...] = jnp.dot(left[...], held[step, :, :PART], preferred_element_type=F32)
-    acc2[...] = jnp.dot(left[...], held[step, :, PART:], preferred_element_type=F32)
     lane = iota((TILE, LANES), 1)
-    for part, (src, mx, my) in enumerate(((acc, fx, fy), (acc2, fx2, fy2))):
-        spread_rows(src, mx, 0)
-        spread_rows(src, my, 1)
-        cells = slice(part * TILE, (part + 1) * TILE)
-        for r in range(BPX):
-            at = slice(r * TILE, (r + 1) * TILE)
+
+    def rows_part(part, carry):
+        width = pl.ds(pl.multiple_of(part * PART, PART), PART)
+        acc[...] = jnp.dot(left[...], held[step, :, width], preferred_element_type=F32)
+        spread_rows(acc, mx, 0)
+        spread_rows(acc, my, 1)
+        cells = pl.ds(pl.multiple_of(part * TILE, TILE), TILE)
+
+        def patch_row(r, carry):
+            at = pl.ds(pl.multiple_of(r * TILE, TILE), TILE)
             mark = pl.multiple_of(r * PATCH + (2 * step + part) * TILE, TILE)
             base = pl.multiple_of(mark + TILE, TILE)
             ends = sides_ref[pl.ds(mark, TILE), :]
@@ -674,12 +676,12 @@
                     hu_ref[g, r, cells, :] - scale * gx + speed * wx,
                     hv_ref[g, r, cells, :] - scale * (nxt - prev) + speed * wy,
                 ]
-                for own, edge, shift in ((0, 0, 1), (GROUPS - 1, LANES - 1, 4)):
+                for own, border, shift in ((0, 0, 1), (GROUPS - 1, LANES - 1, 4)):
                     if g == own:
                         new = [
                             jnp.where(
-                                lane == edge,
-                                a + pltpu.roll(ends, (edge - shift - f) % LANES, 1),
+                                lane == border,
+                                a + pltpu.roll(ends, (border - shift - f) % LANES, 1),
                                 a,
                             )
                             for f, a in enumerate(new)
@@ -687,6 +689,12 @@
                 cut = slice(g * LANES, (g + 1) * LANES)
                 ox_ref[r, cells, cut] = jnp.where(wet, new[0], 0.0)
                 oy_ref[r, cells, cut] = jnp.where(wet, new[1], 0.0)
+            return carry
+
+        lax.fori_loop(0, BPX, patch_row, 0, unroll=4)
+        return carry
+
+    lax.fori_loop(0, 2, rows_part, 0)
 
     @pl.when(step == 1)
     def _():
@@ -742,8 +750,7 @@
             pltpu.SemaphoreType.DMA((steps,)),
             pltpu.VMEM((2 * NPATCH, NW * ABLK), BF16),
             pltpu.VMEM((2 * NPATCH, PART), F32),
-            pltpu.VMEM((2 * NPATCH, PART), F32),
-            field, field, field, field,
+            field, field,
             pltpu.VMEM((TILE, rows), F32),
             pltpu.VMEM((rows, LANES), F32),
             pltpu.VMEM((TILE, cols), F32),

time: 84.6 us -> 87.2 us (1.031)
  Pallas kernels: 49.8 us -> 52.5 us
    pallas_call x1, Pallas kernels: 11.9 us -> 14.6 us  [finish(): pl.pallas_call(finish_kernel, grid=(steps,), out_shape=(shape, shape, jax...]
  transfers between devices with their start and end apart: 7 -> 7, of which waited for: 1 -> 1; matrix products, arithmetic and copies ran while one was open for 0% -> 0% of each run, Pallas kernels for 42% -> 40%
where the time goes in v13:
time: 87.2 us; the launch traced here: 86.4 us
  Pallas kernels  52.5 us (60%)
  starting transfers between devices  29.6 us (34%)
  local copies, waits for them, and re-layouts  2.46 us (3%)
  between operations  1.47 us (2%)
    pallas_call x2, Pallas kernels, stencil(): pl.pallas_call(functools.partial(stencil_kernel, opening, closing), grid=...  19.8 us
    pallas_call x1, Pallas kernels, finish(): pl.pallas_call(finish_kernel, grid=(steps,), out_shape=(shape, shape, jax...  14.6 us
    ppermute x4, starting transfers between devices, send(): return lax.ppermute(value, axis, pairs)  12.3 us
    all_to_all x2, starting transfers between devices, exchange(): got = lax.all_to_all(parts, both, split_axis=0, concat_axis=0, tiled=True)  11.4 us
    pallas_call x1, Pallas kernels, pressure_field(): pl.pallas_call(press_kernel, grid=(steps,), out_shape=tuple((jax.ShapeDty...  7.13 us
    all_to_all x1, starting transfers between devices, body(): lax.all_to_all(want.reshape(devices, 1, capacity), both, split_axis=0, co...  5.99 us
    pallas_call x1, Pallas kernels, edge_cells(): pl.pallas_call(edges_kernel, grid=(1,), out_shape=(line, line, column, co...  4.47 us
    pallas_call x2, Pallas kernels, serve(): pl.pallas_call(serve_kernel, out_shape=jax.ShapeDtypeStruct((slots, tiles...  2.85 us
  transfers between devices with their start and end apart: 7, of which 1 were waited for; matrix products, arithmetic and copies ran while one was open for 0% of the time, Pallas kernels for 40%

profile of v13, /device:TPU:12, one launch (start us, length us, event | category | flops | bytes accessed | tf_op | source)
XLA Modules:
  0.0 86.4 jit_solution(18291008359496336746)
XLA Ops:
  0.6 1.7 %requests.1 = (s32[32,32]{1,0:T(8,128)}, s32[32,32]{1,0:T(8,128)}) custom-call(s32[1,512]{1,0:T(1,128)} %bitcast.29, s32[1,512]{1,0:T(1,128)} %bitcast.30, s32[1,512]{1,0:T(1,128)} %bitcast.31, s32[1,512]{1,0:T(1,128)} %bitcast.32), custom_call_target="tpu_custom_call" | custom-call | tf_op jit(solution)/shard_map/requests/pallas_call | solution.py:82
  2.3 6.0 %all-to-all-start = ((s32[32,1,32]{2,1,0:T(1,128)}), s32[32,1,32]{2,1,0:T(1,128)S(1)}, u32[]{:S(2)}, u32[]{:S(2)}) async-start(s32[32,1,32]{2,1,0:T(1,128)} %bitcast.28), calls=%async_computation | async-start | bytes 32768 | tf_op jit(solution)/shard_map/all_to_all | solution.py:800
  9.0 2.0 %mix.1 = (bf16[256,256]{1,0:T(8,128)(2,1)}, bf16[256,512]{1,0:T(8,128)(2,1)}) custom-call(f32[1]{0:T(128)} %bitcast.19.blend_ref, bf16[6,256,256]{2,1,0:T(8,128)(2,1)} %bitcast.27), custom_call_target="tpu_custom_call" | custom-call | tf_op jit(solution)/shard_map/mix/pallas_call | solution.py:108
  11.0 4.5 %edges.1 = (f32[8,512]{1,0:T(8,128)}, f32[8,512]{1,0:T(8,128)}, f32[8,1024]{1,0:T(8,128)}, f32[8,1024]{1,0:T(8,128)}) custom-call(f32[1024,512]{1,0:T(8,128)} %refs_5_.1, s32[1024,512]{1,0:T(8,128)} %refs_6_.1, f32[1024,512]{1,0:T(8,128)} %refs_7_.1, f32[1024,512]{1,0:T(8,128)} %refs_8_.1, f32[1024,512]{1,0:T(8,128)} %refs_5_.1, s32[1024,512]{1,0:T(8,128)} %refs_6_.1, ...), custom_call_target="tpu_custom_call" | custom-call | tf_op jit(solution)/shard_map/edges/pallas_call | solution.py:194
  15.5 0.7 copy-done.2
  16.2 1.3 %serve.2 = bf16[1024,256]{1,0:T(8,128)(2,1)} custom-call(f32[8,512]{1,0:T(8,128)S(1)} %copy-done.2, s32[32,1,32]{2,1,0:T(1,128)S(1)} %all-to-all-done.asked_ref, bf16[256,256]{1,0:T(8,128)(2,1)S(1)} %copy-done.1), custom_call_target="tpu_custom_call" | custom-call | tf_op jit(solution)/shard_map/serve/pallas_call | solution.py:140
  17.5 5.8 %all-to-all-start.1 = ((bf16[32,32,256]{2,1,0:T(8,128)(2,1)}), bf16[32,32,256]{2,1,0:T(8,128)(2,1)S(1)}, u32[]{:S(2)}, u32[]{:S(2)}) async-start(bf16[32,32,256]{2,1,0:T(8,128)(2,1)} %bitcast.8), calls=%async_computation.1 | async-start | bytes 1048576 | tf_op jit(solution)/shard_map/all_to_all | solution.py:809
  23.4 11.8 %stencil.2 = (f32[1024,512]{1,0:T(8,128)}, f32[4,1024,128]{2,1,0:T(8,128)}, f32[4,1024,128]{2,1,0:T(8,128)}, f32[4,1024,128]{2,1,0:T(8,128)}, f32[8,128]{1,0:T(8,128)}) custom-call(f32[1024,512]{1,0:T(8,128)} %refs_5_.1, s32[1024,512]{1,0:T(8,128)} %refs_6_.1, f32[1024,512]{1,0:T(8,128)} %refs_7_.1, f32[1024,512]{1,0:T(8,128)} %refs_8_.1, ...), custom_call_target="tpu_custom_call" | custom-call | flops 65536000 | bytes 20971520 | tf_op jit(solution)/shard_map/stencil/pallas_call | solution.py:399
  35.2 0.7 copy-done.3
  35.8 1.5 %serve.3 = bf16[1024,512]{1,0:T(8,128)(2,1)} custom-call(f32[8,128]{1,0:T(8,128)S(1)} %copy-done.3, s32[32,1,32]{2,1,0:T(1,128)S(1)} %all-to-all-done.asked_ref, bf16[256,512]{1,0:T(8,128)(2,1)S(1)} %copy-done), custom_call_target="tpu_custom_call" | custom-call | tf_op jit(solution)/shard_map/serve/pallas_call | solution.py:140
  37.4 0.3 all-to-all-done.1
  37.7 5.5 %all-to-all-start.2 = ((bf16[32,32,512]{2,1,0:T(8,128)(2,1)}), bf16[32,32,512]{2,1,0:T(8,128)(2,1)S(1)}, u32[]{:S(2)}, u32[]{:S(2)}) async-start(bf16[32,32,512]{2,1,0:T(8,128)(2,1)} %bitcast.11), calls=%async_computation.2 | async-start | bytes 2097152 | tf_op jit(solution)/shard_map/all_to_all | solution.py:809
  43.2 7.1 %pressure.1 = (f32[4,1040,128]{2,1,0:T(8,128)}, f32[8,512]{1,0:T(8,128)}, f32[8,512]{1,0:T(8,128)}, f32[8,1024]{1,0:T(8,128)}, f32[8,1024]{1,0:T(8,128)}, /*index=5*/s32[1,1024]{1,0:T(1,128)}) custom-call(s32[32,32]{1,0:T(8,128)} %get-tuple-element.29.lab_ref.refs_4_, bf16[1024,256]{1,0:T(8,128)(2,1)} %bitcast.26, bf16[1024,4096]{1,0:T(8,128)(2,1)} %bitcast.20, ...), custom_call_target="tpu_custom_call" | custom-call | flops 1073741824 | bytes 12582912 | tf_op jit(solution)/shard_map/pressure/pallas_call | solution.py:532
  50.4 2.1 %collective-permute-start.2 = (f32[8,1024]{1,0:T(8,128)}, f32[8,1024]{1,0:T(8,128)S(1)}, u32[]{:S(2)}, u32[]{:S(2)}) collective-permute-start(f32[8,1024]{1,0:T(8,128)} %get-tuple-element.42.right_ref), channel_id=1, source_target_pairs={{0,1},{1,2},{2,3},{3,4},{4,5},{5,6},{6,7},{8,9},{9,10},{10,11},{11... | collective-permute-start | bytes 98312 | tf_op jit(solution)/shard_map/ppermute | solution.py:216
  52.4 4.4 %collective-permute-start.3 = (f32[8,1024]{1,0:T(8,128)}, f32[8,1024]{1,0:T(8,128)S(1)}, u32[]{:S(2)}, u32[]{:S(2)}) collective-permute-start(f32[8,1024]{1,0:T(8,128)} %get-tuple-element.43.left_ref), channel_id=1, source_target_pairs={{1,0},{2,1},{3,2},{4,3},{5,4},{6,5},{7,6},{9,8},{10,9},{11,10},{12... | collective-permute-start | bytes 98312 | tf_op jit(solution)/shard_map/ppermute | solution.py:216
  56.8 2.5 %collective-permute-start.1 = (f32[8,512]{1,0:T(8,128)}, f32[8,512]{1,0:T(8,128)S(1)}, u32[]{:S(2)}, u32[]{:S(2)}) collective-permute-start(f32[8,512]{1,0:T(8,128)} %get-tuple-element.41.refs_4_.top_ref), channel_id=1, source_target_pairs={{8,0},{16,8},{24,16},{9,1},{17,9},{25,17},{10,2},{18,10},{26,18},{... | collective-permute-start | bytes 49160 | tf_op jit(solution)/shard_map/ppermute | solution.py:216
  59.3 3.4 %collective-permute-start = (f32[8,512]{1,0:T(8,128)}, f32[8,512]{1,0:T(8,128)S(1)}, u32[]{:S(2)}, u32[]{:S(2)}) collective-permute-start(f32[8,512]{1,0:T(8,128)} %get-tuple-element.40.bottom_ref), channel_id=1, source_target_pairs={{0,8},{8,16},{16,24},{1,9},{9,17},{17,25},{2,10},{10,18},{18,26},{... | collective-permute-start | bytes 49160 | tf_op jit(solution)/shard_map/ppermute | solution.py:216
  62.7 8.0 %stencil.3 = (f32[1024,512]{1,0:T(8,128)}, f32[4,1024,128]{2,1,0:T(8,128)}, f32[4,1024,128]{2,1,0:T(8,128)}, f32[4,1024,128]{2,1,0:T(8,128)}, f32[8,128]{1,0:T(8,128)}) custom-call(f32[1024,512]{1,0:T(8,128)} %refs_5_.1, s32[1024,512]{1,0:T(8,128)} %refs_6_.1, ...), custom_call_target="tpu_custom_call", output_to_operand_aliasing={{0}: (9, {}), {1}: (10, {}), {2}: (11, {}), {3}: (12, {})} | custom-call | flops 39321600 | bytes 12582912 | tf_op jit(solution)/shard_map/stencil/pallas_call | solution.py:399
  70.8 0.5 copy-done.8
  71.3 0.0 copy-done.9
  71.3 0.0 copy-done.6
  71.3 0.0 copy-done.7
  71.4 0.5 copy-done.4
  71.8 14.6 %finish.1 = (f32[16,64,512]{2,1,0:T(8,128)}, f32[16,64,512]{2,1,0:T(8,128)}, f32[1024,512]{1,0:T(8,128)}) custom-call(s32[1,1024]{1,0:T(1,128)} %get-tuple-element.36.lab_ref, bf16[1024,512]{1,0:T(8,128)(2,1)} %bitcast.25, bf16[1024,4096]{1,0:T(8,128)(2,1)} %bitcast.21, f32[4,1040,128]{2,1,0:T(8,128)} %get-tuple-element.39.p_ref, ...), custom_call_target="tpu_custom_call", output_to_operand_aliasing={{2}: (12, {})} | custom-call | flops 2147483648 | bytes 20971520 | tf_op jit(solution)/shard_map/finish/pallas_call | solution.py:736
  (19 shorter events, 0.0 us)
Async XLA Ops:
  2.3 13.1 %all-to-all-start = ((s32[32,1,32]{2,1,0:T(1,128)}), s32[32,1,32]{2,1,0:T(1,128)S(1)}, u32[]{:S(2)}, u32[]{:S(2)}) async-start(s32[32,1,32]{2,1,0:T(1,128)} %bitcast.28), calls=%async_computation | async-start | bytes 32768 | tf_op jit(solution)/shard_map/all_to_all | solution.py:800
  11.0 4.5 %copy-start.1 = (bf16[256,256]{1,0:T(8,128)(2,1)S(1)}, bf16[256,256]{1,0:T(8,128)(2,1)}, u32[]{:S(2)}) copy-start(bf16[256,256]{1,0:T(8,128)(2,1)} %get-tuple-element.32.tiles_ref) | copy-start | bytes 393220
  15.5 0.7 copy-start.2
  17.5 20.2 %all-to-all-start.1 = ((bf16[32,32,256]{2,1,0:T(8,128)(2,1)}), bf16[32,32,256]{2,1,0:T(8,128)(2,1)S(1)}, u32[]{:S(2)}, u32[]{:S(2)}) async-start(bf16[32,32,256]{2,1,0:T(8,128)(2,1)} %bitcast.8), calls=%async_computation.1 | async-start | bytes 1048576 | tf_op jit(solution)/shard_map/all_to_all | solution.py:809
  23.3 11.8 %copy-start = (bf16[256,512]{1,0:T(8,128)(2,1)S(1)}, bf16[256,512]{1,0:T(8,128)(2,1)}, u32[]{:S(2)}) copy-start(bf16[256,512]{1,0:T(8,128)(2,1)} %get-tuple-element.38.tiles_ref) | copy-start | bytes 786436
  35.2 0.7 copy-start.3
  37.7 5.5 %copy-start.5 = (bf16[32,32,256]{2,1,0:T(8,128)(2,1)}, bf16[32,32,256]{2,1,0:T(8,128)(2,1)S(1)}, u32[]{:S(2)}) copy-start(bf16[32,32,256]{2,1,0:T(8,128)(2,1)S(1)} %all-to-all-done.1) | copy-start | bytes 1572868
  37.7 33.1 %all-to-all-start.2 = ((bf16[32,32,512]{2,1,0:T(8,128)(2,1)}), bf16[32,32,512]{2,1,0:T(8,128)(2,1)S(1)}, u32[]{:S(2)}, u32[]{:S(2)}) async-start(bf16[32,32,512]{2,1,0:T(8,128)(2,1)} %bitcast.11), calls=%async_computation.2 | async-start | bytes 2097152 | tf_op jit(solution)/shard_map/all_to_all | solution.py:809
  50.4 20.4 %collective-permute-start.2 = (f32[8,1024]{1,0:T(8,128)}, f32[8,1024]{1,0:T(8,128)S(1)}, u32[]{:S(2)}, u32[]{:S(2)}) collective-permute-start(f32[8,1024]{1,0:T(8,128)} %get-tuple-element.42.right_ref), channel_id=1, source_target_pairs={{0,1},{1,2},{2,3},{3,4},{4,5},{5,6},{6,7},{8,9},{9,10},{10,11},{11... | collective-permute-start | bytes 98312 | tf_op jit(solution)/shard_map/ppermute | solution.py:216
  52.4 18.3 %collective-permute-start.3 = (f32[8,1024]{1,0:T(8,128)}, f32[8,1024]{1,0:T(8,128)S(1)}, u32[]{:S(2)}, u32[]{:S(2)}) collective-permute-start(f32[8,1024]{1,0:T(8,128)} %get-tuple-element.43.left_ref), channel_id=1, source_target_pairs={{1,0},{2,1},{3,2},{4,3},{5,4},{6,5},{7,6},{9,8},{10,9},{11,10},{12... | collective-permute-start | bytes 98312 | tf_op jit(solution)/shard_map/ppermute | solution.py:216
  56.8 13.9 %collective-permute-start.1 = (f32[8,512]{1,0:T(8,128)}, f32[8,512]{1,0:T(8,128)S(1)}, u32[]{:S(2)}, u32[]{:S(2)}) collective-permute-start(f32[8,512]{1,0:T(8,128)} %get-tuple-element.41.refs_4_.top_ref), channel_id=1, source_target_pairs={{8,0},{16,8},{24,16},{9,1},{17,9},{25,17},{10,2},{18,10},{26,18},{... | collective-permute-start | bytes 49160 | tf_op jit(solution)/shard_map/ppermute | solution.py:216
  59.3 11.4 %collective-permute-start = (f32[8,512]{1,0:T(8,128)}, f32[8,512]{1,0:T(8,128)S(1)}, u32[]{:S(2)}, u32[]{:S(2)}) collective-permute-start(f32[8,512]{1,0:T(8,128)} %get-tuple-element.40.bottom_ref), channel_id=1, source_target_pairs={{0,8},{8,16},{16,24},{1,9},{9,17},{17,25},{2,10},{10,18},{18,26},{... | collective-permute-start | bytes 49160 | tf_op jit(solution)/shard_map/ppermute | solution.py:216
  70.7 0.6 copy-start.8
  70.7 0.6 copy-start.9
  70.7 0.6 copy-start.6
  70.8 0.6 copy-start.7
  70.8 1.1 %copy-start.4 = (bf16[32,32,512]{2,1,0:T(8,128)(2,1)}, bf16[32,32,512]{2,1,0:T(8,128)(2,1)S(1)}, u32[]{:S(2)}) copy-start(bf16[32,32,512]{2,1,0:T(8,128)(2,1)S(1)} %all-to-all-done.2) | copy-start | bytes 3145732

commit v14 on v11

--- a/solution.py
+++ b/solution.py
@@ -25,6 +25,7 @@
 VMEM = pl.BlockSpec(memory_space=pltpu.VMEM)
 SMEM = pl.BlockSpec(memory_space=pltpu.SMEM)
 LANES = 128
+TOKEN = jax.ShapeDtypeStruct((1, 1), jnp.int32)
 TILE = 8
 GROUPS = BPY * PATCH // LANES
 HALVES = BPX // TILE
@@ -140,7 +141,7 @@
     return pl.pallas_call(
         serve_kernel,
         out_shape=jax.ShapeDtypeStruct((slots, tiles.shape[1]), BF16),
-        in_specs=[pl.BlockSpec(memory_space=pl.ANY), VMEM, VMEM],
+        in_specs=[SMEM, VMEM, VMEM],
         out_specs=VMEM,
         scratch_shapes=[
             pltpu.VMEM((width, width), jnp.int32),
@@ -153,8 +154,10 @@
 
 def edges_kernel(
     dl, ml, xl, yl, dr, mr, xr, yr, dt, mt, xt, yt, db, mb, xb, yb,
-    top_ref, bottom_ref, left_ref, right_ref,
+    top_ref, bottom_ref, left_ref, right_ref, token_ref,
 ):
+    token_ref[0, 0] = 0
+
     def rows(d, m, x, y, at, out):
         wet = m[...] == 1
         for f, ref in enumerate((d, x, y)):
@@ -194,13 +197,14 @@
     return pl.pallas_call(
         edges_kernel,
         grid=(1,),
-        out_shape=(line, line, column, column),
+        out_shape=(line, line, column, column, TOKEN),
         in_specs=[left] * 4 + [right] * 4 + [top] * 4 + [bottom] * 4,
         out_specs=(
             pl.BlockSpec((TILE, cols), lambda i: (0, 0)),
             pl.BlockSpec((TILE, cols), lambda i: (0, 0)),
             pl.BlockSpec((TILE, rows), lambda i: (0, 0)),
             pl.BlockSpec((TILE, rows), lambda i: (0, 0)),
+            SMEM,
         ),
         compiler_params=params(),
         name="edges",
@@ -304,7 +308,7 @@
 
     @pl.when(step == 0)
     def _():
-        token_ref[...] = jnp.zeros_like(token_ref)
+        token_ref[0, 0] = 0
         if closing:
             for dst in cell:
                 dst[:, dst.shape[1] - BAND:dst.shape[1] - BAND + TILE, :] = jnp.zeros(
@@ -400,14 +404,12 @@
         functools.partial(stencil_kernel, opening, closing),
         grid=(count + 1,),
         out_shape=(
-            jax.ShapeDtypeStruct((rows, cols), F32), plane, plane, plane,
-            jax.ShapeDtypeStruct((TILE, LANES), F32),
+            jax.ShapeDtypeStruct((rows, cols), F32), plane, plane, plane, TOKEN,
         ),
         in_specs=[band] * 4 + [whole] + ([] if opening else [above] * 4 + [whole] * 4),
         out_specs=(
             pl.BlockSpec((BAND, cols), lambda i: (first + jnp.maximum(i - 1, 0), 0)),
-            part, part, part,
-            pl.BlockSpec((TILE, LANES), lambda i: (0, 0)),
+            part, part, part, SMEM,
         ),
         scratch_shapes=[scratch] * (CELL + 3),
         input_output_aliases={} if opening else {9 + n: n for n in range(4)},
@@ -794,7 +796,7 @@
         want.reshape(devices, 1, capacity), both, split_axis=0, concat_axis=0, tiled=True
     )
     press, wind = mix(blend.reshape(1), atm)
-    top, bottom, left, right = edge_cells(depth_field, wet_mask, mom_x, mom_y)
+    top, bottom, left, right, placed = edge_cells(depth_field, wet_mask, mom_x, mom_y)
 
     def exchange(after, tiles):
         rows = serve(after, asked, tiles)
@@ -802,7 +804,7 @@
         got = lax.all_to_all(parts, both, split_axis=0, concat_axis=0, tiled=True)
         return got.reshape(rows.shape)
 
-    press = exchange(top, press)
+    press = exchange(placed, press)
     fields = (depth_field, wet_mask, mom_x, mom_y)
     bands = depth_field.shape[0] // BAND
     ahead = bands * 5 // 8

time: 84.6 us -> 84.3 us (level)
  local copies, waits for them, and re-layouts: 2.46 us -> 1.09 us
  Pallas kernels: 49.8 us -> 51 us
    unnamed x20 -> x16, local copies, waits for them, and re-layouts: 2.46 us -> 1.09 us
    pallas_call x2, Pallas kernels: 2.85 us -> 3.95 us  [serve(): pl.pallas_call(serve_kernel, out_shape=jax.ShapeDtypeStruct((slots, tiles...]
  transfers between devices with their start and end apart: 7 -> 7, of which waited for: 1 -> 1; matrix products, arithmetic and copies ran while one was open for 0% -> 0% of each run, Pallas kernels for 42% -> 43%
where the time goes in v14:
time: 84.3 us; the launch traced here: 83.5 us
  Pallas kernels  51 us (60%)
  starting transfers between devices  29.5 us (35%)
  between operations  1.47 us (2%)
  local copies, waits for them, and re-layouts  1.09 us (1%)
    pallas_call x2, Pallas kernels, stencil(): pl.pallas_call(functools.partial(stencil_kernel, opening, closing), grid=...  19.8 us
    ppermute x4, starting transfers between devices, send(): return lax.ppermute(value, axis, pairs)  12.3 us
    pallas_call x1, Pallas kernels, finish(): pl.pallas_call(finish_kernel, grid=(steps,), out_shape=(shape, shape, jax...  11.9 us
    all_to_all x2, starting transfers between devices, exchange(): got = lax.all_to_all(parts, both, split_axis=0, concat_axis=0, tiled=True)  11.2 us
    pallas_call x1, Pallas kernels, pressure_field(): pl.pallas_call(press_kernel, grid=(steps,), out_shape=tuple((jax.ShapeDty...  7.17 us
    all_to_all x1, starting transfers between devices, body(): lax.all_to_all(want.reshape(devices, 1, capacity), both, split_axis=0, co...  5.99 us
    pallas_call x1, Pallas kernels, edge_cells(): pl.pallas_call(edges_kernel, grid=(1,), out_shape=(line, line, column, co...  4.47 us
    pallas_call x2, Pallas kernels, serve(): pl.pallas_call(serve_kernel, out_shape=jax.ShapeDtypeStruct((slots, tiles...  3.95 us
  transfers between devices with their start and end apart: 7, of which 1 were waited for; matrix products, arithmetic and copies ran while one was open for 0% of the time, Pallas kernels for 43%

profile of v14, /device:TPU:12, one launch (start us, length us, event | category | flops | bytes accessed | tf_op | source)
XLA Modules:
  0.0 83.5 jit_solution(2202559930639933278)
XLA Ops:
  0.6 1.7 %requests.1 = (s32[32,32]{1,0:T(8,128)}, s32[32,32]{1,0:T(8,128)}) custom-call(s32[1,512]{1,0:T(1,128)} %bitcast.29, s32[1,512]{1,0:T(1,128)} %bitcast.30, s32[1,512]{1,0:T(1,128)} %bitcast.31, s32[1,512]{1,0:T(1,128)} %bitcast.32), custom_call_target="tpu_custom_call" | custom-call | tf_op jit(solution)/shard_map/requests/pallas_call | solution.py:83
  2.3 6.0 %all-to-all-start = ((s32[32,1,32]{2,1,0:T(1,128)}), s32[32,1,32]{2,1,0:T(1,128)S(1)}, u32[]{:S(2)}, u32[]{:S(2)}) async-start(s32[32,1,32]{2,1,0:T(1,128)} %bitcast.28), calls=%async_computation | async-start | bytes 32768 | tf_op jit(solution)/shard_map/all_to_all | solution.py:795
  9.0 2.0 %mix.1 = (bf16[256,256]{1,0:T(8,128)(2,1)}, bf16[256,512]{1,0:T(8,128)(2,1)}) custom-call(f32[1]{0:T(128)} %bitcast.19.blend_ref, bf16[6,256,256]{2,1,0:T(8,128)(2,1)} %bitcast.27), custom_call_target="tpu_custom_call" | custom-call | tf_op jit(solution)/shard_map/mix/pallas_call | solution.py:109
  11.0 4.5 %edges.1 = (f32[8,512]{1,0:T(8,128)}, f32[8,512]{1,0:T(8,128)}, f32[8,1024]{1,0:T(8,128)}, f32[8,1024]{1,0:T(8,128)}, s32[1,1]{1,0:T(1,128)}) custom-call(f32[1024,512]{1,0:T(8,128)} %refs_5_.1, s32[1024,512]{1,0:T(8,128)} %refs_6_.1, f32[1024,512]{1,0:T(8,128)} %refs_7_.1, f32[1024,512]{1,0:T(8,128)} %refs_8_.1, f32[1024,512]{1,0:T(8,128)} %refs_5_.1, ...), custom_call_target="tpu_custom_call" | custom-call | tf_op jit(solution)/shard_map/edges/pallas_call | solution.py:197
  15.4 0.0 all-to-all-done.asked_ref
  15.5 1.9 %serve.2 = bf16[1024,256]{1,0:T(8,128)(2,1)} custom-call(s32[1,1]{1,0:T(1,128)} %get-tuple-element.31.after_ref, s32[32,1,32]{2,1,0:T(1,128)S(1)} %all-to-all-done.asked_ref, bf16[256,256]{1,0:T(8,128)(2,1)S(1)} %copy-done.1), custom_call_target="tpu_custom_call" | custom-call | tf_op jit(solution)/shard_map/serve/pallas_call | solution.py:141
  17.3 5.8 %all-to-all-start.1 = ((bf16[32,32,256]{2,1,0:T(8,128)(2,1)}), bf16[32,32,256]{2,1,0:T(8,128)(2,1)S(1)}, u32[]{:S(2)}, u32[]{:S(2)}) async-start(bf16[32,32,256]{2,1,0:T(8,128)(2,1)} %bitcast.8), calls=%async_computation.1 | async-start | bytes 1048576 | tf_op jit(solution)/shard_map/all_to_all | solution.py:804
  23.2 0.0 copy-start
  23.2 11.8 %stencil.2 = (f32[1024,512]{1,0:T(8,128)}, f32[4,1024,128]{2,1,0:T(8,128)}, f32[4,1024,128]{2,1,0:T(8,128)}, f32[4,1024,128]{2,1,0:T(8,128)}, s32[1,1]{1,0:T(1,128)}) custom-call(f32[1024,512]{1,0:T(8,128)} %refs_5_.1, s32[1024,512]{1,0:T(8,128)} %refs_6_.1, f32[1024,512]{1,0:T(8,128)} %refs_7_.1, f32[1024,512]{1,0:T(8,128)} %refs_8_.1, ...), custom_call_target="tpu_custom_call" | custom-call | flops 65536000 | bytes 20971520 | tf_op jit(solution)/shard_map/stencil/pallas_call | solution.py:403
  35.0 2.1 %serve.3 = bf16[1024,512]{1,0:T(8,128)(2,1)} custom-call(s32[1,1]{1,0:T(1,128)} %get-tuple-element.39.after_ref, s32[32,1,32]{2,1,0:T(1,128)S(1)} %all-to-all-done.asked_ref, bf16[256,512]{1,0:T(8,128)(2,1)S(1)} %copy-done), custom_call_target="tpu_custom_call" | custom-call | tf_op jit(solution)/shard_map/serve/pallas_call | solution.py:141
  37.1 0.4 all-to-all-done.1
  37.5 5.4 %all-to-all-start.2 = ((bf16[32,32,512]{2,1,0:T(8,128)(2,1)}), bf16[32,32,512]{2,1,0:T(8,128)(2,1)S(1)}, u32[]{:S(2)}, u32[]{:S(2)}) async-start(bf16[32,32,512]{2,1,0:T(8,128)(2,1)} %bitcast.11), calls=%async_computation.2 | async-start | bytes 2097152 | tf_op jit(solution)/shard_map/all_to_all | solution.py:804
  42.9 7.2 %pressure.1 = (f32[4,1040,128]{2,1,0:T(8,128)}, f32[8,512]{1,0:T(8,128)}, f32[8,512]{1,0:T(8,128)}, f32[8,1024]{1,0:T(8,128)}, f32[8,1024]{1,0:T(8,128)}, /*index=5*/s32[1,1024]{1,0:T(1,128)}) custom-call(s32[32,32]{1,0:T(8,128)} %get-tuple-element.30.lab_ref.refs_4_, bf16[1024,256]{1,0:T(8,128)(2,1)} %bitcast.26, bf16[1024,4096]{1,0:T(8,128)(2,1)} %bitcast.20, ...), custom_call_target="tpu_custom_call" | custom-call | flops 1073741824 | bytes 12582912 | tf_op jit(solution)/shard_map/pressure/pallas_call | solution.py:534
  50.1 2.1 %collective-permute-start.2 = (f32[8,1024]{1,0:T(8,128)}, f32[8,1024]{1,0:T(8,128)S(1)}, u32[]{:S(2)}, u32[]{:S(2)}) collective-permute-start(f32[8,1024]{1,0:T(8,128)} %get-tuple-element.44.right_ref), channel_id=1, source_target_pairs={{0,1},{1,2},{2,3},{3,4},{4,5},{5,6},{6,7},{8,9},{9,10},{10,11},{11... | collective-permute-start | bytes 98312 | tf_op jit(solution)/shard_map/ppermute | solution.py:220
  52.2 4.4 %collective-permute-start.3 = (f32[8,1024]{1,0:T(8,128)}, f32[8,1024]{1,0:T(8,128)S(1)}, u32[]{:S(2)}, u32[]{:S(2)}) collective-permute-start(f32[8,1024]{1,0:T(8,128)} %get-tuple-element.45.left_ref), channel_id=1, source_target_pairs={{1,0},{2,1},{3,2},{4,3},{5,4},{6,5},{7,6},{9,8},{10,9},{11,10},{12... | collective-permute-start | bytes 98312 | tf_op jit(solution)/shard_map/ppermute | solution.py:220
  56.6 2.5 %collective-permute-start.1 = (f32[8,512]{1,0:T(8,128)}, f32[8,512]{1,0:T(8,128)S(1)}, u32[]{:S(2)}, u32[]{:S(2)}) collective-permute-start(f32[8,512]{1,0:T(8,128)} %get-tuple-element.43.refs_4_.top_ref), channel_id=1, source_target_pairs={{8,0},{16,8},{24,16},{9,1},{17,9},{25,17},{10,2},{18,10},{26,18},{... | collective-permute-start | bytes 49160 | tf_op jit(solution)/shard_map/ppermute | solution.py:220
  59.1 3.4 %collective-permute-start = (f32[8,512]{1,0:T(8,128)}, f32[8,512]{1,0:T(8,128)S(1)}, u32[]{:S(2)}, u32[]{:S(2)}) collective-permute-start(f32[8,512]{1,0:T(8,128)} %get-tuple-element.42.bottom_ref), channel_id=1, source_target_pairs={{0,8},{8,16},{16,24},{1,9},{9,17},{17,25},{2,10},{10,18},{18,26},{... | collective-permute-start | bytes 49160 | tf_op jit(solution)/shard_map/ppermute | solution.py:220
  62.5 8.0 %stencil.3 = (f32[1024,512]{1,0:T(8,128)}, f32[4,1024,128]{2,1,0:T(8,128)}, f32[4,1024,128]{2,1,0:T(8,128)}, f32[4,1024,128]{2,1,0:T(8,128)}, s32[1,1]{1,0:T(1,128)}) custom-call(f32[1024,512]{1,0:T(8,128)} %refs_5_.1, s32[1024,512]{1,0:T(8,128)} %refs_6_.1, ...), custom_call_target="tpu_custom_call", output_to_operand_aliasing={{0}: (9, {}), {1}: (10, {}), {2}: (11, {}), {3}: (12, {})} | custom-call | flops 39321600 | bytes 12582912 | tf_op jit(solution)/shard_map/stencil/pallas_call | solution.py:403
  70.5 0.5 copy-done.6
  71.0 0.0 copy-done.7
  71.1 0.0 copy-done.4
  71.1 0.0 copy-done.5
  71.1 0.5 copy-done.2
  71.6 11.9 %finish.1 = (f32[16,64,512]{2,1,0:T(8,128)}, f32[16,64,512]{2,1,0:T(8,128)}, f32[1024,512]{1,0:T(8,128)}) custom-call(s32[1,1024]{1,0:T(1,128)} %get-tuple-element.38.lab_ref, bf16[1024,512]{1,0:T(8,128)(2,1)} %bitcast.25, bf16[1024,4096]{1,0:T(8,128)(2,1)} %bitcast.21, f32[4,1040,128]{2,1,0:T(8,128)} %get-tuple-element.41.p_ref, ...), custom_call_target="tpu_custom_call", output_to_operand_aliasing={{2}: (12, {})} | custom-call | flops 2147483648 | bytes 20971520 | tf_op jit(solution)/shard_map/finish/pallas_call | solution.py:730
  (15 shorter events, 0.0 us)
Async XLA Ops:
  2.3 13.1 %all-to-all-start = ((s32[32,1,32]{2,1,0:T(1,128)}), s32[32,1,32]{2,1,0:T(1,128)S(1)}, u32[]{:S(2)}, u32[]{:S(2)}) async-start(s32[32,1,32]{2,1,0:T(1,128)} %bitcast.28), calls=%async_computation | async-start | bytes 32768 | tf_op jit(solution)/shard_map/all_to_all | solution.py:795
  11.0 4.5 %copy-start.1 = (bf16[256,256]{1,0:T(8,128)(2,1)S(1)}, bf16[256,256]{1,0:T(8,128)(2,1)}, u32[]{:S(2)}) copy-start(bf16[256,256]{1,0:T(8,128)(2,1)} %get-tuple-element.33.tiles_ref) | copy-start | bytes 393220
  17.3 20.2 %all-to-all-start.1 = ((bf16[32,32,256]{2,1,0:T(8,128)(2,1)}), bf16[32,32,256]{2,1,0:T(8,128)(2,1)S(1)}, u32[]{:S(2)}, u32[]{:S(2)}) async-start(bf16[32,32,256]{2,1,0:T(8,128)(2,1)} %bitcast.8), calls=%async_computation.1 | async-start | bytes 1048576 | tf_op jit(solution)/shard_map/all_to_all | solution.py:804
  23.2 11.8 %copy-start = (bf16[256,512]{1,0:T(8,128)(2,1)S(1)}, bf16[256,512]{1,0:T(8,128)(2,1)}, u32[]{:S(2)}) copy-start(bf16[256,512]{1,0:T(8,128)(2,1)} %get-tuple-element.40.tiles_ref) | copy-start | bytes 786436
  37.5 5.4 %copy-start.3 = (bf16[32,32,256]{2,1,0:T(8,128)(2,1)}, bf16[32,32,256]{2,1,0:T(8,128)(2,1)S(1)}, u32[]{:S(2)}) copy-start(bf16[32,32,256]{2,1,0:T(8,128)(2,1)S(1)} %all-to-all-done.1) | copy-start | bytes 1572868
  37.5 33.0 %all-to-all-start.2 = ((bf16[32,32,512]{2,1,0:T(8,128)(2,1)}), bf16[32,32,512]{2,1,0:T(8,128)(2,1)S(1)}, u32[]{:S(2)}, u32[]{:S(2)}) async-start(bf16[32,32,512]{2,1,0:T(8,128)(2,1)} %bitcast.11), calls=%async_computation.2 | async-start | bytes 2097152 | tf_op jit(solution)/shard_map/all_to_all | solution.py:804
  50.1 20.3 %collective-permute-start.2 = (f32[8,1024]{1,0:T(8,128)}, f32[8,1024]{1,0:T(8,128)S(1)}, u32[]{:S(2)}, u32[]{:S(2)}) collective-permute-start(f32[8,1024]{1,0:T(8,128)} %get-tuple-element.44.right_ref), channel_id=1, source_target_pairs={{0,1},{1,2},{2,3},{3,4},{4,5},{5,6},{6,7},{8,9},{9,10},{10,11},{11... | collective-permute-start | bytes 98312 | tf_op jit(solution)/shard_map/ppermute | solution.py:220
  52.2 18.3 %collective-permute-start.3 = (f32[8,1024]{1,0:T(8,128)}, f32[8,1024]{1,0:T(8,128)S(1)}, u32[]{:S(2)}, u32[]{:S(2)}) collective-permute-start(f32[8,1024]{1,0:T(8,128)} %get-tuple-element.45.left_ref), channel_id=1, source_target_pairs={{1,0},{2,1},{3,2},{4,3},{5,4},{6,5},{7,6},{9,8},{10,9},{11,10},{12... | collective-permute-start | bytes 98312 | tf_op jit(solution)/shard_map/ppermute | solution.py:220
  56.6 13.8 %collective-permute-start.1 = (f32[8,512]{1,0:T(8,128)}, f32[8,512]{1,0:T(8,128)S(1)}, u32[]{:S(2)}, u32[]{:S(2)}) collective-permute-start(f32[8,512]{1,0:T(8,128)} %get-tuple-element.43.refs_4_.top_ref), channel_id=1, source_target_pairs={{8,0},{16,8},{24,16},{9,1},{17,9},{25,17},{10,2},{18,10},{26,18},{... | collective-permute-start | bytes 49160 | tf_op jit(solution)/shard_map/ppermute | solution.py:220
  59.1 11.4 %collective-permute-start = (f32[8,512]{1,0:T(8,128)}, f32[8,512]{1,0:T(8,128)S(1)}, u32[]{:S(2)}, u32[]{:S(2)}) collective-permute-start(f32[8,512]{1,0:T(8,128)} %get-tuple-element.42.bottom_ref), channel_id=1, source_target_pairs={{0,8},{8,16},{16,24},{1,9},{9,17},{17,25},{2,10},{10,18},{18,26},{... | collective-permute-start | bytes 49160 | tf_op jit(solution)/shard_map/ppermute | solution.py:220
  70.4 0.6 copy-start.6
  70.5 0.6 copy-start.7
  70.5 0.6 copy-start.4
  70.5 0.6 copy-start.5
  70.5 1.1 %copy-start.2 = (bf16[32,32,512]{2,1,0:T(8,128)(2,1)}, bf16[32,32,512]{2,1,0:T(8,128)(2,1)S(1)}, u32[]{:S(2)}) copy-start(bf16[32,32,512]{2,1,0:T(8,128)(2,1)S(1)} %all-to-all-done.2) | copy-start | bytes 3145732

commit v15 on v14

--- a/solution.py
+++ b/solution.py
@@ -756,7 +756,7 @@
             pltpu.SemaphoreType.DMA((4,)),
             pltpu.SemaphoreType.DMA((4,)),
         ],
-        compiler_params=params(),
+        compiler_params=params(48 << 20),
         cost_estimate=pl.CostEstimate(
             flops=4 * NPATCH * NW * ABLK * PATCH * PATCH, bytes_accessed=20 << 20, transcendentals=0
         ),

time: 84.3 us -> 85.5 us (1.014)
  local copies, waits for them, and re-layouts: 1.09 us -> 3.21 us
  Pallas kernels: 51 us -> 50 us
    unnamed x16 -> x20, local copies, waits for them, and re-layouts: 1.09 us -> 3.21 us
    pallas_call x1, Pallas kernels: 11.9 us -> 10.7 us  [finish(): pl.pallas_call(finish_kernel, grid=(steps,), out_shape=(shape, shape, jax...]
  transfers between devices with their start and end apart: 7 -> 7, of which waited for: 1 -> 1; matrix products, arithmetic and copies ran while one was open for 0% -> 0% of each run, Pallas kernels for 43% -> 42%
where the time goes in v15:
time: 85.5 us; the launch traced here: 84.7 us
  Pallas kernels  50 us (58%)
  starting transfers between devices  29.7 us (35%)
  local copies, waits for them, and re-layouts  3.21 us (4%)
  between operations  1.51 us (2%)
    pallas_call x2, Pallas kernels, stencil(): pl.pallas_call(functools.partial(stencil_kernel, opening, closing), grid=...  19.8 us
    ppermute x4, starting transfers between devices, send(): return lax.ppermute(value, axis, pairs)  12.3 us
    all_to_all x2, starting transfers between devices, exchange(): got = lax.all_to_all(parts, both, split_axis=0, concat_axis=0, tiled=True)  11.4 us
    pallas_call x1, Pallas kernels, finish(): pl.pallas_call(finish_kernel, grid=(steps,), out_shape=(shape, shape, jax...  10.7 us
    pallas_call x1, Pallas kernels, pressure_field(): pl.pallas_call(press_kernel, grid=(steps,), out_shape=tuple((jax.ShapeDty...  7.14 us
    all_to_all x1, starting transfers between devices, body(): lax.all_to_all(want.reshape(devices, 1, capacity), both, split_axis=0, co...  5.99 us
    pallas_call x1, Pallas kernels, edge_cells(): pl.pallas_call(edges_kernel, grid=(1,), out_shape=(line, line, column, co...  4.49 us
    pallas_call x2, Pallas kernels, serve(): pl.pallas_call(serve_kernel, out_shape=jax.ShapeDtypeStruct((slots, tiles...  4.19 us
  transfers between devices with their start and end apart: 7, of which 1 were waited for; matrix products, arithmetic and copies ran while one was open for 0% of the time, Pallas kernels for 42%

profile of v15, /device:TPU:12, one launch (start us, length us, event | category | flops | bytes accessed | tf_op | source)
XLA Modules:
  0.0 84.7 jit_solution(16485477144482607924)
XLA Ops:
  0.6 1.7 %requests.1 = (s32[32,32]{1,0:T(8,128)}, s32[32,32]{1,0:T(8,128)}) custom-call(s32[1,512]{1,0:T(1,128)} %bitcast.29, s32[1,512]{1,0:T(1,128)} %bitcast.30, s32[1,512]{1,0:T(1,128)} %bitcast.31, s32[1,512]{1,0:T(1,128)} %bitcast.32), custom_call_target="tpu_custom_call" | custom-call | tf_op jit(solution)/shard_map/requests/pallas_call | solution.py:83
  2.3 6.0 %all-to-all-start = ((s32[32,1,32]{2,1,0:T(1,128)}), s32[32,1,32]{2,1,0:T(1,128)S(1)}, u32[]{:S(2)}, u32[]{:S(2)}) async-start(s32[32,1,32]{2,1,0:T(1,128)} %bitcast.28), calls=%async_computation | async-start | bytes 32768 | tf_op jit(solution)/shard_map/all_to_all | solution.py:795
  9.0 2.0 %mix.1 = (bf16[256,256]{1,0:T(8,128)(2,1)}, bf16[256,512]{1,0:T(8,128)(2,1)}) custom-call(f32[1]{0:T(128)} %bitcast.19.blend_ref, bf16[6,256,256]{2,1,0:T(8,128)(2,1)} %bitcast.27), custom_call_target="tpu_custom_call" | custom-call | tf_op jit(solution)/shard_map/mix/pallas_call | solution.py:109
  11.0 4.5 %edges.1 = (f32[8,512]{1,0:T(8,128)}, f32[8,512]{1,0:T(8,128)}, f32[8,1024]{1,0:T(8,128)}, f32[8,1024]{1,0:T(8,128)}, s32[1,1]{1,0:T(1,128)}) custom-call(f32[1024,512]{1,0:T(8,128)} %refs_5_.1, s32[1024,512]{1,0:T(8,128)} %refs_6_.1, f32[1024,512]{1,0:T(8,128)} %refs_7_.1, f32[1024,512]{1,0:T(8,128)} %refs_8_.1, f32[1024,512]{1,0:T(8,128)} %refs_5_.1, ...), custom_call_target="tpu_custom_call" | custom-call | tf_op jit(solution)/shard_map/edges/pallas_call | solution.py:197
  15.5 0.0 all-to-all-done.asked_ref
  15.5 2.0 %serve.2 = bf16[1024,256]{1,0:T(8,128)(2,1)} custom-call(s32[1,1]{1,0:T(1,128)} %get-tuple-element.31.after_ref, s32[32,1,32]{2,1,0:T(1,128)S(1)} %all-to-all-done.asked_ref, bf16[256,256]{1,0:T(8,128)(2,1)S(1)} %copy-done.3), custom_call_target="tpu_custom_call" | custom-call | tf_op jit(solution)/shard_map/serve/pallas_call | solution.py:141
  17.4 5.8 %all-to-all-start.1 = ((bf16[32,32,256]{2,1,0:T(8,128)(2,1)}), bf16[32,32,256]{2,1,0:T(8,128)(2,1)S(1)}, u32[]{:S(2)}, u32[]{:S(2)}) async-start(bf16[32,32,256]{2,1,0:T(8,128)(2,1)} %bitcast.8), calls=%async_computation.1 | async-start | bytes 1048576 | tf_op jit(solution)/shard_map/all_to_all | solution.py:804
  23.3 11.8 %stencil.2 = (f32[1024,512]{1,0:T(8,128)}, f32[4,1024,128]{2,1,0:T(8,128)}, f32[4,1024,128]{2,1,0:T(8,128)}, f32[4,1024,128]{2,1,0:T(8,128)}, s32[1,1]{1,0:T(1,128)}) custom-call(f32[1024,512]{1,0:T(8,128)} %refs_5_.1, s32[1024,512]{1,0:T(8,128)} %refs_6_.1, f32[1024,512]{1,0:T(8,128)} %refs_7_.1, f32[1024,512]{1,0:T(8,128)} %refs_8_.1, ...), custom_call_target="tpu_custom_call" | custom-call | flops 65536000 | bytes 20971520 | tf_op jit(solution)/shard_map/stencil/pallas_call | solution.py:403
  35.1 2.2 %serve.3 = bf16[1024,512]{1,0:T(8,128)(2,1)} custom-call(s32[1,1]{1,0:T(1,128)} %get-tuple-element.39.after_ref, s32[32,1,32]{2,1,0:T(1,128)S(1)} %all-to-all-done.asked_ref, bf16[256,512]{1,0:T(8,128)(2,1)S(1)} %copy-done.2), custom_call_target="tpu_custom_call" | custom-call | tf_op jit(solution)/shard_map/serve/pallas_call | solution.py:141
  37.4 0.3 all-to-all-done.1
  37.6 5.6 %all-to-all-start.2 = ((bf16[32,32,512]{2,1,0:T(8,128)(2,1)}), bf16[32,32,512]{2,1,0:T(8,128)(2,1)S(1)}, u32[]{:S(2)}, u32[]{:S(2)}) async-start(bf16[32,32,512]{2,1,0:T(8,128)(2,1)} %bitcast.11), calls=%async_computation.2 | async-start | bytes 2097152 | tf_op jit(solution)/shard_map/all_to_all | solution.py:804
  43.2 7.1 %pressure.1 = (f32[4,1040,128]{2,1,0:T(8,128)}, f32[8,512]{1,0:T(8,128)}, f32[8,512]{1,0:T(8,128)}, f32[8,1024]{1,0:T(8,128)}, f32[8,1024]{1,0:T(8,128)}, /*index=5*/s32[1,1024]{1,0:T(1,128)}) custom-call(s32[32,32]{1,0:T(8,128)} %get-tuple-element.30.lab_ref.refs_4_, bf16[1024,256]{1,0:T(8,128)(2,1)} %bitcast.26, bf16[1024,4096]{1,0:T(8,128)(2,1)} %bitcast.23, ...), custom_call_target="tpu_custom_call" | custom-call | flops 1073741824 | bytes 12582912 | tf_op jit(solution)/shard_map/pressure/pallas_call | solution.py:534
  50.4 2.1 %collective-permute-start.2 = (f32[8,1024]{1,0:T(8,128)}, f32[8,1024]{1,0:T(8,128)S(1)}, u32[]{:S(2)}, u32[]{:S(2)}) collective-permute-start(f32[8,1024]{1,0:T(8,128)} %get-tuple-element.44.right_ref), channel_id=1, source_target_pairs={{0,1},{1,2},{2,3},{3,4},{4,5},{5,6},{6,7},{8,9},{9,10},{10,11},{11... | collective-permute-start | bytes 98312 | tf_op jit(solution)/shard_map/ppermute | solution.py:220
  52.4 4.4 %collective-permute-start.3 = (f32[8,1024]{1,0:T(8,128)}, f32[8,1024]{1,0:T(8,128)S(1)}, u32[]{:S(2)}, u32[]{:S(2)}) collective-permute-start(f32[8,1024]{1,0:T(8,128)} %get-tuple-element.45.left_ref), channel_id=1, source_target_pairs={{1,0},{2,1},{3,2},{4,3},{5,4},{6,5},{7,6},{9,8},{10,9},{11,10},{12... | collective-permute-start | bytes 98312 | tf_op jit(solution)/shard_map/ppermute | solution.py:220
  56.8 2.5 %collective-permute-start.1 = (f32[8,512]{1,0:T(8,128)}, f32[8,512]{1,0:T(8,128)S(1)}, u32[]{:S(2)}, u32[]{:S(2)}) collective-permute-start(f32[8,512]{1,0:T(8,128)} %get-tuple-element.43.refs_4_.top_ref), channel_id=1, source_target_pairs={{8,0},{16,8},{24,16},{9,1},{17,9},{25,17},{10,2},{18,10},{26,18},{... | collective-permute-start | bytes 49160 | tf_op jit(solution)/shard_map/ppermute | solution.py:220
  59.3 3.4 %collective-permute-start = (f32[8,512]{1,0:T(8,128)}, f32[8,512]{1,0:T(8,128)S(1)}, u32[]{:S(2)}, u32[]{:S(2)}) collective-permute-start(f32[8,512]{1,0:T(8,128)} %get-tuple-element.42.bottom_ref), channel_id=1, source_target_pairs={{0,8},{8,16},{16,24},{1,9},{9,17},{17,25},{2,10},{10,18},{18,26},{... | collective-permute-start | bytes 49160 | tf_op jit(solution)/shard_map/ppermute | solution.py:220
  62.7 7.9 %stencil.3 = (f32[1024,512]{1,0:T(8,128)}, f32[4,1024,128]{2,1,0:T(8,128)}, f32[4,1024,128]{2,1,0:T(8,128)}, f32[4,1024,128]{2,1,0:T(8,128)}, s32[1,1]{1,0:T(1,128)}) custom-call(f32[1024,512]{1,0:T(8,128)} %refs_5_.1, s32[1024,512]{1,0:T(8,128)} %refs_6_.1, ...), custom_call_target="tpu_custom_call", output_to_operand_aliasing={{0}: (9, {}), {1}: (10, {}), {2}: (11, {}), {3}: (12, {})} | custom-call | flops 39321600 | bytes 12582912 | tf_op jit(solution)/shard_map/stencil/pallas_call | solution.py:403
  70.7 0.0 collective-permute-done.1.dn_ref
  70.7 0.0 collective-permute-done.2.lh_ref
  70.7 0.0 collective-permute-done.3.rh_ref
  70.8 0.0 copy-start
  70.8 1.6 %copy-done = f32[4,1024,128]{2,1,0:T(8,128)S(1)} copy-done((f32[4,1024,128]{2,1,0:T(8,128)S(1)}, f32[4,1024,128]{2,1,0:T(8,128)}, u32[]{:S(2)}) %copy-start) | copy-done | bytes 2097176
  72.4 1.6 %copy-done.1 = f32[4,1024,128]{2,1,0:T(8,128)S(1)} copy-done((f32[4,1024,128]{2,1,0:T(8,128)S(1)}, f32[4,1024,128]{2,1,0:T(8,128)}, u32[]{:S(2)}) %copy-start.1) | copy-done | bytes 2097176
  74.0 10.7 %finish.1 = (f32[16,64,512]{2,1,0:T(8,128)}, f32[16,64,512]{2,1,0:T(8,128)}, f32[1024,512]{1,0:T(8,128)}) custom-call(s32[1,1024]{1,0:T(1,128)S(1)} %copy-done.8, bf16[1024,512]{1,0:T(8,128)(2,1)S(1)} %bitcast.22, bf16[1024,4096]{1,0:T(8,128)(2,1)} %bitcast.24, f32[4,1040,128]{2,1,0:T(8,128)} %get-tuple-element.41.p_ref, ...), custom_call_target="tpu_custom_call", output_to_operand_aliasing={{2}: (12, {})} | custom-call | flops 2147483648 | bytes 20971520 | tf_op jit(solution)/shard_map/finish/pallas_call | solution.py:730
  (19 shorter events, 0.0 us)
Async XLA Ops:
  2.3 13.1 %all-to-all-start = ((s32[32,1,32]{2,1,0:T(1,128)}), s32[32,1,32]{2,1,0:T(1,128)S(1)}, u32[]{:S(2)}, u32[]{:S(2)}) async-start(s32[32,1,32]{2,1,0:T(1,128)} %bitcast.28), calls=%async_computation | async-start | bytes 32768 | tf_op jit(solution)/shard_map/all_to_all | solution.py:795
  11.0 4.5 %copy-start.3 = (bf16[256,256]{1,0:T(8,128)(2,1)S(1)}, bf16[256,256]{1,0:T(8,128)(2,1)}, u32[]{:S(2)}) copy-start(bf16[256,256]{1,0:T(8,128)(2,1)} %get-tuple-element.33.tiles_ref) | copy-start | bytes 393220
  17.4 20.2 %all-to-all-start.1 = ((bf16[32,32,256]{2,1,0:T(8,128)(2,1)}), bf16[32,32,256]{2,1,0:T(8,128)(2,1)S(1)}, u32[]{:S(2)}, u32[]{:S(2)}) async-start(bf16[32,32,256]{2,1,0:T(8,128)(2,1)} %bitcast.8), calls=%async_computation.1 | async-start | bytes 1048576 | tf_op jit(solution)/shard_map/all_to_all | solution.py:804
  23.3 11.8 %copy-start.2 = (bf16[256,512]{1,0:T(8,128)(2,1)S(1)}, bf16[256,512]{1,0:T(8,128)(2,1)}, u32[]{:S(2)}) copy-start(bf16[256,512]{1,0:T(8,128)(2,1)} %get-tuple-element.40.tiles_ref) | copy-start | bytes 786436
  37.6 5.6 %copy-start.9 = (bf16[32,32,256]{2,1,0:T(8,128)(2,1)}, bf16[32,32,256]{2,1,0:T(8,128)(2,1)S(1)}, u32[]{:S(2)}) copy-start(bf16[32,32,256]{2,1,0:T(8,128)(2,1)S(1)} %all-to-all-done.1) | copy-start | bytes 1572868
  37.6 33.1 %all-to-all-start.2 = ((bf16[32,32,512]{2,1,0:T(8,128)(2,1)}), bf16[32,32,512]{2,1,0:T(8,128)(2,1)S(1)}, u32[]{:S(2)}, u32[]{:S(2)}) async-start(bf16[32,32,512]{2,1,0:T(8,128)(2,1)} %bitcast.11), calls=%async_computation.2 | async-start | bytes 2097152 | tf_op jit(solution)/shard_map/all_to_all | solution.py:804
  50.4 20.4 %collective-permute-start.2 = (f32[8,1024]{1,0:T(8,128)}, f32[8,1024]{1,0:T(8,128)S(1)}, u32[]{:S(2)}, u32[]{:S(2)}) collective-permute-start(f32[8,1024]{1,0:T(8,128)} %get-tuple-element.44.right_ref), channel_id=1, source_target_pairs={{0,1},{1,2},{2,3},{3,4},{4,5},{5,6},{6,7},{8,9},{9,10},{10,11},{11... | collective-permute-start | bytes 98312 | tf_op jit(solution)/shard_map/ppermute | solution.py:220
  52.4 18.3 %collective-permute-start.3 = (f32[8,1024]{1,0:T(8,128)}, f32[8,1024]{1,0:T(8,128)S(1)}, u32[]{:S(2)}, u32[]{:S(2)}) collective-permute-start(f32[8,1024]{1,0:T(8,128)} %get-tuple-element.45.left_ref), channel_id=1, source_target_pairs={{1,0},{2,1},{3,2},{4,3},{5,4},{6,5},{7,6},{9,8},{10,9},{11,10},{12... | collective-permute-start | bytes 98312 | tf_op jit(solution)/shard_map/ppermute | solution.py:220
  56.8 13.9 %collective-permute-start.1 = (f32[8,512]{1,0:T(8,128)}, f32[8,512]{1,0:T(8,128)S(1)}, u32[]{:S(2)}, u32[]{:S(2)}) collective-permute-start(f32[8,512]{1,0:T(8,128)} %get-tuple-element.43.refs_4_.top_ref), channel_id=1, source_target_pairs={{8,0},{16,8},{24,16},{9,1},{17,9},{25,17},{10,2},{18,10},{26,18},{... | collective-permute-start | bytes 49160 | tf_op jit(solution)/shard_map/ppermute | solution.py:220
  59.3 11.4 %collective-permute-start = (f32[8,512]{1,0:T(8,128)}, f32[8,512]{1,0:T(8,128)S(1)}, u32[]{:S(2)}, u32[]{:S(2)}) collective-permute-start(f32[8,512]{1,0:T(8,128)} %get-tuple-element.42.bottom_ref), channel_id=1, source_target_pairs={{0,8},{8,16},{16,24},{1,9},{9,17},{17,25},{2,10},{10,18},{18,26},{... | collective-permute-start | bytes 49160 | tf_op jit(solution)/shard_map/ppermute | solution.py:220
  62.7 8.0 %copy-start.4 = (f32[8,512]{1,0:T(8,128)S(1)}, f32[8,512]{1,0:T(8,128)}, u32[]{:S(2)}) copy-start(f32[8,512]{1,0:T(8,128)} %get-tuple-element.43.refs_4_.top_ref) | copy-start | bytes 49156
  62.7 8.0 %copy-start.5 = (f32[8,1024]{1,0:T(8,128)S(1)}, f32[8,1024]{1,0:T(8,128)}, u32[]{:S(2)}) copy-start(f32[8,1024]{1,0:T(8,128)} %get-tuple-element.45.left_ref) | copy-start | bytes 98308
  62.7 8.0 %copy-start.6 = (f32[8,1024]{1,0:T(8,128)S(1)}, f32[8,1024]{1,0:T(8,128)}, u32[]{:S(2)}) copy-start(f32[8,1024]{1,0:T(8,128)} %get-tuple-element.44.right_ref) | copy-start | bytes 98308
  62.7 8.0 %copy-start.7 = (f32[8,512]{1,0:T(8,128)S(1)}, f32[8,512]{1,0:T(8,128)}, u32[]{:S(2)}) copy-start(f32[8,512]{1,0:T(8,128)} %get-tuple-element.42.bottom_ref) | copy-start | bytes 49156
  62.7 8.0 %copy-start.8 = (s32[1,1024]{1,0:T(1,128)S(1)}, s32[1,1024]{1,0:T(1,128)}, u32[]{:S(2)}) copy-start(s32[1,1024]{1,0:T(1,128)} %get-tuple-element.38.lab_ref) | copy-start | bytes 12292
  70.8 1.6 %copy-start = (f32[4,1024,128]{2,1,0:T(8,128)S(1)}, f32[4,1024,128]{2,1,0:T(8,128)}, u32[]{:S(2)}) copy-start(f32[4,1024,128]{2,1,0:T(8,128)} %get-tuple-element.51) | copy-start | bytes 6291460
  72.4 1.6 %copy-start.1 = (f32[4,1024,128]{2,1,0:T(8,128)S(1)}, f32[4,1024,128]{2,1,0:T(8,128)}, u32[]{:S(2)}) copy-start(f32[4,1024,128]{2,1,0:T(8,128)} %get-tuple-element.52) | copy-start | bytes 6291460
